TPU v7x, 32 devices: a whole 2x2x4 slice. The times are simulated.
32 devices in a mesh: groups: 2 (over y), sec: 4 (over z), tp: 2 (over x), pp: 2 (over core).
Axes of the slice: x: 2, y: 2, z: 4, core: 2. Of those that a mesh axis runs over, the one named last changes fastest.
Arguments:
- query: bfloat16 [512, 4096], P(('groups', 'sec'), ('tp', 'pp')), parts along dimension 0, may hold values from -8 to 8
- keys: bfloat16 [512, 1024], P(('groups', 'sec'), 'tp'), parts along dimension 0, may hold values from -4 to 4
- values: bfloat16 [512, 1024], P(('groups', 'sec'), 'tp'), parts along dimension 0, may hold values from -6 to 6
- residual: bfloat16 [512, 2048], P(('groups', 'sec')), parts along dimension 0, may hold values from -6 to 6
- out_weight: bfloat16 [4096, 2048], P(('tp', 'pp')), may hold values from -0.09375 to 0.09375
- norm_gain: float32 [2048], replicated, may hold values from 0.1 to 1.9
- expert_ids: int32 [512, 2], P(('groups', 'sec')), parts along dimension 0, may hold values from 0 to 7, all different within a row; in each aligned block of 64 rows (0 to 63, 64 to 127, ...) at most 32 rows name the same one
- gate_codes: int32 [512, 2], P(('groups', 'sec')), parts along dimension 0, may hold values from 1 to 255
- doc_lengths: int32 [16], P('groups'), parts along dimension 0, may hold values from 1 to 128, 256 in all
- w_gate: bfloat16 [4, 2048, 16384], P(('tp', 'pp'), None, 'sec'), may hold values from -0.125 to 0.125
- w_up: bfloat16 [4, 2048, 16384], P(('tp', 'pp'), None, 'sec'), may hold values from -0.125 to 0.125
- w_down: bfloat16 [4, 16384, 2048], P(('tp', 'pp'), 'sec'), may hold values from -0.0625 to 0.0625
Outputs:
- scored: bfloat16 [512, 2048], P(('groups', 'sec', 'tp', 'pp')), parts along dimension 0
There are 2 independent parts, one for each index of `groups`. A program takes and returns all parts, laid end to end along the dimension named above; an argument that names none is the same for every part. Nothing has to cross between parts.
Inputs may be any that keep to these rules, and one draw needn't show every extreme that they name: `expert_ids`: each row names two different experts; in each aligned block of 64 rows no expert is named by more than 32 rows, and some block reaches 32. `doc_lengths`: the lengths sum to 256; the longest is exactly 128.
All inputs are finite; a program needn't handle non-finite values.
Results may differ from a plain program's by a relative error of at most 0.015.
Values may be sent and summed in bfloat16 or wider, within the bound.
No kernel may reach another device: no remote copies, remote signals or barrier semaphores. Data moves between devices by JAX's collectives and lax.ppermute only.
A program may use at most 128 MiB of HBM per device.

v0:
```python
import jax
import jax.numpy as jnp
from jax import lax
from jax.sharding import PartitionSpec as P

QUERY_HEAD_COUNT = 32
KEY_VALUE_HEADS = 8
HEAD_DIMENSION = 128
E = 8
MOSTB = 32


neg_fill = -1e30
norm_eps = 1e-05


def doc_index(positions, doc_ends):
    return jnp.sum((positions[:, None] >= doc_ends[None, :]).astype(jnp.int32), axis=1)


def rms_scale(stream, norm_gain):
    meansq = jnp.mean(stream * stream, axis=1, keepdims=True)
    return (stream * lax.rsqrt(meansq + norm_eps) * norm_gain).astype(jnp.bfloat16)


def per_device(
    query,
    keys,
    values,
    residual,
    out_weight,
    norm_gain,
    expert_ids,
    gate_codes,
    doc_lengths,
    w_gate,
    w_up,
    w_down,
):
    block_rows = query.shape[0]
    head_size = HEAD_DIMENSION
    q_heads = query.shape[1] // head_size
    kv_heads = keys.shape[1] // head_size
    group_width = QUERY_HEAD_COUNT // KEY_VALUE_HEADS
    width = residual.shape[1]
    sec_count = lax.axis_size("sec")
    rank_count = lax.axis_size("tp") * lax.axis_size("pp")
    pp_index = lax.axis_index("pp")
    rank_index = lax.axis_index("tp") * lax.axis_size("pp") + pp_index
    own_rows = block_rows // rank_count
    own_start = rank_index * own_rows
    doc_ends = jnp.cumsum(doc_lengths)
    query_pos = lax.axis_index("sec") * block_rows + jnp.arange(block_rows, dtype=jnp.int32)
    query_doc = doc_index(query_pos, doc_ends)
    kv_pick = (pp_index * q_heads + jnp.arange(q_heads, dtype=jnp.int32)) // group_width
    query_heads = query.reshape(block_rows, q_heads, head_size)
    scale = head_size ** (-0.5)
    run_max = jnp.full((q_heads, block_rows), neg_fill, jnp.float32)
    key_piece = lax.all_gather(keys, "sec", axis=0, tiled=True)
    value_piece = lax.all_gather(values, "sec", axis=0, tiled=True)
    count = key_piece.shape[0]
    key_heads = jnp.take(key_piece.reshape(count, kv_heads, head_size), kv_pick, axis=1)
    value_heads = jnp.take(value_piece.reshape(count, kv_heads, head_size), kv_pick, axis=1)
    scores = (
        jnp.einsum("qhd,khd->hqk", query_heads, key_heads, preferred_element_type=jnp.float32)
        * scale
    )
    key_pos = jnp.arange(count, dtype=jnp.int32)
    allowed = (key_pos[None, :] <= query_pos[:, None]) & (
        doc_index(key_pos, doc_ends)[None, :] == query_doc[:, None]
    )
    scores = jnp.where(allowed[None], scores, neg_fill)
    new_max = jnp.maximum(run_max, jnp.max(scores, axis=2))
    probs = jnp.where(allowed[None], jnp.exp(scores - new_max[:, :, None]), 0.0)
    run_total = jnp.sum(probs, axis=2)
    run_acc = jnp.einsum(
        "hqk,khd->hqd", probs.astype(jnp.bfloat16), value_heads, preferred_element_type=jnp.float32
    )
    run_max, run_total, run_acc = (new_max, run_total, run_acc)
    attended = (
        (run_acc / run_total[:, :, None])
        .transpose(1, 0, 2)
        .reshape(block_rows, q_heads * head_size)
        .astype(jnp.bfloat16)
    )
    rows_in = attended
    mixed_own = lax.psum_scatter(
        jnp.dot(rows_in, out_weight, preferred_element_type=jnp.float32).astype(jnp.bfloat16),
        ("tp", "pp"),
        scatter_dimension=0,
        tiled=True,
    ).astype(jnp.float32)
    stream_own = (
        lax.dynamic_slice_in_dim(residual, own_start, own_rows, 0).astype(jnp.float32) + mixed_own
    )
    normed = lax.all_gather(rms_scale(stream_own, norm_gain), ("tp", "pp"), axis=0, tiled=True)
    capacity = MOSTB
    experts_here = max(1, E // sec_count)
    halves = max(1, sec_count // E)
    route_hits = (expert_ids[:, :, None] == jnp.arange(E, dtype=jnp.int32)[None, None, :]).astype(
        jnp.int32
    )
    member = jnp.sum(route_hits, axis=1)
    slots = jnp.cumsum(member, axis=0) - 1
    slot_pick = jnp.sum(route_hits * slots[:, None, :], axis=2)
    codes = gate_codes.astype(jnp.float32)
    shares = codes / jnp.sum(codes, axis=1, keepdims=True)
    slot_range = jnp.arange(capacity, dtype=jnp.int32)
    select = (
        (slots.T[:, None, :] == slot_range[None, :, None]) & (member.T[:, None, :] == 1)
    ).astype(jnp.bfloat16)
    gate_local = w_gate[0].reshape(width, experts_here, -1)
    up_local = w_up[0].reshape(width, experts_here, -1)
    down_local = w_down[0].reshape(experts_here, -1, width)
    packed = jnp.einsum("ecr,rd->ecd", select, normed, preferred_element_type=jnp.float32).astype(
        jnp.bfloat16
    )
    packed = jnp.repeat(packed, halves, axis=0)
    rows_in = lax.all_to_all(
        packed.reshape(sec_count, experts_here, capacity, normed.shape[1]),
        "sec",
        split_axis=0,
        concat_axis=0,
        tiled=True,
    )
    gate = jnp.einsum("sxmd,dxf->sxmf", rows_in, gate_local, preferred_element_type=jnp.float32)
    up = jnp.einsum("sxmd,dxf->sxmf", rows_in, up_local, preferred_element_type=jnp.float32)
    hidden = (jax.nn.silu(gate) * up).astype(jnp.bfloat16)
    partial_out = jnp.einsum(
        "sxmf,xfd->sxmd", hidden, down_local, preferred_element_type=jnp.float32
    )
    returned = lax.all_to_all(
        partial_out.astype(jnp.bfloat16), "sec", split_axis=0, concat_axis=0, tiled=True
    ).astype(partial_out.dtype)
    flat_parts = returned.reshape(sec_count * experts_here * capacity, width)
    half_range = jnp.arange(halves, dtype=jnp.int32)
    top_count = expert_ids.shape[1]
    index = ((expert_ids * halves)[:, :, None] + half_range[None, None, :]) * capacity + slot_pick[
        :, :, None
    ]
    picked = jnp.take(flat_parts, index.reshape(-1), axis=0).reshape(
        own_rows * lax.axis_size(("tp", "pp")), top_count, halves, width
    )
    mixture_own = lax.psum_scatter(
        jnp.sum(picked * shares[:, :, None, None], axis=(1, 2)).astype(jnp.bfloat16),
        ("tp", "pp"),
        scatter_dimension=0,
        tiled=True,
    ).astype(jnp.float32)
    return (stream_own + mixture_own).astype(jnp.bfloat16)


def solution(mesh):
    in_specs = (
        P(("groups", "sec"), ("tp", "pp")),
        P(("groups", "sec"), "tp"),
        P(("groups", "sec"), "tp"),
        P(("groups", "sec"), None),
        P(("tp", "pp"), None),
        P(),
        P(("groups", "sec"), None),
        P(("groups", "sec"), None),
        P("groups"),
        P(("tp", "pp"), None, "sec"),
        P(("tp", "pp"), None, "sec"),
        P(("tp", "pp"), "sec", None),
    )
    out_specs = P(("groups", "sec", "tp", "pp"), None)
    return jax.shard_map(
        per_device, mesh=mesh, in_specs=in_specs, out_specs=out_specs, check_vma=False
    )
```

profile of v0, /device:TPU:0, one launch (start us, length us, event | category | flops | bytes accessed | tf_op | source)
XLA Modules:
  0.0 239.1 jit_solution(17453255772642442494)
XLA Ops:
  6.6 0.9 reduce-window.8
  7.6 15.8 %all_gather.9 = bf16[256,512]{1,0:T(8,128)(2,1)S(1)} all-gather(bf16[64,512]{1,0:T(8,128)(2,1)} %param.15), channel_id=1, replica_groups=mesh['groups'=2,'sec'=4,'tp'=2,'pp'=2] {'sec'}, dimensions={0}, use_global_device_ids=true | all-gather | bytes 327680 | tf_op jit(solution)/shard_map/all_gather | solution.py:59
  23.6 0.2 copy.67
  23.9 0.6 gather_fusion.1
  24.5 0.5 fusion.53
  25.0 14.8 %all_gather.10 = bf16[256,512]{1,0:T(8,128)(2,1)S(1)} all-gather(bf16[64,512]{1,0:T(8,128)(2,1)} %param.16), channel_id=1, replica_groups=mesh['groups'=2,'sec'=4,'tp'=2,'pp'=2] {'sec'}, dimensions={0}, use_global_device_ids=true | all-gather | bytes 327680 | tf_op jit(solution)/shard_map/all_gather | solution.py:60
  39.9 0.2 copy.70
  40.1 0.6 gather_fusion.2
  40.8 0.3 fusion.30
  41.1 0.3 fusion.21
  41.4 3.7 %convolution_convert_fusion.2 = bf16[64,2048]{1,0:T(8,128)(2,1)} fusion(bf16[1024,2048]{1,0:T(8,128)(2,1)} %param.18, bf16[8,8,8,128]{3,2,1,0:T(8,128)(2,1)S(1)} %fusion.21), kind=kOutput, calls=%fused_computation.14 | convolution fusion | flops 268566528 | bytes 4587520 | tf_op jit(solution)/shard_map/dot_general | solution.py:88
  45.4 20.8 %reduce-scatter.3.cloned.1.call-done = bf16[16,2048]{1,0:T(8,128)(2,1)} async-done(((bf16[64,2048]{1,0:T(8,128)(2,1)}), bf16[16,2048]{1,0:T(8,128)(2,1)}) %reduce-scatter.3.cloned.1.call-update) | async-done | bytes 65552 | tf_op jit(solution)/shard_map/reduce_scatter | solution.py:87
  66.2 1.0 multiply_reduce_fusion.1
  67.2 0.9 multiply_convert_fusion
  68.1 5.8 %all_gather.11 = bf16[64,2048]{1,0:T(8,128)(2,1)S(1)} all-gather(bf16[16,2048]{1,0:T(8,128)(2,1)S(1)} %multiply_convert_fusion), channel_id=1, replica_groups=mesh['groups'=2,'sec'=4,'tp'=2,'pp'=2] {'tp','pp'}, dimensions={0}, use_global_device_ids=true | all-gather | bytes 327680 | tf_op jit(solution)/shard_map/all_gather | solution.py:96
  73.9 1.4 convolution_convert_fusion.1
  75.3 4.6 %all-to-all-start = ((bf16[4,2,32,2048]{3,2,1,0:T(8,128)(2,1)}), bf16[4,2,32,2048]{3,2,1,0:T(8,128)(2,1)S(1)}, u32[]{:S(2)}, u32[]{:S(2)}) async-start(bf16[4,2,32,2048]{3,2,1,0:T(8,128)(2,1)} %bitcast.12), calls=%async_computation.1 | async-start | bytes 2097152 | tf_op jit(solution)/shard_map/all_to_all | solution.py:119
  79.9 27.7 %reshape_squeeze.9 = bf16[2048,2,2048]{2,1,0:T(2,128)(2,1)} reshape(bf16[1,2048,4096]{2,1,0:T(8,128)(2,1)} %param.23) | data formatting | bytes 33554432 | tf_op jit(solution)/shard_map/reshape;squeeze | solution.py:112
  107.6 27.7 %reshape_squeeze.10 = bf16[2048,2,2048]{2,1,0:T(2,128)(2,1)} reshape(bf16[1,2048,4096]{2,1,0:T(8,128)(2,1)} %param.24) | data formatting | bytes 33554432 | tf_op jit(solution)/shard_map/reshape;squeeze | solution.py:113
  135.3 15.5 %fusion.4 = f32[4,2,32,2048]{3,2,0,1:T(8,128)S(1)} fusion(bf16[2048,2,2048,1]{2,1,0,3:T(2,128)(2,1)} %bitcast.74, bf16[4,2,32,2048]{3,2,1,0:T(8,128)(2,1)S(1)} %all-to-all-done), kind=kOutput, calls=%fused_computation.7 | convolution fusion | flops 2147483648 | bytes 19922944 | tf_op jit(solution)/shard_map/sxmd,dxf->sxmf/dot_general | solution.py:126
  150.9 16.1 %fusion.14 = bf16[4,2,32,2048]{3,2,0,1:T(8,128)(2,1)S(1)} fusion(bf16[2048,2,2048,1]{2,1,0,3:T(2,128)(2,1)} %bitcast.73, f32[4,2,32,2048]{3,2,0,1:T(8,128)S(1)} %fusion.4, bf16[4,2,32,2048]{3,2,1,0:T(8,128)(2,1)S(1)} %all-to-all-done), kind=kOutput, calls=%fused_computation.13 | convolution fusion | flops 2150629376 | bytes 20971520 | tf_op jit(solution)/shard_map/sxmd,dxf->sxmf/dot_general | solution.py:127
  167.0 8.4 %fusion.10 = bf16[4,2,32,2048]{3,2,0,1:T(8,128)(2,1)S(1)} fusion(bf16[4,2,32,2048]{3,2,0,1:T(8,128)(2,1)S(1)} %fusion.14, bf16[2,2048,2048,1]{2,1,3,0:T(8,128)(2,1)} %bitcast.72), kind=kOutput, calls=%fused_computation.11 | convolution fusion | flops 2148007936 | bytes 18874368 | tf_op jit(solution)/shard_map/sxmf,xfd->sxmd/dot_general | solution.py:129
  175.4 1.1 copy.80
  176.5 5.1 %all-to-all-start.1 = ((bf16[4,2,32,2048]{3,2,1,0:T(8,128)(2,1)}), bf16[4,2,32,2048]{3,2,1,0:T(8,128)(2,1)S(1)}, u32[]{:S(2)}, u32[]{:S(2)}) async-start(bf16[4,2,32,2048]{3,2,1,0:T(8,128)(2,1)} %copy.80), calls=%async_computation.2 | async-start | bytes 2097152 | tf_op jit(solution)/shard_map/all_to_all | solution.py:132
  181.8 0.1 reshape.190
  182.2 25.1 %all-to-all-done.1 = bf16[4,2,32,2048]{3,2,1,0:T(8,128)(2,1)S(1)} async-done(((bf16[4,2,32,2048]{3,2,1,0:T(8,128)(2,1)}), bf16[4,2,32,2048]{3,2,1,0:T(8,128)(2,1)S(1)}, u32[]{:S(2)}, u32[]{:S(2)}) %all-to-all-start.1) | async-done | bytes 1048608 | tf_op jit(solution)/shard_map/all_to_all | solution.py:132
  207.3 0.3 bitcast_convert_fusion
  207.6 1.0 gather_fusion
  208.6 0.6 gather.10
  209.2 3.2 %multiply_reduce_fusion = bf16[64,2048]{1,0:T(8,128)(2,1)} fusion(f32[64,2,1,2048]{3,1,0,2:T(2,128)S(1)} %gather.10, pred[64,2]{1,0:T(8,128)(4,1)S(1)} %copy.74, f32[64,2]{1,0:T(8,128)S(1)} %copy.82), kind=kLoop, calls=%fused_computation.23 | loop fusion | flops 655360 | bytes 1311360 | tf_op jit(solution)/shard_map/reduce_sum | solution.py:145
  212.4 18.3 %reduce-scatter.5.cloned.1.call-done = bf16[16,2048]{1,0:T(8,128)(2,1)} async-done(((bf16[64,2048]{1,0:T(8,128)(2,1)}), bf16[16,2048]{1,0:T(8,128)(2,1)}) %reduce-scatter.5.cloned.1.call-update) | async-done | bytes 65552 | tf_op jit(solution)/shard_map/reduce_scatter | solution.py:144
  230.7 1.5 add_convert_fusion
  (46 shorter events, 1.4 us)
Async XLA Ops:
  6.5 18.0 %copy-start = (bf16[64,1024]{1,0:T(8,128)(2,1)S(1)}, bf16[64,1024]{1,0:T(8,128)(2,1)}, u32[]{:S(2)}) copy-start(bf16[64,1024]{1,0:T(8,128)(2,1)} %param.14) | copy-start | bytes 393220
  6.5 59.7 %reduce-scatter.3.cloned.1.call-start = ((), (), s32[]{:S(2)}) async-start(), calls=%async_computation.4 | async-start | bytes 327680 | tf_op jit(solution)/shard_map/reduce_scatter | solution.py:87
  40.1 5.0 %copy-start.4 = (s32[64,2]{0,1:T(2,128)S(1)}, s32[64,2]{0,1:T(2,128)}, u32[]{:S(2)}) copy-start(s32[64,2]{0,1:T(2,128)} %param.20) | copy-start | bytes 1540
  40.8 25.4 %copy-start.3 = (bf16[64,2048]{1,0:T(8,128)(2,1)S(1)}, bf16[64,2048]{1,0:T(8,128)(2,1)}, u32[]{:S(2)}) copy-start(bf16[64,2048]{1,0:T(8,128)(2,1)} %param.17) | copy-start | bytes 786436
  40.8 26.4 %copy-start.5 = (f32[2048]{0:T(1024)S(1)}, f32[2048]{0:T(1024)}, u32[]{:S(2)}) copy-start(f32[2048]{0:T(1024)} %param.19) | copy-start | bytes 24580
  75.3 60.0 %all-to-all-start = ((bf16[4,2,32,2048]{3,2,1,0:T(8,128)(2,1)}), bf16[4,2,32,2048]{3,2,1,0:T(8,128)(2,1)S(1)}, u32[]{:S(2)}, u32[]{:S(2)}) async-start(bf16[4,2,32,2048]{3,2,1,0:T(8,128)(2,1)} %bitcast.12), calls=%async_computation.1 | async-start | bytes 2097152 | tf_op jit(solution)/shard_map/all_to_all | solution.py:119
  175.4 6.7 %copy-start.6 = (s32[64,2]{0,1:T(2,128)S(1)}, s32[64,2]{0,1:T(2,128)}, u32[]{:S(2)}) copy-start(s32[64,2]{0,1:T(2,128)} %param.21) | copy-start | bytes 1540
  176.5 30.8 %all-to-all-start.1 = ((bf16[4,2,32,2048]{3,2,1,0:T(8,128)(2,1)}), bf16[4,2,32,2048]{3,2,1,0:T(8,128)(2,1)S(1)}, u32[]{:S(2)}, u32[]{:S(2)}) async-start(bf16[4,2,32,2048]{3,2,1,0:T(8,128)(2,1)} %copy.80), calls=%async_computation.2 | async-start | bytes 2097152 | tf_op jit(solution)/shard_map/all_to_all | solution.py:132
  181.6 49.1 %reduce-scatter.5.cloned.1.call-start = ((), (), s32[]{:S(2)}) async-start(), calls=%async_computation.5 | async-start | bytes 327680 | tf_op jit(solution)/shard_map/reduce_scatter | solution.py:144
  207.6 23.1 %copy-start.2 = (bf16[16,2048]{1,0:T(8,128)(2,1)S(1)}, bf16[16,2048]{1,0:T(8,128)(2,1)}, u32[]{:S(2)}) copy-start(bf16[16,2048]{1,0:T(8,128)(2,1)} %reduce-scatter.3.cloned.1.call-done) | copy-start | bytes 196612
  207.6 24.7 %copy-start.1 = (bf16[64,1024]{1,0:T(8,128)(2,1)S(1)}, bf16[64,1024]{1,0:T(8,128)(2,1)}, u32[]{:S(2)}) copy-start(bf16[64,1024]{1,0:T(8,128)(2,1)} %param.14) | copy-start | bytes 393220
Sparse Core Ops, SparseCore 0:
  45.2 20.8 reduce-scatter.2
  212.5 18.1 reduce-scatter.4
where the time goes:
time: 241 us; the launch traced here: 239 us
  waiting for transfers between devices  64.2 us (27%)
  local copies, waits for them, and re-layouts  60.7 us (25%)
  matrix products  45.9 us (19%)
  blocking collectives  36.4 us (15%)
  between operations  13.7 us (6%)
  starting transfers between devices  9.69 us (4%)
  other arithmetic  8.52 us (4%)
    another operation x1, local copies, waits for them, and re-layouts, per_device(): gate_local = w_gate[0].reshape(width, experts_here, -1)  27.7 us
    another operation x1, local copies, waits for them, and re-layouts, per_device(): up_local = w_up[0].reshape(width, experts_here, -1)  27.7 us
    all_to_all x1, waiting for transfers between devices, per_device(): lax.all_to_all(partial_out.astype(jnp.bfloat16), 'sec', split_axis=0, con...  25.1 us
    reduce_scatter x1, waiting for transfers between devices, per_device(): lax.psum_scatter(jnp.dot(rows_in, out_weight, preferred_element_type=jnp....  20.8 us
    reduce_scatter x1, waiting for transfers between devices, per_device(): lax.psum_scatter(jnp.sum(picked * shares[:, :, None, None], axis=(1, 2))....  18.3 us
    dot_general x1, matrix products, per_device(): jnp.einsum('sxmd,dxf->sxmf', rows_in, up_local, preferred_element_type=jn...  16.1 us
    all_gather x1, blocking collectives, per_device(): key_piece = lax.all_gather(keys, 'sec', axis=0, tiled=True)  15.8 us
    dot_general x1, matrix products, per_device(): jnp.einsum('sxmd,dxf->sxmf', rows_in, gate_local, preferred_element_type=...  15.5 us
  transfers between devices with their start and end apart: 4, of which 3 were waited for; matrix products, arithmetic and copies ran while one was open for 24% of the time, Pallas kernels for 0%

commit v1 on v0

v1 whole, which is shorter than its diff:
```python
import functools

import jax
import jax.numpy as jnp
from jax import lax
from jax.experimental import pallas as pl
from jax.experimental.pallas import tpu as pltpu
from jax.sharding import PartitionSpec as P

QUERY_HEAD_COUNT = 32
KEY_VALUE_HEADS = 8
HEAD_DIMENSION = 128
E = 8
MOSTB = 32
LANES = 128

neg_fill = -1e30
norm_eps = 1e-05

VMEM = pl.BlockSpec(memory_space=pltpu.VMEM)
SMEM = pl.BlockSpec(memory_space=pltpu.SMEM)
ANY = pl.BlockSpec(memory_space=pl.ANY)


def dot(a, b):
    return jnp.dot(a, b, preferred_element_type=jnp.float32)


def xor_swap(x, axis, k):
    n = lax.axis_size(axis)
    return lax.ppermute(x, axis, [(i, i ^ k) for i in range(n)])


def attention_kernel(back, kv_heads, group, lengths_ref, sec_ref, q_ref, *refs):
    kv_refs = refs[: back + 1]
    weight_hbm, out_ref, weight_ref, attended_ref, sem = refs[back + 1 :]
    copy = pltpu.make_async_copy(weight_hbm, weight_ref, sem)
    copy.start()
    block = q_ref.shape[0]
    head = HEAD_DIMENSION
    span = (back + 1) * block
    sec = sec_ref[0]
    rows = sec * block + lax.broadcasted_iota(jnp.int32, (block, span), 0)
    cols = (sec - back) * block + lax.broadcasted_iota(jnp.int32, (block, span), 1)
    first = jnp.zeros((block, span), jnp.int32)
    end = jnp.int32(0)
    for d in range(lengths_ref.shape[0]):
        end = end + lengths_ref[d]
        first = jnp.where(rows >= end, end, first)
    allowed = (cols <= rows) & (cols >= first)
    allowed = jnp.concatenate([allowed.astype(jnp.float32)] * group, axis=0) > 0.5
    for g in range(kv_heads):
        q = jnp.concatenate(
            [q_ref[:, (g * group + t) * head : (g * group + t + 1) * head] for t in range(group)],
            axis=0,
        )
        k = jnp.concatenate([r[:, g * head : (g + 1) * head] for r in kv_refs], axis=0)
        v = jnp.concatenate(
            [r[:, (kv_heads + g) * head : (kv_heads + g + 1) * head] for r in kv_refs], axis=0
        )
        scores = lax.dot_general(
            q, k, (((1,), (1,)), ((), ())), preferred_element_type=jnp.float32
        ) * (head**-0.5)
        scores = jnp.where(allowed, scores, neg_fill)
        top = jnp.max(scores, axis=1, keepdims=True)
        weights = jnp.where(allowed, jnp.exp(scores - top), 0.0)
        total = jnp.sum(weights, axis=1, keepdims=True)
        summed = dot(weights.astype(jnp.bfloat16), v) / total
        for t in range(group):
            attended_ref[:, (g * group + t) * head : (g * group + t + 1) * head] = summed[
                t * block : (t + 1) * block
            ].astype(jnp.bfloat16)
    copy.wait()
    out_ref[...] = dot(attended_ref[...], weight_ref[...]).astype(jnp.bfloat16)


def norm_kernel(n_parts, residual_ref, gain_ref, info_ref, *refs):
    parts = refs[:n_parts]
    stream_ref, normed_ref = refs[n_parts:]
    width = residual_ref.shape[1]
    stream = residual_ref[...].astype(jnp.float32)
    mixed = parts[0][...].astype(jnp.float32)
    for p in parts[1:]:
        mixed = mixed + p[...].astype(jnp.float32)
    stream = stream + mixed
    stream_ref[...] = stream
    meansq = jnp.mean(stream * stream, axis=1, keepdims=True)
    normed_ref[:, :width] = (stream * lax.rsqrt(meansq + norm_eps) * gain_ref[...]).astype(
        jnp.bfloat16
    )
    normed_ref[:, width:] = info_ref[...]


def experts_kernel(experts, capacity, tile, expert_ref, *refs):
    n_in = len(refs) - 10
    rows_in = refs[:n_in]
    gate_hbm, up_hbm, down_hbm, out_ref = refs[n_in : n_in + 4]
    rows_ref, gate_ref, up_ref, down_ref, gate_sem, down_sem = refs[n_in + 4 :]
    width = gate_hbm.shape[0]
    hidden_all = gate_hbm.shape[1]
    per_expert = hidden_all // experts
    steps = hidden_all // tile
    copies = []
    for s in range(steps):
        cut = pl.ds(s * tile, tile)
        trio = (
            pltpu.make_async_copy(gate_hbm.at[:, cut], gate_ref.at[s], gate_sem.at[s, 0]),
            pltpu.make_async_copy(up_hbm.at[:, cut], up_ref.at[s], gate_sem.at[s, 1]),
            pltpu.make_async_copy(down_hbm.at[cut, :], down_ref.at[s], down_sem.at[s]),
        )
        for c in trio:
            c.start()
        copies.append(trio)
    start = 0
    for r in rows_in:
        rows_ref[start : start + r.shape[0], :] = r[...]
        start += r.shape[0]
    count = start
    at0 = lax.broadcasted_iota(jnp.int32, (count, count), 0)
    at1 = lax.broadcasted_iota(jnp.int32, (count, count), 1)
    eye = (at0 == at1).astype(jnp.bfloat16)
    before = (at0 < at1).astype(jnp.bfloat16)
    info = lax.dot_general(
        rows_ref[:, width:], eye, (((0,), (0,)), ((), ())), preferred_element_type=jnp.float32
    )
    id0, id1, code0, code1 = (info[i : i + 1, :] for i in range(4))
    slot_of = lax.broadcasted_iota(jnp.int32, (capacity, count), 0).astype(jnp.float32)
    picks, shares, packed = [], [], []
    for x in range(experts):
        e = (expert_ref[0] + x).astype(jnp.float32)
        hit0 = jnp.where(id0 == e, 1.0, 0.0)
        hit1 = jnp.where(id1 == e, 1.0, 0.0)
        member = hit0 + hit1
        share = (hit0 * code0 + hit1 * code1) / (code0 + code1)
        slot = dot(jnp.broadcast_to(member, (8, count)).astype(jnp.bfloat16), before)[:1]
        slot = jnp.where(member > 0.5, slot, -1.0)
        pick = slot == slot_of
        shares.append(jnp.sum(jnp.where(pick, share, 0.0), axis=1, keepdims=True))
        pick = jnp.where(pick, 1.0, 0.0).astype(jnp.bfloat16)
        picks.append(pick)
        packed.append(dot(pick, rows_ref[:, :width]).astype(jnp.bfloat16))
    total = None
    for x in range(experts):
        acc = None
        for s in range(x * steps // experts, (x + 1) * steps // experts):
            gate_copy, up_copy, down_copy = copies[s]
            gate_copy.wait()
            gate = dot(packed[x], gate_ref[s])
            up_copy.wait()
            up = dot(packed[x], up_ref[s])
            hidden = (gate / (1.0 + jnp.exp(-gate)) * up).astype(jnp.bfloat16)
            down_copy.wait()
            part = dot(hidden, down_ref[s])
            acc = part if acc is None else acc + part
        weighted = (acc * shares[x]).astype(jnp.bfloat16)
        spread = lax.dot_general(
            picks[x], weighted, (((0,), (0,)), ((), ())), preferred_element_type=jnp.float32
        )
        total = spread if total is None else total + spread
    out_ref[...] = total.astype(jnp.bfloat16)


def per_device(
    query,
    keys,
    values,
    residual,
    out_weight,
    norm_gain,
    expert_ids,
    gate_codes,
    doc_lengths,
    w_gate,
    w_up,
    w_down,
):
    block, width = residual.shape
    head = HEAD_DIMENSION
    group_width = QUERY_HEAD_COUNT // KEY_VALUE_HEADS
    q_heads = query.shape[1] // head
    sec_count, tp_count, pp_count = (lax.axis_size(a) for a in ("sec", "tp", "pp"))
    sec_index = lax.axis_index("sec")
    pp_index = lax.axis_index("pp")
    ranks = tp_count * pp_count
    rank = lax.axis_index("tp") * pp_count + pp_index
    own_rows = block // ranks

    kv_heads = max(1, q_heads // group_width)
    group = q_heads // kv_heads
    kv_start = pp_index * q_heads // group_width * head
    kv = jnp.concatenate(
        [lax.dynamic_slice_in_dim(a, kv_start, kv_heads * head, 1) for a in (keys, values)], axis=1
    )
    back = -(-(sec_count * block // 2 - 1) // block)
    pieces = [
        lax.ppermute(kv, "sec", [(i, i + k) for i in range(sec_count - k)])
        for k in range(back, 0, -1)
    ] + [kv]
    vmem = 40 * 2**20
    partial = pl.pallas_call(
        functools.partial(attention_kernel, back, kv_heads, group),
        out_shape=jax.ShapeDtypeStruct((block, width), jnp.bfloat16),
        in_specs=[SMEM, SMEM, VMEM] + [VMEM] * (back + 1) + [ANY],
        out_specs=VMEM,
        scratch_shapes=[
            pltpu.VMEM(out_weight.shape, jnp.bfloat16),
            pltpu.VMEM(query.shape, jnp.bfloat16),
            pltpu.SemaphoreType.DMA,
        ],
        compiler_params=pltpu.CompilerParams(vmem_limit_bytes=vmem),
        name="attention",
    )(doc_lengths, sec_index.reshape(1), query, *pieces, out_weight)

    def rows_of(x, r):
        return lax.dynamic_slice_in_dim(x, r * own_rows, own_rows, 0)

    parts = [rows_of(partial, rank)] + [
        xor_swap(rows_of(partial, rank ^ k), ("tp", "pp"), k) for k in range(1, ranks)
    ]
    info = jnp.concatenate([expert_ids, gate_codes], axis=1).astype(jnp.bfloat16)
    info = jnp.pad(rows_of(info, rank), ((0, 0), (0, LANES - info.shape[1])))
    stream, normed = pl.pallas_call(
        functools.partial(norm_kernel, ranks),
        out_shape=(
            jax.ShapeDtypeStruct((own_rows, width), jnp.float32),
            jax.ShapeDtypeStruct((own_rows, width + LANES), jnp.bfloat16),
        ),
        in_specs=[VMEM] * (3 + ranks),
        out_specs=(VMEM, VMEM),
        compiler_params=pltpu.CompilerParams(vmem_limit_bytes=vmem),
        name="norm",
    )(rows_of(residual, rank), norm_gain.reshape(1, width), info, *parts)

    rows = jnp.concatenate(
        [normed] + [xor_swap(normed, "sec", k) for k in range(1, sec_count)], axis=0
    )
    rows = jnp.concatenate([rows] + [xor_swap(rows, "tp", k) for k in range(1, tp_count)], axis=0)
    rows = [rows] + [xor_swap(rows, "pp", k) for k in range(1, pp_count)]

    experts = max(1, E // sec_count)
    halves = max(1, sec_count // E)
    count = sec_count * block
    capacity = sec_count * MOSTB
    hidden_all = w_gate.shape[2]
    tile = min(512, hidden_all // experts)
    steps = hidden_all // tile
    first_expert = (sec_index * experts if halves == 1 else sec_index // halves).reshape(1)
    out = pl.pallas_call(
        functools.partial(experts_kernel, experts, capacity, tile),
        out_shape=jax.ShapeDtypeStruct((count, width), jnp.bfloat16),
        in_specs=[SMEM] + [VMEM] * len(rows) + [ANY] * 3,
        out_specs=VMEM,
        scratch_shapes=[
            pltpu.VMEM((count, width + LANES), jnp.bfloat16),
            pltpu.VMEM((steps, width, tile), jnp.bfloat16),
            pltpu.VMEM((steps, width, tile), jnp.bfloat16),
            pltpu.VMEM((steps, tile, width), jnp.bfloat16),
            pltpu.SemaphoreType.DMA((steps, 2)),
            pltpu.SemaphoreType.DMA((steps,)),
        ],
        compiler_params=pltpu.CompilerParams(vmem_limit_bytes=60 * 2**20),
        name="experts",
    )(first_expert, *rows, w_gate[0], w_up[0], w_down[0])

    def sum_swapped(x, axis):
        n = lax.axis_size(axis)
        x = x.reshape((n, -1) + x.shape[1:])
        total = x[0].astype(jnp.float32)
        for k in range(1, n):
            total = total + xor_swap(x[k], axis, k).astype(jnp.float32)
        return total

    out = sum_swapped(out, "pp").astype(jnp.bfloat16)
    out = sum_swapped(out, "tp").astype(jnp.bfloat16)
    return (stream + sum_swapped(out, "sec")).astype(jnp.bfloat16)


def solution(mesh):
    in_specs = (
        P(("groups", "sec"), ("tp", "pp")),
        P(("groups", "sec"), "tp"),
        P(("groups", "sec"), "tp"),
        P(("groups", "sec"), None),
        P(("tp", "pp"), None),
        P(),
        P(("groups", "sec"), None),
        P(("groups", "sec"), None),
        P("groups"),
        P(("tp", "pp"), None, "sec"),
        P(("tp", "pp"), None, "sec"),
        P(("tp", "pp"), "sec", None),
    )
    out_specs = P(("groups", "sec", "tp", "pp"), None)
    return jax.shard_map(
        per_device, mesh=mesh, in_specs=in_specs, out_specs=out_specs, check_vma=False
    )
```

time: 241 us -> 88.9 us (0.37)
  local copies, waits for them, and re-layouts: 60.7 us -> 7.47 us
  matrix products: 45.9 us -> 0 us
  blocking collectives: 36.4 us -> 0 us
  waiting for transfers between devices: 64.2 us -> 34.6 us
  Pallas kernels: 0 us -> 21.7 us
  between operations: 13.7 us -> 0.18 us
  starting transfers between devices: 9.69 us -> 21.2 us
  other arithmetic: 8.52 us -> 3.32 us
    another operation x2 -> x0, local copies, waits for them, and re-layouts: 55.4 us -> none  [the longest x1 27.7 us: per_device(): gate_local = w_gate[0].reshape(width, experts_here, -1)]
    dot_general x7 -> x0, matrix products: 45.9 us -> none  [the longest x1 16.1 us: per_device(): jnp.einsum('sxmd,dxf->sxmf', rows_in, up_local, preferred_element_type=jn...]
    reduce_scatter x2 -> x0, waiting for transfers between devices: 39.1 us -> none  [the longest x1 20.8 us: per_device(): lax.psum_scatter(jnp.dot(rows_in, out_weight, preferred_element_type=jnp....]
    all_gather x3 -> x0, blocking collectives: 36.4 us -> none  [the longest x1 15.8 us: per_device(): key_piece = lax.all_gather(keys, 'sec', axis=0, tiled=True)]
    ppermute x0 -> x15, waiting for transfers between devices: none -> 34.6 us  [the longest x13 34.2 us: xor_swap(): return lax.ppermute(x, axis, [(i, i ^ k) for i in range(n)])]
    all_to_all x2 -> x0, waiting for transfers between devices: 25.1 us -> none  [the longest x1 25.1 us: per_device(): lax.all_to_all(partial_out.astype(jnp.bfloat16), 'sec', split_axis=0, con...]
    pallas_call x0 -> x3, Pallas kernels: none -> 21.7 us  [the longest x1 19.2 us: per_device(): pl.pallas_call(functools.partial(experts_kernel, experts, capacity, tile)...]
    ppermute x0 -> x15, starting transfers between devices: none -> 21.2 us  [the longest x13 11.8 us: xor_swap(): return lax.ppermute(x, axis, [(i, i ^ k) for i in range(n)])]
  transfers between devices with their start and end apart: 4 -> 15, of which waited for: 3 -> 12; matrix products, arithmetic and copies ran while one was open for 24% -> 2% of each run, Pallas kernels for 0% -> 0%
where the time goes in v1:
time: 88.9 us; the launch traced here: 88.5 us
  waiting for transfers between devices  34.6 us (39%)
  Pallas kernels  21.7 us (24%)
  starting transfers between devices  21.2 us (24%)
  local copies, waits for them, and re-layouts  7.47 us (8%)
  other arithmetic  3.32 us (4%)
    ppermute x13, waiting for transfers between devices, xor_swap(): return lax.ppermute(x, axis, [(i, i ^ k) for i in range(n)])  34.2 us
    pallas_call x1, Pallas kernels, per_device(): pl.pallas_call(functools.partial(experts_kernel, experts, capacity, tile)...  19.2 us
    ppermute x13, starting transfers between devices, xor_swap(): return lax.ppermute(x, axis, [(i, i ^ k) for i in range(n)])  11.8 us
    ppermute x2, starting transfers between devices, per_device(): lax.ppermute(kv, 'sec', [(i, i + k) for i in range(sec_count - k)])  9.43 us
    unnamed x19, local copies, waits for them, and re-layouts  5.39 us
    pallas_call x1, Pallas kernels, per_device(): pl.pallas_call(functools.partial(attention_kernel, back, kv_heads, group)...  2.41 us
  transfers between devices with their start and end apart: 15, of which 12 were waited for; matrix products, arithmetic and copies ran while one was open for 2% of the time, Pallas kernels for 0%

profile of v1, /device:TPU:0, one launch (start us, length us, event | category | flops | bytes accessed | tf_op | source)
XLA Modules:
  0.0 88.5 jit_solution(16115637975581987672)
XLA Ops:
  0.0 0.8 constant_dynamic-slice_fusion.4
  0.8 4.9 %collective-permute-start.1 = (bf16[64,512]{1,0:T(8,128)(2,1)S(1)}, bf16[64,512]{1,0:T(8,128)(2,1)S(1)}, u32[]{:S(2)}, u32[]{:S(2)}) collective-permute-start(bf16[64,512]{1,0:T(8,128)(2,1)S(1)} %pad_maximum_fusion.1.refs_2_), channel_id=1, source_target_pairs={{0,4},{4,8},{8,12},{1,5},{5,9},{9,13},{2,6},{6,10},{10,14},{3,7},{... | collective-permute-start | bytes 196616 | tf_op jit(solution)/shard_map/ppermute | solution.py:196
  5.8 4.5 %collective-permute-start = (bf16[64,512]{1,0:T(8,128)(2,1)S(1)}, bf16[64,512]{1,0:T(8,128)(2,1)S(1)}, u32[]{:S(2)}, u32[]{:S(2)}) collective-permute-start(bf16[64,512]{1,0:T(8,128)(2,1)S(1)} %pad_maximum_fusion.1.refs_2_), channel_id=1, source_target_pairs={{0,8},{4,12},{1,9},{5,13},{2,10},{6,14},{3,11},{7,15},{16,24},{20,... | collective-permute-start | bytes 196616 | tf_op jit(solution)/shard_map/ppermute | solution.py:196
  10.3 0.7 convert.6
  11.0 0.7 convert.7
  12.2 2.2 %copy-done.1 = bf16[1024,2048]{1,0:T(8,128)(2,1)S(1)} copy-done((bf16[1024,2048]{1,0:T(8,128)(2,1)S(1)}, bf16[1024,2048]{1,0:T(8,128)(2,1)}, u32[]{:S(2)}) %copy-start.1) | copy-done | bytes 4194328
  14.4 0.9 %copy-done.2 = bf16[64,1024]{1,0:T(8,128)(2,1)S(1)} copy-done((bf16[64,1024]{1,0:T(8,128)(2,1)S(1)}, bf16[64,1024]{1,0:T(8,128)(2,1)}, u32[]{:S(2)}) %copy-start.2) | copy-done | bytes 131096
  15.9 2.4 %attention.1 = bf16[64,2048]{1,0:T(8,128)(2,1)S(1)} custom-call(s32[8]{0:T(128)S(1)} %copy-done.4, s32[1]{0:T(128)} %bitcast.1.sec_ref, bf16[64,1024]{1,0:T(8,128)(2,1)S(1)} %copy-done.2, bf16[64,512]{1,0:T(8,128)(2,1)S(1)} %collective-permute-done.refs_0_, bf16[64,512]{1,0:T(8,128)(2,1)S(1)} %collective-permute-done.1.refs_1_, ...), custom_call_target="tpu_custom_call" | custom-call | tf_op jit(solution)/shard_map/attention/pallas_call | solution.py:200
  18.4 1.6 %collective-permute-start.3 = (bf16[16,2048]{1,0:T(8,128)(2,1)S(1)}, bf16[16,2048]{1,0:T(8,128)(2,1)S(1)}, u32[]{:S(2)}, u32[]{:S(2)}) collective-permute-start(bf16[16,2048]{1,0:T(8,128)(2,1)S(1)} %get-tuple-element.13), channel_id=1, source_target_pairs={{0,2},{1,3},{2,0},{3,1},{4,6},{5,7},{6,4},{7,5},{8,10},{9,11},{10,... | collective-permute-start | bytes 196616 | tf_op jit(solution)/shard_map/ppermute | solution.py:31
  20.5 2.3 %collective-permute-done.4.refs_3_ = bf16[16,2048]{1,0:T(8,128)(2,1)S(1)} collective-permute-done((bf16[16,2048]{1,0:T(8,128)(2,1)S(1)}, bf16[16,2048]{1,0:T(8,128)(2,1)S(1)}, u32[]{:S(2)}, u32[]{:S(2)}) %collective-permute-start.4) | collective-permute-done | bytes 65568 | tf_op jit(solution)/shard_map/ppermute | solution.py:31
  22.8 1.5 %collective-permute-done.3.refs_2_ = bf16[16,2048]{1,0:T(8,128)(2,1)S(1)} collective-permute-done((bf16[16,2048]{1,0:T(8,128)(2,1)S(1)}, bf16[16,2048]{1,0:T(8,128)(2,1)S(1)}, u32[]{:S(2)}, u32[]{:S(2)}) %collective-permute-start.3) | collective-permute-done | bytes 65568 | tf_op jit(solution)/shard_map/ppermute | solution.py:31
  24.2 0.7 copy-done.3
  25.1 2.2 %collective-permute-start.7 = (bf16[16,2176]{1,0:T(8,128)(2,1)S(1)}, bf16[16,2176]{1,0:T(8,128)(2,1)S(1)}, u32[]{:S(2)}, u32[]{:S(2)}) collective-permute-start(bf16[16,2176]{1,0:T(8,128)(2,1)S(1)} %get-tuple-element.8), channel_id=1, source_target_pairs={{0,12},{4,8},{8,4},{12,0},{1,13},{5,9},{9,5},{13,1},{2,14},{6,10},... | collective-permute-start | bytes 208904 | tf_op jit(solution)/shard_map/ppermute | solution.py:31
  27.2 1.2 %collective-permute-start.6 = (bf16[16,2176]{1,0:T(8,128)(2,1)S(1)}, bf16[16,2176]{1,0:T(8,128)(2,1)S(1)}, u32[]{:S(2)}, u32[]{:S(2)}) collective-permute-start(bf16[16,2176]{1,0:T(8,128)(2,1)S(1)} %get-tuple-element.8), channel_id=1, source_target_pairs={{0,8},{4,12},{8,0},{12,4},{1,9},{5,13},{9,1},{13,5},{2,10},{6,14},... | collective-permute-start | bytes 208904 | tf_op jit(solution)/shard_map/ppermute | solution.py:31
  28.5 1.0 %collective-permute-start.5 = (bf16[16,2176]{1,0:T(8,128)(2,1)S(1)}, bf16[16,2176]{1,0:T(8,128)(2,1)S(1)}, u32[]{:S(2)}, u32[]{:S(2)}) collective-permute-start(bf16[16,2176]{1,0:T(8,128)(2,1)S(1)} %get-tuple-element.8), channel_id=1, source_target_pairs={{0,4},{4,0},{8,12},{12,8},{1,5},{5,1},{9,13},{13,9},{2,6},{6,2},{1... | collective-permute-start | bytes 208904 | tf_op jit(solution)/shard_map/ppermute | solution.py:31
  29.5 1.8 %collective-permute-done.7 = bf16[16,2176]{1,0:T(8,128)(2,1)S(1)} collective-permute-done((bf16[16,2176]{1,0:T(8,128)(2,1)S(1)}, bf16[16,2176]{1,0:T(8,128)(2,1)S(1)}, u32[]{:S(2)}, u32[]{:S(2)}) %collective-permute-start.7) | collective-permute-done | bytes 69664 | tf_op jit(solution)/shard_map/ppermute | solution.py:31
  31.3 4.0 %collective-permute-done.6 = bf16[16,2176]{1,0:T(8,128)(2,1)S(1)} collective-permute-done((bf16[16,2176]{1,0:T(8,128)(2,1)S(1)}, bf16[16,2176]{1,0:T(8,128)(2,1)S(1)}, u32[]{:S(2)}, u32[]{:S(2)}) %collective-permute-start.6) | collective-permute-done | bytes 69664 | tf_op jit(solution)/shard_map/ppermute | solution.py:31
  35.3 0.8 collective-permute-start.8
  36.2 7.6 %collective-permute-done.8 = bf16[64,2176]{1,0:T(8,128)(2,1)S(1)} collective-permute-done((bf16[64,2176]{1,0:T(8,128)(2,1)S(1)}, bf16[64,2176]{1,0:T(8,128)(2,1)S(1)}, u32[]{:S(2)}, u32[]{:S(2)}) %collective-permute-start.8) | collective-permute-done | bytes 278560 | tf_op jit(solution)/shard_map/ppermute | solution.py:31
  43.9 1.9 %collective-permute-done.9.refs_1_ = bf16[128,2176]{1,0:T(8,128)(2,1)S(1)} collective-permute-done((bf16[128,2176]{1,0:T(8,128)(2,1)S(1)}, bf16[128,2176]{1,0:T(8,128)(2,1)S(1)}, u32[]{:S(2)}, u32[]{:S(2)}) %collective-permute-start.9) | collective-permute-done | bytes 557088 | tf_op jit(solution)/shard_map/ppermute | solution.py:31
  45.8 0.8 copy-done.6
  46.6 19.2 %experts.1 = bf16[256,2048]{1,0:T(8,128)(2,1)} custom-call(s32[1]{0:T(128)} %bitcast.2.expert_ref, bf16[128,2176]{1,0:T(8,128)(2,1)} %copy-done.5, bf16[128,2176]{1,0:T(8,128)(2,1)} %copy-done.6, bf16[2048,4096]{1,0:T(8,128)(2,1)} %bitcast.7, bf16[2048,4096]{1,0:T(8,128)(2,1)} %bitcast.8, bf16[4096,2048]{1,0:T(8,128)(2,1)} %bitcast.9), custom_call_target="tpu_custom_call" | custom-call | tf_op jit(solution)/shard_map/experts/pallas_call | solution.py:248
  65.8 1.1 %slice.41 = bf16[128,2048]{1,0:T(8,128)(2,1)S(1)} slice(bf16[256,2048]{1,0:T(8,128)(2,1)} %experts.1), slice={[128:256], [0:2048]} | slice | bytes 1048576 | tf_op jit(solution)/shard_map/slice | solution.py:270
  67.1 1.8 %collective-permute-done.10 = bf16[128,2048]{1,0:T(8,128)(2,1)S(1)} collective-permute-done((bf16[128,2048]{1,0:T(8,128)(2,1)S(1)}, bf16[128,2048]{1,0:T(8,128)(2,1)S(1)}, u32[]{:S(2)}, u32[]{:S(2)}) %collective-permute-start.10) | collective-permute-done | bytes 524320 | tf_op jit(solution)/shard_map/ppermute | solution.py:31
  68.8 1.2 %add_convert_fusion = bf16[128,2048]{1,0:T(8,128)(2,1)S(1)} fusion(bf16[128,2048]{1,0:T(8,128)(2,1)S(1)} %collective-permute-done.10, bf16[256,2048]{1,0:T(8,128)(2,1)} %experts.1), kind=kLoop, calls=%fused_computation | loop fusion | flops 1048576 | bytes 1572864 | tf_op jit(solution)/shard_map/convert_element_type | solution.py:273
  70.0 0.8 collective-permute-start.11
  70.8 7.6 %collective-permute-done.11 = bf16[64,2048]{1,0:T(8,128)(2,1)S(1)} collective-permute-done((bf16[64,2048]{1,0:T(8,128)(2,1)S(1)}, bf16[64,2048]{1,0:T(8,128)(2,1)S(1)}, u32[]{:S(2)}, u32[]{:S(2)}) %collective-permute-start.11) | collective-permute-done | bytes 262176 | tf_op jit(solution)/shard_map/ppermute | solution.py:31
  78.6 2.6 %collective-permute-start.14 = (bf16[16,2048]{1,0:T(8,128)(2,1)S(1)}, bf16[16,2048]{1,0:T(8,128)(2,1)S(1)}, u32[]{:S(2)}, u32[]{:S(2)}) collective-permute-start(bf16[16,2048]{1,0:T(8,128)(2,1)S(1)} %get-tuple-element.10), channel_id=1, source_target_pairs={{0,12},{4,8},{8,4},{12,0},{1,13},{5,9},{9,5},{13,1},{2,14},{6,10},... | collective-permute-start | bytes 196616 | tf_op jit(solution)/shard_map/ppermute | solution.py:31
  81.2 0.9 %collective-permute-start.13 = (bf16[16,2048]{1,0:T(8,128)(2,1)S(1)}, bf16[16,2048]{1,0:T(8,128)(2,1)S(1)}, u32[]{:S(2)}, u32[]{:S(2)}) collective-permute-start(bf16[16,2048]{1,0:T(8,128)(2,1)S(1)} %get-tuple-element.11), channel_id=1, source_target_pairs={{0,8},{4,12},{8,0},{12,4},{1,9},{5,13},{9,1},{13,5},{2,10},{6,14},... | collective-permute-start | bytes 196616 | tf_op jit(solution)/shard_map/ppermute | solution.py:31
  82.1 1.5 %collective-permute-done.12 = bf16[16,2048]{1,0:T(8,128)(2,1)S(1)} collective-permute-done((bf16[16,2048]{1,0:T(8,128)(2,1)S(1)}, bf16[16,2048]{1,0:T(8,128)(2,1)S(1)}, u32[]{:S(2)}, u32[]{:S(2)}) %collective-permute-start.12) | collective-permute-done | bytes 65568 | tf_op jit(solution)/shard_map/ppermute | solution.py:31
  83.6 1.8 %collective-permute-done.14 = bf16[16,2048]{1,0:T(8,128)(2,1)S(1)} collective-permute-done((bf16[16,2048]{1,0:T(8,128)(2,1)S(1)}, bf16[16,2048]{1,0:T(8,128)(2,1)S(1)}, u32[]{:S(2)}, u32[]{:S(2)}) %collective-permute-start.14) | collective-permute-done | bytes 65568 | tf_op jit(solution)/shard_map/ppermute | solution.py:31
  85.3 2.5 %collective-permute-done.13 = bf16[16,2048]{1,0:T(8,128)(2,1)S(1)} collective-permute-done((bf16[16,2048]{1,0:T(8,128)(2,1)S(1)}, bf16[16,2048]{1,0:T(8,128)(2,1)S(1)}, u32[]{:S(2)}, u32[]{:S(2)}) %collective-permute-start.13) | collective-permute-done | bytes 65568 | tf_op jit(solution)/shard_map/ppermute | solution.py:31
  (37 shorter events, 3.1 us)
Async XLA Ops:
  0.0 11.7 %copy-start = (bf16[64,2048]{1,0:T(8,128)(2,1)S(1)}, bf16[64,2048]{1,0:T(8,128)(2,1)}, u32[]{:S(2)}) copy-start(bf16[64,2048]{1,0:T(8,128)(2,1)} %param.15) | copy-start | bytes 786436
  0.8 10.9 %collective-permute-start.1 = (bf16[64,512]{1,0:T(8,128)(2,1)S(1)}, bf16[64,512]{1,0:T(8,128)(2,1)S(1)}, u32[]{:S(2)}, u32[]{:S(2)}) collective-permute-start(bf16[64,512]{1,0:T(8,128)(2,1)S(1)} %pad_maximum_fusion.1.refs_2_), channel_id=1, source_target_pairs={{0,4},{4,8},{8,12},{1,5},{5,9},{9,13},{2,6},{6,10},{10,14},{3,7},{... | collective-permute-start | bytes 196616 | tf_op jit(solution)/shard_map/ppermute | solution.py:196
  5.8 6.4 %collective-permute-start = (bf16[64,512]{1,0:T(8,128)(2,1)S(1)}, bf16[64,512]{1,0:T(8,128)(2,1)S(1)}, u32[]{:S(2)}, u32[]{:S(2)}) collective-permute-start(bf16[64,512]{1,0:T(8,128)(2,1)S(1)} %pad_maximum_fusion.1.refs_2_), channel_id=1, source_target_pairs={{0,8},{4,12},{1,9},{5,13},{2,10},{6,14},{3,11},{7,15},{16,24},{20,... | collective-permute-start | bytes 196616 | tf_op jit(solution)/shard_map/ppermute | solution.py:196
  12.2 2.2 %copy-start.1 = (bf16[1024,2048]{1,0:T(8,128)(2,1)S(1)}, bf16[1024,2048]{1,0:T(8,128)(2,1)}, u32[]{:S(2)}) copy-start(bf16[1024,2048]{1,0:T(8,128)(2,1)} %refs_3_.1) | copy-start | bytes 12582916
  14.4 0.9 %copy-start.2 = (bf16[64,1024]{1,0:T(8,128)(2,1)S(1)}, bf16[64,1024]{1,0:T(8,128)(2,1)}, u32[]{:S(2)}) copy-start(bf16[64,1024]{1,0:T(8,128)(2,1)} %q_ref.1) | copy-start | bytes 393220
  15.3 0.7 copy-start.4
  18.4 4.4 %collective-permute-start.4 = (bf16[16,2048]{1,0:T(8,128)(2,1)S(1)}, bf16[16,2048]{1,0:T(8,128)(2,1)S(1)}, u32[]{:S(2)}, u32[]{:S(2)}) collective-permute-start(bf16[16,2048]{1,0:T(8,128)(2,1)S(1)} %get-tuple-element.12), channel_id=1, source_target_pairs={{0,3},{1,2},{2,1},{3,0},{4,7},{5,6},{6,5},{7,4},{8,11},{9,10},{10,... | collective-permute-start | bytes 196616 | tf_op jit(solution)/shard_map/ppermute | solution.py:31
  18.4 5.8 %collective-permute-start.3 = (bf16[16,2048]{1,0:T(8,128)(2,1)S(1)}, bf16[16,2048]{1,0:T(8,128)(2,1)S(1)}, u32[]{:S(2)}, u32[]{:S(2)}) collective-permute-start(bf16[16,2048]{1,0:T(8,128)(2,1)S(1)} %get-tuple-element.13), channel_id=1, source_target_pairs={{0,2},{1,3},{2,0},{3,1},{4,6},{5,7},{6,4},{7,5},{8,10},{9,11},{10,... | collective-permute-start | bytes 196616 | tf_op jit(solution)/shard_map/ppermute | solution.py:31
  20.0 4.2 %collective-permute-start.2 = (bf16[16,2048]{1,0:T(8,128)(2,1)S(1)}, bf16[16,2048]{1,0:T(8,128)(2,1)S(1)}, u32[]{:S(2)}, u32[]{:S(2)}) collective-permute-start(bf16[16,2048]{1,0:T(8,128)(2,1)S(1)} %get-tuple-element.14), channel_id=1, source_target_pairs={{0,1},{1,0},{2,3},{3,2},{4,5},{5,4},{6,7},{7,6},{8,9},{9,8},{10,11... | collective-permute-start | bytes 196616 | tf_op jit(solution)/shard_map/ppermute | solution.py:31
  24.2 0.7 copy-start.3
  25.1 6.3 %collective-permute-start.7 = (bf16[16,2176]{1,0:T(8,128)(2,1)S(1)}, bf16[16,2176]{1,0:T(8,128)(2,1)S(1)}, u32[]{:S(2)}, u32[]{:S(2)}) collective-permute-start(bf16[16,2176]{1,0:T(8,128)(2,1)S(1)} %get-tuple-element.8), channel_id=1, source_target_pairs={{0,12},{4,8},{8,4},{12,0},{1,13},{5,9},{9,5},{13,1},{2,14},{6,10},... | collective-permute-start | bytes 208904 | tf_op jit(solution)/shard_map/ppermute | solution.py:31
  27.2 8.1 %collective-permute-start.6 = (bf16[16,2176]{1,0:T(8,128)(2,1)S(1)}, bf16[16,2176]{1,0:T(8,128)(2,1)S(1)}, u32[]{:S(2)}, u32[]{:S(2)}) collective-permute-start(bf16[16,2176]{1,0:T(8,128)(2,1)S(1)} %get-tuple-element.8), channel_id=1, source_target_pairs={{0,8},{4,12},{8,0},{12,4},{1,9},{5,13},{9,1},{13,5},{2,10},{6,14},... | collective-permute-start | bytes 208904 | tf_op jit(solution)/shard_map/ppermute | solution.py:31
  28.5 6.8 %collective-permute-start.5 = (bf16[16,2176]{1,0:T(8,128)(2,1)S(1)}, bf16[16,2176]{1,0:T(8,128)(2,1)S(1)}, u32[]{:S(2)}, u32[]{:S(2)}) collective-permute-start(bf16[16,2176]{1,0:T(8,128)(2,1)S(1)} %get-tuple-element.8), channel_id=1, source_target_pairs={{0,4},{4,0},{8,12},{12,8},{1,5},{5,1},{9,13},{13,9},{2,6},{6,2},{1... | collective-permute-start | bytes 208904 | tf_op jit(solution)/shard_map/ppermute | solution.py:31
  35.3 8.4 %collective-permute-start.8 = (bf16[64,2176]{1,0:T(8,128)(2,1)S(1)}, bf16[64,2176]{1,0:T(8,128)(2,1)S(1)}, u32[]{:S(2)}, u32[]{:S(2)}) collective-permute-start(bf16[64,2176]{1,0:T(8,128)(2,1)S(1)} %pad_maximum_fusion), channel_id=1, source_target_pairs={{0,2},{2,0},{1,3},{3,1},{4,6},{6,4},{5,7},{7,5},{8,10},{10,8},{9,1... | collective-permute-start | bytes 835592 | tf_op jit(solution)/shard_map/ppermute | solution.py:31
  43.8 2.0 %copy-start.5 = (bf16[128,2176]{1,0:T(8,128)(2,1)}, bf16[128,2176]{1,0:T(8,128)(2,1)S(1)}, u32[]{:S(2)}) copy-start(bf16[128,2176]{1,0:T(8,128)(2,1)S(1)} %constant_dynamic-update-slice_fusion.refs_0_) | copy-start | bytes 1671172
  43.8 2.0 %collective-permute-start.9 = (bf16[128,2176]{1,0:T(8,128)(2,1)S(1)}, bf16[128,2176]{1,0:T(8,128)(2,1)S(1)}, u32[]{:S(2)}, u32[]{:S(2)}) collective-permute-start(bf16[128,2176]{1,0:T(8,128)(2,1)S(1)} %constant_dynamic-update-slice_fusion.refs_0_), channel_id=1, source_target_pairs={{0,1},{1,0},{2,3},{3,2},{4,5},{5,4},{6,7},{7,6},{8,9},{9,8},{10,11... | collective-permute-start | bytes 1671176 | tf_op jit(solution)/shard_map/ppermute | solution.py:31
  45.8 0.8 copy-start.6
  66.9 2.0 %collective-permute-start.10 = (bf16[128,2048]{1,0:T(8,128)(2,1)S(1)}, bf16[128,2048]{1,0:T(8,128)(2,1)S(1)}, u32[]{:S(2)}, u32[]{:S(2)}) collective-permute-start(bf16[128,2048]{1,0:T(8,128)(2,1)S(1)} %slice.41), channel_id=1, source_target_pairs={{0,1},{1,0},{2,3},{3,2},{4,5},{5,4},{6,7},{7,6},{8,9},{9,8},{10,11... | collective-permute-start | bytes 1572872 | tf_op jit(solution)/shard_map/ppermute | solution.py:31
  70.0 8.4 %collective-permute-start.11 = (bf16[64,2048]{1,0:T(8,128)(2,1)S(1)}, bf16[64,2048]{1,0:T(8,128)(2,1)S(1)}, u32[]{:S(2)}, u32[]{:S(2)}) collective-permute-start(bf16[64,2048]{1,0:T(8,128)(2,1)S(1)} %slice.43), channel_id=1, source_target_pairs={{0,2},{2,0},{1,3},{3,1},{4,6},{6,4},{5,7},{7,5},{8,10},{10,8},{9,1... | collective-permute-start | bytes 786440 | tf_op jit(solution)/shard_map/ppermute | solution.py:31
  78.5 5.0 %collective-permute-start.12 = (bf16[16,2048]{1,0:T(8,128)(2,1)S(1)}, bf16[16,2048]{1,0:T(8,128)(2,1)S(1)}, u32[]{:S(2)}, u32[]{:S(2)}) collective-permute-start(bf16[16,2048]{1,0:T(8,128)(2,1)S(1)} %get-tuple-element.9), channel_id=1, source_target_pairs={{0,4},{4,0},{8,12},{12,8},{1,5},{5,1},{9,13},{13,9},{2,6},{6,2},{1... | collective-permute-start | bytes 196616 | tf_op jit(solution)/shard_map/ppermute | solution.py:31
  78.6 6.7 %collective-permute-start.14 = (bf16[16,2048]{1,0:T(8,128)(2,1)S(1)}, bf16[16,2048]{1,0:T(8,128)(2,1)S(1)}, u32[]{:S(2)}, u32[]{:S(2)}) collective-permute-start(bf16[16,2048]{1,0:T(8,128)(2,1)S(1)} %get-tuple-element.10), channel_id=1, source_target_pairs={{0,12},{4,8},{8,4},{12,0},{1,13},{5,9},{9,5},{13,1},{2,14},{6,10},... | collective-permute-start | bytes 196616 | tf_op jit(solution)/shard_map/ppermute | solution.py:31
  81.2 6.6 %collective-permute-start.13 = (bf16[16,2048]{1,0:T(8,128)(2,1)S(1)}, bf16[16,2048]{1,0:T(8,128)(2,1)S(1)}, u32[]{:S(2)}, u32[]{:S(2)}) collective-permute-start(bf16[16,2048]{1,0:T(8,128)(2,1)S(1)} %get-tuple-element.11), channel_id=1, source_target_pairs={{0,8},{4,12},{8,0},{12,4},{1,9},{5,13},{9,1},{13,5},{2,10},{6,14},... | collective-permute-start | bytes 196616 | tf_op jit(solution)/shard_map/ppermute | solution.py:31

commit v2 on v1

v2 whole, which is shorter than its diff:
```python
import functools

import jax
import jax.numpy as jnp
from jax import lax
from jax.experimental import pallas as pl
from jax.experimental.pallas import tpu as pltpu
from jax.sharding import PartitionSpec as P

QUERY_HEAD_COUNT = 32
KEY_VALUE_HEADS = 8
HEAD_DIMENSION = 128
E = 8
MOSTB = 32
LANES = 128

neg_fill = -1e30
norm_eps = 1e-05

VMEM = pl.BlockSpec(memory_space=pltpu.VMEM)
SMEM = pl.BlockSpec(memory_space=pltpu.SMEM)
HBM = pl.BlockSpec(memory_space=pltpu.HBM)
ANY = pl.BlockSpec(memory_space=pl.ANY)
MIB = 2**20


def dot(a, b):
    return jnp.dot(a, b, preferred_element_type=jnp.float32)


def xor_swap(x, axis, k):
    n = lax.axis_size(axis)
    return lax.ppermute(x, axis, [(i, i ^ k) for i in range(n)])


def call(kernel, out_shape, args, scratch=(), vmem=8, name=None, cost_us=1.0):
    args = [
        (s, pltpu.with_memory_space_constraint(a, pltpu.HBM) if s is HBM else a) for s, a in args
    ]
    single = not isinstance(out_shape, (tuple, list))
    return pl.pallas_call(
        kernel,
        out_shape=out_shape,
        in_specs=[s for s, _ in args],
        out_specs=VMEM if single else [VMEM] * len(out_shape),
        scratch_shapes=list(scratch),
        compiler_params=pltpu.CompilerParams(vmem_limit_bytes=vmem * MIB),
        cost_estimate=pl.CostEstimate(
            flops=0, bytes_accessed=int(cost_us * 3.4e6), transcendentals=0
        ),
        name=name,
    )(*[a for _, a in args])


def sds(shape, dtype):
    return jax.ShapeDtypeStruct(shape, dtype)


def position():
    rank = lax.axis_index("tp") * lax.axis_size("pp") + lax.axis_index("pp")
    return lax.axis_index("sec"), rank


def columns(source, targets, first=0):
    per = targets[0].shape[1] if targets else 0
    return [(source.at[:, pl.ds((first + i) * per, per)], t) for i, t in enumerate(targets)]


def prepare_kernel(
    back, tp_count, pp_count, lengths_hbm, ids_hbm, codes_hbm, query_hbm, weight_hbm, residual_hbm,
    gain_hbm, *refs
):
    gate_hbm, query_ref, weight_ref, gain_ref, mask_ref, order_ref, residual_ref, info_ref = refs[
        :8
    ]
    gate_refs = refs[8:-5]
    lengths, ids, codes, residual_all, sem = refs[-5:]
    pairs = [
        (lengths_hbm, lengths),
        (ids_hbm, ids),
        (codes_hbm, codes),
        (residual_hbm, residual_all),
        (query_hbm, query_ref),
        (gain_hbm, gain_ref),
        (weight_hbm, weight_ref),
    ] + columns(gate_hbm, gate_refs)
    copies = [pltpu.make_async_copy(a, b, sem.at[i]) for i, (a, b) in enumerate(pairs)]
    for c in copies:
        c.start()
    sec, rank = position()
    block = query_ref.shape[0]
    own_rows = residual_ref.shape[0]
    at = lax.broadcasted_iota(jnp.int32, (block, block), 0)
    to = lax.broadcasted_iota(jnp.int32, (block, block), 1)
    chunk = lax.div(at, own_rows)
    flip = lax.rem(chunk, tp_count) * pp_count + lax.div(chunk, tp_count)
    source = (rank ^ flip) * own_rows + lax.rem(at, own_rows)
    order_ref[...] = jnp.where(to == source, 1.0, 0.0).astype(jnp.bfloat16)
    own = lax.broadcasted_iota(jnp.int32, (own_rows, block), 0) + rank * own_rows
    own = jnp.where(own == lax.broadcasted_iota(jnp.int32, (own_rows, block), 1), 1.0, 0.0)
    own = own.astype(jnp.bfloat16)
    for c in copies[:4]:
        c.wait()
    span = (back + 1) * block
    rows = sec * block + lax.broadcasted_iota(jnp.int32, (block, span), 0)
    cols = (sec - back) * block + lax.broadcasted_iota(jnp.int32, (block, span), 1)
    first = jnp.zeros((block, span), jnp.int32)
    end = jnp.int32(0)
    for d in range(lengths.shape[0]):
        end = end + lengths[d]
        first = jnp.where(rows >= end, end, first)
    mask_ref[...] = jnp.where((cols <= rows) & (cols >= first), 1.0, 0.0)
    residual_ref[...] = dot(own, residual_all[...])
    info = jnp.concatenate(
        [ids[...], codes[...], jnp.zeros((LANES - 4, block), jnp.int32)], axis=0
    ).astype(jnp.float32)
    info_ref[...] = lax.dot_general(
        own, info.astype(jnp.bfloat16), (((1,), (1,)), ((), ())), preferred_element_type=jnp.float32
    ).astype(jnp.bfloat16)
    for c in copies[4:]:
        c.wait()


def load_kernel(n_after, source, *refs):
    *targets, token_ref, sem = refs[n_after:]
    copies = [
        pltpu.make_async_copy(a, b, sem.at[i])
        for i, (a, b) in enumerate(columns(source, targets))
    ]
    for c in copies:
        c.start()
    token_ref[...] = jnp.zeros_like(token_ref)
    for c in copies:
        c.wait()


def load(array, parts, wanted, after, name):
    rows, cols = array.shape
    out = call(
        functools.partial(load_kernel, len(after)),
        [sds((rows, cols // parts), array.dtype)] * wanted + [sds((8, LANES), jnp.float32)],
        [(HBM, array)] + [(ANY, a) for a in after],
        scratch=[pltpu.SemaphoreType.DMA((wanted,))],
        vmem=1,
        name=name,
        cost_us=array.size * wanted / parts * 2 / 3.4e6,
    )
    return out[:-1], out[-1]


def attention_kernel(back, kv_heads, group, q_ref, mask_ref, order_ref, *refs):
    kv_refs = refs[: back + 1]
    weight_ref, keep_ref, send_ref, attended_ref = refs[back + 1 :]
    block = q_ref.shape[0]
    head = HEAD_DIMENSION
    allowed = jnp.concatenate([mask_ref[...]] * group, axis=0) > 0.5
    for g in range(kv_heads):
        q = jnp.concatenate(
            [q_ref[:, (g * group + t) * head : (g * group + t + 1) * head] for t in range(group)],
            axis=0,
        )
        k = jnp.concatenate([r[:, g * head : (g + 1) * head] for r in kv_refs], axis=0)
        v = jnp.concatenate(
            [r[:, (kv_heads + g) * head : (kv_heads + g + 1) * head] for r in kv_refs], axis=0
        )
        scores = lax.dot_general(
            q, k, (((1,), (1,)), ((), ())), preferred_element_type=jnp.float32
        ) * (head**-0.5)
        scores = jnp.where(allowed, scores, neg_fill)
        top = jnp.max(scores, axis=1, keepdims=True)
        weights = jnp.where(allowed, jnp.exp(scores - top), 0.0)
        total = jnp.sum(weights, axis=1, keepdims=True)
        summed = dot(weights.astype(jnp.bfloat16), v) / total
        for t in range(group):
            attended_ref[:, (g * group + t) * head : (g * group + t + 1) * head] = summed[
                t * block : (t + 1) * block
            ].astype(jnp.bfloat16)
    attended = dot(order_ref[...], attended_ref[...]).astype(jnp.bfloat16)
    mixed = dot(attended, weight_ref[...])
    kept = keep_ref.shape[0]
    keep_ref[...] = mixed[:kept]
    send_ref[...] = mixed[kept:].astype(jnp.bfloat16)


def add_kernel(keep_rows, n_in, *refs):
    total = refs[0][...].astype(jnp.float32)
    for r in refs[1:n_in]:
        total = total + r[...].astype(jnp.float32)
    start = 0
    for r in refs[n_in:]:
        r[...] = total[start : start + r.shape[0]].astype(r.dtype)
        start += r.shape[0]


def add(arrays, keep, send, name):
    width = arrays[0].shape[1]
    out = [sds((r, width), jnp.float32) for r in keep]
    out += [sds((r, width), jnp.bfloat16) for r in send]
    out = call(
        functools.partial(add_kernel, sum(keep), len(arrays)),
        out,
        [(VMEM, a) for a in arrays],
        name=name,
        cost_us=0.2,
    )
    return out[: len(keep)], out[len(keep) :]


def norm_kernel(n_parts, residual_ref, gain_ref, info_ref, *refs):
    parts = refs[:n_parts]
    stream_ref, normed_ref = refs[-2:]
    width = residual_ref.shape[1]
    mixed = parts[0][...].astype(jnp.float32)
    for p in parts[1:]:
        mixed = mixed + p[...].astype(jnp.float32)
    stream = residual_ref[...] + mixed
    stream_ref[...] = stream
    meansq = jnp.mean(stream * stream, axis=1, keepdims=True)
    normed_ref[:, :width] = (stream * lax.rsqrt(meansq + norm_eps) * gain_ref[...]).astype(
        jnp.bfloat16
    )
    normed_ref[:, width:] = info_ref[...]


def experts_kernel(experts, capacity, tile, halves, n_rows, n_gate, n_up, *refs):
    rows_in = refs[:n_rows]
    gate_refs = list(refs[n_rows : n_rows + n_gate])
    up_refs = list(refs[n_rows + n_gate : n_rows + n_gate + n_up])
    refs = refs[n_rows + n_gate + n_up :]
    up_hbm, down_hbm, keep_ref, send_ref, rows_ref, pick_ref, packed_ref, hidden_ref = refs[:8]
    up_late = list(refs[8 : 8 + experts - n_up])
    down_ref, up_sem, down_sem = refs[8 + experts - n_up :]
    per_expert, width = down_hbm.shape[0] // experts, down_hbm.shape[1]
    up_copies = [
        pltpu.make_async_copy(a, b, up_sem.at[i])
        for i, (a, b) in enumerate(columns(up_hbm, up_late, n_up))
    ]
    up_refs += up_late
    down_copies = [
        pltpu.make_async_copy(
            down_hbm.at[pl.ds(x * per_expert, per_expert)], down_ref, down_sem.at[x]
        )
        for x in range(experts)
    ]
    for c in down_copies[:1] + up_copies:
        c.start()
    count = 0
    for r in rows_in:
        rows_ref[count : count + r.shape[0], :] = r[...]
        count += r.shape[0]
    at0 = lax.broadcasted_iota(jnp.int32, (count, count), 0)
    at1 = lax.broadcasted_iota(jnp.int32, (count, count), 1)
    eye = jnp.where(at0 == at1, 1.0, 0.0).astype(jnp.bfloat16)
    before = jnp.where(at0 < at1, 1.0, 0.0).astype(jnp.bfloat16)
    info = lax.dot_general(
        rows_ref[:, width:], eye, (((0,), (0,)), ((), ())), preferred_element_type=jnp.float32
    )
    id0, id1, code0, code1 = (info[i : i + 1, :] for i in range(4))
    slot_of = lax.broadcasted_iota(jnp.int32, (capacity, count), 0).astype(jnp.float32)
    first = lax.axis_index("sec") * experts if halves == 1 else lax.axis_index("sec") // halves
    picks, shares = [], []
    for x in range(experts):
        e = (first + x).astype(jnp.float32)
        hit0 = jnp.where(id0 == e, 1.0, 0.0)
        hit1 = jnp.where(id1 == e, 1.0, 0.0)
        member = hit0 + hit1
        share = (hit0 * code0 + hit1 * code1) / (code0 + code1)
        slot = dot(jnp.broadcast_to(member, (8, count)).astype(jnp.bfloat16), before)[:1]
        slot = jnp.where(member > 0.5, slot, -1.0)
        pick = slot == slot_of
        shares.append(jnp.sum(jnp.where(pick, share, 0.0), axis=1, keepdims=True))
        picks.append(jnp.where(pick, 1.0, 0.0).astype(jnp.bfloat16))
    pick_ref[...] = jnp.concatenate(picks, axis=0)
    column = min(512, width)

    def pack(c, _):
        cut = pl.ds(pl.multiple_of(c * column, column), column)
        packed_ref[:, cut] = dot(pick_ref[...], rows_ref[:, cut]).astype(jnp.bfloat16)
        return 0

    lax.fori_loop(0, width // column, pack, 0)
    for x in range(experts):
        mine = slice(x * capacity, (x + 1) * capacity)
        if x >= n_up:
            up_copies[x - n_up].wait()
        gate_ref, up_ref = gate_refs[x], up_refs[x]

        def inner(s, _):
            cut = pl.ds(pl.multiple_of(s * tile, tile), tile)
            gate = dot(packed_ref[mine, :], gate_ref[:, cut])
            up = dot(packed_ref[mine, :], up_ref[:, cut])
            hidden_ref[mine, cut] = (gate / (1.0 + jnp.exp(-gate)) * up).astype(jnp.bfloat16)
            return 0

        lax.fori_loop(0, per_expert // tile, inner, 0)
        down_copies[x].wait()

        def outer(c, _):
            cut = pl.ds(pl.multiple_of(c * column, column), column)
            out = dot(hidden_ref[mine, :], down_ref[:, cut])
            packed_ref[mine, cut] = (out * shares[x]).astype(jnp.bfloat16)
            return 0

        lax.fori_loop(0, width // column, outer, 0)
        if x + 1 < experts:
            down_copies[x + 1].start()
    kept = keep_ref.shape[0]

    def spread(c, _):
        cut = pl.ds(pl.multiple_of(c * column, column), column)
        out = lax.dot_general(
            pick_ref[...], packed_ref[:, cut], (((0,), (0,)), ((), ())),
            preferred_element_type=jnp.float32,
        )
        keep_ref[:, cut] = out[:kept]
        send_ref[:, cut] = out[kept:].astype(jnp.bfloat16)
        return 0

    lax.fori_loop(0, width // column, spread, 0)


def per_device(
    query,
    keys,
    values,
    residual,
    out_weight,
    norm_gain,
    expert_ids,
    gate_codes,
    doc_lengths,
    w_gate,
    w_up,
    w_down,
):
    block, width = residual.shape
    head = HEAD_DIMENSION
    group_width = QUERY_HEAD_COUNT // KEY_VALUE_HEADS
    q_heads = query.shape[1] // head
    sec_count, tp_count, pp_count = (lax.axis_size(a) for a in ("sec", "tp", "pp"))
    own_rows = block // (tp_count * pp_count)
    bf16, f32 = jnp.bfloat16, jnp.float32

    kv_heads = max(1, q_heads // group_width)
    group = q_heads // kv_heads
    kv_start = lax.axis_index("pp") * q_heads // group_width * head
    kv = jnp.concatenate(
        [lax.dynamic_slice_in_dim(a, kv_start, kv_heads * head, 1) for a in (keys, values)], axis=1
    )
    back = -(-(sec_count * block // 2 - 1) // block)
    pieces = [
        lax.ppermute(kv, "sec", [(i, i + k) for i in range(sec_count - k)])
        for k in range(back, 0, -1)
    ] + [kv]

    experts = max(1, E // sec_count)
    per_expert = w_gate.shape[2] // experts
    span = (back + 1) * block
    query_v, weight_v, gain_v, mask, order, residual_own, info, *gate_v = call(
        functools.partial(prepare_kernel, back, tp_count, pp_count),
        [
            sds(query.shape, bf16),
            sds(out_weight.shape, bf16),
            sds((1, width), f32),
            sds((block, span), f32),
            sds((block, block), bf16),
            sds((own_rows, width), f32),
            sds((own_rows, LANES), bf16),
        ]
        + [sds((width, per_expert), bf16)] * experts,
        [
            (HBM, a)
            for a in (
                doc_lengths, expert_ids.T, gate_codes.T, query, out_weight, residual,
                norm_gain.reshape(1, width), w_gate[0],
            )
        ],
        scratch=[
            pltpu.SMEM(doc_lengths.shape, jnp.int32),
            pltpu.VMEM((2, block), jnp.int32),
            pltpu.VMEM((2, block), jnp.int32),
            pltpu.VMEM(residual.shape, bf16),
            pltpu.SemaphoreType.DMA((7 + experts,)),
        ],
        vmem=6,
        name="prepare",
        cost_us=6.0,
    )
    half = block // pp_count
    keep, send = call(
        functools.partial(attention_kernel, back, kv_heads, group),
        [sds((half, width), f32), sds((block - half, width), bf16)],
        [(VMEM, a) for a in (query_v, mask, order, *pieces, weight_v)],
        scratch=[pltpu.VMEM(query.shape, bf16)],
        name="attention",
        cost_us=2.4,
    )

    (own,), sends = add(
        [keep] + [xor_swap(send, "pp", 1)], [own_rows], [own_rows] * (tp_count - 1), "sum_cores"
    )
    got = [xor_swap(sends[k - 1], "tp", k) for k in range(1, tp_count)]
    up_v, token = load(w_up[0], experts, 1, [own], "load_up")
    stream, normed = call(
        functools.partial(norm_kernel, tp_count),
        [sds((own_rows, width), f32), sds((own_rows, width + LANES), bf16)],
        [(VMEM, a) for a in (residual_own, gain_v, info, own, *got)] + [(ANY, token)],
        name="norm",
        cost_us=0.2,
    )

    groups = min(4, sec_count)
    near = [normed] + [xor_swap(normed, "sec", k) for k in range(1, sec_count)]
    per_group = sec_count // groups
    near = [
        jnp.concatenate(near[g * per_group : (g + 1) * per_group], axis=0)
        if per_group > 1
        else near[g]
        for g in range(groups)
    ]
    rows = [[r] + [xor_swap(r, "tp", k) for k in range(1, tp_count)] for r in near]
    rows = [rows[g][k] for k in range(tp_count) for g in range(groups)]
    rows = rows + [xor_swap(r, "pp", k) for k in range(1, pp_count) for r in rows]

    halves = max(1, sec_count // E)
    count = sec_count * block
    capacity = sec_count * MOSTB
    down = w_down[0]
    tile = min(512, down.shape[0] // experts)
    kept = count // pp_count
    keep, send = call(
        functools.partial(experts_kernel, experts, capacity, tile, halves, len(rows), experts, 1),
        [sds((kept, width), f32), sds((count - kept, width), bf16)],
        [(VMEM, a) for a in (*rows, *gate_v, *up_v)] + [(HBM, w_up[0]), (HBM, down)],
        scratch=[
            pltpu.VMEM((count, width + LANES), bf16),
            pltpu.VMEM((experts * capacity, count), bf16),
            pltpu.VMEM((experts * capacity, width), bf16),
            pltpu.VMEM((experts * capacity, down.shape[0] // experts), bf16),
            *[pltpu.VMEM((width, per_expert), bf16)] * (experts - 1),
            pltpu.VMEM((per_expert, width), bf16),
            pltpu.SemaphoreType.DMA((experts,)),
            pltpu.SemaphoreType.DMA((experts,)),
        ],
        vmem=20,
        name="experts",
        cost_us=12.0,
    )

    piece = kept // (tp_count * groups)
    own, sends = add(
        [keep, xor_swap(send, "pp", 1)], [piece] * groups, [piece] * (groups * (tp_count - 1)), "sum_cores2"
    )
    final = [stream]
    for g in list(range(1, groups)) + [0]:
        got = [xor_swap(sends[(k - 1) * groups + g], "tp", k) for k in range(1, tp_count)]
        if g == 0 and per_group == 1:
            final += [own[0]] + got
            continue
        kept_rows = own_rows if g == 0 else 0
        mine, out = add(
            [own[g]] + got,
            [own_rows] if g == 0 else [],
            [own_rows] * (per_group - (g == 0)),
            "sum_x%d" % g,
        )
        final += list(mine)
        for j, o in enumerate(out):
            final.append(xor_swap(o, "sec", g * per_group + j + (g == 0)))
    return call(
        functools.partial(add_kernel, 0, len(final)),
        [sds((own_rows, width), bf16)],
        [(VMEM, a) for a in final],
        name="total",
        cost_us=0.2,
    )[0]


def solution(mesh):
    in_specs = (
        P(("groups", "sec"), ("tp", "pp")),
        P(("groups", "sec"), "tp"),
        P(("groups", "sec"), "tp"),
        P(("groups", "sec"), None),
        P(("tp", "pp"), None),
        P(),
        P(("groups", "sec"), None),
        P(("groups", "sec"), None),
        P("groups"),
        P(("tp", "pp"), None, "sec"),
        P(("tp", "pp"), None, "sec"),
        P(("tp", "pp"), "sec", None),
    )
    out_specs = P(("groups", "sec", "tp", "pp"), None)
    return jax.shard_map(
        per_device, mesh=mesh, in_specs=in_specs, out_specs=out_specs, check_vma=False
    )
```

time: 88.9 us -> 71.7 us (0.81)
  waiting for transfers between devices: 34.6 us -> 18.7 us
  local copies, waits for them, and re-layouts: 7.47 us -> 0.78 us
  starting transfers between devices: 21.2 us -> 26.3 us
  Pallas kernels: 21.7 us -> 25.4 us
  other arithmetic: 3.32 us -> 0.01 us
    ppermute x13 -> x25, waiting for transfers between devices: 34.2 us -> 18.7 us  [xor_swap(): return lax.ppermute(x, axis, [(i, i ^ k) for i in range(n)])]
    unnamed x19 -> x0, local copies, waits for them, and re-layouts: 5.39 us -> none
    ppermute x13 -> x25, starting transfers between devices: 11.8 us -> 16.9 us  [xor_swap(): return lax.ppermute(x, axis, [(i, i ^ k) for i in range(n)])]
    pallas_call x3 -> x11, Pallas kernels: 21.7 us -> 25.4 us  [call(): pl.pallas_call(kernel, out_shape=out_shape, in_specs=[s for s, _ in args]...]
    convert_element_type x3 -> x0, other arithmetic: 1.91 us -> none  [the longest x1 1.17 us: per_device(): out = sum_swapped(out, 'pp').astype(jnp.bfloat16)]
    another operation x2 -> x0, other arithmetic: 1.37 us -> none
    slice x3 -> x0, local copies, waits for them, and re-layouts: 1.11 us -> none  [sum_swapped(): total = total + xor_swap(x[k], axis, k).astype(jnp.float32)]
  transfers between devices with their start and end apart: 15 -> 27, of which waited for: 12 -> 14; matrix products, arithmetic and copies ran while one was open for 2% -> 0% of each run, Pallas kernels for 0% -> 15%
where the time goes in v2:
time: 71.7 us; the launch traced here: 71.4 us
  starting transfers between devices  26.3 us (37%)
  Pallas kernels  25.4 us (35%)
  waiting for transfers between devices  18.7 us (26%)
  local copies, waits for them, and re-layouts  0.78 us (1%)
    pallas_call x11, Pallas kernels, call(): pl.pallas_call(kernel, out_shape=out_shape, in_specs=[s for s, _ in args]...  25.4 us
    ppermute x25, waiting for transfers between devices, xor_swap(): return lax.ppermute(x, axis, [(i, i ^ k) for i in range(n)])  18.7 us
    ppermute x25, starting transfers between devices, xor_swap(): return lax.ppermute(x, axis, [(i, i ^ k) for i in range(n)])  16.9 us
    ppermute x2, starting transfers between devices, per_device(): lax.ppermute(kv, 'sec', [(i, i + k) for i in range(sec_count - k)])  9.43 us
  transfers between devices with their start and end apart: 27, of which 14 were waited for; matrix products, arithmetic and copies ran while one was open for 0% of the time, Pallas kernels for 15%

profile of v2, /device:TPU:0, one launch (start us, length us, event | category | flops | bytes accessed | tf_op | source)
XLA Modules:
  0.0 71.4 jit_solution(3067715912023910633)
XLA Ops:
  0.0 0.8 %constant_dynamic-slice_fusion = (bf16[64,256]{1,0:T(8,128)(2,1)S(1)}, bf16[64,256]{1,0:T(8,128)(2,1)S(1)}) fusion(bf16[64,512]{1,0:T(8,128)(2,1)} %param.14, s32[]{:T(128)S(6)} %select_n.10, bf16[64,512]{1,0:T(8,128)(2,1)} %param.13), kind=kLoop, calls=%fused_computation.1 | loop fusion | bytes 131076 | tf_op jit(solution)/shard_map/dynamic_slice | solution.py:348
  0.8 4.9 %collective-permute-start.1 = (bf16[64,512]{1,0:T(8,128)(2,1)S(1)}, bf16[64,512]{1,0:T(8,128)(2,1)S(1)}, u32[]{:S(2)}, u32[]{:S(2)}) collective-permute-start(bf16[64,512]{1,0:T(8,128)(2,1)S(1)} %pad_maximum_fusion.refs_2_), channel_id=1, source_target_pairs={{0,4},{4,8},{8,12},{1,5},{5,9},{9,13},{2,6},{6,10},{10,14},{3,7},{... | collective-permute-start | bytes 196616 | tf_op jit(solution)/shard_map/ppermute | solution.py:352
  5.7 4.5 %collective-permute-start = (bf16[64,512]{1,0:T(8,128)(2,1)S(1)}, bf16[64,512]{1,0:T(8,128)(2,1)S(1)}, u32[]{:S(2)}, u32[]{:S(2)}) collective-permute-start(bf16[64,512]{1,0:T(8,128)(2,1)S(1)} %pad_maximum_fusion.refs_2_), channel_id=1, source_target_pairs={{0,8},{4,12},{1,9},{5,13},{2,10},{6,14},{3,11},{7,15},{16,24},{20,... | collective-permute-start | bytes 196616 | tf_op jit(solution)/shard_map/ppermute | solution.py:352
  10.2 7.3 %prepare.1 = (bf16[64,1024]{1,0:T(8,128)(2,1)S(1)}, bf16[1024,2048]{1,0:T(8,128)(2,1)S(1)}, f32[1,2048]{1,0:T(1,128)S(1)}, f32[64,192]{1,0:T(8,128)S(1)}, bf16[6...) custom-call(s32[8]{0:T(128)} %lengths_hbm.1, ...), custom_call_target="tpu_custom_call" | custom-call | bytes 20400000 | tf_op jit(solution)/shard_map/prepare/pallas_call | solution.py:41
  17.6 1.4 %attention.1 = (f32[32,2048]{1,0:T(8,128)S(1)}, bf16[32,2048]{1,0:T(8,128)(2,1)S(1)}) custom-call(bf16[64,1024]{1,0:T(8,128)(2,1)S(1)} %get-tuple-element.35.q_ref, f32[64,192]{1,0:T(8,128)S(1)} %get-tuple-element.36.mask_ref, bf16[64,64]{1,0:T(8,128)(2,1)S(1)} %get-tuple-element.37.order_ref, bf16[64,512]{1,0:T(8,128)(2,1)S(1)} %collective-permute-done.refs_0_, ...), custom_call_target="tpu_custom_call" | custom-call | bytes 8160000 | tf_op jit(solution)/shard_map/attention/pallas_call | solution.py:41
  19.1 1.3 %collective-permute-done.2.refs_1_ = bf16[32,2048]{1,0:T(8,128)(2,1)S(1)} collective-permute-done((bf16[32,2048]{1,0:T(8,128)(2,1)S(1)}, bf16[32,2048]{1,0:T(8,128)(2,1)S(1)}, u32[]{:S(2)}, u32[]{:S(2)}) %collective-permute-start.2) | collective-permute-done | bytes 131104 | tf_op jit(solution)/shard_map/ppermute | solution.py:33
  20.5 1.6 %collective-permute-start.3 = (bf16[16,2048]{1,0:T(8,128)(2,1)S(1)}, bf16[16,2048]{1,0:T(8,128)(2,1)S(1)}, u32[]{:S(2)}, u32[]{:S(2)}) collective-permute-start(bf16[16,2048]{1,0:T(8,128)(2,1)S(1)} %get-tuple-element.42), channel_id=1, source_target_pairs={{0,2},{2,0},{1,3},{3,1},{4,6},{6,4},{5,7},{7,5},{8,10},{10,8},{9,1... | collective-permute-start | bytes 196616 | tf_op jit(solution)/shard_map/ppermute | solution.py:33
  22.0 3.4 %load_up.1 = (bf16[2048,2048]{1,0:T(8,128)(2,1)S(1)}, f32[8,128]{1,0:T(8,128)S(1)}) custom-call(bf16[2048,4096]{1,0:T(8,128)(2,1)} %bitcast.6, f32[16,2048]{1,0:T(8,128)S(1)} %get-tuple-element.41.refs_0_), custom_call_target="tpu_custom_call" | custom-call | bytes 8388607 | tf_op jit(solution)/shard_map/load_up/pallas_call | solution.py:41
  25.6 0.9 %collective-permute-start.7 = (bf16[16,2176]{1,0:T(8,128)(2,1)S(1)}, bf16[16,2176]{1,0:T(8,128)(2,1)S(1)}, u32[]{:S(2)}, u32[]{:S(2)}) collective-permute-start(bf16[16,2176]{1,0:T(8,128)(2,1)S(1)} %get-tuple-element.45.refs_0_), channel_id=1, source_target_pairs={{0,2},{2,0},{1,3},{3,1},{4,6},{6,4},{5,7},{7,5},{8,10},{10,8},{9,1... | collective-permute-start | bytes 208904 | tf_op jit(solution)/shard_map/ppermute | solution.py:33
  26.5 0.8 %collective-permute-start.5 = (bf16[16,2176]{1,0:T(8,128)(2,1)S(1)}, bf16[16,2176]{1,0:T(8,128)(2,1)S(1)}, u32[]{:S(2)}, u32[]{:S(2)}) collective-permute-start(bf16[16,2176]{1,0:T(8,128)(2,1)S(1)} %get-tuple-element.45.refs_0_), channel_id=1, source_target_pairs={{0,8},{4,12},{8,0},{12,4},{1,9},{5,13},{9,1},{13,5},{2,10},{6,14},... | collective-permute-start | bytes 208904 | tf_op jit(solution)/shard_map/ppermute | solution.py:33
  27.4 3.5 %collective-permute-start.4 = (bf16[16,2176]{1,0:T(8,128)(2,1)S(1)}, bf16[16,2176]{1,0:T(8,128)(2,1)S(1)}, u32[]{:S(2)}, u32[]{:S(2)}) collective-permute-start(bf16[16,2176]{1,0:T(8,128)(2,1)S(1)} %get-tuple-element.45.refs_0_), channel_id=1, source_target_pairs={{0,4},{4,0},{8,12},{12,8},{1,5},{5,1},{9,13},{13,9},{2,6},{6,2},{1... | collective-permute-start | bytes 208904 | tf_op jit(solution)/shard_map/ppermute | solution.py:33
  30.9 2.6 %collective-permute-done.6.refs_3_ = bf16[16,2176]{1,0:T(8,128)(2,1)S(1)} collective-permute-done((bf16[16,2176]{1,0:T(8,128)(2,1)S(1)}, bf16[16,2176]{1,0:T(8,128)(2,1)S(1)}, u32[]{:S(2)}, u32[]{:S(2)}) %collective-permute-start.6) | collective-permute-done | bytes 69664 | tf_op jit(solution)/shard_map/ppermute | solution.py:33
  33.5 1.1 %collective-permute-start.10 = (bf16[16,2176]{1,0:T(8,128)(2,1)S(1)}, bf16[16,2176]{1,0:T(8,128)(2,1)S(1)}, u32[]{:S(2)}, u32[]{:S(2)}) collective-permute-start(bf16[16,2176]{1,0:T(8,128)(2,1)S(1)} %collective-permute-done.6.refs_3_), channel_id=1, source_target_pairs={{0,2},{2,0},{1,3},{3,1},{4,6},{6,4},{5,7},{7,5},{8,10},{10,8},{9,1... | collective-permute-start | bytes 208904 | tf_op jit(solution)/shard_map/ppermute | solution.py:33
  34.6 1.5 %collective-permute-start.9 = (bf16[16,2176]{1,0:T(8,128)(2,1)S(1)}, bf16[16,2176]{1,0:T(8,128)(2,1)S(1)}, u32[]{:S(2)}, u32[]{:S(2)}) collective-permute-start(bf16[16,2176]{1,0:T(8,128)(2,1)S(1)} %collective-permute-done.5.refs_2_), channel_id=1, source_target_pairs={{0,2},{2,0},{1,3},{3,1},{4,6},{6,4},{5,7},{7,5},{8,10},{10,8},{9,1... | collective-permute-start | bytes 208904 | tf_op jit(solution)/shard_map/ppermute | solution.py:33
  36.2 0.5 collective-permute-start.8
  37.2 1.3 %collective-permute-done.10.refs_7_ = bf16[16,2176]{1,0:T(8,128)(2,1)S(1)} collective-permute-done((bf16[16,2176]{1,0:T(8,128)(2,1)S(1)}, bf16[16,2176]{1,0:T(8,128)(2,1)S(1)}, u32[]{:S(2)}, u32[]{:S(2)}) %collective-permute-start.10) | collective-permute-done | bytes 69664 | tf_op jit(solution)/shard_map/ppermute | solution.py:33
  38.5 1.5 %collective-permute-done.9.refs_6_ = bf16[16,2176]{1,0:T(8,128)(2,1)S(1)} collective-permute-done((bf16[16,2176]{1,0:T(8,128)(2,1)S(1)}, bf16[16,2176]{1,0:T(8,128)(2,1)S(1)}, u32[]{:S(2)}, u32[]{:S(2)}) %collective-permute-start.9) | collective-permute-done | bytes 69664 | tf_op jit(solution)/shard_map/ppermute | solution.py:33
  40.0 1.1 %collective-permute-done.8.refs_5_ = bf16[16,2176]{1,0:T(8,128)(2,1)S(1)} collective-permute-done((bf16[16,2176]{1,0:T(8,128)(2,1)S(1)}, bf16[16,2176]{1,0:T(8,128)(2,1)S(1)}, u32[]{:S(2)}, u32[]{:S(2)}) %collective-permute-start.8) | collective-permute-done | bytes 69664 | tf_op jit(solution)/shard_map/ppermute | solution.py:33
  41.2 1.1 %collective-permute-done.16.refs_13_ = bf16[16,2176]{1,0:T(8,128)(2,1)S(1)} collective-permute-done((bf16[16,2176]{1,0:T(8,128)(2,1)S(1)}, bf16[16,2176]{1,0:T(8,128)(2,1)S(1)}, u32[]{:S(2)}, u32[]{:S(2)}) %collective-permute-start.16) | collective-permute-done | bytes 69664 | tf_op jit(solution)/shard_map/ppermute | solution.py:33
  42.3 12.3 %experts.1 = (f32[128,2048]{1,0:T(8,128)S(1)}, bf16[128,2048]{1,0:T(8,128)(2,1)S(1)}) custom-call(bf16[16,2176]{1,0:T(8,128)(2,1)S(1)} %get-tuple-element.45.refs_0_, bf16[16,2176]{1,0:T(8,128)(2,1)S(1)} %collective-permute-done.4.refs_1_, bf16[16,2176]{1,0:T(8,128)(2,1)S(1)} %collective-permute-done.5.refs_2_, ...), custom_call_target="tpu_custom_call" | custom-call | bytes 40800000 | tf_op jit(solution)/shard_map/experts/pallas_call | solution.py:41
  54.8 1.8 %collective-permute-done.19.refs_1_ = bf16[128,2048]{1,0:T(8,128)(2,1)S(1)} collective-permute-done((bf16[128,2048]{1,0:T(8,128)(2,1)S(1)}, bf16[128,2048]{1,0:T(8,128)(2,1)S(1)}, u32[]{:S(2)}, u32[]{:S(2)}) %collective-permute-start.19) | collective-permute-done | bytes 524320 | tf_op jit(solution)/shard_map/ppermute | solution.py:33
  56.7 1.2 %collective-permute-start.20 = (bf16[16,2048]{1,0:T(8,128)(2,1)S(1)}, bf16[16,2048]{1,0:T(8,128)(2,1)S(1)}, u32[]{:S(2)}, u32[]{:S(2)}) collective-permute-start(bf16[16,2048]{1,0:T(8,128)(2,1)S(1)} %get-tuple-element.52), channel_id=1, source_target_pairs={{0,2},{2,0},{1,3},{3,1},{4,6},{6,4},{5,7},{7,5},{8,10},{10,8},{9,1... | collective-permute-start | bytes 196616 | tf_op jit(solution)/shard_map/ppermute | solution.py:33
  57.9 0.9 %collective-permute-start.22 = (bf16[16,2048]{1,0:T(8,128)(2,1)S(1)}, bf16[16,2048]{1,0:T(8,128)(2,1)S(1)}, u32[]{:S(2)}, u32[]{:S(2)}) collective-permute-start(bf16[16,2048]{1,0:T(8,128)(2,1)S(1)} %get-tuple-element.54), channel_id=1, source_target_pairs={{0,2},{2,0},{1,3},{3,1},{4,6},{6,4},{5,7},{7,5},{8,10},{10,8},{9,1... | collective-permute-start | bytes 196616 | tf_op jit(solution)/shard_map/ppermute | solution.py:33
  58.8 1.1 %collective-permute-start.24 = (bf16[16,2048]{1,0:T(8,128)(2,1)S(1)}, bf16[16,2048]{1,0:T(8,128)(2,1)S(1)}, u32[]{:S(2)}, u32[]{:S(2)}) collective-permute-start(bf16[16,2048]{1,0:T(8,128)(2,1)S(1)} %get-tuple-element.56), channel_id=1, source_target_pairs={{0,2},{2,0},{1,3},{3,1},{4,6},{6,4},{5,7},{7,5},{8,10},{10,8},{9,1... | collective-permute-start | bytes 196616 | tf_op jit(solution)/shard_map/ppermute | solution.py:33
  59.9 0.9 %collective-permute-start.26 = (bf16[16,2048]{1,0:T(8,128)(2,1)S(1)}, bf16[16,2048]{1,0:T(8,128)(2,1)S(1)}, u32[]{:S(2)}, u32[]{:S(2)}) collective-permute-start(bf16[16,2048]{1,0:T(8,128)(2,1)S(1)} %get-tuple-element.58), channel_id=1, source_target_pairs={{0,2},{2,0},{1,3},{3,1},{4,6},{6,4},{5,7},{7,5},{8,10},{10,8},{9,1... | collective-permute-start | bytes 196616 | tf_op jit(solution)/shard_map/ppermute | solution.py:33
  60.8 0.9 %collective-permute-done.20.refs_1_ = bf16[16,2048]{1,0:T(8,128)(2,1)S(1)} collective-permute-done((bf16[16,2048]{1,0:T(8,128)(2,1)S(1)}, bf16[16,2048]{1,0:T(8,128)(2,1)S(1)}, u32[]{:S(2)}, u32[]{:S(2)}) %collective-permute-start.20) | collective-permute-done | bytes 65568 | tf_op jit(solution)/shard_map/ppermute | solution.py:33
  61.8 1.3 %collective-permute-done.22.refs_1_ = bf16[16,2048]{1,0:T(8,128)(2,1)S(1)} collective-permute-done((bf16[16,2048]{1,0:T(8,128)(2,1)S(1)}, bf16[16,2048]{1,0:T(8,128)(2,1)S(1)}, u32[]{:S(2)}, u32[]{:S(2)}) %collective-permute-start.22) | collective-permute-done | bytes 65568 | tf_op jit(solution)/shard_map/ppermute | solution.py:33
  63.2 1.3 %collective-permute-done.24.refs_1_ = bf16[16,2048]{1,0:T(8,128)(2,1)S(1)} collective-permute-done((bf16[16,2048]{1,0:T(8,128)(2,1)S(1)}, bf16[16,2048]{1,0:T(8,128)(2,1)S(1)}, u32[]{:S(2)}, u32[]{:S(2)}) %collective-permute-start.24) | collective-permute-done | bytes 65568 | tf_op jit(solution)/shard_map/ppermute | solution.py:33
  64.5 1.8 %collective-permute-start.25 = (bf16[16,2048]{1,0:T(8,128)(2,1)S(1)}, bf16[16,2048]{1,0:T(8,128)(2,1)S(1)}, u32[]{:S(2)}, u32[]{:S(2)}) collective-permute-start(bf16[16,2048]{1,0:T(8,128)(2,1)S(1)} %sum_x3.1), channel_id=1, source_target_pairs={{0,12},{4,8},{8,4},{12,0},{1,13},{5,9},{9,5},{13,1},{2,14},{6,10},... | collective-permute-start | bytes 196616 | tf_op jit(solution)/shard_map/ppermute | solution.py:33
  66.7 3.0 %collective-permute-done.23.refs_2_ = bf16[16,2048]{1,0:T(8,128)(2,1)S(1)} collective-permute-done((bf16[16,2048]{1,0:T(8,128)(2,1)S(1)}, bf16[16,2048]{1,0:T(8,128)(2,1)S(1)}, u32[]{:S(2)}, u32[]{:S(2)}) %collective-permute-start.23) | collective-permute-done | bytes 65568 | tf_op jit(solution)/shard_map/ppermute | solution.py:33
  69.7 1.0 %collective-permute-done.25.refs_3_ = bf16[16,2048]{1,0:T(8,128)(2,1)S(1)} collective-permute-done((bf16[16,2048]{1,0:T(8,128)(2,1)S(1)}, bf16[16,2048]{1,0:T(8,128)(2,1)S(1)}, u32[]{:S(2)}, u32[]{:S(2)}) %collective-permute-start.25) | collective-permute-done | bytes 65568 | tf_op jit(solution)/shard_map/ppermute | solution.py:33
  70.7 0.7 total.1
  (35 shorter events, 1.8 us)
Async XLA Ops:
  0.8 16.8 %collective-permute-start.1 = (bf16[64,512]{1,0:T(8,128)(2,1)S(1)}, bf16[64,512]{1,0:T(8,128)(2,1)S(1)}, u32[]{:S(2)}, u32[]{:S(2)}) collective-permute-start(bf16[64,512]{1,0:T(8,128)(2,1)S(1)} %pad_maximum_fusion.refs_2_), channel_id=1, source_target_pairs={{0,4},{4,8},{8,12},{1,5},{5,9},{9,13},{2,6},{6,10},{10,14},{3,7},{... | collective-permute-start | bytes 196616 | tf_op jit(solution)/shard_map/ppermute | solution.py:352
  5.7 11.9 %collective-permute-start = (bf16[64,512]{1,0:T(8,128)(2,1)S(1)}, bf16[64,512]{1,0:T(8,128)(2,1)S(1)}, u32[]{:S(2)}, u32[]{:S(2)}) collective-permute-start(bf16[64,512]{1,0:T(8,128)(2,1)S(1)} %pad_maximum_fusion.refs_2_), channel_id=1, source_target_pairs={{0,8},{4,12},{1,9},{5,13},{2,10},{6,14},{3,11},{7,15},{16,24},{20,... | collective-permute-start | bytes 196616 | tf_op jit(solution)/shard_map/ppermute | solution.py:352
  19.0 1.4 %collective-permute-start.2 = (bf16[32,2048]{1,0:T(8,128)(2,1)S(1)}, bf16[32,2048]{1,0:T(8,128)(2,1)S(1)}, u32[]{:S(2)}, u32[]{:S(2)}) collective-permute-start(bf16[32,2048]{1,0:T(8,128)(2,1)S(1)} %get-tuple-element.40), channel_id=1, source_target_pairs={{0,1},{1,0},{2,3},{3,2},{4,5},{5,4},{6,7},{7,6},{8,9},{9,8},{10,11... | collective-permute-start | bytes 393224 | tf_op jit(solution)/shard_map/ppermute | solution.py:33
  20.5 5.0 %collective-permute-start.3 = (bf16[16,2048]{1,0:T(8,128)(2,1)S(1)}, bf16[16,2048]{1,0:T(8,128)(2,1)S(1)}, u32[]{:S(2)}, u32[]{:S(2)}) collective-permute-start(bf16[16,2048]{1,0:T(8,128)(2,1)S(1)} %get-tuple-element.42), channel_id=1, source_target_pairs={{0,2},{2,0},{1,3},{3,1},{4,6},{6,4},{5,7},{7,5},{8,10},{10,8},{9,1... | collective-permute-start | bytes 196616 | tf_op jit(solution)/shard_map/ppermute | solution.py:33
  25.6 5.3 %collective-permute-start.7 = (bf16[16,2176]{1,0:T(8,128)(2,1)S(1)}, bf16[16,2176]{1,0:T(8,128)(2,1)S(1)}, u32[]{:S(2)}, u32[]{:S(2)}) collective-permute-start(bf16[16,2176]{1,0:T(8,128)(2,1)S(1)} %get-tuple-element.45.refs_0_), channel_id=1, source_target_pairs={{0,2},{2,0},{1,3},{3,1},{4,6},{6,4},{5,7},{7,5},{8,10},{10,8},{9,1... | collective-permute-start | bytes 208904 | tf_op jit(solution)/shard_map/ppermute | solution.py:33
  26.5 7.0 %collective-permute-start.6 = (bf16[16,2176]{1,0:T(8,128)(2,1)S(1)}, bf16[16,2176]{1,0:T(8,128)(2,1)S(1)}, u32[]{:S(2)}, u32[]{:S(2)}) collective-permute-start(bf16[16,2176]{1,0:T(8,128)(2,1)S(1)} %get-tuple-element.45.refs_0_), channel_id=1, source_target_pairs={{0,12},{4,8},{8,4},{12,0},{1,13},{5,9},{9,5},{13,1},{2,14},{6,10},... | collective-permute-start | bytes 208904 | tf_op jit(solution)/shard_map/ppermute | solution.py:33
  26.5 7.0 %collective-permute-start.11 = (bf16[16,2176]{1,0:T(8,128)(2,1)S(1)}, bf16[16,2176]{1,0:T(8,128)(2,1)S(1)}, u32[]{:S(2)}, u32[]{:S(2)}) collective-permute-start(bf16[16,2176]{1,0:T(8,128)(2,1)S(1)} %get-tuple-element.45.refs_0_), channel_id=1, source_target_pairs={{0,1},{1,0},{2,3},{3,2},{4,5},{5,4},{6,7},{7,6},{8,9},{9,8},{10,11... | collective-permute-start | bytes 208904 | tf_op jit(solution)/shard_map/ppermute | solution.py:33
  26.5 8.1 %collective-permute-start.5 = (bf16[16,2176]{1,0:T(8,128)(2,1)S(1)}, bf16[16,2176]{1,0:T(8,128)(2,1)S(1)}, u32[]{:S(2)}, u32[]{:S(2)}) collective-permute-start(bf16[16,2176]{1,0:T(8,128)(2,1)S(1)} %get-tuple-element.45.refs_0_), channel_id=1, source_target_pairs={{0,8},{4,12},{8,0},{12,4},{1,9},{5,13},{9,1},{13,5},{2,10},{6,14},... | collective-permute-start | bytes 208904 | tf_op jit(solution)/shard_map/ppermute | solution.py:33
  27.4 8.8 %collective-permute-start.4 = (bf16[16,2176]{1,0:T(8,128)(2,1)S(1)}, bf16[16,2176]{1,0:T(8,128)(2,1)S(1)}, u32[]{:S(2)}, u32[]{:S(2)}) collective-permute-start(bf16[16,2176]{1,0:T(8,128)(2,1)S(1)} %get-tuple-element.45.refs_0_), channel_id=1, source_target_pairs={{0,4},{4,0},{8,12},{12,8},{1,5},{5,1},{9,13},{13,9},{2,6},{6,2},{1... | collective-permute-start | bytes 208904 | tf_op jit(solution)/shard_map/ppermute | solution.py:33
  30.9 5.8 %collective-permute-start.15 = (bf16[16,2176]{1,0:T(8,128)(2,1)S(1)}, bf16[16,2176]{1,0:T(8,128)(2,1)S(1)}, u32[]{:S(2)}, u32[]{:S(2)}) collective-permute-start(bf16[16,2176]{1,0:T(8,128)(2,1)S(1)} %collective-permute-done.7.refs_4_), channel_id=1, source_target_pairs={{0,1},{1,0},{2,3},{3,2},{4,5},{5,4},{6,7},{7,6},{8,9},{9,8},{10,11... | collective-permute-start | bytes 208904 | tf_op jit(solution)/shard_map/ppermute | solution.py:33
  33.5 3.2 %collective-permute-start.14 = (bf16[16,2176]{1,0:T(8,128)(2,1)S(1)}, bf16[16,2176]{1,0:T(8,128)(2,1)S(1)}, u32[]{:S(2)}, u32[]{:S(2)}) collective-permute-start(bf16[16,2176]{1,0:T(8,128)(2,1)S(1)} %collective-permute-done.6.refs_3_), channel_id=1, source_target_pairs={{0,1},{1,0},{2,3},{3,2},{4,5},{5,4},{6,7},{7,6},{8,9},{9,8},{10,11... | collective-permute-start | bytes 208904 | tf_op jit(solution)/shard_map/ppermute | solution.py:33
  33.5 5.0 %collective-permute-start.10 = (bf16[16,2176]{1,0:T(8,128)(2,1)S(1)}, bf16[16,2176]{1,0:T(8,128)(2,1)S(1)}, u32[]{:S(2)}, u32[]{:S(2)}) collective-permute-start(bf16[16,2176]{1,0:T(8,128)(2,1)S(1)} %collective-permute-done.6.refs_3_), channel_id=1, source_target_pairs={{0,2},{2,0},{1,3},{3,1},{4,6},{6,4},{5,7},{7,5},{8,10},{10,8},{9,1... | collective-permute-start | bytes 208904 | tf_op jit(solution)/shard_map/ppermute | solution.py:33
  34.6 5.3 %collective-permute-start.9 = (bf16[16,2176]{1,0:T(8,128)(2,1)S(1)}, bf16[16,2176]{1,0:T(8,128)(2,1)S(1)}, u32[]{:S(2)}, u32[]{:S(2)}) collective-permute-start(bf16[16,2176]{1,0:T(8,128)(2,1)S(1)} %collective-permute-done.5.refs_2_), channel_id=1, source_target_pairs={{0,2},{2,0},{1,3},{3,1},{4,6},{6,4},{5,7},{7,5},{8,10},{10,8},{9,1... | collective-permute-start | bytes 208904 | tf_op jit(solution)/shard_map/ppermute | solution.py:33
  36.2 4.9 %collective-permute-start.8 = (bf16[16,2176]{1,0:T(8,128)(2,1)S(1)}, bf16[16,2176]{1,0:T(8,128)(2,1)S(1)}, u32[]{:S(2)}, u32[]{:S(2)}) collective-permute-start(bf16[16,2176]{1,0:T(8,128)(2,1)S(1)} %collective-permute-done.4.refs_1_), channel_id=1, source_target_pairs={{0,2},{2,0},{1,3},{3,1},{4,6},{6,4},{5,7},{7,5},{8,10},{10,8},{9,1... | collective-permute-start | bytes 208904 | tf_op jit(solution)/shard_map/ppermute | solution.py:33
  36.7 4.4 %collective-permute-start.13 = (bf16[16,2176]{1,0:T(8,128)(2,1)S(1)}, bf16[16,2176]{1,0:T(8,128)(2,1)S(1)}, u32[]{:S(2)}, u32[]{:S(2)}) collective-permute-start(bf16[16,2176]{1,0:T(8,128)(2,1)S(1)} %collective-permute-done.5.refs_2_), channel_id=1, source_target_pairs={{0,1},{1,0},{2,3},{3,2},{4,5},{5,4},{6,7},{7,6},{8,9},{9,8},{10,11... | collective-permute-start | bytes 208904 | tf_op jit(solution)/shard_map/ppermute | solution.py:33
  36.7 4.4 %collective-permute-start.12 = (bf16[16,2176]{1,0:T(8,128)(2,1)S(1)}, bf16[16,2176]{1,0:T(8,128)(2,1)S(1)}, u32[]{:S(2)}, u32[]{:S(2)}) collective-permute-start(bf16[16,2176]{1,0:T(8,128)(2,1)S(1)} %collective-permute-done.4.refs_1_), channel_id=1, source_target_pairs={{0,1},{1,0},{2,3},{3,2},{4,5},{5,4},{6,7},{7,6},{8,9},{9,8},{10,11... | collective-permute-start | bytes 208904 | tf_op jit(solution)/shard_map/ppermute | solution.py:33
  38.5 2.6 %collective-permute-start.18 = (bf16[16,2176]{1,0:T(8,128)(2,1)S(1)}, bf16[16,2176]{1,0:T(8,128)(2,1)S(1)}, u32[]{:S(2)}, u32[]{:S(2)}) collective-permute-start(bf16[16,2176]{1,0:T(8,128)(2,1)S(1)} %collective-permute-done.10.refs_7_), channel_id=1, source_target_pairs={{0,1},{1,0},{2,3},{3,2},{4,5},{5,4},{6,7},{7,6},{8,9},{9,8},{10,11... | collective-permute-start | bytes 208904 | tf_op jit(solution)/shard_map/ppermute | solution.py:33
  40.0 1.3 %collective-permute-start.17 = (bf16[16,2176]{1,0:T(8,128)(2,1)S(1)}, bf16[16,2176]{1,0:T(8,128)(2,1)S(1)}, u32[]{:S(2)}, u32[]{:S(2)}) collective-permute-start(bf16[16,2176]{1,0:T(8,128)(2,1)S(1)} %collective-permute-done.9.refs_6_), channel_id=1, source_target_pairs={{0,1},{1,0},{2,3},{3,2},{4,5},{5,4},{6,7},{7,6},{8,9},{9,8},{10,11... | collective-permute-start | bytes 208904 | tf_op jit(solution)/shard_map/ppermute | solution.py:33
  41.1 1.3 %collective-permute-start.16 = (bf16[16,2176]{1,0:T(8,128)(2,1)S(1)}, bf16[16,2176]{1,0:T(8,128)(2,1)S(1)}, u32[]{:S(2)}, u32[]{:S(2)}) collective-permute-start(bf16[16,2176]{1,0:T(8,128)(2,1)S(1)} %collective-permute-done.8.refs_5_), channel_id=1, source_target_pairs={{0,1},{1,0},{2,3},{3,2},{4,5},{5,4},{6,7},{7,6},{8,9},{9,8},{10,11... | collective-permute-start | bytes 208904 | tf_op jit(solution)/shard_map/ppermute | solution.py:33
  54.6 2.0 %collective-permute-start.19 = (bf16[128,2048]{1,0:T(8,128)(2,1)S(1)}, bf16[128,2048]{1,0:T(8,128)(2,1)S(1)}, u32[]{:S(2)}, u32[]{:S(2)}) collective-permute-start(bf16[128,2048]{1,0:T(8,128)(2,1)S(1)} %get-tuple-element.50), channel_id=1, source_target_pairs={{0,1},{1,0},{2,3},{3,2},{4,5},{5,4},{6,7},{7,6},{8,9},{9,8},{10,11... | collective-permute-start | bytes 1572872 | tf_op jit(solution)/shard_map/ppermute | solution.py:33
  56.7 5.0 %collective-permute-start.20 = (bf16[16,2048]{1,0:T(8,128)(2,1)S(1)}, bf16[16,2048]{1,0:T(8,128)(2,1)S(1)}, u32[]{:S(2)}, u32[]{:S(2)}) collective-permute-start(bf16[16,2048]{1,0:T(8,128)(2,1)S(1)} %get-tuple-element.52), channel_id=1, source_target_pairs={{0,2},{2,0},{1,3},{3,1},{4,6},{6,4},{5,7},{7,5},{8,10},{10,8},{9,1... | collective-permute-start | bytes 196616 | tf_op jit(solution)/shard_map/ppermute | solution.py:33
  57.9 5.2 %collective-permute-start.22 = (bf16[16,2048]{1,0:T(8,128)(2,1)S(1)}, bf16[16,2048]{1,0:T(8,128)(2,1)S(1)}, u32[]{:S(2)}, u32[]{:S(2)}) collective-permute-start(bf16[16,2048]{1,0:T(8,128)(2,1)S(1)} %get-tuple-element.54), channel_id=1, source_target_pairs={{0,2},{2,0},{1,3},{3,1},{4,6},{6,4},{5,7},{7,5},{8,10},{10,8},{9,1... | collective-permute-start | bytes 196616 | tf_op jit(solution)/shard_map/ppermute | solution.py:33
  58.8 5.7 %collective-permute-start.24 = (bf16[16,2048]{1,0:T(8,128)(2,1)S(1)}, bf16[16,2048]{1,0:T(8,128)(2,1)S(1)}, u32[]{:S(2)}, u32[]{:S(2)}) collective-permute-start(bf16[16,2048]{1,0:T(8,128)(2,1)S(1)} %get-tuple-element.56), channel_id=1, source_target_pairs={{0,2},{2,0},{1,3},{3,1},{4,6},{6,4},{5,7},{7,5},{8,10},{10,8},{9,1... | collective-permute-start | bytes 196616 | tf_op jit(solution)/shard_map/ppermute | solution.py:33
  59.9 6.4 %collective-permute-start.26 = (bf16[16,2048]{1,0:T(8,128)(2,1)S(1)}, bf16[16,2048]{1,0:T(8,128)(2,1)S(1)}, u32[]{:S(2)}, u32[]{:S(2)}) collective-permute-start(bf16[16,2048]{1,0:T(8,128)(2,1)S(1)} %get-tuple-element.58), channel_id=1, source_target_pairs={{0,2},{2,0},{1,3},{3,1},{4,6},{6,4},{5,7},{7,5},{8,10},{10,8},{9,1... | collective-permute-start | bytes 196616 | tf_op jit(solution)/shard_map/ppermute | solution.py:33
  61.7 5.0 %collective-permute-start.21 = (bf16[16,2048]{1,0:T(8,128)(2,1)S(1)}, bf16[16,2048]{1,0:T(8,128)(2,1)S(1)}, u32[]{:S(2)}, u32[]{:S(2)}) collective-permute-start(bf16[16,2048]{1,0:T(8,128)(2,1)S(1)} %sum_x1.1), channel_id=1, source_target_pairs={{0,4},{4,0},{8,12},{12,8},{1,5},{5,1},{9,13},{13,9},{2,6},{6,2},{1... | collective-permute-start | bytes 196616 | tf_op jit(solution)/shard_map/ppermute | solution.py:33
  63.1 6.6 %collective-permute-start.23 = (bf16[16,2048]{1,0:T(8,128)(2,1)S(1)}, bf16[16,2048]{1,0:T(8,128)(2,1)S(1)}, u32[]{:S(2)}, u32[]{:S(2)}) collective-permute-start(bf16[16,2048]{1,0:T(8,128)(2,1)S(1)} %sum_x2.1), channel_id=1, source_target_pairs={{0,8},{4,12},{8,0},{12,4},{1,9},{5,13},{9,1},{13,5},{2,10},{6,14},... | collective-permute-start | bytes 196616 | tf_op jit(solution)/shard_map/ppermute | solution.py:33
  64.5 6.2 %collective-permute-start.25 = (bf16[16,2048]{1,0:T(8,128)(2,1)S(1)}, bf16[16,2048]{1,0:T(8,128)(2,1)S(1)}, u32[]{:S(2)}, u32[]{:S(2)}) collective-permute-start(bf16[16,2048]{1,0:T(8,128)(2,1)S(1)} %sum_x3.1), channel_id=1, source_target_pairs={{0,12},{4,8},{8,4},{12,0},{1,13},{5,9},{9,5},{13,1},{2,14},{6,10},... | collective-permute-start | bytes 196616 | tf_op jit(solution)/shard_map/ppermute | solution.py:33

commit v3 on v2

--- a/solution.py
+++ b/solution.py
@@ -70,11 +70,8 @@
     back, tp_count, pp_count, lengths_hbm, ids_hbm, codes_hbm, query_hbm, weight_hbm, residual_hbm,
     gain_hbm, *refs
 ):
-    gate_hbm, query_ref, weight_ref, gain_ref, mask_ref, order_ref, residual_ref, info_ref = refs[
-        :8
-    ]
-    gate_refs = refs[8:-5]
-    lengths, ids, codes, residual_all, sem = refs[-5:]
+    query_ref, weight_ref, gain_ref, mask_ref, order_ref, residual_ref, info_ref = refs[:7]
+    lengths, ids, codes, residual_all, sem = refs[7:]
     pairs = [
         (lengths_hbm, lengths),
         (ids_hbm, ids),
@@ -83,7 +80,7 @@
         (query_hbm, query_ref),
         (gain_hbm, gain_ref),
         (weight_hbm, weight_ref),
-    ] + columns(gate_hbm, gate_refs)
+    ]
     copies = [pltpu.make_async_copy(a, b, sem.at[i]) for i, (a, b) in enumerate(pairs)]
     for c in copies:
         c.start()
@@ -121,31 +118,44 @@
         c.wait()
 
 
-def load_kernel(n_after, source, *refs):
-    *targets, token_ref, sem = refs[n_after:]
-    copies = [
-        pltpu.make_async_copy(a, b, sem.at[i])
-        for i, (a, b) in enumerate(columns(source, targets))
-    ]
-    for c in copies:
-        c.start()
-    token_ref[...] = jnp.zeros_like(token_ref)
-    for c in copies:
-        c.wait()
-
-
-def load(array, parts, wanted, after, name):
-    rows, cols = array.shape
-    out = call(
-        functools.partial(load_kernel, len(after)),
-        [sds((rows, cols // parts), array.dtype)] * wanted + [sds((8, LANES), jnp.float32)],
+def load_kernel(first, n_after, source, *refs):
+    target, sem = refs[n_after:]
+    copy = pltpu.make_async_copy(
+        source.at[:, pl.ds(first, target.shape[1])], target, sem
+    )
+    copy.start()
+    copy.wait()
+
+
+def load(array, first, columns, after, name):
+    rows = array.shape[0]
+    return call(
+        functools.partial(load_kernel, first, len(after)),
+        sds((rows, columns), array.dtype),
         [(HBM, array)] + [(ANY, a) for a in after],
-        scratch=[pltpu.SemaphoreType.DMA((wanted,))],
+        scratch=[pltpu.SemaphoreType.DMA],
         vmem=1,
         name=name,
-        cost_us=array.size * wanted / parts * 2 / 3.4e6,
-    )
-    return out[:-1], out[-1]
+        cost_us=rows * columns * 2 / 3.4e6,
+    )
+
+
+def join_kernel(n, n_after, *refs):
+    start = 0
+    for r in refs[:n]:
+        refs[n + n_after][start : start + r.shape[0], :] = r[...]
+        start += r.shape[0]
+
+
+def join(arrays, after, name):
+    rows = sum(a.shape[0] for a in arrays)
+    return call(
+        functools.partial(join_kernel, len(arrays), len(after)),
+        sds((rows, arrays[0].shape[1]), arrays[0].dtype),
+        [(VMEM, a) for a in arrays] + [(ANY, a) for a in after],
+        name=name,
+        cost_us=0.1,
+    )
 
 
 def attention_kernel(back, kv_heads, group, q_ref, mask_ref, order_ref, *refs):
@@ -356,7 +366,7 @@
     experts = max(1, E // sec_count)
     per_expert = w_gate.shape[2] // experts
     span = (back + 1) * block
-    query_v, weight_v, gain_v, mask, order, residual_own, info, *gate_v = call(
+    query_v, weight_v, gain_v, mask, order, residual_own, info = call(
         functools.partial(prepare_kernel, back, tp_count, pp_count),
         [
             sds(query.shape, bf16),
@@ -366,13 +376,12 @@
             sds((block, block), bf16),
             sds((own_rows, width), f32),
             sds((own_rows, LANES), bf16),
-        ]
-        + [sds((width, per_expert), bf16)] * experts,
+        ],
         [
             (HBM, a)
             for a in (
                 doc_lengths, expert_ids.T, gate_codes.T, query, out_weight, residual,
-                norm_gain.reshape(1, width), w_gate[0],
+                norm_gain.reshape(1, width),
             )
         ],
         scratch=[
@@ -380,11 +389,11 @@
             pltpu.VMEM((2, block), jnp.int32),
             pltpu.VMEM((2, block), jnp.int32),
             pltpu.VMEM(residual.shape, bf16),
-            pltpu.SemaphoreType.DMA((7 + experts,)),
+            pltpu.SemaphoreType.DMA((7,)),
         ],
         vmem=6,
         name="prepare",
-        cost_us=6.0,
+        cost_us=2.0,
     )
     half = block // pp_count
     keep, send = call(
@@ -400,27 +409,42 @@
         [keep] + [xor_swap(send, "pp", 1)], [own_rows], [own_rows] * (tp_count - 1), "sum_cores"
     )
     got = [xor_swap(sends[k - 1], "tp", k) for k in range(1, tp_count)]
-    up_v, token = load(w_up[0], experts, 1, [own], "load_up")
     stream, normed = call(
         functools.partial(norm_kernel, tp_count),
         [sds((own_rows, width), f32), sds((own_rows, width + LANES), bf16)],
-        [(VMEM, a) for a in (residual_own, gain_v, info, own, *got)] + [(ANY, token)],
+        [(VMEM, a) for a in (residual_own, gain_v, info, own, *got)],
         name="norm",
         cost_us=0.2,
     )
 
-    groups = min(4, sec_count)
-    near = [normed] + [xor_swap(normed, "sec", k) for k in range(1, sec_count)]
-    per_group = sec_count // groups
-    near = [
-        jnp.concatenate(near[g * per_group : (g + 1) * per_group], axis=0)
-        if per_group > 1
-        else near[g]
-        for g in range(groups)
-    ]
-    rows = [[r] + [xor_swap(r, "tp", k) for k in range(1, tp_count)] for r in near]
-    rows = [rows[g][k] for k in range(tp_count) for g in range(groups)]
-    rows = rows + [xor_swap(r, "pp", k) for k in range(1, pp_count) for r in rows]
+    near = {k: xor_swap(normed, "sec", k) for k in range(sec_count - 1, 0, -1)}
+    near[0] = normed
+    split = max(1, sec_count // 2)
+    groups = [g for g in ([0], list(range(1, split)), list(range(split, sec_count))) if g]
+    gate_v = [load(w_gate[0], 0, per_expert, [normed], "load_gate")]
+    up_v = []
+    last_load = gate_v[0]
+    rows = []
+    for i, g in enumerate(groups):
+        piece = near[0] if i == 0 else join([near[k] for k in g], [last_load], "join_z")
+        rows.append([piece] + [xor_swap(piece, "tp", k) for k in range(1, tp_count)])
+        if i == 1 or (i == 0 and len(groups) == 1):
+            last_load = load(w_up[0], 0, per_expert, [piece, last_load], "load_up")
+            up_v.append(last_load)
+        if i == len(groups) - 1:
+            for x in range(1, experts):
+                last_load = load(
+                    w_gate[0], x * per_expert, per_expert, [piece, last_load], "load_gate"
+                )
+                gate_v.append(last_load)
+    rows = [[rows[g][k] for g in range(len(groups))] for k in range(tp_count)]
+    early = join(
+        rows[0] + [r for k in range(1, tp_count) for r in rows[k][:-1]], [], "join_early"
+    )
+    late = join([rows[k][-1] for k in range(1, tp_count)], [last_load], "join_late")
+    early = [early] + [xor_swap(early, "pp", k) for k in range(1, pp_count)]
+    late = [late] + [xor_swap(late, "pp", k) for k in range(1, pp_count)]
+    rows = [r for pair in zip(early, late) for r in pair]
 
     halves = max(1, sec_count // E)
     count = sec_count * block
@@ -447,26 +471,26 @@
         cost_us=12.0,
     )
 
-    piece = kept // (tp_count * groups)
-    own, sends = add(
-        [keep, xor_swap(send, "pp", 1)], [piece] * groups, [piece] * (groups * (tp_count - 1)), "sum_cores2"
-    )
+    sizes = [len(g) * own_rows for g in groups]
+    last = len(groups) - 1
+    outs = add(
+        [keep, xor_swap(send, "pp", 1)],
+        sizes,
+        [z for k in range(1, tp_count) for z in sizes[:-1]] + sizes[-1:] * (tp_count - 1),
+        "sum_cores2",
+    )
+    mine, sends = outs
+    theirs = [
+        [sends[(k - 1) * last + g] for k in range(1, tp_count)] for g in range(last)
+    ] + [sends[(tp_count - 1) * last :]]
     final = [stream]
-    for g in list(range(1, groups)) + [0]:
-        got = [xor_swap(sends[(k - 1) * groups + g], "tp", k) for k in range(1, tp_count)]
-        if g == 0 and per_group == 1:
-            final += [own[0]] + got
+    for g in range(last, -1, -1):
+        got = [xor_swap(theirs[g][k - 1], "tp", k) for k in range(1, tp_count)]
+        if g == 0:
+            final += [mine[0]] + got
             continue
-        kept_rows = own_rows if g == 0 else 0
-        mine, out = add(
-            [own[g]] + got,
-            [own_rows] if g == 0 else [],
-            [own_rows] * (per_group - (g == 0)),
-            "sum_x%d" % g,
-        )
-        final += list(mine)
-        for j, o in enumerate(out):
-            final.append(xor_swap(o, "sec", g * per_group + j + (g == 0)))
+        _, out = add([mine[g]] + got, [], [own_rows] * len(groups[g]), "sum_x%d" % g)
+        final += [xor_swap(o, "sec", k) for k, o in zip(groups[g], out)]
     return call(
         functools.partial(add_kernel, 0, len(final)),
         [sds((own_rows, width), bf16)],

time: 71.7 us -> 73.6 us (1.026)
  Pallas kernels: 25.4 us -> 27.3 us
    pallas_call x11 -> x16, Pallas kernels: 25.4 us -> 27.3 us  [call(): pl.pallas_call(kernel, out_shape=out_shape, in_specs=[s for s, _ in args]...]
    ppermute x25 -> x17, waiting for transfers between devices: 18.7 us -> 18.1 us  [xor_swap(): return lax.ppermute(x, axis, [(i, i ^ k) for i in range(n)])]
    ppermute x25 -> x17, starting transfers between devices: 16.9 us -> 17.3 us  [xor_swap(): return lax.ppermute(x, axis, [(i, i ^ k) for i in range(n)])]
  transfers between devices with their start and end apart: 27 -> 19, of which waited for: 14 -> 9; matrix products, arithmetic and copies ran while one was open for 0% -> 0% of each run, Pallas kernels for 15% -> 17%
where the time goes in v3:
time: 73.6 us; the launch traced here: 73.2 us
  Pallas kernels  27.3 us (37%)
  starting transfers between devices  26.7 us (36%)
  waiting for transfers between devices  18.1 us (25%)
  local copies, waits for them, and re-layouts  0.78 us (1%)
    pallas_call x16, Pallas kernels, call(): pl.pallas_call(kernel, out_shape=out_shape, in_specs=[s for s, _ in args]...  27.3 us
    ppermute x17, waiting for transfers between devices, xor_swap(): return lax.ppermute(x, axis, [(i, i ^ k) for i in range(n)])  18.1 us
    ppermute x17, starting transfers between devices, xor_swap(): return lax.ppermute(x, axis, [(i, i ^ k) for i in range(n)])  17.3 us
    ppermute x2, starting transfers between devices, per_device(): lax.ppermute(kv, 'sec', [(i, i + k) for i in range(sec_count - k)])  9.43 us
  transfers between devices with their start and end apart: 19, of which 9 were waited for; matrix products, arithmetic and copies ran while one was open for 0% of the time, Pallas kernels for 17%

profile of v3, /device:TPU:0, one launch (start us, length us, event | category | flops | bytes accessed | tf_op | source)
XLA Modules:
  0.0 73.2 jit_solution(14762496177165071263)
XLA Ops:
  0.0 0.8 %constant_dynamic-slice_fusion = (bf16[64,256]{1,0:T(8,128)(2,1)S(1)}, bf16[64,256]{1,0:T(8,128)(2,1)S(1)}) fusion(bf16[64,512]{1,0:T(8,128)(2,1)} %param.14, s32[]{:T(128)S(6)} %select_n.10, bf16[64,512]{1,0:T(8,128)(2,1)} %param.13), kind=kLoop, calls=%fused_computation.1 | loop fusion | bytes 131076 | tf_op jit(solution)/shard_map/dynamic_slice | solution.py:358
  0.8 4.9 %collective-permute-start.1 = (bf16[64,512]{1,0:T(8,128)(2,1)S(1)}, bf16[64,512]{1,0:T(8,128)(2,1)S(1)}, u32[]{:S(2)}, u32[]{:S(2)}) collective-permute-start(bf16[64,512]{1,0:T(8,128)(2,1)S(1)} %pad_maximum_fusion.refs_2_), channel_id=1, source_target_pairs={{0,4},{4,8},{8,12},{1,5},{5,9},{9,13},{2,6},{6,10},{10,14},{3,7},{... | collective-permute-start | bytes 196616 | tf_op jit(solution)/shard_map/ppermute | solution.py:362
  5.7 4.5 %collective-permute-start = (bf16[64,512]{1,0:T(8,128)(2,1)S(1)}, bf16[64,512]{1,0:T(8,128)(2,1)S(1)}, u32[]{:S(2)}, u32[]{:S(2)}) collective-permute-start(bf16[64,512]{1,0:T(8,128)(2,1)S(1)} %pad_maximum_fusion.refs_2_), channel_id=1, source_target_pairs={{0,8},{4,12},{1,9},{5,13},{2,10},{6,14},{3,11},{7,15},{16,24},{20,... | collective-permute-start | bytes 196616 | tf_op jit(solution)/shard_map/ppermute | solution.py:362
  10.2 2.5 %prepare.1 = (bf16[64,1024]{1,0:T(8,128)(2,1)S(1)}, bf16[1024,2048]{1,0:T(8,128)(2,1)S(1)}, f32[1,2048]{1,0:T(1,128)S(1)}, f32[64,192]{1,0:T(8,128)S(1)}, bf16[6...) custom-call(s32[8]{0:T(128)} %lengths_hbm.1, s32[2,64]{1,0:T(2,128)} %bitcast.12, ...), custom_call_target="tpu_custom_call" | custom-call | bytes 6800000 | tf_op jit(solution)/shard_map/prepare/pallas_call | solution.py:41
  12.7 1.4 %attention.1 = (f32[32,2048]{1,0:T(8,128)S(1)}, bf16[32,2048]{1,0:T(8,128)(2,1)S(1)}) custom-call(bf16[64,1024]{1,0:T(8,128)(2,1)S(1)} %get-tuple-element.31.q_ref, f32[64,192]{1,0:T(8,128)S(1)} %get-tuple-element.32.mask_ref, bf16[64,64]{1,0:T(8,128)(2,1)S(1)} %get-tuple-element.33.order_ref, bf16[64,512]{1,0:T(8,128)(2,1)S(1)} %collective-permute-done.refs_0_, ...), custom_call_target="tpu_custom_call" | custom-call | bytes 8160000 | tf_op jit(solution)/shard_map/attention/pallas_call | solution.py:41
  14.2 1.3 %collective-permute-done.2.refs_1_ = bf16[32,2048]{1,0:T(8,128)(2,1)S(1)} collective-permute-done((bf16[32,2048]{1,0:T(8,128)(2,1)S(1)}, bf16[32,2048]{1,0:T(8,128)(2,1)S(1)}, u32[]{:S(2)}, u32[]{:S(2)}) %collective-permute-start.2) | collective-permute-done | bytes 131104 | tf_op jit(solution)/shard_map/ppermute | solution.py:33
  15.6 1.6 %collective-permute-start.3 = (bf16[16,2048]{1,0:T(8,128)(2,1)S(1)}, bf16[16,2048]{1,0:T(8,128)(2,1)S(1)}, u32[]{:S(2)}, u32[]{:S(2)}) collective-permute-start(bf16[16,2048]{1,0:T(8,128)(2,1)S(1)} %get-tuple-element.38), channel_id=1, source_target_pairs={{0,2},{2,0},{1,3},{3,1},{4,6},{6,4},{5,7},{7,5},{8,10},{10,8},{9,1... | collective-permute-start | bytes 196616 | tf_op jit(solution)/shard_map/ppermute | solution.py:33
  17.2 2.8 %collective-permute-done.3.refs_1_ = bf16[16,2048]{1,0:T(8,128)(2,1)S(1)} collective-permute-done((bf16[16,2048]{1,0:T(8,128)(2,1)S(1)}, bf16[16,2048]{1,0:T(8,128)(2,1)S(1)}, u32[]{:S(2)}, u32[]{:S(2)}) %collective-permute-start.3) | collective-permute-done | bytes 65568 | tf_op jit(solution)/shard_map/ppermute | solution.py:33
  19.9 0.1 norm.1
  20.1 1.6 %collective-permute-start.7 = (bf16[16,2176]{1,0:T(8,128)(2,1)S(1)}, bf16[16,2176]{1,0:T(8,128)(2,1)S(1)}, u32[]{:S(2)}, u32[]{:S(2)}) collective-permute-start(bf16[16,2176]{1,0:T(8,128)(2,1)S(1)} %get-tuple-element.40.refs_0_), channel_id=1, source_target_pairs={{0,2},{2,0},{1,3},{3,1},{4,6},{6,4},{5,7},{7,5},{8,10},{10,8},{9,1... | collective-permute-start | bytes 208904 | tf_op jit(solution)/shard_map/ppermute | solution.py:33
  21.7 4.0 %collective-permute-start.6 = (bf16[16,2176]{1,0:T(8,128)(2,1)S(1)}, bf16[16,2176]{1,0:T(8,128)(2,1)S(1)}, u32[]{:S(2)}, u32[]{:S(2)}) collective-permute-start(bf16[16,2176]{1,0:T(8,128)(2,1)S(1)} %get-tuple-element.40.refs_0_), channel_id=1, source_target_pairs={{0,12},{4,8},{8,4},{12,0},{1,13},{5,9},{9,5},{13,1},{2,14},{6,10},... | collective-permute-start | bytes 208904 | tf_op jit(solution)/shard_map/ppermute | solution.py:33
  25.7 3.4 %load_gate.2.refs_1_.refs_4_ = bf16[2048,2048]{1,0:T(8,128)(2,1)S(1)} custom-call(bf16[2048,4096]{1,0:T(8,128)(2,1)} %bitcast.8, bf16[16,2176]{1,0:T(8,128)(2,1)S(1)} %get-tuple-element.40.refs_0_), custom_call_target="tpu_custom_call" | custom-call | bytes 8388607 | tf_op jit(solution)/shard_map/load_gate/pallas_call | solution.py:41
  29.2 0.6 collective-permute-start.8
  29.8 3.4 %load_up.1.refs_2_.refs_1_.refs_6_ = bf16[2048,2048]{1,0:T(8,128)(2,1)S(1)} custom-call(bf16[2048,4096]{1,0:T(8,128)(2,1)} %bitcast.6, bf16[16,2176]{1,0:T(8,128)(2,1)S(1)} %join_z.2.refs_0_.refs_1_, bf16[2048,2048]{1,0:T(8,128)(2,1)S(1)} %load_gate.2.refs_1_.refs_4_), custom_call_target="tpu_custom_call" | custom-call | bytes 8388607 | tf_op jit(solution)/shard_map/load_up/pallas_call | solution.py:41
  33.2 0.3 collective-permute-done.8.refs_4_
  33.7 1.2 %collective-permute-start.9 = (bf16[32,2176]{1,0:T(8,128)(2,1)S(1)}, bf16[32,2176]{1,0:T(8,128)(2,1)S(1)}, u32[]{:S(2)}, u32[]{:S(2)}) collective-permute-start(bf16[32,2176]{1,0:T(8,128)(2,1)S(1)} %join_z.3.refs_2_.refs_0_), channel_id=1, source_target_pairs={{0,2},{2,0},{1,3},{3,1},{4,6},{6,4},{5,7},{7,5},{8,10},{10,8},{9,1... | collective-permute-start | bytes 417800 | tf_op jit(solution)/shard_map/ppermute | solution.py:33
  34.9 3.4 %load_gate.3.refs_1_.refs_5_ = bf16[2048,2048]{1,0:T(8,128)(2,1)S(1)} custom-call(bf16[2048,4096]{1,0:T(8,128)(2,1)} %bitcast.9, bf16[32,2176]{1,0:T(8,128)(2,1)S(1)} %join_z.3.refs_2_.refs_0_, bf16[2048,2048]{1,0:T(8,128)(2,1)S(1)} %load_up.1.refs_2_.refs_1_.refs_6_), custom_call_target="tpu_custom_call" | custom-call | bytes 8388607 | tf_op jit(solution)/shard_map/load_gate/pallas_call | solution.py:41
  38.3 1.4 %collective-permute-done.9.refs_0_ = bf16[32,2176]{1,0:T(8,128)(2,1)S(1)} collective-permute-done((bf16[32,2176]{1,0:T(8,128)(2,1)S(1)}, bf16[32,2176]{1,0:T(8,128)(2,1)S(1)}, u32[]{:S(2)}, u32[]{:S(2)}) %collective-permute-start.9) | collective-permute-done | bytes 139296 | tf_op jit(solution)/shard_map/ppermute | solution.py:33
  39.8 1.3 %collective-permute-done.11.refs_3_ = bf16[32,2176]{1,0:T(8,128)(2,1)S(1)} collective-permute-done((bf16[32,2176]{1,0:T(8,128)(2,1)S(1)}, bf16[32,2176]{1,0:T(8,128)(2,1)S(1)}, u32[]{:S(2)}, u32[]{:S(2)}) %collective-permute-start.11) | collective-permute-done | bytes 139296 | tf_op jit(solution)/shard_map/ppermute | solution.py:33
  41.2 12.3 %experts.1 = (f32[128,2048]{1,0:T(8,128)S(1)}, bf16[128,2048]{1,0:T(8,128)(2,1)S(1)}) custom-call(bf16[96,2176]{1,0:T(8,128)(2,1)S(1)} %join_early.1.refs_0_, bf16[32,2176]{1,0:T(8,128)(2,1)S(1)} %join_late.1.refs_1_, bf16[96,2176]{1,0:T(8,128)(2,1)S(1)} %collective-permute-done.10.refs_2_, bf16[32,2176]{1,0:T(8,128)(2,1)S(1)} %collective-permute-done.11.refs_3_, ...), custom_call_target="tpu_custom_call" | custom-call | bytes 40800000 | tf_op jit(solution)/shard_map/experts/pallas_call | solution.py:41
  53.5 0.2 collective-permute-start.12
  53.7 1.8 %collective-permute-done.12.refs_1_ = bf16[128,2048]{1,0:T(8,128)(2,1)S(1)} collective-permute-done((bf16[128,2048]{1,0:T(8,128)(2,1)S(1)}, bf16[128,2048]{1,0:T(8,128)(2,1)S(1)}, u32[]{:S(2)}, u32[]{:S(2)}) %collective-permute-start.12) | collective-permute-done | bytes 524320 | tf_op jit(solution)/shard_map/ppermute | solution.py:33
  55.5 1.2 %collective-permute-start.13 = (bf16[32,2048]{1,0:T(8,128)(2,1)S(1)}, bf16[32,2048]{1,0:T(8,128)(2,1)S(1)}, u32[]{:S(2)}, u32[]{:S(2)}) collective-permute-start(bf16[32,2048]{1,0:T(8,128)(2,1)S(1)} %get-tuple-element.44), channel_id=1, source_target_pairs={{0,2},{2,0},{1,3},{3,1},{4,6},{6,4},{5,7},{7,5},{8,10},{10,8},{9,1... | collective-permute-start | bytes 393224 | tf_op jit(solution)/shard_map/ppermute | solution.py:33
  56.8 0.9 %collective-permute-start.16 = (bf16[16,2048]{1,0:T(8,128)(2,1)S(1)}, bf16[16,2048]{1,0:T(8,128)(2,1)S(1)}, u32[]{:S(2)}, u32[]{:S(2)}) collective-permute-start(bf16[16,2048]{1,0:T(8,128)(2,1)S(1)} %get-tuple-element.48), channel_id=1, source_target_pairs={{0,2},{2,0},{1,3},{3,1},{4,6},{6,4},{5,7},{7,5},{8,10},{10,8},{9,1... | collective-permute-start | bytes 196616 | tf_op jit(solution)/shard_map/ppermute | solution.py:33
  57.6 1.2 %collective-permute-start.18 = (bf16[16,2048]{1,0:T(8,128)(2,1)S(1)}, bf16[16,2048]{1,0:T(8,128)(2,1)S(1)}, u32[]{:S(2)}, u32[]{:S(2)}) collective-permute-start(bf16[16,2048]{1,0:T(8,128)(2,1)S(1)} %get-tuple-element.50), channel_id=1, source_target_pairs={{0,2},{2,0},{1,3},{3,1},{4,6},{6,4},{5,7},{7,5},{8,10},{10,8},{9,1... | collective-permute-start | bytes 196616 | tf_op jit(solution)/shard_map/ppermute | solution.py:33
  58.8 4.5 %collective-permute-done.16.refs_1_ = bf16[16,2048]{1,0:T(8,128)(2,1)S(1)} collective-permute-done((bf16[16,2048]{1,0:T(8,128)(2,1)S(1)}, bf16[16,2048]{1,0:T(8,128)(2,1)S(1)}, u32[]{:S(2)}, u32[]{:S(2)}) %collective-permute-start.16) | collective-permute-done | bytes 65568 | tf_op jit(solution)/shard_map/ppermute | solution.py:33
  63.3 0.6 collective-permute-start.17
  63.9 2.5 %collective-permute-start.14 = (bf16[16,2048]{1,0:T(8,128)(2,1)S(1)}, bf16[16,2048]{1,0:T(8,128)(2,1)S(1)}, u32[]{:S(2)}, u32[]{:S(2)}) collective-permute-start(bf16[16,2048]{1,0:T(8,128)(2,1)S(1)} %get-tuple-element.45), channel_id=1, source_target_pairs={{0,8},{4,12},{8,0},{12,4},{1,9},{5,13},{9,1},{13,5},{2,10},{6,14},... | collective-permute-start | bytes 196616 | tf_op jit(solution)/shard_map/ppermute | solution.py:33
  66.4 1.5 %collective-permute-start.15 = (bf16[16,2048]{1,0:T(8,128)(2,1)S(1)}, bf16[16,2048]{1,0:T(8,128)(2,1)S(1)}, u32[]{:S(2)}, u32[]{:S(2)}) collective-permute-start(bf16[16,2048]{1,0:T(8,128)(2,1)S(1)} %get-tuple-element.46), channel_id=1, source_target_pairs={{0,12},{4,8},{8,4},{12,0},{1,13},{5,9},{9,5},{13,1},{2,14},{6,10},... | collective-permute-start | bytes 196616 | tf_op jit(solution)/shard_map/ppermute | solution.py:33
  67.9 2.6 %collective-permute-done.14.refs_1_ = bf16[16,2048]{1,0:T(8,128)(2,1)S(1)} collective-permute-done((bf16[16,2048]{1,0:T(8,128)(2,1)S(1)}, bf16[16,2048]{1,0:T(8,128)(2,1)S(1)}, u32[]{:S(2)}, u32[]{:S(2)}) %collective-permute-start.14) | collective-permute-done | bytes 65568 | tf_op jit(solution)/shard_map/ppermute | solution.py:33
  70.5 2.0 %collective-permute-done.15.refs_2_ = bf16[16,2048]{1,0:T(8,128)(2,1)S(1)} collective-permute-done((bf16[16,2048]{1,0:T(8,128)(2,1)S(1)}, bf16[16,2048]{1,0:T(8,128)(2,1)S(1)}, u32[]{:S(2)}, u32[]{:S(2)}) %collective-permute-start.15) | collective-permute-done | bytes 65568 | tf_op jit(solution)/shard_map/ppermute | solution.py:33
  72.5 0.7 total.1
  (24 shorter events, 0.5 us)
Async XLA Ops:
  0.8 11.9 %collective-permute-start.1 = (bf16[64,512]{1,0:T(8,128)(2,1)S(1)}, bf16[64,512]{1,0:T(8,128)(2,1)S(1)}, u32[]{:S(2)}, u32[]{:S(2)}) collective-permute-start(bf16[64,512]{1,0:T(8,128)(2,1)S(1)} %pad_maximum_fusion.refs_2_), channel_id=1, source_target_pairs={{0,4},{4,8},{8,12},{1,5},{5,9},{9,13},{2,6},{6,10},{10,14},{3,7},{... | collective-permute-start | bytes 196616 | tf_op jit(solution)/shard_map/ppermute | solution.py:362
  5.7 7.0 %collective-permute-start = (bf16[64,512]{1,0:T(8,128)(2,1)S(1)}, bf16[64,512]{1,0:T(8,128)(2,1)S(1)}, u32[]{:S(2)}, u32[]{:S(2)}) collective-permute-start(bf16[64,512]{1,0:T(8,128)(2,1)S(1)} %pad_maximum_fusion.refs_2_), channel_id=1, source_target_pairs={{0,8},{4,12},{1,9},{5,13},{2,10},{6,14},{3,11},{7,15},{16,24},{20,... | collective-permute-start | bytes 196616 | tf_op jit(solution)/shard_map/ppermute | solution.py:362
  14.2 1.4 %collective-permute-start.2 = (bf16[32,2048]{1,0:T(8,128)(2,1)S(1)}, bf16[32,2048]{1,0:T(8,128)(2,1)S(1)}, u32[]{:S(2)}, u32[]{:S(2)}) collective-permute-start(bf16[32,2048]{1,0:T(8,128)(2,1)S(1)} %get-tuple-element.36), channel_id=1, source_target_pairs={{0,1},{1,0},{2,3},{3,2},{4,5},{5,4},{6,7},{7,6},{8,9},{9,8},{10,11... | collective-permute-start | bytes 393224 | tf_op jit(solution)/shard_map/ppermute | solution.py:33
  15.6 4.3 %collective-permute-start.3 = (bf16[16,2048]{1,0:T(8,128)(2,1)S(1)}, bf16[16,2048]{1,0:T(8,128)(2,1)S(1)}, u32[]{:S(2)}, u32[]{:S(2)}) collective-permute-start(bf16[16,2048]{1,0:T(8,128)(2,1)S(1)} %get-tuple-element.38), channel_id=1, source_target_pairs={{0,2},{2,0},{1,3},{3,1},{4,6},{6,4},{5,7},{7,5},{8,10},{10,8},{9,1... | collective-permute-start | bytes 196616 | tf_op jit(solution)/shard_map/ppermute | solution.py:33
  20.1 9.1 %collective-permute-start.4 = (bf16[16,2176]{1,0:T(8,128)(2,1)S(1)}, bf16[16,2176]{1,0:T(8,128)(2,1)S(1)}, u32[]{:S(2)}, u32[]{:S(2)}) collective-permute-start(bf16[16,2176]{1,0:T(8,128)(2,1)S(1)} %get-tuple-element.40.refs_0_), channel_id=1, source_target_pairs={{0,4},{4,0},{8,12},{12,8},{1,5},{5,1},{9,13},{13,9},{2,6},{6,2},{1... | collective-permute-start | bytes 208904 | tf_op jit(solution)/shard_map/ppermute | solution.py:33
  20.1 13.1 %collective-permute-start.7 = (bf16[16,2176]{1,0:T(8,128)(2,1)S(1)}, bf16[16,2176]{1,0:T(8,128)(2,1)S(1)}, u32[]{:S(2)}, u32[]{:S(2)}) collective-permute-start(bf16[16,2176]{1,0:T(8,128)(2,1)S(1)} %get-tuple-element.40.refs_0_), channel_id=1, source_target_pairs={{0,2},{2,0},{1,3},{3,1},{4,6},{6,4},{5,7},{7,5},{8,10},{10,8},{9,1... | collective-permute-start | bytes 208904 | tf_op jit(solution)/shard_map/ppermute | solution.py:33
  21.7 11.5 %collective-permute-start.6 = (bf16[16,2176]{1,0:T(8,128)(2,1)S(1)}, bf16[16,2176]{1,0:T(8,128)(2,1)S(1)}, u32[]{:S(2)}, u32[]{:S(2)}) collective-permute-start(bf16[16,2176]{1,0:T(8,128)(2,1)S(1)} %get-tuple-element.40.refs_0_), channel_id=1, source_target_pairs={{0,12},{4,8},{8,4},{12,0},{1,13},{5,9},{9,5},{13,1},{2,14},{6,10},... | collective-permute-start | bytes 208904 | tf_op jit(solution)/shard_map/ppermute | solution.py:33
  25.7 7.4 %collective-permute-start.5 = (bf16[16,2176]{1,0:T(8,128)(2,1)S(1)}, bf16[16,2176]{1,0:T(8,128)(2,1)S(1)}, u32[]{:S(2)}, u32[]{:S(2)}) collective-permute-start(bf16[16,2176]{1,0:T(8,128)(2,1)S(1)} %get-tuple-element.40.refs_0_), channel_id=1, source_target_pairs={{0,8},{4,12},{8,0},{12,4},{1,9},{5,13},{9,1},{13,5},{2,10},{6,14},... | collective-permute-start | bytes 208904 | tf_op jit(solution)/shard_map/ppermute | solution.py:33
  29.2 4.4 %collective-permute-start.8 = (bf16[16,2176]{1,0:T(8,128)(2,1)S(1)}, bf16[16,2176]{1,0:T(8,128)(2,1)S(1)}, u32[]{:S(2)}, u32[]{:S(2)}) collective-permute-start(bf16[16,2176]{1,0:T(8,128)(2,1)S(1)} %join_z.2.refs_0_.refs_1_), channel_id=1, source_target_pairs={{0,2},{2,0},{1,3},{3,1},{4,6},{6,4},{5,7},{7,5},{8,10},{10,8},{9,1... | collective-permute-start | bytes 208904 | tf_op jit(solution)/shard_map/ppermute | solution.py:33
  33.6 7.6 %collective-permute-start.10 = (bf16[96,2176]{1,0:T(8,128)(2,1)S(1)}, bf16[96,2176]{1,0:T(8,128)(2,1)S(1)}, u32[]{:S(2)}, u32[]{:S(2)}) collective-permute-start(bf16[96,2176]{1,0:T(8,128)(2,1)S(1)} %join_early.1.refs_0_), channel_id=1, source_target_pairs={{0,1},{1,0},{2,3},{3,2},{4,5},{5,4},{6,7},{7,6},{8,9},{9,8},{10,11... | collective-permute-start | bytes 1253384 | tf_op jit(solution)/shard_map/ppermute | solution.py:33
  33.7 6.1 %collective-permute-start.9 = (bf16[32,2176]{1,0:T(8,128)(2,1)S(1)}, bf16[32,2176]{1,0:T(8,128)(2,1)S(1)}, u32[]{:S(2)}, u32[]{:S(2)}) collective-permute-start(bf16[32,2176]{1,0:T(8,128)(2,1)S(1)} %join_z.3.refs_2_.refs_0_), channel_id=1, source_target_pairs={{0,2},{2,0},{1,3},{3,1},{4,6},{6,4},{5,7},{7,5},{8,10},{10,8},{9,1... | collective-permute-start | bytes 417800 | tf_op jit(solution)/shard_map/ppermute | solution.py:33
  39.8 1.4 %collective-permute-start.11 = (bf16[32,2176]{1,0:T(8,128)(2,1)S(1)}, bf16[32,2176]{1,0:T(8,128)(2,1)S(1)}, u32[]{:S(2)}, u32[]{:S(2)}) collective-permute-start(bf16[32,2176]{1,0:T(8,128)(2,1)S(1)} %join_late.1.refs_1_), channel_id=1, source_target_pairs={{0,1},{1,0},{2,3},{3,2},{4,5},{5,4},{6,7},{7,6},{8,9},{9,8},{10,11... | collective-permute-start | bytes 417800 | tf_op jit(solution)/shard_map/ppermute | solution.py:33
  53.5 2.0 %collective-permute-start.12 = (bf16[128,2048]{1,0:T(8,128)(2,1)S(1)}, bf16[128,2048]{1,0:T(8,128)(2,1)S(1)}, u32[]{:S(2)}, u32[]{:S(2)}) collective-permute-start(bf16[128,2048]{1,0:T(8,128)(2,1)S(1)} %get-tuple-element.42), channel_id=1, source_target_pairs={{0,1},{1,0},{2,3},{3,2},{4,5},{5,4},{6,7},{7,6},{8,9},{9,8},{10,11... | collective-permute-start | bytes 1572872 | tf_op jit(solution)/shard_map/ppermute | solution.py:33
  55.5 8.4 %collective-permute-start.13 = (bf16[32,2048]{1,0:T(8,128)(2,1)S(1)}, bf16[32,2048]{1,0:T(8,128)(2,1)S(1)}, u32[]{:S(2)}, u32[]{:S(2)}) collective-permute-start(bf16[32,2048]{1,0:T(8,128)(2,1)S(1)} %get-tuple-element.44), channel_id=1, source_target_pairs={{0,2},{2,0},{1,3},{3,1},{4,6},{6,4},{5,7},{7,5},{8,10},{10,8},{9,1... | collective-permute-start | bytes 393224 | tf_op jit(solution)/shard_map/ppermute | solution.py:33
  56.8 6.5 %collective-permute-start.16 = (bf16[16,2048]{1,0:T(8,128)(2,1)S(1)}, bf16[16,2048]{1,0:T(8,128)(2,1)S(1)}, u32[]{:S(2)}, u32[]{:S(2)}) collective-permute-start(bf16[16,2048]{1,0:T(8,128)(2,1)S(1)} %get-tuple-element.48), channel_id=1, source_target_pairs={{0,2},{2,0},{1,3},{3,1},{4,6},{6,4},{5,7},{7,5},{8,10},{10,8},{9,1... | collective-permute-start | bytes 196616 | tf_op jit(solution)/shard_map/ppermute | solution.py:33
  57.6 10.3 %collective-permute-start.18 = (bf16[16,2048]{1,0:T(8,128)(2,1)S(1)}, bf16[16,2048]{1,0:T(8,128)(2,1)S(1)}, u32[]{:S(2)}, u32[]{:S(2)}) collective-permute-start(bf16[16,2048]{1,0:T(8,128)(2,1)S(1)} %get-tuple-element.50), channel_id=1, source_target_pairs={{0,2},{2,0},{1,3},{3,1},{4,6},{6,4},{5,7},{7,5},{8,10},{10,8},{9,1... | collective-permute-start | bytes 196616 | tf_op jit(solution)/shard_map/ppermute | solution.py:33
  63.3 4.6 %collective-permute-start.17 = (bf16[16,2048]{1,0:T(8,128)(2,1)S(1)}, bf16[16,2048]{1,0:T(8,128)(2,1)S(1)}, u32[]{:S(2)}, u32[]{:S(2)}) collective-permute-start(bf16[16,2048]{1,0:T(8,128)(2,1)S(1)} %sum_x1.1), channel_id=1, source_target_pairs={{0,4},{4,0},{8,12},{12,8},{1,5},{5,1},{9,13},{13,9},{2,6},{6,2},{1... | collective-permute-start | bytes 196616 | tf_op jit(solution)/shard_map/ppermute | solution.py:33
  63.9 6.6 %collective-permute-start.14 = (bf16[16,2048]{1,0:T(8,128)(2,1)S(1)}, bf16[16,2048]{1,0:T(8,128)(2,1)S(1)}, u32[]{:S(2)}, u32[]{:S(2)}) collective-permute-start(bf16[16,2048]{1,0:T(8,128)(2,1)S(1)} %get-tuple-element.45), channel_id=1, source_target_pairs={{0,8},{4,12},{8,0},{12,4},{1,9},{5,13},{9,1},{13,5},{2,10},{6,14},... | collective-permute-start | bytes 196616 | tf_op jit(solution)/shard_map/ppermute | solution.py:33
  66.4 6.2 %collective-permute-start.15 = (bf16[16,2048]{1,0:T(8,128)(2,1)S(1)}, bf16[16,2048]{1,0:T(8,128)(2,1)S(1)}, u32[]{:S(2)}, u32[]{:S(2)}) collective-permute-start(bf16[16,2048]{1,0:T(8,128)(2,1)S(1)} %get-tuple-element.46), channel_id=1, source_target_pairs={{0,12},{4,8},{8,4},{12,0},{1,13},{5,9},{9,5},{13,1},{2,14},{6,10},... | collective-permute-start | bytes 196616 | tf_op jit(solution)/shard_map/ppermute | solution.py:33

commit v4 on v2

--- a/solution.py
+++ b/solution.py
@@ -222,27 +222,28 @@
     normed_ref[:, width:] = info_ref[...]
 
 
-def experts_kernel(experts, capacity, tile, halves, n_rows, n_gate, n_up, *refs):
+def experts_kernel(experts, capacity, tile, halves, n_rows, *refs):
     rows_in = refs[:n_rows]
-    gate_refs = list(refs[n_rows : n_rows + n_gate])
-    up_refs = list(refs[n_rows + n_gate : n_rows + n_gate + n_up])
-    refs = refs[n_rows + n_gate + n_up :]
-    up_hbm, down_hbm, keep_ref, send_ref, rows_ref, pick_ref, packed_ref, hidden_ref = refs[:8]
-    up_late = list(refs[8 : 8 + experts - n_up])
-    down_ref, up_sem, down_sem = refs[8 + experts - n_up :]
+    gate_first, up_first, gate_hbm, up_hbm, down_hbm, keep_ref, send_ref = refs[
+        n_rows : n_rows + 7
+    ]
+    rows_ref, pick_ref, packed_ref, hidden_ref, gate_ref, up_ref, down_ref, sem = refs[n_rows + 7 :]
     per_expert, width = down_hbm.shape[0] // experts, down_hbm.shape[1]
-    up_copies = [
-        pltpu.make_async_copy(a, b, up_sem.at[i])
-        for i, (a, b) in enumerate(columns(up_hbm, up_late, n_up))
-    ]
-    up_refs += up_late
-    down_copies = [
-        pltpu.make_async_copy(
-            down_hbm.at[pl.ds(x * per_expert, per_expert)], down_ref, down_sem.at[x]
-        )
-        for x in range(experts)
-    ]
-    for c in down_copies[:1] + up_copies:
+    steps = per_expert // tile
+    column = min(512, width)
+    gates, ups, downs = [], [], []
+    for x in range(experts):
+        for s in range(steps if x else 0):
+            cut = pl.ds(x * per_expert + s * tile, tile)
+            at = (x - 1) * steps + s
+            gates.append(pltpu.make_async_copy(gate_hbm.at[:, cut], gate_ref.at[at], sem.at[0, at]))
+            ups.append(pltpu.make_async_copy(up_hbm.at[:, cut], up_ref.at[at], sem.at[1, at]))
+        for c in range(width // column):
+            source = down_hbm.at[pl.ds(x * per_expert, per_expert), pl.ds(c * column, column)]
+            at = x * (width // column) + c
+            downs.append(pltpu.make_async_copy(source, down_ref.at[c], sem.at[2, at]))
+    first_downs = downs[: width // column]
+    for c in first_downs + [c for pair in zip(gates, ups) for c in pair]:
         c.start()
     count = 0
     for r in rows_in:
@@ -271,52 +272,37 @@
         shares.append(jnp.sum(jnp.where(pick, share, 0.0), axis=1, keepdims=True))
         picks.append(jnp.where(pick, 1.0, 0.0).astype(jnp.bfloat16))
     pick_ref[...] = jnp.concatenate(picks, axis=0)
-    column = min(512, width)
-
-    def pack(c, _):
-        cut = pl.ds(pl.multiple_of(c * column, column), column)
-        packed_ref[:, cut] = dot(pick_ref[...], rows_ref[:, cut]).astype(jnp.bfloat16)
-        return 0
-
-    lax.fori_loop(0, width // column, pack, 0)
+    for c in range(0, width, column):
+        packed_ref[:, c : c + column] = dot(pick_ref[...], rows_ref[:, c : c + column]).astype(
+            jnp.bfloat16
+        )
     for x in range(experts):
         mine = slice(x * capacity, (x + 1) * capacity)
-        if x >= n_up:
-            up_copies[x - n_up].wait()
-        gate_ref, up_ref = gate_refs[x], up_refs[x]
-
-        def inner(s, _):
-            cut = pl.ds(pl.multiple_of(s * tile, tile), tile)
-            gate = dot(packed_ref[mine, :], gate_ref[:, cut])
-            up = dot(packed_ref[mine, :], up_ref[:, cut])
-            hidden_ref[mine, cut] = (gate / (1.0 + jnp.exp(-gate)) * up).astype(jnp.bfloat16)
-            return 0
-
-        lax.fori_loop(0, per_expert // tile, inner, 0)
-        down_copies[x].wait()
-
-        def outer(c, _):
-            cut = pl.ds(pl.multiple_of(c * column, column), column)
-            out = dot(hidden_ref[mine, :], down_ref[:, cut])
+        for s in range(steps):
+            cut = slice(s * tile, (s + 1) * tile)
+            at = (x - 1) * steps + s
+            if x:
+                gates[at].wait()
+                ups[at].wait()
+            gate = dot(packed_ref[mine, :], gate_ref[at] if x else gate_first[:, cut])
+            up = dot(packed_ref[mine, :], up_ref[at] if x else up_first[:, cut])
+            half = 0.5 * gate
+            hidden_ref[mine, cut] = ((half + half * jnp.tanh(half)) * up).astype(jnp.bfloat16)
+        for c in range(width // column):
+            cut = slice(c * column, (c + 1) * column)
+            downs[x * (width // column) + c].wait()
+            out = dot(hidden_ref[mine, :], down_ref[c])
             packed_ref[mine, cut] = (out * shares[x]).astype(jnp.bfloat16)
-            return 0
-
-        lax.fori_loop(0, width // column, outer, 0)
-        if x + 1 < experts:
-            down_copies[x + 1].start()
+            if x + 1 < experts:
+                downs[(x + 1) * (width // column) + c].start()
     kept = keep_ref.shape[0]
-
-    def spread(c, _):
-        cut = pl.ds(pl.multiple_of(c * column, column), column)
+    for c in range(0, width, column):
         out = lax.dot_general(
-            pick_ref[...], packed_ref[:, cut], (((0,), (0,)), ((), ())),
+            pick_ref[...], packed_ref[:, c : c + column], (((0,), (0,)), ((), ())),
             preferred_element_type=jnp.float32,
         )
-        keep_ref[:, cut] = out[:kept]
-        send_ref[:, cut] = out[kept:].astype(jnp.bfloat16)
-        return 0
-
-    lax.fori_loop(0, width // column, spread, 0)
+        keep_ref[:, c : c + column] = out[:kept]
+        send_ref[:, c : c + column] = out[kept:].astype(jnp.bfloat16)
 
 
 def per_device(
@@ -367,7 +353,7 @@
             sds((own_rows, width), f32),
             sds((own_rows, LANES), bf16),
         ]
-        + [sds((width, per_expert), bf16)] * experts,
+        + [sds((width, per_expert), bf16)],
         [
             (HBM, a)
             for a in (
@@ -380,11 +366,11 @@
             pltpu.VMEM((2, block), jnp.int32),
             pltpu.VMEM((2, block), jnp.int32),
             pltpu.VMEM(residual.shape, bf16),
-            pltpu.SemaphoreType.DMA((7 + experts,)),
+            pltpu.SemaphoreType.DMA((8,)),
         ],
         vmem=6,
         name="prepare",
-        cost_us=6.0,
+        cost_us=4.0,
     )
     half = block // pp_count
     keep, send = call(
@@ -427,22 +413,24 @@
     capacity = sec_count * MOSTB
     down = w_down[0]
     tile = min(512, down.shape[0] // experts)
+    late = max(1, (experts - 1) * (per_expert // tile))
+    column = min(512, width)
     kept = count // pp_count
     keep, send = call(
-        functools.partial(experts_kernel, experts, capacity, tile, halves, len(rows), experts, 1),
+        functools.partial(experts_kernel, experts, capacity, tile, halves, len(rows)),
         [sds((kept, width), f32), sds((count - kept, width), bf16)],
-        [(VMEM, a) for a in (*rows, *gate_v, *up_v)] + [(HBM, w_up[0]), (HBM, down)],
+        [(VMEM, a) for a in (*rows, *gate_v, *up_v)] + [(HBM, a) for a in (w_gate[0], w_up[0], down)],
         scratch=[
             pltpu.VMEM((count, width + LANES), bf16),
             pltpu.VMEM((experts * capacity, count), bf16),
             pltpu.VMEM((experts * capacity, width), bf16),
             pltpu.VMEM((experts * capacity, down.shape[0] // experts), bf16),
-            *[pltpu.VMEM((width, per_expert), bf16)] * (experts - 1),
-            pltpu.VMEM((per_expert, width), bf16),
-            pltpu.SemaphoreType.DMA((experts,)),
-            pltpu.SemaphoreType.DMA((experts,)),
+            pltpu.VMEM((late, width, tile), bf16),
+            pltpu.VMEM((late, width, tile), bf16),
+            pltpu.VMEM((width // column, per_expert, column), bf16),
+            pltpu.SemaphoreType.DMA((3, max(late, experts * (width // column)))),
         ],
-        vmem=20,
+        vmem=30,
         name="experts",
         cost_us=12.0,
     )

time: 71.7 us -> 71.8 us (level)
  transfers between devices with their start and end apart: 27 -> 27, of which waited for: 14 -> 14; matrix products, arithmetic and copies ran while one was open for 0% -> 0% of each run, Pallas kernels for 15% -> 12%
where the time goes in v4:
time: 71.8 us; the launch traced here: 71.6 us
  starting transfers between devices  26.4 us (37%)
  Pallas kernels  25.6 us (36%)
  waiting for transfers between devices  18.7 us (26%)
  local copies, waits for them, and re-layouts  0.78 us (1%)
    pallas_call x11, Pallas kernels, call(): pl.pallas_call(kernel, out_shape=out_shape, in_specs=[s for s, _ in args]...  25.6 us
    ppermute x25, waiting for transfers between devices, xor_swap(): return lax.ppermute(x, axis, [(i, i ^ k) for i in range(n)])  18.7 us
    ppermute x25, starting transfers between devices, xor_swap(): return lax.ppermute(x, axis, [(i, i ^ k) for i in range(n)])  16.9 us
    ppermute x2, starting transfers between devices, per_device(): lax.ppermute(kv, 'sec', [(i, i + k) for i in range(sec_count - k)])  9.43 us
  transfers between devices with their start and end apart: 27, of which 14 were waited for; matrix products, arithmetic and copies ran while one was open for 0% of the time, Pallas kernels for 12%

profile of v4, /device:TPU:0, one launch (start us, length us, event | category | flops | bytes accessed | tf_op | source)
XLA Modules:
  0.0 71.6 jit_solution(16043551280039858131)
XLA Ops:
  0.0 0.8 %constant_dynamic-slice_fusion = (bf16[64,256]{1,0:T(8,128)(2,1)S(1)}, bf16[64,256]{1,0:T(8,128)(2,1)S(1)}) fusion(bf16[64,512]{1,0:T(8,128)(2,1)} %param.14, s32[]{:T(128)S(6)} %select_n.10, bf16[64,512]{1,0:T(8,128)(2,1)} %param.13), kind=kLoop, calls=%fused_computation.1 | loop fusion | bytes 131076 | tf_op jit(solution)/shard_map/dynamic_slice | solution.py:334
  0.8 4.9 %collective-permute-start.1 = (bf16[64,512]{1,0:T(8,128)(2,1)S(1)}, bf16[64,512]{1,0:T(8,128)(2,1)S(1)}, u32[]{:S(2)}, u32[]{:S(2)}) collective-permute-start(bf16[64,512]{1,0:T(8,128)(2,1)S(1)} %pad_maximum_fusion.refs_2_), channel_id=1, source_target_pairs={{0,4},{4,8},{8,12},{1,5},{5,9},{9,13},{2,6},{6,10},{10,14},{3,7},{... | collective-permute-start | bytes 196616 | tf_op jit(solution)/shard_map/ppermute | solution.py:338
  5.7 4.5 %collective-permute-start = (bf16[64,512]{1,0:T(8,128)(2,1)S(1)}, bf16[64,512]{1,0:T(8,128)(2,1)S(1)}, u32[]{:S(2)}, u32[]{:S(2)}) collective-permute-start(bf16[64,512]{1,0:T(8,128)(2,1)S(1)} %pad_maximum_fusion.refs_2_), channel_id=1, source_target_pairs={{0,8},{4,12},{1,9},{5,13},{2,10},{6,14},{3,11},{7,15},{16,24},{20,... | collective-permute-start | bytes 196616 | tf_op jit(solution)/shard_map/ppermute | solution.py:338
  10.2 4.9 %prepare.1 = (bf16[64,1024]{1,0:T(8,128)(2,1)S(1)}, bf16[1024,2048]{1,0:T(8,128)(2,1)S(1)}, f32[1,2048]{1,0:T(1,128)S(1)}, f32[64,192]{1,0:T(8,128)S(1)}, bf16[6...) custom-call(s32[8]{0:T(128)} %lengths_hbm.1, ...), custom_call_target="tpu_custom_call" | custom-call | bytes 13600000 | tf_op jit(solution)/shard_map/prepare/pallas_call | solution.py:41
  15.2 1.4 %attention.1 = (f32[32,2048]{1,0:T(8,128)S(1)}, bf16[32,2048]{1,0:T(8,128)(2,1)S(1)}) custom-call(bf16[64,1024]{1,0:T(8,128)(2,1)S(1)} %get-tuple-element.34.q_ref, f32[64,192]{1,0:T(8,128)S(1)} %get-tuple-element.35.mask_ref, bf16[64,64]{1,0:T(8,128)(2,1)S(1)} %get-tuple-element.36.order_ref, bf16[64,512]{1,0:T(8,128)(2,1)S(1)} %collective-permute-done.refs_0_, ...), custom_call_target="tpu_custom_call" | custom-call | bytes 8160000 | tf_op jit(solution)/shard_map/attention/pallas_call | solution.py:41
  16.7 1.3 %collective-permute-done.2.refs_1_ = bf16[32,2048]{1,0:T(8,128)(2,1)S(1)} collective-permute-done((bf16[32,2048]{1,0:T(8,128)(2,1)S(1)}, bf16[32,2048]{1,0:T(8,128)(2,1)S(1)}, u32[]{:S(2)}, u32[]{:S(2)}) %collective-permute-start.2) | collective-permute-done | bytes 131104 | tf_op jit(solution)/shard_map/ppermute | solution.py:33
  18.1 1.6 %collective-permute-start.3 = (bf16[16,2048]{1,0:T(8,128)(2,1)S(1)}, bf16[16,2048]{1,0:T(8,128)(2,1)S(1)}, u32[]{:S(2)}, u32[]{:S(2)}) collective-permute-start(bf16[16,2048]{1,0:T(8,128)(2,1)S(1)} %get-tuple-element.41), channel_id=1, source_target_pairs={{0,2},{2,0},{1,3},{3,1},{4,6},{6,4},{5,7},{7,5},{8,10},{10,8},{9,1... | collective-permute-start | bytes 196616 | tf_op jit(solution)/shard_map/ppermute | solution.py:33
  19.6 3.4 %load_up.1 = (bf16[2048,2048]{1,0:T(8,128)(2,1)S(1)}, f32[8,128]{1,0:T(8,128)S(1)}) custom-call(bf16[2048,4096]{1,0:T(8,128)(2,1)} %bitcast.8, f32[16,2048]{1,0:T(8,128)S(1)} %get-tuple-element.40.refs_0_), custom_call_target="tpu_custom_call" | custom-call | bytes 8388607 | tf_op jit(solution)/shard_map/load_up/pallas_call | solution.py:41
  23.2 0.9 %collective-permute-start.7 = (bf16[16,2176]{1,0:T(8,128)(2,1)S(1)}, bf16[16,2176]{1,0:T(8,128)(2,1)S(1)}, u32[]{:S(2)}, u32[]{:S(2)}) collective-permute-start(bf16[16,2176]{1,0:T(8,128)(2,1)S(1)} %get-tuple-element.44.refs_0_), channel_id=1, source_target_pairs={{0,2},{2,0},{1,3},{3,1},{4,6},{6,4},{5,7},{7,5},{8,10},{10,8},{9,1... | collective-permute-start | bytes 208904 | tf_op jit(solution)/shard_map/ppermute | solution.py:33
  24.1 0.8 %collective-permute-start.5 = (bf16[16,2176]{1,0:T(8,128)(2,1)S(1)}, bf16[16,2176]{1,0:T(8,128)(2,1)S(1)}, u32[]{:S(2)}, u32[]{:S(2)}) collective-permute-start(bf16[16,2176]{1,0:T(8,128)(2,1)S(1)} %get-tuple-element.44.refs_0_), channel_id=1, source_target_pairs={{0,8},{4,12},{8,0},{12,4},{1,9},{5,13},{9,1},{13,5},{2,10},{6,14},... | collective-permute-start | bytes 208904 | tf_op jit(solution)/shard_map/ppermute | solution.py:33
  25.0 3.5 %collective-permute-start.4 = (bf16[16,2176]{1,0:T(8,128)(2,1)S(1)}, bf16[16,2176]{1,0:T(8,128)(2,1)S(1)}, u32[]{:S(2)}, u32[]{:S(2)}) collective-permute-start(bf16[16,2176]{1,0:T(8,128)(2,1)S(1)} %get-tuple-element.44.refs_0_), channel_id=1, source_target_pairs={{0,4},{4,0},{8,12},{12,8},{1,5},{5,1},{9,13},{13,9},{2,6},{6,2},{1... | collective-permute-start | bytes 208904 | tf_op jit(solution)/shard_map/ppermute | solution.py:33
  28.5 2.6 %collective-permute-done.6.refs_3_ = bf16[16,2176]{1,0:T(8,128)(2,1)S(1)} collective-permute-done((bf16[16,2176]{1,0:T(8,128)(2,1)S(1)}, bf16[16,2176]{1,0:T(8,128)(2,1)S(1)}, u32[]{:S(2)}, u32[]{:S(2)}) %collective-permute-start.6) | collective-permute-done | bytes 69664 | tf_op jit(solution)/shard_map/ppermute | solution.py:33
  31.1 1.1 %collective-permute-start.10 = (bf16[16,2176]{1,0:T(8,128)(2,1)S(1)}, bf16[16,2176]{1,0:T(8,128)(2,1)S(1)}, u32[]{:S(2)}, u32[]{:S(2)}) collective-permute-start(bf16[16,2176]{1,0:T(8,128)(2,1)S(1)} %collective-permute-done.6.refs_3_), channel_id=1, source_target_pairs={{0,2},{2,0},{1,3},{3,1},{4,6},{6,4},{5,7},{7,5},{8,10},{10,8},{9,1... | collective-permute-start | bytes 208904 | tf_op jit(solution)/shard_map/ppermute | solution.py:33
  32.2 1.5 %collective-permute-start.9 = (bf16[16,2176]{1,0:T(8,128)(2,1)S(1)}, bf16[16,2176]{1,0:T(8,128)(2,1)S(1)}, u32[]{:S(2)}, u32[]{:S(2)}) collective-permute-start(bf16[16,2176]{1,0:T(8,128)(2,1)S(1)} %collective-permute-done.5.refs_2_), channel_id=1, source_target_pairs={{0,2},{2,0},{1,3},{3,1},{4,6},{6,4},{5,7},{7,5},{8,10},{10,8},{9,1... | collective-permute-start | bytes 208904 | tf_op jit(solution)/shard_map/ppermute | solution.py:33
  33.8 0.5 collective-permute-start.8
  34.8 1.3 %collective-permute-done.10.refs_7_ = bf16[16,2176]{1,0:T(8,128)(2,1)S(1)} collective-permute-done((bf16[16,2176]{1,0:T(8,128)(2,1)S(1)}, bf16[16,2176]{1,0:T(8,128)(2,1)S(1)}, u32[]{:S(2)}, u32[]{:S(2)}) %collective-permute-start.10) | collective-permute-done | bytes 69664 | tf_op jit(solution)/shard_map/ppermute | solution.py:33
  36.1 1.5 %collective-permute-done.9.refs_6_ = bf16[16,2176]{1,0:T(8,128)(2,1)S(1)} collective-permute-done((bf16[16,2176]{1,0:T(8,128)(2,1)S(1)}, bf16[16,2176]{1,0:T(8,128)(2,1)S(1)}, u32[]{:S(2)}, u32[]{:S(2)}) %collective-permute-start.9) | collective-permute-done | bytes 69664 | tf_op jit(solution)/shard_map/ppermute | solution.py:33
  37.6 1.1 %collective-permute-done.8.refs_5_ = bf16[16,2176]{1,0:T(8,128)(2,1)S(1)} collective-permute-done((bf16[16,2176]{1,0:T(8,128)(2,1)S(1)}, bf16[16,2176]{1,0:T(8,128)(2,1)S(1)}, u32[]{:S(2)}, u32[]{:S(2)}) %collective-permute-start.8) | collective-permute-done | bytes 69664 | tf_op jit(solution)/shard_map/ppermute | solution.py:33
  38.8 1.1 %collective-permute-done.16.refs_13_ = bf16[16,2176]{1,0:T(8,128)(2,1)S(1)} collective-permute-done((bf16[16,2176]{1,0:T(8,128)(2,1)S(1)}, bf16[16,2176]{1,0:T(8,128)(2,1)S(1)}, u32[]{:S(2)}, u32[]{:S(2)}) %collective-permute-start.16) | collective-permute-done | bytes 69664 | tf_op jit(solution)/shard_map/ppermute | solution.py:33
  40.0 14.8 %experts.1 = (f32[128,2048]{1,0:T(8,128)S(1)}, bf16[128,2048]{1,0:T(8,128)(2,1)S(1)}) custom-call(bf16[16,2176]{1,0:T(8,128)(2,1)S(1)} %get-tuple-element.44.refs_0_, bf16[16,2176]{1,0:T(8,128)(2,1)S(1)} %collective-permute-done.4.refs_1_, bf16[16,2176]{1,0:T(8,128)(2,1)S(1)} %collective-permute-done.5.refs_2_, ...), custom_call_target="tpu_custom_call" | custom-call | bytes 40800000 | tf_op jit(solution)/shard_map/experts/pallas_call | solution.py:41
  55.0 1.7 %collective-permute-done.19.refs_1_ = bf16[128,2048]{1,0:T(8,128)(2,1)S(1)} collective-permute-done((bf16[128,2048]{1,0:T(8,128)(2,1)S(1)}, bf16[128,2048]{1,0:T(8,128)(2,1)S(1)}, u32[]{:S(2)}, u32[]{:S(2)}) %collective-permute-start.19) | collective-permute-done | bytes 524320 | tf_op jit(solution)/shard_map/ppermute | solution.py:33
  56.9 1.2 %collective-permute-start.20 = (bf16[16,2048]{1,0:T(8,128)(2,1)S(1)}, bf16[16,2048]{1,0:T(8,128)(2,1)S(1)}, u32[]{:S(2)}, u32[]{:S(2)}) collective-permute-start(bf16[16,2048]{1,0:T(8,128)(2,1)S(1)} %get-tuple-element.50), channel_id=1, source_target_pairs={{0,2},{2,0},{1,3},{3,1},{4,6},{6,4},{5,7},{7,5},{8,10},{10,8},{9,1... | collective-permute-start | bytes 196616 | tf_op jit(solution)/shard_map/ppermute | solution.py:33
  58.1 0.9 %collective-permute-start.22 = (bf16[16,2048]{1,0:T(8,128)(2,1)S(1)}, bf16[16,2048]{1,0:T(8,128)(2,1)S(1)}, u32[]{:S(2)}, u32[]{:S(2)}) collective-permute-start(bf16[16,2048]{1,0:T(8,128)(2,1)S(1)} %get-tuple-element.52), channel_id=1, source_target_pairs={{0,2},{2,0},{1,3},{3,1},{4,6},{6,4},{5,7},{7,5},{8,10},{10,8},{9,1... | collective-permute-start | bytes 196616 | tf_op jit(solution)/shard_map/ppermute | solution.py:33
  59.0 1.1 %collective-permute-start.24 = (bf16[16,2048]{1,0:T(8,128)(2,1)S(1)}, bf16[16,2048]{1,0:T(8,128)(2,1)S(1)}, u32[]{:S(2)}, u32[]{:S(2)}) collective-permute-start(bf16[16,2048]{1,0:T(8,128)(2,1)S(1)} %get-tuple-element.54), channel_id=1, source_target_pairs={{0,2},{2,0},{1,3},{3,1},{4,6},{6,4},{5,7},{7,5},{8,10},{10,8},{9,1... | collective-permute-start | bytes 196616 | tf_op jit(solution)/shard_map/ppermute | solution.py:33
  60.1 0.9 %collective-permute-start.26 = (bf16[16,2048]{1,0:T(8,128)(2,1)S(1)}, bf16[16,2048]{1,0:T(8,128)(2,1)S(1)}, u32[]{:S(2)}, u32[]{:S(2)}) collective-permute-start(bf16[16,2048]{1,0:T(8,128)(2,1)S(1)} %get-tuple-element.56), channel_id=1, source_target_pairs={{0,2},{2,0},{1,3},{3,1},{4,6},{6,4},{5,7},{7,5},{8,10},{10,8},{9,1... | collective-permute-start | bytes 196616 | tf_op jit(solution)/shard_map/ppermute | solution.py:33
  61.0 0.9 %collective-permute-done.20.refs_1_ = bf16[16,2048]{1,0:T(8,128)(2,1)S(1)} collective-permute-done((bf16[16,2048]{1,0:T(8,128)(2,1)S(1)}, bf16[16,2048]{1,0:T(8,128)(2,1)S(1)}, u32[]{:S(2)}, u32[]{:S(2)}) %collective-permute-start.20) | collective-permute-done | bytes 65568 | tf_op jit(solution)/shard_map/ppermute | solution.py:33
  62.0 1.3 %collective-permute-done.22.refs_1_ = bf16[16,2048]{1,0:T(8,128)(2,1)S(1)} collective-permute-done((bf16[16,2048]{1,0:T(8,128)(2,1)S(1)}, bf16[16,2048]{1,0:T(8,128)(2,1)S(1)}, u32[]{:S(2)}, u32[]{:S(2)}) %collective-permute-start.22) | collective-permute-done | bytes 65568 | tf_op jit(solution)/shard_map/ppermute | solution.py:33
  63.4 1.3 %collective-permute-done.24.refs_1_ = bf16[16,2048]{1,0:T(8,128)(2,1)S(1)} collective-permute-done((bf16[16,2048]{1,0:T(8,128)(2,1)S(1)}, bf16[16,2048]{1,0:T(8,128)(2,1)S(1)}, u32[]{:S(2)}, u32[]{:S(2)}) %collective-permute-start.24) | collective-permute-done | bytes 65568 | tf_op jit(solution)/shard_map/ppermute | solution.py:33
  64.7 1.8 %collective-permute-start.25 = (bf16[16,2048]{1,0:T(8,128)(2,1)S(1)}, bf16[16,2048]{1,0:T(8,128)(2,1)S(1)}, u32[]{:S(2)}, u32[]{:S(2)}) collective-permute-start(bf16[16,2048]{1,0:T(8,128)(2,1)S(1)} %sum_x3.1), channel_id=1, source_target_pairs={{0,12},{4,8},{8,4},{12,0},{1,13},{5,9},{9,5},{13,1},{2,14},{6,10},... | collective-permute-start | bytes 196616 | tf_op jit(solution)/shard_map/ppermute | solution.py:33
  66.9 3.0 %collective-permute-done.23.refs_2_ = bf16[16,2048]{1,0:T(8,128)(2,1)S(1)} collective-permute-done((bf16[16,2048]{1,0:T(8,128)(2,1)S(1)}, bf16[16,2048]{1,0:T(8,128)(2,1)S(1)}, u32[]{:S(2)}, u32[]{:S(2)}) %collective-permute-start.23) | collective-permute-done | bytes 65568 | tf_op jit(solution)/shard_map/ppermute | solution.py:33
  69.9 1.0 %collective-permute-done.25.refs_3_ = bf16[16,2048]{1,0:T(8,128)(2,1)S(1)} collective-permute-done((bf16[16,2048]{1,0:T(8,128)(2,1)S(1)}, bf16[16,2048]{1,0:T(8,128)(2,1)S(1)}, u32[]{:S(2)}, u32[]{:S(2)}) %collective-permute-start.25) | collective-permute-done | bytes 65568 | tf_op jit(solution)/shard_map/ppermute | solution.py:33
  70.9 0.7 total.1
  (35 shorter events, 1.8 us)
Async XLA Ops:
  0.8 14.4 %collective-permute-start.1 = (bf16[64,512]{1,0:T(8,128)(2,1)S(1)}, bf16[64,512]{1,0:T(8,128)(2,1)S(1)}, u32[]{:S(2)}, u32[]{:S(2)}) collective-permute-start(bf16[64,512]{1,0:T(8,128)(2,1)S(1)} %pad_maximum_fusion.refs_2_), channel_id=1, source_target_pairs={{0,4},{4,8},{8,12},{1,5},{5,9},{9,13},{2,6},{6,10},{10,14},{3,7},{... | collective-permute-start | bytes 196616 | tf_op jit(solution)/shard_map/ppermute | solution.py:338
  5.7 9.5 %collective-permute-start = (bf16[64,512]{1,0:T(8,128)(2,1)S(1)}, bf16[64,512]{1,0:T(8,128)(2,1)S(1)}, u32[]{:S(2)}, u32[]{:S(2)}) collective-permute-start(bf16[64,512]{1,0:T(8,128)(2,1)S(1)} %pad_maximum_fusion.refs_2_), channel_id=1, source_target_pairs={{0,8},{4,12},{1,9},{5,13},{2,10},{6,14},{3,11},{7,15},{16,24},{20,... | collective-permute-start | bytes 196616 | tf_op jit(solution)/shard_map/ppermute | solution.py:338
  16.6 1.4 %collective-permute-start.2 = (bf16[32,2048]{1,0:T(8,128)(2,1)S(1)}, bf16[32,2048]{1,0:T(8,128)(2,1)S(1)}, u32[]{:S(2)}, u32[]{:S(2)}) collective-permute-start(bf16[32,2048]{1,0:T(8,128)(2,1)S(1)} %get-tuple-element.39), channel_id=1, source_target_pairs={{0,1},{1,0},{2,3},{3,2},{4,5},{5,4},{6,7},{7,6},{8,9},{9,8},{10,11... | collective-permute-start | bytes 393224 | tf_op jit(solution)/shard_map/ppermute | solution.py:33
  18.1 5.0 %collective-permute-start.3 = (bf16[16,2048]{1,0:T(8,128)(2,1)S(1)}, bf16[16,2048]{1,0:T(8,128)(2,1)S(1)}, u32[]{:S(2)}, u32[]{:S(2)}) collective-permute-start(bf16[16,2048]{1,0:T(8,128)(2,1)S(1)} %get-tuple-element.41), channel_id=1, source_target_pairs={{0,2},{2,0},{1,3},{3,1},{4,6},{6,4},{5,7},{7,5},{8,10},{10,8},{9,1... | collective-permute-start | bytes 196616 | tf_op jit(solution)/shard_map/ppermute | solution.py:33
  23.2 5.3 %collective-permute-start.7 = (bf16[16,2176]{1,0:T(8,128)(2,1)S(1)}, bf16[16,2176]{1,0:T(8,128)(2,1)S(1)}, u32[]{:S(2)}, u32[]{:S(2)}) collective-permute-start(bf16[16,2176]{1,0:T(8,128)(2,1)S(1)} %get-tuple-element.44.refs_0_), channel_id=1, source_target_pairs={{0,2},{2,0},{1,3},{3,1},{4,6},{6,4},{5,7},{7,5},{8,10},{10,8},{9,1... | collective-permute-start | bytes 208904 | tf_op jit(solution)/shard_map/ppermute | solution.py:33
  24.1 7.0 %collective-permute-start.6 = (bf16[16,2176]{1,0:T(8,128)(2,1)S(1)}, bf16[16,2176]{1,0:T(8,128)(2,1)S(1)}, u32[]{:S(2)}, u32[]{:S(2)}) collective-permute-start(bf16[16,2176]{1,0:T(8,128)(2,1)S(1)} %get-tuple-element.44.refs_0_), channel_id=1, source_target_pairs={{0,12},{4,8},{8,4},{12,0},{1,13},{5,9},{9,5},{13,1},{2,14},{6,10},... | collective-permute-start | bytes 208904 | tf_op jit(solution)/shard_map/ppermute | solution.py:33
  24.1 7.0 %collective-permute-start.11 = (bf16[16,2176]{1,0:T(8,128)(2,1)S(1)}, bf16[16,2176]{1,0:T(8,128)(2,1)S(1)}, u32[]{:S(2)}, u32[]{:S(2)}) collective-permute-start(bf16[16,2176]{1,0:T(8,128)(2,1)S(1)} %get-tuple-element.44.refs_0_), channel_id=1, source_target_pairs={{0,1},{1,0},{2,3},{3,2},{4,5},{5,4},{6,7},{7,6},{8,9},{9,8},{10,11... | collective-permute-start | bytes 208904 | tf_op jit(solution)/shard_map/ppermute | solution.py:33
  24.1 8.1 %collective-permute-start.5 = (bf16[16,2176]{1,0:T(8,128)(2,1)S(1)}, bf16[16,2176]{1,0:T(8,128)(2,1)S(1)}, u32[]{:S(2)}, u32[]{:S(2)}) collective-permute-start(bf16[16,2176]{1,0:T(8,128)(2,1)S(1)} %get-tuple-element.44.refs_0_), channel_id=1, source_target_pairs={{0,8},{4,12},{8,0},{12,4},{1,9},{5,13},{9,1},{13,5},{2,10},{6,14},... | collective-permute-start | bytes 208904 | tf_op jit(solution)/shard_map/ppermute | solution.py:33
  25.0 8.8 %collective-permute-start.4 = (bf16[16,2176]{1,0:T(8,128)(2,1)S(1)}, bf16[16,2176]{1,0:T(8,128)(2,1)S(1)}, u32[]{:S(2)}, u32[]{:S(2)}) collective-permute-start(bf16[16,2176]{1,0:T(8,128)(2,1)S(1)} %get-tuple-element.44.refs_0_), channel_id=1, source_target_pairs={{0,4},{4,0},{8,12},{12,8},{1,5},{5,1},{9,13},{13,9},{2,6},{6,2},{1... | collective-permute-start | bytes 208904 | tf_op jit(solution)/shard_map/ppermute | solution.py:33
  28.5 5.8 %collective-permute-start.15 = (bf16[16,2176]{1,0:T(8,128)(2,1)S(1)}, bf16[16,2176]{1,0:T(8,128)(2,1)S(1)}, u32[]{:S(2)}, u32[]{:S(2)}) collective-permute-start(bf16[16,2176]{1,0:T(8,128)(2,1)S(1)} %collective-permute-done.7.refs_4_), channel_id=1, source_target_pairs={{0,1},{1,0},{2,3},{3,2},{4,5},{5,4},{6,7},{7,6},{8,9},{9,8},{10,11... | collective-permute-start | bytes 208904 | tf_op jit(solution)/shard_map/ppermute | solution.py:33
  31.1 3.2 %collective-permute-start.14 = (bf16[16,2176]{1,0:T(8,128)(2,1)S(1)}, bf16[16,2176]{1,0:T(8,128)(2,1)S(1)}, u32[]{:S(2)}, u32[]{:S(2)}) collective-permute-start(bf16[16,2176]{1,0:T(8,128)(2,1)S(1)} %collective-permute-done.6.refs_3_), channel_id=1, source_target_pairs={{0,1},{1,0},{2,3},{3,2},{4,5},{5,4},{6,7},{7,6},{8,9},{9,8},{10,11... | collective-permute-start | bytes 208904 | tf_op jit(solution)/shard_map/ppermute | solution.py:33
  31.1 5.0 %collective-permute-start.10 = (bf16[16,2176]{1,0:T(8,128)(2,1)S(1)}, bf16[16,2176]{1,0:T(8,128)(2,1)S(1)}, u32[]{:S(2)}, u32[]{:S(2)}) collective-permute-start(bf16[16,2176]{1,0:T(8,128)(2,1)S(1)} %collective-permute-done.6.refs_3_), channel_id=1, source_target_pairs={{0,2},{2,0},{1,3},{3,1},{4,6},{6,4},{5,7},{7,5},{8,10},{10,8},{9,1... | collective-permute-start | bytes 208904 | tf_op jit(solution)/shard_map/ppermute | solution.py:33
  32.2 5.3 %collective-permute-start.9 = (bf16[16,2176]{1,0:T(8,128)(2,1)S(1)}, bf16[16,2176]{1,0:T(8,128)(2,1)S(1)}, u32[]{:S(2)}, u32[]{:S(2)}) collective-permute-start(bf16[16,2176]{1,0:T(8,128)(2,1)S(1)} %collective-permute-done.5.refs_2_), channel_id=1, source_target_pairs={{0,2},{2,0},{1,3},{3,1},{4,6},{6,4},{5,7},{7,5},{8,10},{10,8},{9,1... | collective-permute-start | bytes 208904 | tf_op jit(solution)/shard_map/ppermute | solution.py:33
  33.8 4.9 %collective-permute-start.8 = (bf16[16,2176]{1,0:T(8,128)(2,1)S(1)}, bf16[16,2176]{1,0:T(8,128)(2,1)S(1)}, u32[]{:S(2)}, u32[]{:S(2)}) collective-permute-start(bf16[16,2176]{1,0:T(8,128)(2,1)S(1)} %collective-permute-done.4.refs_1_), channel_id=1, source_target_pairs={{0,2},{2,0},{1,3},{3,1},{4,6},{6,4},{5,7},{7,5},{8,10},{10,8},{9,1... | collective-permute-start | bytes 208904 | tf_op jit(solution)/shard_map/ppermute | solution.py:33
  34.3 4.4 %collective-permute-start.13 = (bf16[16,2176]{1,0:T(8,128)(2,1)S(1)}, bf16[16,2176]{1,0:T(8,128)(2,1)S(1)}, u32[]{:S(2)}, u32[]{:S(2)}) collective-permute-start(bf16[16,2176]{1,0:T(8,128)(2,1)S(1)} %collective-permute-done.5.refs_2_), channel_id=1, source_target_pairs={{0,1},{1,0},{2,3},{3,2},{4,5},{5,4},{6,7},{7,6},{8,9},{9,8},{10,11... | collective-permute-start | bytes 208904 | tf_op jit(solution)/shard_map/ppermute | solution.py:33
  34.3 4.4 %collective-permute-start.12 = (bf16[16,2176]{1,0:T(8,128)(2,1)S(1)}, bf16[16,2176]{1,0:T(8,128)(2,1)S(1)}, u32[]{:S(2)}, u32[]{:S(2)}) collective-permute-start(bf16[16,2176]{1,0:T(8,128)(2,1)S(1)} %collective-permute-done.4.refs_1_), channel_id=1, source_target_pairs={{0,1},{1,0},{2,3},{3,2},{4,5},{5,4},{6,7},{7,6},{8,9},{9,8},{10,11... | collective-permute-start | bytes 208904 | tf_op jit(solution)/shard_map/ppermute | solution.py:33
  36.1 2.6 %collective-permute-start.18 = (bf16[16,2176]{1,0:T(8,128)(2,1)S(1)}, bf16[16,2176]{1,0:T(8,128)(2,1)S(1)}, u32[]{:S(2)}, u32[]{:S(2)}) collective-permute-start(bf16[16,2176]{1,0:T(8,128)(2,1)S(1)} %collective-permute-done.10.refs_7_), channel_id=1, source_target_pairs={{0,1},{1,0},{2,3},{3,2},{4,5},{5,4},{6,7},{7,6},{8,9},{9,8},{10,11... | collective-permute-start | bytes 208904 | tf_op jit(solution)/shard_map/ppermute | solution.py:33
  37.6 1.3 %collective-permute-start.17 = (bf16[16,2176]{1,0:T(8,128)(2,1)S(1)}, bf16[16,2176]{1,0:T(8,128)(2,1)S(1)}, u32[]{:S(2)}, u32[]{:S(2)}) collective-permute-start(bf16[16,2176]{1,0:T(8,128)(2,1)S(1)} %collective-permute-done.9.refs_6_), channel_id=1, source_target_pairs={{0,1},{1,0},{2,3},{3,2},{4,5},{5,4},{6,7},{7,6},{8,9},{9,8},{10,11... | collective-permute-start | bytes 208904 | tf_op jit(solution)/shard_map/ppermute | solution.py:33
  38.7 1.3 %collective-permute-start.16 = (bf16[16,2176]{1,0:T(8,128)(2,1)S(1)}, bf16[16,2176]{1,0:T(8,128)(2,1)S(1)}, u32[]{:S(2)}, u32[]{:S(2)}) collective-permute-start(bf16[16,2176]{1,0:T(8,128)(2,1)S(1)} %collective-permute-done.8.refs_5_), channel_id=1, source_target_pairs={{0,1},{1,0},{2,3},{3,2},{4,5},{5,4},{6,7},{7,6},{8,9},{9,8},{10,11... | collective-permute-start | bytes 208904 | tf_op jit(solution)/shard_map/ppermute | solution.py:33
  54.8 2.0 %collective-permute-start.19 = (bf16[128,2048]{1,0:T(8,128)(2,1)S(1)}, bf16[128,2048]{1,0:T(8,128)(2,1)S(1)}, u32[]{:S(2)}, u32[]{:S(2)}) collective-permute-start(bf16[128,2048]{1,0:T(8,128)(2,1)S(1)} %get-tuple-element.48), channel_id=1, source_target_pairs={{0,1},{1,0},{2,3},{3,2},{4,5},{5,4},{6,7},{7,6},{8,9},{9,8},{10,11... | collective-permute-start | bytes 1572872 | tf_op jit(solution)/shard_map/ppermute | solution.py:33
  56.9 5.0 %collective-permute-start.20 = (bf16[16,2048]{1,0:T(8,128)(2,1)S(1)}, bf16[16,2048]{1,0:T(8,128)(2,1)S(1)}, u32[]{:S(2)}, u32[]{:S(2)}) collective-permute-start(bf16[16,2048]{1,0:T(8,128)(2,1)S(1)} %get-tuple-element.50), channel_id=1, source_target_pairs={{0,2},{2,0},{1,3},{3,1},{4,6},{6,4},{5,7},{7,5},{8,10},{10,8},{9,1... | collective-permute-start | bytes 196616 | tf_op jit(solution)/shard_map/ppermute | solution.py:33
  58.1 5.2 %collective-permute-start.22 = (bf16[16,2048]{1,0:T(8,128)(2,1)S(1)}, bf16[16,2048]{1,0:T(8,128)(2,1)S(1)}, u32[]{:S(2)}, u32[]{:S(2)}) collective-permute-start(bf16[16,2048]{1,0:T(8,128)(2,1)S(1)} %get-tuple-element.52), channel_id=1, source_target_pairs={{0,2},{2,0},{1,3},{3,1},{4,6},{6,4},{5,7},{7,5},{8,10},{10,8},{9,1... | collective-permute-start | bytes 196616 | tf_op jit(solution)/shard_map/ppermute | solution.py:33
  59.0 5.7 %collective-permute-start.24 = (bf16[16,2048]{1,0:T(8,128)(2,1)S(1)}, bf16[16,2048]{1,0:T(8,128)(2,1)S(1)}, u32[]{:S(2)}, u32[]{:S(2)}) collective-permute-start(bf16[16,2048]{1,0:T(8,128)(2,1)S(1)} %get-tuple-element.54), channel_id=1, source_target_pairs={{0,2},{2,0},{1,3},{3,1},{4,6},{6,4},{5,7},{7,5},{8,10},{10,8},{9,1... | collective-permute-start | bytes 196616 | tf_op jit(solution)/shard_map/ppermute | solution.py:33
  60.1 6.4 %collective-permute-start.26 = (bf16[16,2048]{1,0:T(8,128)(2,1)S(1)}, bf16[16,2048]{1,0:T(8,128)(2,1)S(1)}, u32[]{:S(2)}, u32[]{:S(2)}) collective-permute-start(bf16[16,2048]{1,0:T(8,128)(2,1)S(1)} %get-tuple-element.56), channel_id=1, source_target_pairs={{0,2},{2,0},{1,3},{3,1},{4,6},{6,4},{5,7},{7,5},{8,10},{10,8},{9,1... | collective-permute-start | bytes 196616 | tf_op jit(solution)/shard_map/ppermute | solution.py:33
  61.9 5.0 %collective-permute-start.21 = (bf16[16,2048]{1,0:T(8,128)(2,1)S(1)}, bf16[16,2048]{1,0:T(8,128)(2,1)S(1)}, u32[]{:S(2)}, u32[]{:S(2)}) collective-permute-start(bf16[16,2048]{1,0:T(8,128)(2,1)S(1)} %sum_x1.1), channel_id=1, source_target_pairs={{0,4},{4,0},{8,12},{12,8},{1,5},{5,1},{9,13},{13,9},{2,6},{6,2},{1... | collective-permute-start | bytes 196616 | tf_op jit(solution)/shard_map/ppermute | solution.py:33
  63.3 6.6 %collective-permute-start.23 = (bf16[16,2048]{1,0:T(8,128)(2,1)S(1)}, bf16[16,2048]{1,0:T(8,128)(2,1)S(1)}, u32[]{:S(2)}, u32[]{:S(2)}) collective-permute-start(bf16[16,2048]{1,0:T(8,128)(2,1)S(1)} %sum_x2.1), channel_id=1, source_target_pairs={{0,8},{4,12},{8,0},{12,4},{1,9},{5,13},{9,1},{13,5},{2,10},{6,14},... | collective-permute-start | bytes 196616 | tf_op jit(solution)/shard_map/ppermute | solution.py:33
  64.7 6.2 %collective-permute-start.25 = (bf16[16,2048]{1,0:T(8,128)(2,1)S(1)}, bf16[16,2048]{1,0:T(8,128)(2,1)S(1)}, u32[]{:S(2)}, u32[]{:S(2)}) collective-permute-start(bf16[16,2048]{1,0:T(8,128)(2,1)S(1)} %sum_x3.1), channel_id=1, source_target_pairs={{0,12},{4,8},{8,4},{12,0},{1,13},{5,9},{9,5},{13,1},{2,14},{6,10},... | collective-permute-start | bytes 196616 | tf_op jit(solution)/shard_map/ppermute | solution.py:33

commit v5 on v2

--- a/solution.py
+++ b/solution.py
@@ -273,50 +273,38 @@
     pick_ref[...] = jnp.concatenate(picks, axis=0)
     column = min(512, width)
 
-    def pack(c, _):
-        cut = pl.ds(pl.multiple_of(c * column, column), column)
-        packed_ref[:, cut] = dot(pick_ref[...], rows_ref[:, cut]).astype(jnp.bfloat16)
-        return 0
-
-    lax.fori_loop(0, width // column, pack, 0)
+    for c in range(0, width, column):
+        packed_ref[:, c : c + column] = dot(pick_ref[...], rows_ref[:, c : c + column]).astype(
+            jnp.bfloat16
+        )
     for x in range(experts):
         mine = slice(x * capacity, (x + 1) * capacity)
         if x >= n_up:
             up_copies[x - n_up].wait()
         gate_ref, up_ref = gate_refs[x], up_refs[x]
 
-        def inner(s, _):
-            cut = pl.ds(pl.multiple_of(s * tile, tile), tile)
+        for s in range(0, per_expert, tile):
+            cut = slice(s, s + tile)
             gate = dot(packed_ref[mine, :], gate_ref[:, cut])
             up = dot(packed_ref[mine, :], up_ref[:, cut])
-            hidden_ref[mine, cut] = (gate / (1.0 + jnp.exp(-gate)) * up).astype(jnp.bfloat16)
-            return 0
-
-        lax.fori_loop(0, per_expert // tile, inner, 0)
+            half = 0.5 * gate
+            hidden_ref[mine, cut] = ((half + half * jnp.tanh(half)) * up).astype(jnp.bfloat16)
         down_copies[x].wait()
 
-        def outer(c, _):
-            cut = pl.ds(pl.multiple_of(c * column, column), column)
-            out = dot(hidden_ref[mine, :], down_ref[:, cut])
-            packed_ref[mine, cut] = (out * shares[x]).astype(jnp.bfloat16)
-            return 0
-
-        lax.fori_loop(0, width // column, outer, 0)
+        for c in range(0, width, column):
+            out = dot(hidden_ref[mine, :], down_ref[:, c : c + column])
+            packed_ref[mine, c : c + column] = (out * shares[x]).astype(jnp.bfloat16)
         if x + 1 < experts:
             down_copies[x + 1].start()
     kept = keep_ref.shape[0]
 
-    def spread(c, _):
-        cut = pl.ds(pl.multiple_of(c * column, column), column)
+    for c in range(0, width, column):
         out = lax.dot_general(
-            pick_ref[...], packed_ref[:, cut], (((0,), (0,)), ((), ())),
+            pick_ref[...], packed_ref[:, c : c + column], (((0,), (0,)), ((), ())),
             preferred_element_type=jnp.float32,
         )
-        keep_ref[:, cut] = out[:kept]
-        send_ref[:, cut] = out[kept:].astype(jnp.bfloat16)
-        return 0
-
-    lax.fori_loop(0, width // column, spread, 0)
+        keep_ref[:, c : c + column] = out[:kept]
+        send_ref[:, c : c + column] = out[kept:].astype(jnp.bfloat16)
 
 
 def per_device(
@@ -442,7 +430,7 @@
             pltpu.SemaphoreType.DMA((experts,)),
             pltpu.SemaphoreType.DMA((experts,)),
         ],
-        vmem=20,
+        vmem=24,
         name="experts",
         cost_us=12.0,
     )

time: 71.7 us -> 72 us (level)
  no operation moved by 1% of the time
where the time goes in v5:
time: 72 us; the launch traced here: 71.7 us
  starting transfers between devices  26.3 us (37%)
  Pallas kernels  25.7 us (36%)
  waiting for transfers between devices  18.7 us (26%)
  local copies, waits for them, and re-layouts  0.78 us (1%)
    pallas_call x11, Pallas kernels, call(): pl.pallas_call(kernel, out_shape=out_shape, in_specs=[s for s, _ in args]...  25.7 us
    ppermute x25, waiting for transfers between devices, xor_swap(): return lax.ppermute(x, axis, [(i, i ^ k) for i in range(n)])  18.7 us
    ppermute x25, starting transfers between devices, xor_swap(): return lax.ppermute(x, axis, [(i, i ^ k) for i in range(n)])  16.9 us
    ppermute x2, starting transfers between devices, per_device(): lax.ppermute(kv, 'sec', [(i, i + k) for i in range(sec_count - k)])  9.43 us
  transfers between devices with their start and end apart: 27, of which 14 were waited for; matrix products, arithmetic and copies ran while one was open for 0% of the time, Pallas kernels for 15%

profile of v5, /device:TPU:0, one launch (start us, length us, event | category | flops | bytes accessed | tf_op | source)
XLA Modules:
  0.0 71.7 jit_solution(9941104241418165289)
XLA Ops:
  0.0 0.8 %constant_dynamic-slice_fusion = (bf16[64,256]{1,0:T(8,128)(2,1)S(1)}, bf16[64,256]{1,0:T(8,128)(2,1)S(1)}) fusion(bf16[64,512]{1,0:T(8,128)(2,1)} %param.14, s32[]{:T(128)S(6)} %select_n.10, bf16[64,512]{1,0:T(8,128)(2,1)} %param.13), kind=kLoop, calls=%fused_computation.1 | loop fusion | bytes 131076 | tf_op jit(solution)/shard_map/dynamic_slice | solution.py:336
  0.8 4.9 %collective-permute-start.1 = (bf16[64,512]{1,0:T(8,128)(2,1)S(1)}, bf16[64,512]{1,0:T(8,128)(2,1)S(1)}, u32[]{:S(2)}, u32[]{:S(2)}) collective-permute-start(bf16[64,512]{1,0:T(8,128)(2,1)S(1)} %pad_maximum_fusion.refs_2_), channel_id=1, source_target_pairs={{0,4},{4,8},{8,12},{1,5},{5,9},{9,13},{2,6},{6,10},{10,14},{3,7},{... | collective-permute-start | bytes 196616 | tf_op jit(solution)/shard_map/ppermute | solution.py:340
  5.7 4.5 %collective-permute-start = (bf16[64,512]{1,0:T(8,128)(2,1)S(1)}, bf16[64,512]{1,0:T(8,128)(2,1)S(1)}, u32[]{:S(2)}, u32[]{:S(2)}) collective-permute-start(bf16[64,512]{1,0:T(8,128)(2,1)S(1)} %pad_maximum_fusion.refs_2_), channel_id=1, source_target_pairs={{0,8},{4,12},{1,9},{5,13},{2,10},{6,14},{3,11},{7,15},{16,24},{20,... | collective-permute-start | bytes 196616 | tf_op jit(solution)/shard_map/ppermute | solution.py:340
  10.2 7.3 %prepare.1 = (bf16[64,1024]{1,0:T(8,128)(2,1)S(1)}, bf16[1024,2048]{1,0:T(8,128)(2,1)S(1)}, f32[1,2048]{1,0:T(1,128)S(1)}, f32[64,192]{1,0:T(8,128)S(1)}, bf16[6...) custom-call(s32[8]{0:T(128)} %lengths_hbm.1, ...), custom_call_target="tpu_custom_call" | custom-call | bytes 20400000 | tf_op jit(solution)/shard_map/prepare/pallas_call | solution.py:41
  17.6 1.4 %attention.1 = (f32[32,2048]{1,0:T(8,128)S(1)}, bf16[32,2048]{1,0:T(8,128)(2,1)S(1)}) custom-call(bf16[64,1024]{1,0:T(8,128)(2,1)S(1)} %get-tuple-element.35.q_ref, f32[64,192]{1,0:T(8,128)S(1)} %get-tuple-element.36.mask_ref, bf16[64,64]{1,0:T(8,128)(2,1)S(1)} %get-tuple-element.37.order_ref, bf16[64,512]{1,0:T(8,128)(2,1)S(1)} %collective-permute-done.refs_0_, ...), custom_call_target="tpu_custom_call" | custom-call | bytes 8160000 | tf_op jit(solution)/shard_map/attention/pallas_call | solution.py:41
  19.1 1.3 %collective-permute-done.2.refs_1_ = bf16[32,2048]{1,0:T(8,128)(2,1)S(1)} collective-permute-done((bf16[32,2048]{1,0:T(8,128)(2,1)S(1)}, bf16[32,2048]{1,0:T(8,128)(2,1)S(1)}, u32[]{:S(2)}, u32[]{:S(2)}) %collective-permute-start.2) | collective-permute-done | bytes 131104 | tf_op jit(solution)/shard_map/ppermute | solution.py:33
  20.5 1.6 %collective-permute-start.3 = (bf16[16,2048]{1,0:T(8,128)(2,1)S(1)}, bf16[16,2048]{1,0:T(8,128)(2,1)S(1)}, u32[]{:S(2)}, u32[]{:S(2)}) collective-permute-start(bf16[16,2048]{1,0:T(8,128)(2,1)S(1)} %get-tuple-element.42), channel_id=1, source_target_pairs={{0,2},{2,0},{1,3},{3,1},{4,6},{6,4},{5,7},{7,5},{8,10},{10,8},{9,1... | collective-permute-start | bytes 196616 | tf_op jit(solution)/shard_map/ppermute | solution.py:33
  22.0 3.4 %load_up.1 = (bf16[2048,2048]{1,0:T(8,128)(2,1)S(1)}, f32[8,128]{1,0:T(8,128)S(1)}) custom-call(bf16[2048,4096]{1,0:T(8,128)(2,1)} %bitcast.6, f32[16,2048]{1,0:T(8,128)S(1)} %get-tuple-element.41.refs_0_), custom_call_target="tpu_custom_call" | custom-call | bytes 8388607 | tf_op jit(solution)/shard_map/load_up/pallas_call | solution.py:41
  25.6 0.9 %collective-permute-start.7 = (bf16[16,2176]{1,0:T(8,128)(2,1)S(1)}, bf16[16,2176]{1,0:T(8,128)(2,1)S(1)}, u32[]{:S(2)}, u32[]{:S(2)}) collective-permute-start(bf16[16,2176]{1,0:T(8,128)(2,1)S(1)} %get-tuple-element.45.refs_0_), channel_id=1, source_target_pairs={{0,2},{2,0},{1,3},{3,1},{4,6},{6,4},{5,7},{7,5},{8,10},{10,8},{9,1... | collective-permute-start | bytes 208904 | tf_op jit(solution)/shard_map/ppermute | solution.py:33
  26.5 0.8 %collective-permute-start.5 = (bf16[16,2176]{1,0:T(8,128)(2,1)S(1)}, bf16[16,2176]{1,0:T(8,128)(2,1)S(1)}, u32[]{:S(2)}, u32[]{:S(2)}) collective-permute-start(bf16[16,2176]{1,0:T(8,128)(2,1)S(1)} %get-tuple-element.45.refs_0_), channel_id=1, source_target_pairs={{0,8},{4,12},{8,0},{12,4},{1,9},{5,13},{9,1},{13,5},{2,10},{6,14},... | collective-permute-start | bytes 208904 | tf_op jit(solution)/shard_map/ppermute | solution.py:33
  27.4 3.5 %collective-permute-start.4 = (bf16[16,2176]{1,0:T(8,128)(2,1)S(1)}, bf16[16,2176]{1,0:T(8,128)(2,1)S(1)}, u32[]{:S(2)}, u32[]{:S(2)}) collective-permute-start(bf16[16,2176]{1,0:T(8,128)(2,1)S(1)} %get-tuple-element.45.refs_0_), channel_id=1, source_target_pairs={{0,4},{4,0},{8,12},{12,8},{1,5},{5,1},{9,13},{13,9},{2,6},{6,2},{1... | collective-permute-start | bytes 208904 | tf_op jit(solution)/shard_map/ppermute | solution.py:33
  30.9 2.6 %collective-permute-done.6.refs_3_ = bf16[16,2176]{1,0:T(8,128)(2,1)S(1)} collective-permute-done((bf16[16,2176]{1,0:T(8,128)(2,1)S(1)}, bf16[16,2176]{1,0:T(8,128)(2,1)S(1)}, u32[]{:S(2)}, u32[]{:S(2)}) %collective-permute-start.6) | collective-permute-done | bytes 69664 | tf_op jit(solution)/shard_map/ppermute | solution.py:33
  33.5 1.1 %collective-permute-start.10 = (bf16[16,2176]{1,0:T(8,128)(2,1)S(1)}, bf16[16,2176]{1,0:T(8,128)(2,1)S(1)}, u32[]{:S(2)}, u32[]{:S(2)}) collective-permute-start(bf16[16,2176]{1,0:T(8,128)(2,1)S(1)} %collective-permute-done.6.refs_3_), channel_id=1, source_target_pairs={{0,2},{2,0},{1,3},{3,1},{4,6},{6,4},{5,7},{7,5},{8,10},{10,8},{9,1... | collective-permute-start | bytes 208904 | tf_op jit(solution)/shard_map/ppermute | solution.py:33
  34.6 1.5 %collective-permute-start.9 = (bf16[16,2176]{1,0:T(8,128)(2,1)S(1)}, bf16[16,2176]{1,0:T(8,128)(2,1)S(1)}, u32[]{:S(2)}, u32[]{:S(2)}) collective-permute-start(bf16[16,2176]{1,0:T(8,128)(2,1)S(1)} %collective-permute-done.5.refs_2_), channel_id=1, source_target_pairs={{0,2},{2,0},{1,3},{3,1},{4,6},{6,4},{5,7},{7,5},{8,10},{10,8},{9,1... | collective-permute-start | bytes 208904 | tf_op jit(solution)/shard_map/ppermute | solution.py:33
  36.2 0.5 collective-permute-start.8
  37.2 1.3 %collective-permute-done.10.refs_7_ = bf16[16,2176]{1,0:T(8,128)(2,1)S(1)} collective-permute-done((bf16[16,2176]{1,0:T(8,128)(2,1)S(1)}, bf16[16,2176]{1,0:T(8,128)(2,1)S(1)}, u32[]{:S(2)}, u32[]{:S(2)}) %collective-permute-start.10) | collective-permute-done | bytes 69664 | tf_op jit(solution)/shard_map/ppermute | solution.py:33
  38.5 1.5 %collective-permute-done.9.refs_6_ = bf16[16,2176]{1,0:T(8,128)(2,1)S(1)} collective-permute-done((bf16[16,2176]{1,0:T(8,128)(2,1)S(1)}, bf16[16,2176]{1,0:T(8,128)(2,1)S(1)}, u32[]{:S(2)}, u32[]{:S(2)}) %collective-permute-start.9) | collective-permute-done | bytes 69664 | tf_op jit(solution)/shard_map/ppermute | solution.py:33
  40.0 1.1 %collective-permute-done.8.refs_5_ = bf16[16,2176]{1,0:T(8,128)(2,1)S(1)} collective-permute-done((bf16[16,2176]{1,0:T(8,128)(2,1)S(1)}, bf16[16,2176]{1,0:T(8,128)(2,1)S(1)}, u32[]{:S(2)}, u32[]{:S(2)}) %collective-permute-start.8) | collective-permute-done | bytes 69664 | tf_op jit(solution)/shard_map/ppermute | solution.py:33
  41.2 1.1 %collective-permute-done.16.refs_13_ = bf16[16,2176]{1,0:T(8,128)(2,1)S(1)} collective-permute-done((bf16[16,2176]{1,0:T(8,128)(2,1)S(1)}, bf16[16,2176]{1,0:T(8,128)(2,1)S(1)}, u32[]{:S(2)}, u32[]{:S(2)}) %collective-permute-start.16) | collective-permute-done | bytes 69664 | tf_op jit(solution)/shard_map/ppermute | solution.py:33
  42.3 12.6 %experts.1 = (f32[128,2048]{1,0:T(8,128)S(1)}, bf16[128,2048]{1,0:T(8,128)(2,1)S(1)}) custom-call(bf16[16,2176]{1,0:T(8,128)(2,1)S(1)} %get-tuple-element.45.refs_0_, bf16[16,2176]{1,0:T(8,128)(2,1)S(1)} %collective-permute-done.4.refs_1_, bf16[16,2176]{1,0:T(8,128)(2,1)S(1)} %collective-permute-done.5.refs_2_, ...), custom_call_target="tpu_custom_call" | custom-call | bytes 40800000 | tf_op jit(solution)/shard_map/experts/pallas_call | solution.py:41
  55.1 1.8 %collective-permute-done.19.refs_1_ = bf16[128,2048]{1,0:T(8,128)(2,1)S(1)} collective-permute-done((bf16[128,2048]{1,0:T(8,128)(2,1)S(1)}, bf16[128,2048]{1,0:T(8,128)(2,1)S(1)}, u32[]{:S(2)}, u32[]{:S(2)}) %collective-permute-start.19) | collective-permute-done | bytes 524320 | tf_op jit(solution)/shard_map/ppermute | solution.py:33
  57.0 1.2 %collective-permute-start.20 = (bf16[16,2048]{1,0:T(8,128)(2,1)S(1)}, bf16[16,2048]{1,0:T(8,128)(2,1)S(1)}, u32[]{:S(2)}, u32[]{:S(2)}) collective-permute-start(bf16[16,2048]{1,0:T(8,128)(2,1)S(1)} %get-tuple-element.52), channel_id=1, source_target_pairs={{0,2},{2,0},{1,3},{3,1},{4,6},{6,4},{5,7},{7,5},{8,10},{10,8},{9,1... | collective-permute-start | bytes 196616 | tf_op jit(solution)/shard_map/ppermute | solution.py:33
  58.2 0.9 %collective-permute-start.22 = (bf16[16,2048]{1,0:T(8,128)(2,1)S(1)}, bf16[16,2048]{1,0:T(8,128)(2,1)S(1)}, u32[]{:S(2)}, u32[]{:S(2)}) collective-permute-start(bf16[16,2048]{1,0:T(8,128)(2,1)S(1)} %get-tuple-element.54), channel_id=1, source_target_pairs={{0,2},{2,0},{1,3},{3,1},{4,6},{6,4},{5,7},{7,5},{8,10},{10,8},{9,1... | collective-permute-start | bytes 196616 | tf_op jit(solution)/shard_map/ppermute | solution.py:33
  59.1 1.1 %collective-permute-start.24 = (bf16[16,2048]{1,0:T(8,128)(2,1)S(1)}, bf16[16,2048]{1,0:T(8,128)(2,1)S(1)}, u32[]{:S(2)}, u32[]{:S(2)}) collective-permute-start(bf16[16,2048]{1,0:T(8,128)(2,1)S(1)} %get-tuple-element.56), channel_id=1, source_target_pairs={{0,2},{2,0},{1,3},{3,1},{4,6},{6,4},{5,7},{7,5},{8,10},{10,8},{9,1... | collective-permute-start | bytes 196616 | tf_op jit(solution)/shard_map/ppermute | solution.py:33
  60.2 0.9 %collective-permute-start.26 = (bf16[16,2048]{1,0:T(8,128)(2,1)S(1)}, bf16[16,2048]{1,0:T(8,128)(2,1)S(1)}, u32[]{:S(2)}, u32[]{:S(2)}) collective-permute-start(bf16[16,2048]{1,0:T(8,128)(2,1)S(1)} %get-tuple-element.58), channel_id=1, source_target_pairs={{0,2},{2,0},{1,3},{3,1},{4,6},{6,4},{5,7},{7,5},{8,10},{10,8},{9,1... | collective-permute-start | bytes 196616 | tf_op jit(solution)/shard_map/ppermute | solution.py:33
  61.1 0.9 %collective-permute-done.20.refs_1_ = bf16[16,2048]{1,0:T(8,128)(2,1)S(1)} collective-permute-done((bf16[16,2048]{1,0:T(8,128)(2,1)S(1)}, bf16[16,2048]{1,0:T(8,128)(2,1)S(1)}, u32[]{:S(2)}, u32[]{:S(2)}) %collective-permute-start.20) | collective-permute-done | bytes 65568 | tf_op jit(solution)/shard_map/ppermute | solution.py:33
  62.1 1.3 %collective-permute-done.22.refs_1_ = bf16[16,2048]{1,0:T(8,128)(2,1)S(1)} collective-permute-done((bf16[16,2048]{1,0:T(8,128)(2,1)S(1)}, bf16[16,2048]{1,0:T(8,128)(2,1)S(1)}, u32[]{:S(2)}, u32[]{:S(2)}) %collective-permute-start.22) | collective-permute-done | bytes 65568 | tf_op jit(solution)/shard_map/ppermute | solution.py:33
  63.5 1.3 %collective-permute-done.24.refs_1_ = bf16[16,2048]{1,0:T(8,128)(2,1)S(1)} collective-permute-done((bf16[16,2048]{1,0:T(8,128)(2,1)S(1)}, bf16[16,2048]{1,0:T(8,128)(2,1)S(1)}, u32[]{:S(2)}, u32[]{:S(2)}) %collective-permute-start.24) | collective-permute-done | bytes 65568 | tf_op jit(solution)/shard_map/ppermute | solution.py:33
  64.8 1.8 %collective-permute-start.25 = (bf16[16,2048]{1,0:T(8,128)(2,1)S(1)}, bf16[16,2048]{1,0:T(8,128)(2,1)S(1)}, u32[]{:S(2)}, u32[]{:S(2)}) collective-permute-start(bf16[16,2048]{1,0:T(8,128)(2,1)S(1)} %sum_x3.1), channel_id=1, source_target_pairs={{0,12},{4,8},{8,4},{12,0},{1,13},{5,9},{9,5},{13,1},{2,14},{6,10},... | collective-permute-start | bytes 196616 | tf_op jit(solution)/shard_map/ppermute | solution.py:33
  67.0 3.0 %collective-permute-done.23.refs_2_ = bf16[16,2048]{1,0:T(8,128)(2,1)S(1)} collective-permute-done((bf16[16,2048]{1,0:T(8,128)(2,1)S(1)}, bf16[16,2048]{1,0:T(8,128)(2,1)S(1)}, u32[]{:S(2)}, u32[]{:S(2)}) %collective-permute-start.23) | collective-permute-done | bytes 65568 | tf_op jit(solution)/shard_map/ppermute | solution.py:33
  70.0 1.0 %collective-permute-done.25.refs_3_ = bf16[16,2048]{1,0:T(8,128)(2,1)S(1)} collective-permute-done((bf16[16,2048]{1,0:T(8,128)(2,1)S(1)}, bf16[16,2048]{1,0:T(8,128)(2,1)S(1)}, u32[]{:S(2)}, u32[]{:S(2)}) %collective-permute-start.25) | collective-permute-done | bytes 65568 | tf_op jit(solution)/shard_map/ppermute | solution.py:33
  71.0 0.7 total.1
  (35 shorter events, 1.8 us)
Async XLA Ops:
  0.8 16.8 %collective-permute-start.1 = (bf16[64,512]{1,0:T(8,128)(2,1)S(1)}, bf16[64,512]{1,0:T(8,128)(2,1)S(1)}, u32[]{:S(2)}, u32[]{:S(2)}) collective-permute-start(bf16[64,512]{1,0:T(8,128)(2,1)S(1)} %pad_maximum_fusion.refs_2_), channel_id=1, source_target_pairs={{0,4},{4,8},{8,12},{1,5},{5,9},{9,13},{2,6},{6,10},{10,14},{3,7},{... | collective-permute-start | bytes 196616 | tf_op jit(solution)/shard_map/ppermute | solution.py:340
  5.7 11.9 %collective-permute-start = (bf16[64,512]{1,0:T(8,128)(2,1)S(1)}, bf16[64,512]{1,0:T(8,128)(2,1)S(1)}, u32[]{:S(2)}, u32[]{:S(2)}) collective-permute-start(bf16[64,512]{1,0:T(8,128)(2,1)S(1)} %pad_maximum_fusion.refs_2_), channel_id=1, source_target_pairs={{0,8},{4,12},{1,9},{5,13},{2,10},{6,14},{3,11},{7,15},{16,24},{20,... | collective-permute-start | bytes 196616 | tf_op jit(solution)/shard_map/ppermute | solution.py:340
  19.0 1.4 %collective-permute-start.2 = (bf16[32,2048]{1,0:T(8,128)(2,1)S(1)}, bf16[32,2048]{1,0:T(8,128)(2,1)S(1)}, u32[]{:S(2)}, u32[]{:S(2)}) collective-permute-start(bf16[32,2048]{1,0:T(8,128)(2,1)S(1)} %get-tuple-element.40), channel_id=1, source_target_pairs={{0,1},{1,0},{2,3},{3,2},{4,5},{5,4},{6,7},{7,6},{8,9},{9,8},{10,11... | collective-permute-start | bytes 393224 | tf_op jit(solution)/shard_map/ppermute | solution.py:33
  20.5 5.0 %collective-permute-start.3 = (bf16[16,2048]{1,0:T(8,128)(2,1)S(1)}, bf16[16,2048]{1,0:T(8,128)(2,1)S(1)}, u32[]{:S(2)}, u32[]{:S(2)}) collective-permute-start(bf16[16,2048]{1,0:T(8,128)(2,1)S(1)} %get-tuple-element.42), channel_id=1, source_target_pairs={{0,2},{2,0},{1,3},{3,1},{4,6},{6,4},{5,7},{7,5},{8,10},{10,8},{9,1... | collective-permute-start | bytes 196616 | tf_op jit(solution)/shard_map/ppermute | solution.py:33
  25.6 5.3 %collective-permute-start.7 = (bf16[16,2176]{1,0:T(8,128)(2,1)S(1)}, bf16[16,2176]{1,0:T(8,128)(2,1)S(1)}, u32[]{:S(2)}, u32[]{:S(2)}) collective-permute-start(bf16[16,2176]{1,0:T(8,128)(2,1)S(1)} %get-tuple-element.45.refs_0_), channel_id=1, source_target_pairs={{0,2},{2,0},{1,3},{3,1},{4,6},{6,4},{5,7},{7,5},{8,10},{10,8},{9,1... | collective-permute-start | bytes 208904 | tf_op jit(solution)/shard_map/ppermute | solution.py:33
  26.5 7.0 %collective-permute-start.6 = (bf16[16,2176]{1,0:T(8,128)(2,1)S(1)}, bf16[16,2176]{1,0:T(8,128)(2,1)S(1)}, u32[]{:S(2)}, u32[]{:S(2)}) collective-permute-start(bf16[16,2176]{1,0:T(8,128)(2,1)S(1)} %get-tuple-element.45.refs_0_), channel_id=1, source_target_pairs={{0,12},{4,8},{8,4},{12,0},{1,13},{5,9},{9,5},{13,1},{2,14},{6,10},... | collective-permute-start | bytes 208904 | tf_op jit(solution)/shard_map/ppermute | solution.py:33
  26.5 7.0 %collective-permute-start.11 = (bf16[16,2176]{1,0:T(8,128)(2,1)S(1)}, bf16[16,2176]{1,0:T(8,128)(2,1)S(1)}, u32[]{:S(2)}, u32[]{:S(2)}) collective-permute-start(bf16[16,2176]{1,0:T(8,128)(2,1)S(1)} %get-tuple-element.45.refs_0_), channel_id=1, source_target_pairs={{0,1},{1,0},{2,3},{3,2},{4,5},{5,4},{6,7},{7,6},{8,9},{9,8},{10,11... | collective-permute-start | bytes 208904 | tf_op jit(solution)/shard_map/ppermute | solution.py:33
  26.5 8.1 %collective-permute-start.5 = (bf16[16,2176]{1,0:T(8,128)(2,1)S(1)}, bf16[16,2176]{1,0:T(8,128)(2,1)S(1)}, u32[]{:S(2)}, u32[]{:S(2)}) collective-permute-start(bf16[16,2176]{1,0:T(8,128)(2,1)S(1)} %get-tuple-element.45.refs_0_), channel_id=1, source_target_pairs={{0,8},{4,12},{8,0},{12,4},{1,9},{5,13},{9,1},{13,5},{2,10},{6,14},... | collective-permute-start | bytes 208904 | tf_op jit(solution)/shard_map/ppermute | solution.py:33
  27.4 8.8 %collective-permute-start.4 = (bf16[16,2176]{1,0:T(8,128)(2,1)S(1)}, bf16[16,2176]{1,0:T(8,128)(2,1)S(1)}, u32[]{:S(2)}, u32[]{:S(2)}) collective-permute-start(bf16[16,2176]{1,0:T(8,128)(2,1)S(1)} %get-tuple-element.45.refs_0_), channel_id=1, source_target_pairs={{0,4},{4,0},{8,12},{12,8},{1,5},{5,1},{9,13},{13,9},{2,6},{6,2},{1... | collective-permute-start | bytes 208904 | tf_op jit(solution)/shard_map/ppermute | solution.py:33
  30.9 5.8 %collective-permute-start.15 = (bf16[16,2176]{1,0:T(8,128)(2,1)S(1)}, bf16[16,2176]{1,0:T(8,128)(2,1)S(1)}, u32[]{:S(2)}, u32[]{:S(2)}) collective-permute-start(bf16[16,2176]{1,0:T(8,128)(2,1)S(1)} %collective-permute-done.7.refs_4_), channel_id=1, source_target_pairs={{0,1},{1,0},{2,3},{3,2},{4,5},{5,4},{6,7},{7,6},{8,9},{9,8},{10,11... | collective-permute-start | bytes 208904 | tf_op jit(solution)/shard_map/ppermute | solution.py:33
  33.5 3.2 %collective-permute-start.14 = (bf16[16,2176]{1,0:T(8,128)(2,1)S(1)}, bf16[16,2176]{1,0:T(8,128)(2,1)S(1)}, u32[]{:S(2)}, u32[]{:S(2)}) collective-permute-start(bf16[16,2176]{1,0:T(8,128)(2,1)S(1)} %collective-permute-done.6.refs_3_), channel_id=1, source_target_pairs={{0,1},{1,0},{2,3},{3,2},{4,5},{5,4},{6,7},{7,6},{8,9},{9,8},{10,11... | collective-permute-start | bytes 208904 | tf_op jit(solution)/shard_map/ppermute | solution.py:33
  33.5 5.0 %collective-permute-start.10 = (bf16[16,2176]{1,0:T(8,128)(2,1)S(1)}, bf16[16,2176]{1,0:T(8,128)(2,1)S(1)}, u32[]{:S(2)}, u32[]{:S(2)}) collective-permute-start(bf16[16,2176]{1,0:T(8,128)(2,1)S(1)} %collective-permute-done.6.refs_3_), channel_id=1, source_target_pairs={{0,2},{2,0},{1,3},{3,1},{4,6},{6,4},{5,7},{7,5},{8,10},{10,8},{9,1... | collective-permute-start | bytes 208904 | tf_op jit(solution)/shard_map/ppermute | solution.py:33
  34.6 5.3 %collective-permute-start.9 = (bf16[16,2176]{1,0:T(8,128)(2,1)S(1)}, bf16[16,2176]{1,0:T(8,128)(2,1)S(1)}, u32[]{:S(2)}, u32[]{:S(2)}) collective-permute-start(bf16[16,2176]{1,0:T(8,128)(2,1)S(1)} %collective-permute-done.5.refs_2_), channel_id=1, source_target_pairs={{0,2},{2,0},{1,3},{3,1},{4,6},{6,4},{5,7},{7,5},{8,10},{10,8},{9,1... | collective-permute-start | bytes 208904 | tf_op jit(solution)/shard_map/ppermute | solution.py:33
  36.2 4.9 %collective-permute-start.8 = (bf16[16,2176]{1,0:T(8,128)(2,1)S(1)}, bf16[16,2176]{1,0:T(8,128)(2,1)S(1)}, u32[]{:S(2)}, u32[]{:S(2)}) collective-permute-start(bf16[16,2176]{1,0:T(8,128)(2,1)S(1)} %collective-permute-done.4.refs_1_), channel_id=1, source_target_pairs={{0,2},{2,0},{1,3},{3,1},{4,6},{6,4},{5,7},{7,5},{8,10},{10,8},{9,1... | collective-permute-start | bytes 208904 | tf_op jit(solution)/shard_map/ppermute | solution.py:33
  36.7 4.4 %collective-permute-start.13 = (bf16[16,2176]{1,0:T(8,128)(2,1)S(1)}, bf16[16,2176]{1,0:T(8,128)(2,1)S(1)}, u32[]{:S(2)}, u32[]{:S(2)}) collective-permute-start(bf16[16,2176]{1,0:T(8,128)(2,1)S(1)} %collective-permute-done.5.refs_2_), channel_id=1, source_target_pairs={{0,1},{1,0},{2,3},{3,2},{4,5},{5,4},{6,7},{7,6},{8,9},{9,8},{10,11... | collective-permute-start | bytes 208904 | tf_op jit(solution)/shard_map/ppermute | solution.py:33
  36.7 4.4 %collective-permute-start.12 = (bf16[16,2176]{1,0:T(8,128)(2,1)S(1)}, bf16[16,2176]{1,0:T(8,128)(2,1)S(1)}, u32[]{:S(2)}, u32[]{:S(2)}) collective-permute-start(bf16[16,2176]{1,0:T(8,128)(2,1)S(1)} %collective-permute-done.4.refs_1_), channel_id=1, source_target_pairs={{0,1},{1,0},{2,3},{3,2},{4,5},{5,4},{6,7},{7,6},{8,9},{9,8},{10,11... | collective-permute-start | bytes 208904 | tf_op jit(solution)/shard_map/ppermute | solution.py:33
  38.5 2.6 %collective-permute-start.18 = (bf16[16,2176]{1,0:T(8,128)(2,1)S(1)}, bf16[16,2176]{1,0:T(8,128)(2,1)S(1)}, u32[]{:S(2)}, u32[]{:S(2)}) collective-permute-start(bf16[16,2176]{1,0:T(8,128)(2,1)S(1)} %collective-permute-done.10.refs_7_), channel_id=1, source_target_pairs={{0,1},{1,0},{2,3},{3,2},{4,5},{5,4},{6,7},{7,6},{8,9},{9,8},{10,11... | collective-permute-start | bytes 208904 | tf_op jit(solution)/shard_map/ppermute | solution.py:33
  40.0 1.3 %collective-permute-start.17 = (bf16[16,2176]{1,0:T(8,128)(2,1)S(1)}, bf16[16,2176]{1,0:T(8,128)(2,1)S(1)}, u32[]{:S(2)}, u32[]{:S(2)}) collective-permute-start(bf16[16,2176]{1,0:T(8,128)(2,1)S(1)} %collective-permute-done.9.refs_6_), channel_id=1, source_target_pairs={{0,1},{1,0},{2,3},{3,2},{4,5},{5,4},{6,7},{7,6},{8,9},{9,8},{10,11... | collective-permute-start | bytes 208904 | tf_op jit(solution)/shard_map/ppermute | solution.py:33
  41.1 1.3 %collective-permute-start.16 = (bf16[16,2176]{1,0:T(8,128)(2,1)S(1)}, bf16[16,2176]{1,0:T(8,128)(2,1)S(1)}, u32[]{:S(2)}, u32[]{:S(2)}) collective-permute-start(bf16[16,2176]{1,0:T(8,128)(2,1)S(1)} %collective-permute-done.8.refs_5_), channel_id=1, source_target_pairs={{0,1},{1,0},{2,3},{3,2},{4,5},{5,4},{6,7},{7,6},{8,9},{9,8},{10,11... | collective-permute-start | bytes 208904 | tf_op jit(solution)/shard_map/ppermute | solution.py:33
  54.9 2.0 %collective-permute-start.19 = (bf16[128,2048]{1,0:T(8,128)(2,1)S(1)}, bf16[128,2048]{1,0:T(8,128)(2,1)S(1)}, u32[]{:S(2)}, u32[]{:S(2)}) collective-permute-start(bf16[128,2048]{1,0:T(8,128)(2,1)S(1)} %get-tuple-element.50), channel_id=1, source_target_pairs={{0,1},{1,0},{2,3},{3,2},{4,5},{5,4},{6,7},{7,6},{8,9},{9,8},{10,11... | collective-permute-start | bytes 1572872 | tf_op jit(solution)/shard_map/ppermute | solution.py:33
  57.0 5.0 %collective-permute-start.20 = (bf16[16,2048]{1,0:T(8,128)(2,1)S(1)}, bf16[16,2048]{1,0:T(8,128)(2,1)S(1)}, u32[]{:S(2)}, u32[]{:S(2)}) collective-permute-start(bf16[16,2048]{1,0:T(8,128)(2,1)S(1)} %get-tuple-element.52), channel_id=1, source_target_pairs={{0,2},{2,0},{1,3},{3,1},{4,6},{6,4},{5,7},{7,5},{8,10},{10,8},{9,1... | collective-permute-start | bytes 196616 | tf_op jit(solution)/shard_map/ppermute | solution.py:33
  58.2 5.2 %collective-permute-start.22 = (bf16[16,2048]{1,0:T(8,128)(2,1)S(1)}, bf16[16,2048]{1,0:T(8,128)(2,1)S(1)}, u32[]{:S(2)}, u32[]{:S(2)}) collective-permute-start(bf16[16,2048]{1,0:T(8,128)(2,1)S(1)} %get-tuple-element.54), channel_id=1, source_target_pairs={{0,2},{2,0},{1,3},{3,1},{4,6},{6,4},{5,7},{7,5},{8,10},{10,8},{9,1... | collective-permute-start | bytes 196616 | tf_op jit(solution)/shard_map/ppermute | solution.py:33
  59.1 5.7 %collective-permute-start.24 = (bf16[16,2048]{1,0:T(8,128)(2,1)S(1)}, bf16[16,2048]{1,0:T(8,128)(2,1)S(1)}, u32[]{:S(2)}, u32[]{:S(2)}) collective-permute-start(bf16[16,2048]{1,0:T(8,128)(2,1)S(1)} %get-tuple-element.56), channel_id=1, source_target_pairs={{0,2},{2,0},{1,3},{3,1},{4,6},{6,4},{5,7},{7,5},{8,10},{10,8},{9,1... | collective-permute-start | bytes 196616 | tf_op jit(solution)/shard_map/ppermute | solution.py:33
  60.2 6.4 %collective-permute-start.26 = (bf16[16,2048]{1,0:T(8,128)(2,1)S(1)}, bf16[16,2048]{1,0:T(8,128)(2,1)S(1)}, u32[]{:S(2)}, u32[]{:S(2)}) collective-permute-start(bf16[16,2048]{1,0:T(8,128)(2,1)S(1)} %get-tuple-element.58), channel_id=1, source_target_pairs={{0,2},{2,0},{1,3},{3,1},{4,6},{6,4},{5,7},{7,5},{8,10},{10,8},{9,1... | collective-permute-start | bytes 196616 | tf_op jit(solution)/shard_map/ppermute | solution.py:33
  62.0 5.0 %collective-permute-start.21 = (bf16[16,2048]{1,0:T(8,128)(2,1)S(1)}, bf16[16,2048]{1,0:T(8,128)(2,1)S(1)}, u32[]{:S(2)}, u32[]{:S(2)}) collective-permute-start(bf16[16,2048]{1,0:T(8,128)(2,1)S(1)} %sum_x1.1), channel_id=1, source_target_pairs={{0,4},{4,0},{8,12},{12,8},{1,5},{5,1},{9,13},{13,9},{2,6},{6,2},{1... | collective-permute-start | bytes 196616 | tf_op jit(solution)/shard_map/ppermute | solution.py:33
  63.4 6.6 %collective-permute-start.23 = (bf16[16,2048]{1,0:T(8,128)(2,1)S(1)}, bf16[16,2048]{1,0:T(8,128)(2,1)S(1)}, u32[]{:S(2)}, u32[]{:S(2)}) collective-permute-start(bf16[16,2048]{1,0:T(8,128)(2,1)S(1)} %sum_x2.1), channel_id=1, source_target_pairs={{0,8},{4,12},{8,0},{12,4},{1,9},{5,13},{9,1},{13,5},{2,10},{6,14},... | collective-permute-start | bytes 196616 | tf_op jit(solution)/shard_map/ppermute | solution.py:33
  64.8 6.2 %collective-permute-start.25 = (bf16[16,2048]{1,0:T(8,128)(2,1)S(1)}, bf16[16,2048]{1,0:T(8,128)(2,1)S(1)}, u32[]{:S(2)}, u32[]{:S(2)}) collective-permute-start(bf16[16,2048]{1,0:T(8,128)(2,1)S(1)} %sum_x3.1), channel_id=1, source_target_pairs={{0,12},{4,8},{8,4},{12,0},{1,13},{5,9},{9,5},{13,1},{2,14},{6,10},... | collective-permute-start | bytes 196616 | tf_op jit(solution)/shard_map/ppermute | solution.py:33

commit v6 on v5

--- a/solution.py
+++ b/solution.py
@@ -121,36 +121,32 @@
         c.wait()
 
 
-def load_kernel(n_after, source, *refs):
-    *targets, token_ref, sem = refs[n_after:]
-    copies = [
-        pltpu.make_async_copy(a, b, sem.at[i])
-        for i, (a, b) in enumerate(columns(source, targets))
-    ]
-    for c in copies:
-        c.start()
+def load_kernel(first, n_after, source, *refs):
+    target, token_ref, sem = refs[n_after:]
+    copy = pltpu.make_async_copy(source.at[:, pl.ds(first, target.shape[1])], target, sem)
+    copy.start()
     token_ref[...] = jnp.zeros_like(token_ref)
-    for c in copies:
-        c.wait()
-
-
-def load(array, parts, wanted, after, name):
-    rows, cols = array.shape
-    out = call(
-        functools.partial(load_kernel, len(after)),
-        [sds((rows, cols // parts), array.dtype)] * wanted + [sds((8, LANES), jnp.float32)],
+    copy.wait()
+
+
+def load(array, first, columns, after, name):
+    rows = array.shape[0]
+    return call(
+        functools.partial(load_kernel, first, len(after)),
+        [sds((rows, columns), array.dtype), sds((8, LANES), jnp.float32)],
         [(HBM, array)] + [(ANY, a) for a in after],
-        scratch=[pltpu.SemaphoreType.DMA((wanted,))],
+        scratch=[pltpu.SemaphoreType.DMA],
         vmem=1,
         name=name,
-        cost_us=array.size * wanted / parts * 2 / 3.4e6,
-    )
-    return out[:-1], out[-1]
+        cost_us=rows * columns * 2 / 3.4e6,
+    )
 
 
 def attention_kernel(back, kv_heads, group, q_ref, mask_ref, order_ref, *refs):
     kv_refs = refs[: back + 1]
-    weight_ref, keep_ref, send_ref, attended_ref = refs[back + 1 :]
+    weight_ref, up_hbm, keep_ref, send_ref, up_ref, attended_ref, sem = refs[back + 1 :]
+    copy = pltpu.make_async_copy(up_hbm.at[:, pl.ds(0, up_ref.shape[1])], up_ref, sem)
+    copy.start()
     block = q_ref.shape[0]
     head = HEAD_DIMENSION
     allowed = jnp.concatenate([mask_ref[...]] * group, axis=0) > 0.5
@@ -180,6 +176,7 @@
     kept = keep_ref.shape[0]
     keep_ref[...] = mixed[:kept]
     send_ref[...] = mixed[kept:].astype(jnp.bfloat16)
+    copy.wait()
 
 
 def add_kernel(keep_rows, n_in, *refs):
@@ -222,27 +219,25 @@
     normed_ref[:, width:] = info_ref[...]
 
 
-def experts_kernel(experts, capacity, tile, halves, n_rows, n_gate, n_up, *refs):
+def experts_kernel(experts, capacity, tile, halves, n_rows, *refs):
     rows_in = refs[:n_rows]
-    gate_refs = list(refs[n_rows : n_rows + n_gate])
-    up_refs = list(refs[n_rows + n_gate : n_rows + n_gate + n_up])
-    refs = refs[n_rows + n_gate + n_up :]
-    up_hbm, down_hbm, keep_ref, send_ref, rows_ref, pick_ref, packed_ref, hidden_ref = refs[:8]
-    up_late = list(refs[8 : 8 + experts - n_up])
-    down_ref, up_sem, down_sem = refs[8 + experts - n_up :]
+    gate_first, up_early, up_late, gate_hbm, up_hbm, down_hbm, keep_ref, send_ref = refs[
+        n_rows : n_rows + 8
+    ]
+    rows_ref, pick_ref, packed_ref, hidden_ref, half_ref, gate_ref, up_ref, down_ref, sem = refs[
+        n_rows + 8 :
+    ]
     per_expert, width = down_hbm.shape[0] // experts, down_hbm.shape[1]
-    up_copies = [
-        pltpu.make_async_copy(a, b, up_sem.at[i])
-        for i, (a, b) in enumerate(columns(up_hbm, up_late, n_up))
-    ]
-    up_refs += up_late
-    down_copies = [
-        pltpu.make_async_copy(
-            down_hbm.at[pl.ds(x * per_expert, per_expert)], down_ref, down_sem.at[x]
-        )
-        for x in range(experts)
-    ]
-    for c in down_copies[:1] + up_copies:
+    early = up_early.shape[1]
+    column = min(512, width)
+    gates, ups, downs = [], [], []
+    for x in range(experts):
+        cut = pl.ds(x * per_expert, per_expert)
+        downs.append(pltpu.make_async_copy(down_hbm.at[cut], down_ref, sem.at[0, x]))
+        if x:
+            gates.append(pltpu.make_async_copy(gate_hbm.at[:, cut], gate_ref.at[x - 1], sem.at[1, x]))
+            ups.append(pltpu.make_async_copy(up_hbm.at[:, cut], up_ref.at[x - 1], sem.at[2, x]))
+    for c in downs[:1] + [c for pair in zip(gates, ups) for c in pair]:
         c.start()
     count = 0
     for r in rows_in:
@@ -279,23 +274,31 @@
         )
     for x in range(experts):
         mine = slice(x * capacity, (x + 1) * capacity)
-        if x >= n_up:
-            up_copies[x - n_up].wait()
-        gate_ref, up_ref = gate_refs[x], up_refs[x]
-
+        if x:
+            gates[x - 1].wait()
         for s in range(0, per_expert, tile):
             cut = slice(s, s + tile)
-            gate = dot(packed_ref[mine, :], gate_ref[:, cut])
-            up = dot(packed_ref[mine, :], up_ref[:, cut])
+            gate = dot(packed_ref[mine, :], gate_ref[x - 1, :, cut] if x else gate_first[:, cut])
             half = 0.5 * gate
-            hidden_ref[mine, cut] = ((half + half * jnp.tanh(half)) * up).astype(jnp.bfloat16)
-        down_copies[x].wait()
-
+            half_ref[:, cut] = half + half * jnp.tanh(half)
+        if x:
+            ups[x - 1].wait()
+        for s in range(0, per_expert, tile):
+            cut = slice(s, s + tile)
+            if x:
+                weight = up_ref[x - 1, :, cut]
+            elif s < early:
+                weight = up_early[:, cut]
+            else:
+                weight = up_late[:, s - early : s - early + tile]
+            up = dot(packed_ref[mine, :], weight)
+            hidden_ref[mine, cut] = (half_ref[:, cut] * up).astype(jnp.bfloat16)
+        downs[x].wait()
         for c in range(0, width, column):
             out = dot(hidden_ref[mine, :], down_ref[:, c : c + column])
             packed_ref[mine, c : c + column] = (out * shares[x]).astype(jnp.bfloat16)
         if x + 1 < experts:
-            down_copies[x + 1].start()
+            downs[x + 1].start()
     kept = keep_ref.shape[0]
 
     for c in range(0, width, column):
@@ -355,7 +358,7 @@
             sds((own_rows, width), f32),
             sds((own_rows, LANES), bf16),
         ]
-        + [sds((width, per_expert), bf16)] * experts,
+        + [sds((width, per_expert), bf16)],
         [
             (HBM, a)
             for a in (
@@ -368,18 +371,19 @@
             pltpu.VMEM((2, block), jnp.int32),
             pltpu.VMEM((2, block), jnp.int32),
             pltpu.VMEM(residual.shape, bf16),
-            pltpu.SemaphoreType.DMA((7 + experts,)),
+            pltpu.SemaphoreType.DMA((8,)),
         ],
         vmem=6,
         name="prepare",
-        cost_us=6.0,
+        cost_us=4.0,
     )
     half = block // pp_count
-    keep, send = call(
+    early = max(LANES, per_expert // 2)
+    keep, send, up_early = call(
         functools.partial(attention_kernel, back, kv_heads, group),
-        [sds((half, width), f32), sds((block - half, width), bf16)],
-        [(VMEM, a) for a in (query_v, mask, order, *pieces, weight_v)],
-        scratch=[pltpu.VMEM(query.shape, bf16)],
+        [sds((half, width), f32), sds((block - half, width), bf16), sds((width, early), bf16)],
+        [(VMEM, a) for a in (query_v, mask, order, *pieces, weight_v)] + [(HBM, w_up[0])],
+        scratch=[pltpu.VMEM(query.shape, bf16), pltpu.SemaphoreType.DMA],
         name="attention",
         cost_us=2.4,
     )
@@ -388,7 +392,7 @@
         [keep] + [xor_swap(send, "pp", 1)], [own_rows], [own_rows] * (tp_count - 1), "sum_cores"
     )
     got = [xor_swap(sends[k - 1], "tp", k) for k in range(1, tp_count)]
-    up_v, token = load(w_up[0], experts, 1, [own], "load_up")
+    up_late, token = load(w_up[0], early, per_expert - early, [own], "load_up")
     stream, normed = call(
         functools.partial(norm_kernel, tp_count),
         [sds((own_rows, width), f32), sds((own_rows, width + LANES), bf16)],
@@ -414,23 +418,25 @@
     count = sec_count * block
     capacity = sec_count * MOSTB
     down = w_down[0]
-    tile = min(512, down.shape[0] // experts)
+    tile = min(512, early, per_expert - early)
     kept = count // pp_count
     keep, send = call(
-        functools.partial(experts_kernel, experts, capacity, tile, halves, len(rows), experts, 1),
+        functools.partial(experts_kernel, experts, capacity, tile, halves, len(rows)),
         [sds((kept, width), f32), sds((count - kept, width), bf16)],
-        [(VMEM, a) for a in (*rows, *gate_v, *up_v)] + [(HBM, w_up[0]), (HBM, down)],
+        [(VMEM, a) for a in (*rows, *gate_v, up_early, up_late)]
+        + [(HBM, a) for a in (w_gate[0], w_up[0], down)],
         scratch=[
             pltpu.VMEM((count, width + LANES), bf16),
             pltpu.VMEM((experts * capacity, count), bf16),
             pltpu.VMEM((experts * capacity, width), bf16),
             pltpu.VMEM((experts * capacity, down.shape[0] // experts), bf16),
-            *[pltpu.VMEM((width, per_expert), bf16)] * (experts - 1),
+            pltpu.VMEM((capacity, per_expert), f32),
+            pltpu.VMEM((max(1, experts - 1), width, per_expert), bf16),
+            pltpu.VMEM((max(1, experts - 1), width, per_expert), bf16),
             pltpu.VMEM((per_expert, width), bf16),
-            pltpu.SemaphoreType.DMA((experts,)),
-            pltpu.SemaphoreType.DMA((experts,)),
+            pltpu.SemaphoreType.DMA((3, experts)),
         ],
-        vmem=24,
+        vmem=33,
         name="experts",
         cost_us=12.0,
     )

time: 72 us -> 73.4 us (1.019)
  waiting for transfers between devices: 18.7 us -> 19.7 us
    ppermute x25, waiting for transfers between devices: 18.7 us -> 19.7 us  [xor_swap(): return lax.ppermute(x, axis, [(i, i ^ k) for i in range(n)])]
  transfers between devices with their start and end apart: 27 -> 27, of which waited for: 14 -> 15; matrix products, arithmetic and copies ran while one was open for 0% -> 0% of each run, Pallas kernels for 15% -> 10%
where the time goes in v6:
time: 73.4 us; the launch traced here: 73.1 us
  starting transfers between devices  26.5 us (36%)
  Pallas kernels  25.9 us (35%)
  waiting for transfers between devices  19.7 us (27%)
  local copies, waits for them, and re-layouts  0.78 us (1%)
    pallas_call x11, Pallas kernels, call(): pl.pallas_call(kernel, out_shape=out_shape, in_specs=[s for s, _ in args]...  25.9 us
    ppermute x25, waiting for transfers between devices, xor_swap(): return lax.ppermute(x, axis, [(i, i ^ k) for i in range(n)])  19.7 us
    ppermute x25, starting transfers between devices, xor_swap(): return lax.ppermute(x, axis, [(i, i ^ k) for i in range(n)])  17 us
    ppermute x2, starting transfers between devices, per_device(): lax.ppermute(kv, 'sec', [(i, i + k) for i in range(sec_count - k)])  9.43 us
  transfers between devices with their start and end apart: 27, of which 15 were waited for; matrix products, arithmetic and copies ran while one was open for 0% of the time, Pallas kernels for 10%

profile of v6, /device:TPU:0, one launch (start us, length us, event | category | flops | bytes accessed | tf_op | source)
XLA Modules:
  0.0 73.1 jit_solution(6843532266510930967)
XLA Ops:
  0.0 0.8 %constant_dynamic-slice_fusion = (bf16[64,256]{1,0:T(8,128)(2,1)S(1)}, bf16[64,256]{1,0:T(8,128)(2,1)S(1)}) fusion(bf16[64,512]{1,0:T(8,128)(2,1)} %param.14, s32[]{:T(128)S(6)} %select_n.10, bf16[64,512]{1,0:T(8,128)(2,1)} %param.13), kind=kLoop, calls=%fused_computation.1 | loop fusion | bytes 131076 | tf_op jit(solution)/shard_map/dynamic_slice | solution.py:339
  0.8 4.9 %collective-permute-start.1 = (bf16[64,512]{1,0:T(8,128)(2,1)S(1)}, bf16[64,512]{1,0:T(8,128)(2,1)S(1)}, u32[]{:S(2)}, u32[]{:S(2)}) collective-permute-start(bf16[64,512]{1,0:T(8,128)(2,1)S(1)} %pad_maximum_fusion.refs_2_), channel_id=1, source_target_pairs={{0,4},{4,8},{8,12},{1,5},{5,9},{9,13},{2,6},{6,10},{10,14},{3,7},{... | collective-permute-start | bytes 196616 | tf_op jit(solution)/shard_map/ppermute | solution.py:343
  5.7 4.5 %collective-permute-start = (bf16[64,512]{1,0:T(8,128)(2,1)S(1)}, bf16[64,512]{1,0:T(8,128)(2,1)S(1)}, u32[]{:S(2)}, u32[]{:S(2)}) collective-permute-start(bf16[64,512]{1,0:T(8,128)(2,1)S(1)} %pad_maximum_fusion.refs_2_), channel_id=1, source_target_pairs={{0,8},{4,12},{1,9},{5,13},{2,10},{6,14},{3,11},{7,15},{16,24},{20,... | collective-permute-start | bytes 196616 | tf_op jit(solution)/shard_map/ppermute | solution.py:343
  10.2 4.9 %prepare.1 = (bf16[64,1024]{1,0:T(8,128)(2,1)S(1)}, bf16[1024,2048]{1,0:T(8,128)(2,1)S(1)}, f32[1,2048]{1,0:T(1,128)S(1)}, f32[64,192]{1,0:T(8,128)S(1)}, bf16[6...) custom-call(s32[8]{0:T(128)} %lengths_hbm.1, ...), custom_call_target="tpu_custom_call" | custom-call | bytes 13600000 | tf_op jit(solution)/shard_map/prepare/pallas_call | solution.py:41
  15.2 2.7 %attention.1 = (f32[32,2048]{1,0:T(8,128)S(1)}, bf16[32,2048]{1,0:T(8,128)(2,1)S(1)}, bf16[2048,1024]{1,0:T(8,128)(2,1)S(1)}) custom-call(bf16[64,1024]{1,0:T(8,128)(2,1)S(1)} %get-tuple-element.35.q_ref, f32[64,192]{1,0:T(8,128)S(1)} %get-tuple-element.36.mask_ref, bf16[64,64]{1,0:T(8,128)(2,1)S(1)} %get-tuple-element.37.order_ref, ...), custom_call_target="tpu_custom_call" | custom-call | bytes 8160000 | tf_op jit(solution)/shard_map/attention/pallas_call | solution.py:41
  18.0 1.3 %collective-permute-done.2.refs_1_ = bf16[32,2048]{1,0:T(8,128)(2,1)S(1)} collective-permute-done((bf16[32,2048]{1,0:T(8,128)(2,1)S(1)}, bf16[32,2048]{1,0:T(8,128)(2,1)S(1)}, u32[]{:S(2)}, u32[]{:S(2)}) %collective-permute-start.2) | collective-permute-done | bytes 131104 | tf_op jit(solution)/shard_map/ppermute | solution.py:33
  19.3 1.6 %collective-permute-start.3 = (bf16[16,2048]{1,0:T(8,128)(2,1)S(1)}, bf16[16,2048]{1,0:T(8,128)(2,1)S(1)}, u32[]{:S(2)}, u32[]{:S(2)}) collective-permute-start(bf16[16,2048]{1,0:T(8,128)(2,1)S(1)} %get-tuple-element.42), channel_id=1, source_target_pairs={{0,2},{2,0},{1,3},{3,1},{4,6},{6,4},{5,7},{7,5},{8,10},{10,8},{9,1... | collective-permute-start | bytes 196616 | tf_op jit(solution)/shard_map/ppermute | solution.py:33
  20.9 2.2 %load_up.1 = (bf16[2048,1024]{1,0:T(8,128)(2,1)S(1)}, f32[8,128]{1,0:T(8,128)S(1)}) custom-call(bf16[2048,4096]{1,0:T(8,128)(2,1)} %bitcast.7, f32[16,2048]{1,0:T(8,128)S(1)} %get-tuple-element.41.refs_0_), custom_call_target="tpu_custom_call" | custom-call | bytes 4194303 | tf_op jit(solution)/shard_map/load_up/pallas_call | solution.py:41
  23.1 0.6 collective-permute-done.3.refs_1_
  23.8 1.6 %collective-permute-start.7 = (bf16[16,2176]{1,0:T(8,128)(2,1)S(1)}, bf16[16,2176]{1,0:T(8,128)(2,1)S(1)}, u32[]{:S(2)}, u32[]{:S(2)}) collective-permute-start(bf16[16,2176]{1,0:T(8,128)(2,1)S(1)} %get-tuple-element.45.refs_0_), channel_id=1, source_target_pairs={{0,2},{2,0},{1,3},{3,1},{4,6},{6,4},{5,7},{7,5},{8,10},{10,8},{9,1... | collective-permute-start | bytes 208904 | tf_op jit(solution)/shard_map/ppermute | solution.py:33
  25.3 0.8 %collective-permute-start.5 = (bf16[16,2176]{1,0:T(8,128)(2,1)S(1)}, bf16[16,2176]{1,0:T(8,128)(2,1)S(1)}, u32[]{:S(2)}, u32[]{:S(2)}) collective-permute-start(bf16[16,2176]{1,0:T(8,128)(2,1)S(1)} %get-tuple-element.45.refs_0_), channel_id=1, source_target_pairs={{0,8},{4,12},{8,0},{12,4},{1,9},{5,13},{9,1},{13,5},{2,10},{6,14},... | collective-permute-start | bytes 208904 | tf_op jit(solution)/shard_map/ppermute | solution.py:33
  26.2 3.5 %collective-permute-start.4 = (bf16[16,2176]{1,0:T(8,128)(2,1)S(1)}, bf16[16,2176]{1,0:T(8,128)(2,1)S(1)}, u32[]{:S(2)}, u32[]{:S(2)}) collective-permute-start(bf16[16,2176]{1,0:T(8,128)(2,1)S(1)} %get-tuple-element.45.refs_0_), channel_id=1, source_target_pairs={{0,4},{4,0},{8,12},{12,8},{1,5},{5,1},{9,13},{13,9},{2,6},{6,2},{1... | collective-permute-start | bytes 208904 | tf_op jit(solution)/shard_map/ppermute | solution.py:33
  29.7 2.6 %collective-permute-done.6.refs_3_ = bf16[16,2176]{1,0:T(8,128)(2,1)S(1)} collective-permute-done((bf16[16,2176]{1,0:T(8,128)(2,1)S(1)}, bf16[16,2176]{1,0:T(8,128)(2,1)S(1)}, u32[]{:S(2)}, u32[]{:S(2)}) %collective-permute-start.6) | collective-permute-done | bytes 69664 | tf_op jit(solution)/shard_map/ppermute | solution.py:33
  32.3 0.5 collective-permute-start.10
  32.9 1.5 %collective-permute-start.9 = (bf16[16,2176]{1,0:T(8,128)(2,1)S(1)}, bf16[16,2176]{1,0:T(8,128)(2,1)S(1)}, u32[]{:S(2)}, u32[]{:S(2)}) collective-permute-start(bf16[16,2176]{1,0:T(8,128)(2,1)S(1)} %collective-permute-done.5.refs_2_), channel_id=1, source_target_pairs={{0,2},{2,0},{1,3},{3,1},{4,6},{6,4},{5,7},{7,5},{8,10},{10,8},{9,1... | collective-permute-start | bytes 208904 | tf_op jit(solution)/shard_map/ppermute | solution.py:33
  34.4 0.5 collective-permute-start.8
  35.4 1.9 %collective-permute-done.10.refs_7_ = bf16[16,2176]{1,0:T(8,128)(2,1)S(1)} collective-permute-done((bf16[16,2176]{1,0:T(8,128)(2,1)S(1)}, bf16[16,2176]{1,0:T(8,128)(2,1)S(1)}, u32[]{:S(2)}, u32[]{:S(2)}) %collective-permute-start.10) | collective-permute-done | bytes 69664 | tf_op jit(solution)/shard_map/ppermute | solution.py:33
  37.3 1.5 %collective-permute-done.9.refs_6_ = bf16[16,2176]{1,0:T(8,128)(2,1)S(1)} collective-permute-done((bf16[16,2176]{1,0:T(8,128)(2,1)S(1)}, bf16[16,2176]{1,0:T(8,128)(2,1)S(1)}, u32[]{:S(2)}, u32[]{:S(2)}) %collective-permute-start.9) | collective-permute-done | bytes 69664 | tf_op jit(solution)/shard_map/ppermute | solution.py:33
  38.8 1.1 %collective-permute-done.8.refs_5_ = bf16[16,2176]{1,0:T(8,128)(2,1)S(1)} collective-permute-done((bf16[16,2176]{1,0:T(8,128)(2,1)S(1)}, bf16[16,2176]{1,0:T(8,128)(2,1)S(1)}, u32[]{:S(2)}, u32[]{:S(2)}) %collective-permute-start.8) | collective-permute-done | bytes 69664 | tf_op jit(solution)/shard_map/ppermute | solution.py:33
  40.1 1.1 %collective-permute-done.16.refs_13_ = bf16[16,2176]{1,0:T(8,128)(2,1)S(1)} collective-permute-done((bf16[16,2176]{1,0:T(8,128)(2,1)S(1)}, bf16[16,2176]{1,0:T(8,128)(2,1)S(1)}, u32[]{:S(2)}, u32[]{:S(2)}) %collective-permute-start.16) | collective-permute-done | bytes 69664 | tf_op jit(solution)/shard_map/ppermute | solution.py:33
  41.2 15.2 %experts.1 = (f32[128,2048]{1,0:T(8,128)S(1)}, bf16[128,2048]{1,0:T(8,128)(2,1)S(1)}) custom-call(bf16[16,2176]{1,0:T(8,128)(2,1)S(1)} %get-tuple-element.45.refs_0_, bf16[16,2176]{1,0:T(8,128)(2,1)S(1)} %collective-permute-done.4.refs_1_, bf16[16,2176]{1,0:T(8,128)(2,1)S(1)} %collective-permute-done.5.refs_2_, ...), custom_call_target="tpu_custom_call" | custom-call | bytes 40800000 | tf_op jit(solution)/shard_map/experts/pallas_call | solution.py:41
  56.6 1.8 %collective-permute-done.19.refs_1_ = bf16[128,2048]{1,0:T(8,128)(2,1)S(1)} collective-permute-done((bf16[128,2048]{1,0:T(8,128)(2,1)S(1)}, bf16[128,2048]{1,0:T(8,128)(2,1)S(1)}, u32[]{:S(2)}, u32[]{:S(2)}) %collective-permute-start.19) | collective-permute-done | bytes 524320 | tf_op jit(solution)/shard_map/ppermute | solution.py:33
  58.4 0.6 collective-permute-start.20
  59.0 1.5 %collective-permute-start.22 = (bf16[16,2048]{1,0:T(8,128)(2,1)S(1)}, bf16[16,2048]{1,0:T(8,128)(2,1)S(1)}, u32[]{:S(2)}, u32[]{:S(2)}) collective-permute-start(bf16[16,2048]{1,0:T(8,128)(2,1)S(1)} %get-tuple-element.54), channel_id=1, source_target_pairs={{0,2},{2,0},{1,3},{3,1},{4,6},{6,4},{5,7},{7,5},{8,10},{10,8},{9,1... | collective-permute-start | bytes 196616 | tf_op jit(solution)/shard_map/ppermute | solution.py:33
  61.1 1.5 %collective-permute-start.26 = (bf16[16,2048]{1,0:T(8,128)(2,1)S(1)}, bf16[16,2048]{1,0:T(8,128)(2,1)S(1)}, u32[]{:S(2)}, u32[]{:S(2)}) collective-permute-start(bf16[16,2048]{1,0:T(8,128)(2,1)S(1)} %get-tuple-element.58), channel_id=1, source_target_pairs={{0,2},{2,0},{1,3},{3,1},{4,6},{6,4},{5,7},{7,5},{8,10},{10,8},{9,1... | collective-permute-start | bytes 196616 | tf_op jit(solution)/shard_map/ppermute | solution.py:33
  62.6 0.9 %collective-permute-done.20.refs_1_ = bf16[16,2048]{1,0:T(8,128)(2,1)S(1)} collective-permute-done((bf16[16,2048]{1,0:T(8,128)(2,1)S(1)}, bf16[16,2048]{1,0:T(8,128)(2,1)S(1)}, u32[]{:S(2)}, u32[]{:S(2)}) %collective-permute-start.20) | collective-permute-done | bytes 65568 | tf_op jit(solution)/shard_map/ppermute | solution.py:33
  63.5 1.3 %collective-permute-done.22.refs_1_ = bf16[16,2048]{1,0:T(8,128)(2,1)S(1)} collective-permute-done((bf16[16,2048]{1,0:T(8,128)(2,1)S(1)}, bf16[16,2048]{1,0:T(8,128)(2,1)S(1)}, u32[]{:S(2)}, u32[]{:S(2)}) %collective-permute-start.22) | collective-permute-done | bytes 65568 | tf_op jit(solution)/shard_map/ppermute | solution.py:33
  65.0 1.2 %collective-permute-done.24.refs_1_ = bf16[16,2048]{1,0:T(8,128)(2,1)S(1)} collective-permute-done((bf16[16,2048]{1,0:T(8,128)(2,1)S(1)}, bf16[16,2048]{1,0:T(8,128)(2,1)S(1)}, u32[]{:S(2)}, u32[]{:S(2)}) %collective-permute-start.24) | collective-permute-done | bytes 65568 | tf_op jit(solution)/shard_map/ppermute | solution.py:33
  66.2 1.9 %collective-permute-start.25 = (bf16[16,2048]{1,0:T(8,128)(2,1)S(1)}, bf16[16,2048]{1,0:T(8,128)(2,1)S(1)}, u32[]{:S(2)}, u32[]{:S(2)}) collective-permute-start(bf16[16,2048]{1,0:T(8,128)(2,1)S(1)} %sum_x3.1), channel_id=1, source_target_pairs={{0,12},{4,8},{8,4},{12,0},{1,13},{5,9},{9,5},{13,1},{2,14},{6,10},... | collective-permute-start | bytes 196616 | tf_op jit(solution)/shard_map/ppermute | solution.py:33
  68.5 2.9 %collective-permute-done.23.refs_2_ = bf16[16,2048]{1,0:T(8,128)(2,1)S(1)} collective-permute-done((bf16[16,2048]{1,0:T(8,128)(2,1)S(1)}, bf16[16,2048]{1,0:T(8,128)(2,1)S(1)}, u32[]{:S(2)}, u32[]{:S(2)}) %collective-permute-start.23) | collective-permute-done | bytes 65568 | tf_op jit(solution)/shard_map/ppermute | solution.py:33
  71.4 1.0 %collective-permute-done.25.refs_3_ = bf16[16,2048]{1,0:T(8,128)(2,1)S(1)} collective-permute-done((bf16[16,2048]{1,0:T(8,128)(2,1)S(1)}, bf16[16,2048]{1,0:T(8,128)(2,1)S(1)}, u32[]{:S(2)}, u32[]{:S(2)}) %collective-permute-start.25) | collective-permute-done | bytes 65568 | tf_op jit(solution)/shard_map/ppermute | solution.py:33
  72.4 0.7 total.1
  (35 shorter events, 2.3 us)
Async XLA Ops:
  0.8 14.4 %collective-permute-start.1 = (bf16[64,512]{1,0:T(8,128)(2,1)S(1)}, bf16[64,512]{1,0:T(8,128)(2,1)S(1)}, u32[]{:S(2)}, u32[]{:S(2)}) collective-permute-start(bf16[64,512]{1,0:T(8,128)(2,1)S(1)} %pad_maximum_fusion.refs_2_), channel_id=1, source_target_pairs={{0,4},{4,8},{8,12},{1,5},{5,9},{9,13},{2,6},{6,10},{10,14},{3,7},{... | collective-permute-start | bytes 196616 | tf_op jit(solution)/shard_map/ppermute | solution.py:343
  5.7 9.5 %collective-permute-start = (bf16[64,512]{1,0:T(8,128)(2,1)S(1)}, bf16[64,512]{1,0:T(8,128)(2,1)S(1)}, u32[]{:S(2)}, u32[]{:S(2)}) collective-permute-start(bf16[64,512]{1,0:T(8,128)(2,1)S(1)} %pad_maximum_fusion.refs_2_), channel_id=1, source_target_pairs={{0,8},{4,12},{1,9},{5,13},{2,10},{6,14},{3,11},{7,15},{16,24},{20,... | collective-permute-start | bytes 196616 | tf_op jit(solution)/shard_map/ppermute | solution.py:343
  17.9 1.4 %collective-permute-start.2 = (bf16[32,2048]{1,0:T(8,128)(2,1)S(1)}, bf16[32,2048]{1,0:T(8,128)(2,1)S(1)}, u32[]{:S(2)}, u32[]{:S(2)}) collective-permute-start(bf16[32,2048]{1,0:T(8,128)(2,1)S(1)} %get-tuple-element.40), channel_id=1, source_target_pairs={{0,1},{1,0},{2,3},{3,2},{4,5},{5,4},{6,7},{7,6},{8,9},{9,8},{10,11... | collective-permute-start | bytes 393224 | tf_op jit(solution)/shard_map/ppermute | solution.py:33
  19.3 4.3 %collective-permute-start.3 = (bf16[16,2048]{1,0:T(8,128)(2,1)S(1)}, bf16[16,2048]{1,0:T(8,128)(2,1)S(1)}, u32[]{:S(2)}, u32[]{:S(2)}) collective-permute-start(bf16[16,2048]{1,0:T(8,128)(2,1)S(1)} %get-tuple-element.42), channel_id=1, source_target_pairs={{0,2},{2,0},{1,3},{3,1},{4,6},{6,4},{5,7},{7,5},{8,10},{10,8},{9,1... | collective-permute-start | bytes 196616 | tf_op jit(solution)/shard_map/ppermute | solution.py:33
  23.8 6.0 %collective-permute-start.7 = (bf16[16,2176]{1,0:T(8,128)(2,1)S(1)}, bf16[16,2176]{1,0:T(8,128)(2,1)S(1)}, u32[]{:S(2)}, u32[]{:S(2)}) collective-permute-start(bf16[16,2176]{1,0:T(8,128)(2,1)S(1)} %get-tuple-element.45.refs_0_), channel_id=1, source_target_pairs={{0,2},{2,0},{1,3},{3,1},{4,6},{6,4},{5,7},{7,5},{8,10},{10,8},{9,1... | collective-permute-start | bytes 208904 | tf_op jit(solution)/shard_map/ppermute | solution.py:33
  25.3 7.0 %collective-permute-start.6 = (bf16[16,2176]{1,0:T(8,128)(2,1)S(1)}, bf16[16,2176]{1,0:T(8,128)(2,1)S(1)}, u32[]{:S(2)}, u32[]{:S(2)}) collective-permute-start(bf16[16,2176]{1,0:T(8,128)(2,1)S(1)} %get-tuple-element.45.refs_0_), channel_id=1, source_target_pairs={{0,12},{4,8},{8,4},{12,0},{1,13},{5,9},{9,5},{13,1},{2,14},{6,10},... | collective-permute-start | bytes 208904 | tf_op jit(solution)/shard_map/ppermute | solution.py:33
  25.3 7.0 %collective-permute-start.11 = (bf16[16,2176]{1,0:T(8,128)(2,1)S(1)}, bf16[16,2176]{1,0:T(8,128)(2,1)S(1)}, u32[]{:S(2)}, u32[]{:S(2)}) collective-permute-start(bf16[16,2176]{1,0:T(8,128)(2,1)S(1)} %get-tuple-element.45.refs_0_), channel_id=1, source_target_pairs={{0,1},{1,0},{2,3},{3,2},{4,5},{5,4},{6,7},{7,6},{8,9},{9,8},{10,11... | collective-permute-start | bytes 208904 | tf_op jit(solution)/shard_map/ppermute | solution.py:33
  25.3 7.5 %collective-permute-start.5 = (bf16[16,2176]{1,0:T(8,128)(2,1)S(1)}, bf16[16,2176]{1,0:T(8,128)(2,1)S(1)}, u32[]{:S(2)}, u32[]{:S(2)}) collective-permute-start(bf16[16,2176]{1,0:T(8,128)(2,1)S(1)} %get-tuple-element.45.refs_0_), channel_id=1, source_target_pairs={{0,8},{4,12},{8,0},{12,4},{1,9},{5,13},{9,1},{13,5},{2,10},{6,14},... | collective-permute-start | bytes 208904 | tf_op jit(solution)/shard_map/ppermute | solution.py:33
  26.2 8.2 %collective-permute-start.4 = (bf16[16,2176]{1,0:T(8,128)(2,1)S(1)}, bf16[16,2176]{1,0:T(8,128)(2,1)S(1)}, u32[]{:S(2)}, u32[]{:S(2)}) collective-permute-start(bf16[16,2176]{1,0:T(8,128)(2,1)S(1)} %get-tuple-element.45.refs_0_), channel_id=1, source_target_pairs={{0,4},{4,0},{8,12},{12,8},{1,5},{5,1},{9,13},{13,9},{2,6},{6,2},{1... | collective-permute-start | bytes 208904 | tf_op jit(solution)/shard_map/ppermute | solution.py:33
  29.7 5.2 %collective-permute-start.15 = (bf16[16,2176]{1,0:T(8,128)(2,1)S(1)}, bf16[16,2176]{1,0:T(8,128)(2,1)S(1)}, u32[]{:S(2)}, u32[]{:S(2)}) collective-permute-start(bf16[16,2176]{1,0:T(8,128)(2,1)S(1)} %collective-permute-done.7.refs_4_), channel_id=1, source_target_pairs={{0,1},{1,0},{2,3},{3,2},{4,5},{5,4},{6,7},{7,6},{8,9},{9,8},{10,11... | collective-permute-start | bytes 208904 | tf_op jit(solution)/shard_map/ppermute | solution.py:33
  32.3 2.6 %collective-permute-start.14 = (bf16[16,2176]{1,0:T(8,128)(2,1)S(1)}, bf16[16,2176]{1,0:T(8,128)(2,1)S(1)}, u32[]{:S(2)}, u32[]{:S(2)}) collective-permute-start(bf16[16,2176]{1,0:T(8,128)(2,1)S(1)} %collective-permute-done.6.refs_3_), channel_id=1, source_target_pairs={{0,1},{1,0},{2,3},{3,2},{4,5},{5,4},{6,7},{7,6},{8,9},{9,8},{10,11... | collective-permute-start | bytes 208904 | tf_op jit(solution)/shard_map/ppermute | solution.py:33
  32.3 5.0 %collective-permute-start.10 = (bf16[16,2176]{1,0:T(8,128)(2,1)S(1)}, bf16[16,2176]{1,0:T(8,128)(2,1)S(1)}, u32[]{:S(2)}, u32[]{:S(2)}) collective-permute-start(bf16[16,2176]{1,0:T(8,128)(2,1)S(1)} %collective-permute-done.6.refs_3_), channel_id=1, source_target_pairs={{0,2},{2,0},{1,3},{3,1},{4,6},{6,4},{5,7},{7,5},{8,10},{10,8},{9,1... | collective-permute-start | bytes 208904 | tf_op jit(solution)/shard_map/ppermute | solution.py:33
  32.9 5.9 %collective-permute-start.9 = (bf16[16,2176]{1,0:T(8,128)(2,1)S(1)}, bf16[16,2176]{1,0:T(8,128)(2,1)S(1)}, u32[]{:S(2)}, u32[]{:S(2)}) collective-permute-start(bf16[16,2176]{1,0:T(8,128)(2,1)S(1)} %collective-permute-done.5.refs_2_), channel_id=1, source_target_pairs={{0,2},{2,0},{1,3},{3,1},{4,6},{6,4},{5,7},{7,5},{8,10},{10,8},{9,1... | collective-permute-start | bytes 208904 | tf_op jit(solution)/shard_map/ppermute | solution.py:33
  34.4 5.5 %collective-permute-start.8 = (bf16[16,2176]{1,0:T(8,128)(2,1)S(1)}, bf16[16,2176]{1,0:T(8,128)(2,1)S(1)}, u32[]{:S(2)}, u32[]{:S(2)}) collective-permute-start(bf16[16,2176]{1,0:T(8,128)(2,1)S(1)} %collective-permute-done.4.refs_1_), channel_id=1, source_target_pairs={{0,2},{2,0},{1,3},{3,1},{4,6},{6,4},{5,7},{7,5},{8,10},{10,8},{9,1... | collective-permute-start | bytes 208904 | tf_op jit(solution)/shard_map/ppermute | solution.py:33
  34.9 5.0 %collective-permute-start.13 = (bf16[16,2176]{1,0:T(8,128)(2,1)S(1)}, bf16[16,2176]{1,0:T(8,128)(2,1)S(1)}, u32[]{:S(2)}, u32[]{:S(2)}) collective-permute-start(bf16[16,2176]{1,0:T(8,128)(2,1)S(1)} %collective-permute-done.5.refs_2_), channel_id=1, source_target_pairs={{0,1},{1,0},{2,3},{3,2},{4,5},{5,4},{6,7},{7,6},{8,9},{9,8},{10,11... | collective-permute-start | bytes 208904 | tf_op jit(solution)/shard_map/ppermute | solution.py:33
  34.9 5.0 %collective-permute-start.12 = (bf16[16,2176]{1,0:T(8,128)(2,1)S(1)}, bf16[16,2176]{1,0:T(8,128)(2,1)S(1)}, u32[]{:S(2)}, u32[]{:S(2)}) collective-permute-start(bf16[16,2176]{1,0:T(8,128)(2,1)S(1)} %collective-permute-done.4.refs_1_), channel_id=1, source_target_pairs={{0,1},{1,0},{2,3},{3,2},{4,5},{5,4},{6,7},{7,6},{8,9},{9,8},{10,11... | collective-permute-start | bytes 208904 | tf_op jit(solution)/shard_map/ppermute | solution.py:33
  37.3 2.6 %collective-permute-start.18 = (bf16[16,2176]{1,0:T(8,128)(2,1)S(1)}, bf16[16,2176]{1,0:T(8,128)(2,1)S(1)}, u32[]{:S(2)}, u32[]{:S(2)}) collective-permute-start(bf16[16,2176]{1,0:T(8,128)(2,1)S(1)} %collective-permute-done.10.refs_7_), channel_id=1, source_target_pairs={{0,1},{1,0},{2,3},{3,2},{4,5},{5,4},{6,7},{7,6},{8,9},{9,8},{10,11... | collective-permute-start | bytes 208904 | tf_op jit(solution)/shard_map/ppermute | solution.py:33
  38.8 1.3 %collective-permute-start.17 = (bf16[16,2176]{1,0:T(8,128)(2,1)S(1)}, bf16[16,2176]{1,0:T(8,128)(2,1)S(1)}, u32[]{:S(2)}, u32[]{:S(2)}) collective-permute-start(bf16[16,2176]{1,0:T(8,128)(2,1)S(1)} %collective-permute-done.9.refs_6_), channel_id=1, source_target_pairs={{0,1},{1,0},{2,3},{3,2},{4,5},{5,4},{6,7},{7,6},{8,9},{9,8},{10,11... | collective-permute-start | bytes 208904 | tf_op jit(solution)/shard_map/ppermute | solution.py:33
  39.9 1.3 %collective-permute-start.16 = (bf16[16,2176]{1,0:T(8,128)(2,1)S(1)}, bf16[16,2176]{1,0:T(8,128)(2,1)S(1)}, u32[]{:S(2)}, u32[]{:S(2)}) collective-permute-start(bf16[16,2176]{1,0:T(8,128)(2,1)S(1)} %collective-permute-done.8.refs_5_), channel_id=1, source_target_pairs={{0,1},{1,0},{2,3},{3,2},{4,5},{5,4},{6,7},{7,6},{8,9},{9,8},{10,11... | collective-permute-start | bytes 208904 | tf_op jit(solution)/shard_map/ppermute | solution.py:33
  56.4 2.0 %collective-permute-start.19 = (bf16[128,2048]{1,0:T(8,128)(2,1)S(1)}, bf16[128,2048]{1,0:T(8,128)(2,1)S(1)}, u32[]{:S(2)}, u32[]{:S(2)}) collective-permute-start(bf16[128,2048]{1,0:T(8,128)(2,1)S(1)} %get-tuple-element.50), channel_id=1, source_target_pairs={{0,1},{1,0},{2,3},{3,2},{4,5},{5,4},{6,7},{7,6},{8,9},{9,8},{10,11... | collective-permute-start | bytes 1572872 | tf_op jit(solution)/shard_map/ppermute | solution.py:33
  58.4 5.0 %collective-permute-start.20 = (bf16[16,2048]{1,0:T(8,128)(2,1)S(1)}, bf16[16,2048]{1,0:T(8,128)(2,1)S(1)}, u32[]{:S(2)}, u32[]{:S(2)}) collective-permute-start(bf16[16,2048]{1,0:T(8,128)(2,1)S(1)} %get-tuple-element.52), channel_id=1, source_target_pairs={{0,2},{2,0},{1,3},{3,1},{4,6},{6,4},{5,7},{7,5},{8,10},{10,8},{9,1... | collective-permute-start | bytes 196616 | tf_op jit(solution)/shard_map/ppermute | solution.py:33
  59.0 5.8 %collective-permute-start.22 = (bf16[16,2048]{1,0:T(8,128)(2,1)S(1)}, bf16[16,2048]{1,0:T(8,128)(2,1)S(1)}, u32[]{:S(2)}, u32[]{:S(2)}) collective-permute-start(bf16[16,2048]{1,0:T(8,128)(2,1)S(1)} %get-tuple-element.54), channel_id=1, source_target_pairs={{0,2},{2,0},{1,3},{3,1},{4,6},{6,4},{5,7},{7,5},{8,10},{10,8},{9,1... | collective-permute-start | bytes 196616 | tf_op jit(solution)/shard_map/ppermute | solution.py:33
  60.5 5.6 %collective-permute-start.24 = (bf16[16,2048]{1,0:T(8,128)(2,1)S(1)}, bf16[16,2048]{1,0:T(8,128)(2,1)S(1)}, u32[]{:S(2)}, u32[]{:S(2)}) collective-permute-start(bf16[16,2048]{1,0:T(8,128)(2,1)S(1)} %get-tuple-element.56), channel_id=1, source_target_pairs={{0,2},{2,0},{1,3},{3,1},{4,6},{6,4},{5,7},{7,5},{8,10},{10,8},{9,1... | collective-permute-start | bytes 196616 | tf_op jit(solution)/shard_map/ppermute | solution.py:33
  61.1 7.0 %collective-permute-start.26 = (bf16[16,2048]{1,0:T(8,128)(2,1)S(1)}, bf16[16,2048]{1,0:T(8,128)(2,1)S(1)}, u32[]{:S(2)}, u32[]{:S(2)}) collective-permute-start(bf16[16,2048]{1,0:T(8,128)(2,1)S(1)} %get-tuple-element.58), channel_id=1, source_target_pairs={{0,2},{2,0},{1,3},{3,1},{4,6},{6,4},{5,7},{7,5},{8,10},{10,8},{9,1... | collective-permute-start | bytes 196616 | tf_op jit(solution)/shard_map/ppermute | solution.py:33
  63.5 5.0 %collective-permute-start.21 = (bf16[16,2048]{1,0:T(8,128)(2,1)S(1)}, bf16[16,2048]{1,0:T(8,128)(2,1)S(1)}, u32[]{:S(2)}, u32[]{:S(2)}) collective-permute-start(bf16[16,2048]{1,0:T(8,128)(2,1)S(1)} %sum_x1.1), channel_id=1, source_target_pairs={{0,4},{4,0},{8,12},{12,8},{1,5},{5,1},{9,13},{13,9},{2,6},{6,2},{1... | collective-permute-start | bytes 196616 | tf_op jit(solution)/shard_map/ppermute | solution.py:33
  64.9 6.5 %collective-permute-start.23 = (bf16[16,2048]{1,0:T(8,128)(2,1)S(1)}, bf16[16,2048]{1,0:T(8,128)(2,1)S(1)}, u32[]{:S(2)}, u32[]{:S(2)}) collective-permute-start(bf16[16,2048]{1,0:T(8,128)(2,1)S(1)} %sum_x2.1), channel_id=1, source_target_pairs={{0,8},{4,12},{8,0},{12,4},{1,9},{5,13},{9,1},{13,5},{2,10},{6,14},... | collective-permute-start | bytes 196616 | tf_op jit(solution)/shard_map/ppermute | solution.py:33
  66.2 6.2 %collective-permute-start.25 = (bf16[16,2048]{1,0:T(8,128)(2,1)S(1)}, bf16[16,2048]{1,0:T(8,128)(2,1)S(1)}, u32[]{:S(2)}, u32[]{:S(2)}) collective-permute-start(bf16[16,2048]{1,0:T(8,128)(2,1)S(1)} %sum_x3.1), channel_id=1, source_target_pairs={{0,12},{4,8},{8,4},{12,0},{1,13},{5,9},{9,5},{13,1},{2,14},{6,10},... | collective-permute-start | bytes 196616 | tf_op jit(solution)/shard_map/ppermute | solution.py:33

commit v7 on v5

--- a/solution.py
+++ b/solution.py
@@ -222,14 +222,14 @@
     normed_ref[:, width:] = info_ref[...]
 
 
-def experts_kernel(experts, capacity, tile, halves, n_rows, n_gate, n_up, *refs):
+def experts_kernel(experts, tile, halves, n_rows, n_gate, n_up, *refs):
     rows_in = refs[:n_rows]
     gate_refs = list(refs[n_rows : n_rows + n_gate])
     up_refs = list(refs[n_rows + n_gate : n_rows + n_gate + n_up])
     refs = refs[n_rows + n_gate + n_up :]
-    up_hbm, down_hbm, keep_ref, send_ref, rows_ref, pick_ref, packed_ref, hidden_ref = refs[:8]
-    up_late = list(refs[8 : 8 + experts - n_up])
-    down_ref, up_sem, down_sem = refs[8 + experts - n_up :]
+    up_hbm, down_hbm, keep_ref, send_ref, rows_ref, sum_ref, hidden_ref = refs[:7]
+    up_late = list(refs[7 : 7 + experts - n_up])
+    down_ref, up_sem, down_sem = refs[7 + experts - n_up :]
     per_expert, width = down_hbm.shape[0] // experts, down_hbm.shape[1]
     up_copies = [
         pltpu.make_async_copy(a, b, up_sem.at[i])
@@ -248,63 +248,36 @@
     for r in rows_in:
         rows_ref[count : count + r.shape[0], :] = r[...]
         count += r.shape[0]
-    at0 = lax.broadcasted_iota(jnp.int32, (count, count), 0)
-    at1 = lax.broadcasted_iota(jnp.int32, (count, count), 1)
-    eye = jnp.where(at0 == at1, 1.0, 0.0).astype(jnp.bfloat16)
-    before = jnp.where(at0 < at1, 1.0, 0.0).astype(jnp.bfloat16)
-    info = lax.dot_general(
-        rows_ref[:, width:], eye, (((0,), (0,)), ((), ())), preferred_element_type=jnp.float32
-    )
-    id0, id1, code0, code1 = (info[i : i + 1, :] for i in range(4))
-    slot_of = lax.broadcasted_iota(jnp.int32, (capacity, count), 0).astype(jnp.float32)
+    info = rows_ref[:, width:].astype(jnp.float32)
+    id0, id1, code0, code1 = (info[:, i : i + 1] for i in range(4))
     first = lax.axis_index("sec") * experts if halves == 1 else lax.axis_index("sec") // halves
-    picks, shares = [], []
+    kept = keep_ref.shape[0]
+    column = min(512, width)
     for x in range(experts):
         e = (first + x).astype(jnp.float32)
-        hit0 = jnp.where(id0 == e, 1.0, 0.0)
-        hit1 = jnp.where(id1 == e, 1.0, 0.0)
-        member = hit0 + hit1
-        share = (hit0 * code0 + hit1 * code1) / (code0 + code1)
-        slot = dot(jnp.broadcast_to(member, (8, count)).astype(jnp.bfloat16), before)[:1]
-        slot = jnp.where(member > 0.5, slot, -1.0)
-        pick = slot == slot_of
-        shares.append(jnp.sum(jnp.where(pick, share, 0.0), axis=1, keepdims=True))
-        picks.append(jnp.where(pick, 1.0, 0.0).astype(jnp.bfloat16))
-    pick_ref[...] = jnp.concatenate(picks, axis=0)
-    column = min(512, width)
-
-    for c in range(0, width, column):
-        packed_ref[:, c : c + column] = dot(pick_ref[...], rows_ref[:, c : c + column]).astype(
-            jnp.bfloat16
-        )
-    for x in range(experts):
-        mine = slice(x * capacity, (x + 1) * capacity)
+        named = jnp.where(id0 == e, code0, 0.0) + jnp.where(id1 == e, code1, 0.0)
+        share = 0.5 * named / (code0 + code1)
         if x >= n_up:
             up_copies[x - n_up].wait()
         gate_ref, up_ref = gate_refs[x], up_refs[x]
-
         for s in range(0, per_expert, tile):
             cut = slice(s, s + tile)
-            gate = dot(packed_ref[mine, :], gate_ref[:, cut])
-            up = dot(packed_ref[mine, :], up_ref[:, cut])
-            half = 0.5 * gate
-            hidden_ref[mine, cut] = ((half + half * jnp.tanh(half)) * up).astype(jnp.bfloat16)
+            gate = dot(rows_ref[:, :width], gate_ref[:, cut])
+            up = dot(rows_ref[:, :width], up_ref[:, cut]) * share
+            hidden_ref[:, cut] = ((gate + gate * jnp.tanh(0.5 * gate)) * up).astype(jnp.bfloat16)
         down_copies[x].wait()
-
         for c in range(0, width, column):
-            out = dot(hidden_ref[mine, :], down_ref[:, c : c + column])
-            packed_ref[mine, c : c + column] = (out * shares[x]).astype(jnp.bfloat16)
+            cut = slice(c, c + column)
+            out = dot(hidden_ref[...], down_ref[:, cut])
+            if x:
+                out = out + sum_ref[:, cut]
+            if x + 1 < experts:
+                sum_ref[:, cut] = out
+            else:
+                keep_ref[:, cut] = out[:kept]
+                send_ref[:, cut] = out[kept:].astype(jnp.bfloat16)
         if x + 1 < experts:
             down_copies[x + 1].start()
-    kept = keep_ref.shape[0]
-
-    for c in range(0, width, column):
-        out = lax.dot_general(
-            pick_ref[...], packed_ref[:, c : c + column], (((0,), (0,)), ((), ())),
-            preferred_element_type=jnp.float32,
-        )
-        keep_ref[:, c : c + column] = out[:kept]
-        send_ref[:, c : c + column] = out[kept:].astype(jnp.bfloat16)
 
 
 def per_device(
@@ -412,19 +385,17 @@
 
     halves = max(1, sec_count // E)
     count = sec_count * block
-    capacity = sec_count * MOSTB
     down = w_down[0]
     tile = min(512, down.shape[0] // experts)
     kept = count // pp_count
     keep, send = call(
-        functools.partial(experts_kernel, experts, capacity, tile, halves, len(rows), experts, 1),
+        functools.partial(experts_kernel, experts, tile, halves, len(rows), experts, 1),
         [sds((kept, width), f32), sds((count - kept, width), bf16)],
         [(VMEM, a) for a in (*rows, *gate_v, *up_v)] + [(HBM, w_up[0]), (HBM, down)],
         scratch=[
             pltpu.VMEM((count, width + LANES), bf16),
-            pltpu.VMEM((experts * capacity, count), bf16),
-            pltpu.VMEM((experts * capacity, width), bf16),
-            pltpu.VMEM((experts * capacity, down.shape[0] // experts), bf16),
+            pltpu.VMEM((count, width), f32),
+            pltpu.VMEM((count, per_expert), bf16),
             *[pltpu.VMEM((width, per_expert), bf16)] * (experts - 1),
             pltpu.VMEM((per_expert, width), bf16),
             pltpu.SemaphoreType.DMA((experts,)),

time: 72 us -> 78.5 us (1.090)
  Pallas kernels: 25.7 us -> 32.2 us
    pallas_call x11, Pallas kernels: 25.7 us -> 32.2 us  [call(): pl.pallas_call(kernel, out_shape=out_shape, in_specs=[s for s, _ in args]...]
  transfers between devices with their start and end apart: 27 -> 27, of which waited for: 14 -> 14; matrix products, arithmetic and copies ran while one was open for 0% -> 0% of each run, Pallas kernels for 15% -> 14%
where the time goes in v7:
time: 78.5 us; the launch traced here: 78.3 us
  Pallas kernels  32.2 us (41%)
  starting transfers between devices  26.3 us (34%)
  waiting for transfers between devices  18.7 us (24%)
    pallas_call x11, Pallas kernels, call(): pl.pallas_call(kernel, out_shape=out_shape, in_specs=[s for s, _ in args]...  32.2 us
    ppermute x25, waiting for transfers between devices, xor_swap(): return lax.ppermute(x, axis, [(i, i ^ k) for i in range(n)])  18.7 us
    ppermute x25, starting transfers between devices, xor_swap(): return lax.ppermute(x, axis, [(i, i ^ k) for i in range(n)])  16.9 us
    ppermute x2, starting transfers between devices, per_device(): lax.ppermute(kv, 'sec', [(i, i + k) for i in range(sec_count - k)])  9.43 us
  transfers between devices with their start and end apart: 27, of which 14 were waited for; matrix products, arithmetic and copies ran while one was open for 0% of the time, Pallas kernels for 14%

profile of v7, /device:TPU:0, one launch (start us, length us, event | category | flops | bytes accessed | tf_op | source)
XLA Modules:
  0.0 78.3 jit_solution(2060897018449476094)
XLA Ops:
  0.0 0.8 constant_dynamic-slice_fusion
  0.8 4.9 %collective-permute-start.1 = (bf16[64,512]{1,0:T(8,128)(2,1)S(1)}, bf16[64,512]{1,0:T(8,128)(2,1)S(1)}, u32[]{:S(2)}, u32[]{:S(2)}) collective-permute-start(bf16[64,512]{1,0:T(8,128)(2,1)S(1)} %pad_maximum_fusion.refs_2_), channel_id=1, source_target_pairs={{0,4},{4,8},{8,12},{1,5},{5,9},{9,13},{2,6},{6,10},{10,14},{3,7},{... | collective-permute-start | bytes 196616 | tf_op jit(solution)/shard_map/ppermute | solution.py:313
  5.7 4.5 %collective-permute-start = (bf16[64,512]{1,0:T(8,128)(2,1)S(1)}, bf16[64,512]{1,0:T(8,128)(2,1)S(1)}, u32[]{:S(2)}, u32[]{:S(2)}) collective-permute-start(bf16[64,512]{1,0:T(8,128)(2,1)S(1)} %pad_maximum_fusion.refs_2_), channel_id=1, source_target_pairs={{0,8},{4,12},{1,9},{5,13},{2,10},{6,14},{3,11},{7,15},{16,24},{20,... | collective-permute-start | bytes 196616 | tf_op jit(solution)/shard_map/ppermute | solution.py:313
  10.2 7.3 %prepare.1 = (bf16[64,1024]{1,0:T(8,128)(2,1)S(1)}, bf16[1024,2048]{1,0:T(8,128)(2,1)S(1)}, f32[1,2048]{1,0:T(1,128)S(1)}, f32[64,192]{1,0:T(8,128)S(1)}, bf16[6...) custom-call(s32[8]{0:T(128)} %lengths_hbm.1, ...), custom_call_target="tpu_custom_call" | custom-call | bytes 20400000 | tf_op jit(solution)/shard_map/prepare/pallas_call | solution.py:41
  17.6 1.4 %attention.1 = (f32[32,2048]{1,0:T(8,128)S(1)}, bf16[32,2048]{1,0:T(8,128)(2,1)S(1)}) custom-call(bf16[64,1024]{1,0:T(8,128)(2,1)S(1)} %get-tuple-element.35.q_ref, f32[64,192]{1,0:T(8,128)S(1)} %get-tuple-element.36.mask_ref, bf16[64,64]{1,0:T(8,128)(2,1)S(1)} %get-tuple-element.37.order_ref, bf16[64,512]{1,0:T(8,128)(2,1)S(1)} %collective-permute-done.refs_0_, ...), custom_call_target="tpu_custom_call" | custom-call | bytes 8160000 | tf_op jit(solution)/shard_map/attention/pallas_call | solution.py:41
  19.1 1.3 %collective-permute-done.2.refs_1_ = bf16[32,2048]{1,0:T(8,128)(2,1)S(1)} collective-permute-done((bf16[32,2048]{1,0:T(8,128)(2,1)S(1)}, bf16[32,2048]{1,0:T(8,128)(2,1)S(1)}, u32[]{:S(2)}, u32[]{:S(2)}) %collective-permute-start.2) | collective-permute-done | bytes 131104 | tf_op jit(solution)/shard_map/ppermute | solution.py:33
  20.5 1.6 %collective-permute-start.3 = (bf16[16,2048]{1,0:T(8,128)(2,1)S(1)}, bf16[16,2048]{1,0:T(8,128)(2,1)S(1)}, u32[]{:S(2)}, u32[]{:S(2)}) collective-permute-start(bf16[16,2048]{1,0:T(8,128)(2,1)S(1)} %get-tuple-element.42), channel_id=1, source_target_pairs={{0,2},{2,0},{1,3},{3,1},{4,6},{6,4},{5,7},{7,5},{8,10},{10,8},{9,1... | collective-permute-start | bytes 196616 | tf_op jit(solution)/shard_map/ppermute | solution.py:33
  22.0 3.4 %load_up.1 = (bf16[2048,2048]{1,0:T(8,128)(2,1)S(1)}, f32[8,128]{1,0:T(8,128)S(1)}) custom-call(bf16[2048,4096]{1,0:T(8,128)(2,1)} %bitcast.6, f32[16,2048]{1,0:T(8,128)S(1)} %get-tuple-element.41.refs_0_), custom_call_target="tpu_custom_call" | custom-call | bytes 8388607 | tf_op jit(solution)/shard_map/load_up/pallas_call | solution.py:41
  25.6 0.9 %collective-permute-start.7 = (bf16[16,2176]{1,0:T(8,128)(2,1)S(1)}, bf16[16,2176]{1,0:T(8,128)(2,1)S(1)}, u32[]{:S(2)}, u32[]{:S(2)}) collective-permute-start(bf16[16,2176]{1,0:T(8,128)(2,1)S(1)} %get-tuple-element.45.refs_0_), channel_id=1, source_target_pairs={{0,2},{2,0},{1,3},{3,1},{4,6},{6,4},{5,7},{7,5},{8,10},{10,8},{9,1... | collective-permute-start | bytes 208904 | tf_op jit(solution)/shard_map/ppermute | solution.py:33
  26.5 0.8 %collective-permute-start.5 = (bf16[16,2176]{1,0:T(8,128)(2,1)S(1)}, bf16[16,2176]{1,0:T(8,128)(2,1)S(1)}, u32[]{:S(2)}, u32[]{:S(2)}) collective-permute-start(bf16[16,2176]{1,0:T(8,128)(2,1)S(1)} %get-tuple-element.45.refs_0_), channel_id=1, source_target_pairs={{0,8},{4,12},{8,0},{12,4},{1,9},{5,13},{9,1},{13,5},{2,10},{6,14},... | collective-permute-start | bytes 208904 | tf_op jit(solution)/shard_map/ppermute | solution.py:33
  27.4 3.5 %collective-permute-start.4 = (bf16[16,2176]{1,0:T(8,128)(2,1)S(1)}, bf16[16,2176]{1,0:T(8,128)(2,1)S(1)}, u32[]{:S(2)}, u32[]{:S(2)}) collective-permute-start(bf16[16,2176]{1,0:T(8,128)(2,1)S(1)} %get-tuple-element.45.refs_0_), channel_id=1, source_target_pairs={{0,4},{4,0},{8,12},{12,8},{1,5},{5,1},{9,13},{13,9},{2,6},{6,2},{1... | collective-permute-start | bytes 208904 | tf_op jit(solution)/shard_map/ppermute | solution.py:33
  30.9 2.6 %collective-permute-done.6.refs_3_ = bf16[16,2176]{1,0:T(8,128)(2,1)S(1)} collective-permute-done((bf16[16,2176]{1,0:T(8,128)(2,1)S(1)}, bf16[16,2176]{1,0:T(8,128)(2,1)S(1)}, u32[]{:S(2)}, u32[]{:S(2)}) %collective-permute-start.6) | collective-permute-done | bytes 69664 | tf_op jit(solution)/shard_map/ppermute | solution.py:33
  33.5 1.1 %collective-permute-start.10 = (bf16[16,2176]{1,0:T(8,128)(2,1)S(1)}, bf16[16,2176]{1,0:T(8,128)(2,1)S(1)}, u32[]{:S(2)}, u32[]{:S(2)}) collective-permute-start(bf16[16,2176]{1,0:T(8,128)(2,1)S(1)} %collective-permute-done.6.refs_3_), channel_id=1, source_target_pairs={{0,2},{2,0},{1,3},{3,1},{4,6},{6,4},{5,7},{7,5},{8,10},{10,8},{9,1... | collective-permute-start | bytes 208904 | tf_op jit(solution)/shard_map/ppermute | solution.py:33
  34.6 1.5 %collective-permute-start.9 = (bf16[16,2176]{1,0:T(8,128)(2,1)S(1)}, bf16[16,2176]{1,0:T(8,128)(2,1)S(1)}, u32[]{:S(2)}, u32[]{:S(2)}) collective-permute-start(bf16[16,2176]{1,0:T(8,128)(2,1)S(1)} %collective-permute-done.5.refs_2_), channel_id=1, source_target_pairs={{0,2},{2,0},{1,3},{3,1},{4,6},{6,4},{5,7},{7,5},{8,10},{10,8},{9,1... | collective-permute-start | bytes 208904 | tf_op jit(solution)/shard_map/ppermute | solution.py:33
  36.2 0.5 collective-permute-start.8
  37.2 1.3 %collective-permute-done.10.refs_7_ = bf16[16,2176]{1,0:T(8,128)(2,1)S(1)} collective-permute-done((bf16[16,2176]{1,0:T(8,128)(2,1)S(1)}, bf16[16,2176]{1,0:T(8,128)(2,1)S(1)}, u32[]{:S(2)}, u32[]{:S(2)}) %collective-permute-start.10) | collective-permute-done | bytes 69664 | tf_op jit(solution)/shard_map/ppermute | solution.py:33
  38.5 1.5 %collective-permute-done.9.refs_6_ = bf16[16,2176]{1,0:T(8,128)(2,1)S(1)} collective-permute-done((bf16[16,2176]{1,0:T(8,128)(2,1)S(1)}, bf16[16,2176]{1,0:T(8,128)(2,1)S(1)}, u32[]{:S(2)}, u32[]{:S(2)}) %collective-permute-start.9) | collective-permute-done | bytes 69664 | tf_op jit(solution)/shard_map/ppermute | solution.py:33
  40.0 1.1 %collective-permute-done.8.refs_5_ = bf16[16,2176]{1,0:T(8,128)(2,1)S(1)} collective-permute-done((bf16[16,2176]{1,0:T(8,128)(2,1)S(1)}, bf16[16,2176]{1,0:T(8,128)(2,1)S(1)}, u32[]{:S(2)}, u32[]{:S(2)}) %collective-permute-start.8) | collective-permute-done | bytes 69664 | tf_op jit(solution)/shard_map/ppermute | solution.py:33
  41.2 1.1 %collective-permute-done.16.refs_13_ = bf16[16,2176]{1,0:T(8,128)(2,1)S(1)} collective-permute-done((bf16[16,2176]{1,0:T(8,128)(2,1)S(1)}, bf16[16,2176]{1,0:T(8,128)(2,1)S(1)}, u32[]{:S(2)}, u32[]{:S(2)}) %collective-permute-start.16) | collective-permute-done | bytes 69664 | tf_op jit(solution)/shard_map/ppermute | solution.py:33
  42.3 19.1 %experts.1 = (f32[128,2048]{1,0:T(8,128)S(1)}, bf16[128,2048]{1,0:T(8,128)(2,1)S(1)}) custom-call(bf16[16,2176]{1,0:T(8,128)(2,1)S(1)} %get-tuple-element.45.refs_0_, bf16[16,2176]{1,0:T(8,128)(2,1)S(1)} %collective-permute-done.4.refs_1_, bf16[16,2176]{1,0:T(8,128)(2,1)S(1)} %collective-permute-done.5.refs_2_, ...), custom_call_target="tpu_custom_call" | custom-call | bytes 40800000 | tf_op jit(solution)/shard_map/experts/pallas_call | solution.py:41
  61.7 1.8 %collective-permute-done.19.refs_1_ = bf16[128,2048]{1,0:T(8,128)(2,1)S(1)} collective-permute-done((bf16[128,2048]{1,0:T(8,128)(2,1)S(1)}, bf16[128,2048]{1,0:T(8,128)(2,1)S(1)}, u32[]{:S(2)}, u32[]{:S(2)}) %collective-permute-start.19) | collective-permute-done | bytes 524320 | tf_op jit(solution)/shard_map/ppermute | solution.py:33
  63.5 1.2 %collective-permute-start.20 = (bf16[16,2048]{1,0:T(8,128)(2,1)S(1)}, bf16[16,2048]{1,0:T(8,128)(2,1)S(1)}, u32[]{:S(2)}, u32[]{:S(2)}) collective-permute-start(bf16[16,2048]{1,0:T(8,128)(2,1)S(1)} %get-tuple-element.52), channel_id=1, source_target_pairs={{0,2},{2,0},{1,3},{3,1},{4,6},{6,4},{5,7},{7,5},{8,10},{10,8},{9,1... | collective-permute-start | bytes 196616 | tf_op jit(solution)/shard_map/ppermute | solution.py:33
  64.7 0.9 %collective-permute-start.22 = (bf16[16,2048]{1,0:T(8,128)(2,1)S(1)}, bf16[16,2048]{1,0:T(8,128)(2,1)S(1)}, u32[]{:S(2)}, u32[]{:S(2)}) collective-permute-start(bf16[16,2048]{1,0:T(8,128)(2,1)S(1)} %get-tuple-element.54), channel_id=1, source_target_pairs={{0,2},{2,0},{1,3},{3,1},{4,6},{6,4},{5,7},{7,5},{8,10},{10,8},{9,1... | collective-permute-start | bytes 196616 | tf_op jit(solution)/shard_map/ppermute | solution.py:33
  65.6 1.1 %collective-permute-start.24 = (bf16[16,2048]{1,0:T(8,128)(2,1)S(1)}, bf16[16,2048]{1,0:T(8,128)(2,1)S(1)}, u32[]{:S(2)}, u32[]{:S(2)}) collective-permute-start(bf16[16,2048]{1,0:T(8,128)(2,1)S(1)} %get-tuple-element.56), channel_id=1, source_target_pairs={{0,2},{2,0},{1,3},{3,1},{4,6},{6,4},{5,7},{7,5},{8,10},{10,8},{9,1... | collective-permute-start | bytes 196616 | tf_op jit(solution)/shard_map/ppermute | solution.py:33
  66.8 0.9 %collective-permute-start.26 = (bf16[16,2048]{1,0:T(8,128)(2,1)S(1)}, bf16[16,2048]{1,0:T(8,128)(2,1)S(1)}, u32[]{:S(2)}, u32[]{:S(2)}) collective-permute-start(bf16[16,2048]{1,0:T(8,128)(2,1)S(1)} %get-tuple-element.58), channel_id=1, source_target_pairs={{0,2},{2,0},{1,3},{3,1},{4,6},{6,4},{5,7},{7,5},{8,10},{10,8},{9,1... | collective-permute-start | bytes 196616 | tf_op jit(solution)/shard_map/ppermute | solution.py:33
  67.7 0.9 %collective-permute-done.20.refs_1_ = bf16[16,2048]{1,0:T(8,128)(2,1)S(1)} collective-permute-done((bf16[16,2048]{1,0:T(8,128)(2,1)S(1)}, bf16[16,2048]{1,0:T(8,128)(2,1)S(1)}, u32[]{:S(2)}, u32[]{:S(2)}) %collective-permute-start.20) | collective-permute-done | bytes 65568 | tf_op jit(solution)/shard_map/ppermute | solution.py:33
  68.6 1.3 %collective-permute-done.22.refs_1_ = bf16[16,2048]{1,0:T(8,128)(2,1)S(1)} collective-permute-done((bf16[16,2048]{1,0:T(8,128)(2,1)S(1)}, bf16[16,2048]{1,0:T(8,128)(2,1)S(1)}, u32[]{:S(2)}, u32[]{:S(2)}) %collective-permute-start.22) | collective-permute-done | bytes 65568 | tf_op jit(solution)/shard_map/ppermute | solution.py:33
  70.0 1.3 %collective-permute-done.24.refs_1_ = bf16[16,2048]{1,0:T(8,128)(2,1)S(1)} collective-permute-done((bf16[16,2048]{1,0:T(8,128)(2,1)S(1)}, bf16[16,2048]{1,0:T(8,128)(2,1)S(1)}, u32[]{:S(2)}, u32[]{:S(2)}) %collective-permute-start.24) | collective-permute-done | bytes 65568 | tf_op jit(solution)/shard_map/ppermute | solution.py:33
  71.4 1.8 %collective-permute-start.25 = (bf16[16,2048]{1,0:T(8,128)(2,1)S(1)}, bf16[16,2048]{1,0:T(8,128)(2,1)S(1)}, u32[]{:S(2)}, u32[]{:S(2)}) collective-permute-start(bf16[16,2048]{1,0:T(8,128)(2,1)S(1)} %sum_x3.1), channel_id=1, source_target_pairs={{0,12},{4,8},{8,4},{12,0},{1,13},{5,9},{9,5},{13,1},{2,14},{6,10},... | collective-permute-start | bytes 196616 | tf_op jit(solution)/shard_map/ppermute | solution.py:33
  73.6 3.0 %collective-permute-done.23.refs_2_ = bf16[16,2048]{1,0:T(8,128)(2,1)S(1)} collective-permute-done((bf16[16,2048]{1,0:T(8,128)(2,1)S(1)}, bf16[16,2048]{1,0:T(8,128)(2,1)S(1)}, u32[]{:S(2)}, u32[]{:S(2)}) %collective-permute-start.23) | collective-permute-done | bytes 65568 | tf_op jit(solution)/shard_map/ppermute | solution.py:33
  76.6 1.0 %collective-permute-done.25.refs_3_ = bf16[16,2048]{1,0:T(8,128)(2,1)S(1)} collective-permute-done((bf16[16,2048]{1,0:T(8,128)(2,1)S(1)}, bf16[16,2048]{1,0:T(8,128)(2,1)S(1)}, u32[]{:S(2)}, u32[]{:S(2)}) %collective-permute-start.25) | collective-permute-done | bytes 65568 | tf_op jit(solution)/shard_map/ppermute | solution.py:33
  77.6 0.7 total.1
  (35 shorter events, 1.8 us)
Async XLA Ops:
  0.8 16.8 %collective-permute-start.1 = (bf16[64,512]{1,0:T(8,128)(2,1)S(1)}, bf16[64,512]{1,0:T(8,128)(2,1)S(1)}, u32[]{:S(2)}, u32[]{:S(2)}) collective-permute-start(bf16[64,512]{1,0:T(8,128)(2,1)S(1)} %pad_maximum_fusion.refs_2_), channel_id=1, source_target_pairs={{0,4},{4,8},{8,12},{1,5},{5,9},{9,13},{2,6},{6,10},{10,14},{3,7},{... | collective-permute-start | bytes 196616 | tf_op jit(solution)/shard_map/ppermute | solution.py:313
  5.7 11.9 %collective-permute-start = (bf16[64,512]{1,0:T(8,128)(2,1)S(1)}, bf16[64,512]{1,0:T(8,128)(2,1)S(1)}, u32[]{:S(2)}, u32[]{:S(2)}) collective-permute-start(bf16[64,512]{1,0:T(8,128)(2,1)S(1)} %pad_maximum_fusion.refs_2_), channel_id=1, source_target_pairs={{0,8},{4,12},{1,9},{5,13},{2,10},{6,14},{3,11},{7,15},{16,24},{20,... | collective-permute-start | bytes 196616 | tf_op jit(solution)/shard_map/ppermute | solution.py:313
  19.0 1.4 %collective-permute-start.2 = (bf16[32,2048]{1,0:T(8,128)(2,1)S(1)}, bf16[32,2048]{1,0:T(8,128)(2,1)S(1)}, u32[]{:S(2)}, u32[]{:S(2)}) collective-permute-start(bf16[32,2048]{1,0:T(8,128)(2,1)S(1)} %get-tuple-element.40), channel_id=1, source_target_pairs={{0,1},{1,0},{2,3},{3,2},{4,5},{5,4},{6,7},{7,6},{8,9},{9,8},{10,11... | collective-permute-start | bytes 393224 | tf_op jit(solution)/shard_map/ppermute | solution.py:33
  20.5 5.0 %collective-permute-start.3 = (bf16[16,2048]{1,0:T(8,128)(2,1)S(1)}, bf16[16,2048]{1,0:T(8,128)(2,1)S(1)}, u32[]{:S(2)}, u32[]{:S(2)}) collective-permute-start(bf16[16,2048]{1,0:T(8,128)(2,1)S(1)} %get-tuple-element.42), channel_id=1, source_target_pairs={{0,2},{2,0},{1,3},{3,1},{4,6},{6,4},{5,7},{7,5},{8,10},{10,8},{9,1... | collective-permute-start | bytes 196616 | tf_op jit(solution)/shard_map/ppermute | solution.py:33
  25.6 5.3 %collective-permute-start.7 = (bf16[16,2176]{1,0:T(8,128)(2,1)S(1)}, bf16[16,2176]{1,0:T(8,128)(2,1)S(1)}, u32[]{:S(2)}, u32[]{:S(2)}) collective-permute-start(bf16[16,2176]{1,0:T(8,128)(2,1)S(1)} %get-tuple-element.45.refs_0_), channel_id=1, source_target_pairs={{0,2},{2,0},{1,3},{3,1},{4,6},{6,4},{5,7},{7,5},{8,10},{10,8},{9,1... | collective-permute-start | bytes 208904 | tf_op jit(solution)/shard_map/ppermute | solution.py:33
  26.5 7.0 %collective-permute-start.6 = (bf16[16,2176]{1,0:T(8,128)(2,1)S(1)}, bf16[16,2176]{1,0:T(8,128)(2,1)S(1)}, u32[]{:S(2)}, u32[]{:S(2)}) collective-permute-start(bf16[16,2176]{1,0:T(8,128)(2,1)S(1)} %get-tuple-element.45.refs_0_), channel_id=1, source_target_pairs={{0,12},{4,8},{8,4},{12,0},{1,13},{5,9},{9,5},{13,1},{2,14},{6,10},... | collective-permute-start | bytes 208904 | tf_op jit(solution)/shard_map/ppermute | solution.py:33
  26.5 7.0 %collective-permute-start.11 = (bf16[16,2176]{1,0:T(8,128)(2,1)S(1)}, bf16[16,2176]{1,0:T(8,128)(2,1)S(1)}, u32[]{:S(2)}, u32[]{:S(2)}) collective-permute-start(bf16[16,2176]{1,0:T(8,128)(2,1)S(1)} %get-tuple-element.45.refs_0_), channel_id=1, source_target_pairs={{0,1},{1,0},{2,3},{3,2},{4,5},{5,4},{6,7},{7,6},{8,9},{9,8},{10,11... | collective-permute-start | bytes 208904 | tf_op jit(solution)/shard_map/ppermute | solution.py:33
  26.5 8.1 %collective-permute-start.5 = (bf16[16,2176]{1,0:T(8,128)(2,1)S(1)}, bf16[16,2176]{1,0:T(8,128)(2,1)S(1)}, u32[]{:S(2)}, u32[]{:S(2)}) collective-permute-start(bf16[16,2176]{1,0:T(8,128)(2,1)S(1)} %get-tuple-element.45.refs_0_), channel_id=1, source_target_pairs={{0,8},{4,12},{8,0},{12,4},{1,9},{5,13},{9,1},{13,5},{2,10},{6,14},... | collective-permute-start | bytes 208904 | tf_op jit(solution)/shard_map/ppermute | solution.py:33
  27.4 8.8 %collective-permute-start.4 = (bf16[16,2176]{1,0:T(8,128)(2,1)S(1)}, bf16[16,2176]{1,0:T(8,128)(2,1)S(1)}, u32[]{:S(2)}, u32[]{:S(2)}) collective-permute-start(bf16[16,2176]{1,0:T(8,128)(2,1)S(1)} %get-tuple-element.45.refs_0_), channel_id=1, source_target_pairs={{0,4},{4,0},{8,12},{12,8},{1,5},{5,1},{9,13},{13,9},{2,6},{6,2},{1... | collective-permute-start | bytes 208904 | tf_op jit(solution)/shard_map/ppermute | solution.py:33
  30.9 5.8 %collective-permute-start.15 = (bf16[16,2176]{1,0:T(8,128)(2,1)S(1)}, bf16[16,2176]{1,0:T(8,128)(2,1)S(1)}, u32[]{:S(2)}, u32[]{:S(2)}) collective-permute-start(bf16[16,2176]{1,0:T(8,128)(2,1)S(1)} %collective-permute-done.7.refs_4_), channel_id=1, source_target_pairs={{0,1},{1,0},{2,3},{3,2},{4,5},{5,4},{6,7},{7,6},{8,9},{9,8},{10,11... | collective-permute-start | bytes 208904 | tf_op jit(solution)/shard_map/ppermute | solution.py:33
  33.5 3.2 %collective-permute-start.14 = (bf16[16,2176]{1,0:T(8,128)(2,1)S(1)}, bf16[16,2176]{1,0:T(8,128)(2,1)S(1)}, u32[]{:S(2)}, u32[]{:S(2)}) collective-permute-start(bf16[16,2176]{1,0:T(8,128)(2,1)S(1)} %collective-permute-done.6.refs_3_), channel_id=1, source_target_pairs={{0,1},{1,0},{2,3},{3,2},{4,5},{5,4},{6,7},{7,6},{8,9},{9,8},{10,11... | collective-permute-start | bytes 208904 | tf_op jit(solution)/shard_map/ppermute | solution.py:33
  33.5 5.0 %collective-permute-start.10 = (bf16[16,2176]{1,0:T(8,128)(2,1)S(1)}, bf16[16,2176]{1,0:T(8,128)(2,1)S(1)}, u32[]{:S(2)}, u32[]{:S(2)}) collective-permute-start(bf16[16,2176]{1,0:T(8,128)(2,1)S(1)} %collective-permute-done.6.refs_3_), channel_id=1, source_target_pairs={{0,2},{2,0},{1,3},{3,1},{4,6},{6,4},{5,7},{7,5},{8,10},{10,8},{9,1... | collective-permute-start | bytes 208904 | tf_op jit(solution)/shard_map/ppermute | solution.py:33
  34.6 5.3 %collective-permute-start.9 = (bf16[16,2176]{1,0:T(8,128)(2,1)S(1)}, bf16[16,2176]{1,0:T(8,128)(2,1)S(1)}, u32[]{:S(2)}, u32[]{:S(2)}) collective-permute-start(bf16[16,2176]{1,0:T(8,128)(2,1)S(1)} %collective-permute-done.5.refs_2_), channel_id=1, source_target_pairs={{0,2},{2,0},{1,3},{3,1},{4,6},{6,4},{5,7},{7,5},{8,10},{10,8},{9,1... | collective-permute-start | bytes 208904 | tf_op jit(solution)/shard_map/ppermute | solution.py:33
  36.2 4.9 %collective-permute-start.8 = (bf16[16,2176]{1,0:T(8,128)(2,1)S(1)}, bf16[16,2176]{1,0:T(8,128)(2,1)S(1)}, u32[]{:S(2)}, u32[]{:S(2)}) collective-permute-start(bf16[16,2176]{1,0:T(8,128)(2,1)S(1)} %collective-permute-done.4.refs_1_), channel_id=1, source_target_pairs={{0,2},{2,0},{1,3},{3,1},{4,6},{6,4},{5,7},{7,5},{8,10},{10,8},{9,1... | collective-permute-start | bytes 208904 | tf_op jit(solution)/shard_map/ppermute | solution.py:33
  36.7 4.4 %collective-permute-start.13 = (bf16[16,2176]{1,0:T(8,128)(2,1)S(1)}, bf16[16,2176]{1,0:T(8,128)(2,1)S(1)}, u32[]{:S(2)}, u32[]{:S(2)}) collective-permute-start(bf16[16,2176]{1,0:T(8,128)(2,1)S(1)} %collective-permute-done.5.refs_2_), channel_id=1, source_target_pairs={{0,1},{1,0},{2,3},{3,2},{4,5},{5,4},{6,7},{7,6},{8,9},{9,8},{10,11... | collective-permute-start | bytes 208904 | tf_op jit(solution)/shard_map/ppermute | solution.py:33
  36.7 4.4 %collective-permute-start.12 = (bf16[16,2176]{1,0:T(8,128)(2,1)S(1)}, bf16[16,2176]{1,0:T(8,128)(2,1)S(1)}, u32[]{:S(2)}, u32[]{:S(2)}) collective-permute-start(bf16[16,2176]{1,0:T(8,128)(2,1)S(1)} %collective-permute-done.4.refs_1_), channel_id=1, source_target_pairs={{0,1},{1,0},{2,3},{3,2},{4,5},{5,4},{6,7},{7,6},{8,9},{9,8},{10,11... | collective-permute-start | bytes 208904 | tf_op jit(solution)/shard_map/ppermute | solution.py:33
  38.5 2.6 %collective-permute-start.18 = (bf16[16,2176]{1,0:T(8,128)(2,1)S(1)}, bf16[16,2176]{1,0:T(8,128)(2,1)S(1)}, u32[]{:S(2)}, u32[]{:S(2)}) collective-permute-start(bf16[16,2176]{1,0:T(8,128)(2,1)S(1)} %collective-permute-done.10.refs_7_), channel_id=1, source_target_pairs={{0,1},{1,0},{2,3},{3,2},{4,5},{5,4},{6,7},{7,6},{8,9},{9,8},{10,11... | collective-permute-start | bytes 208904 | tf_op jit(solution)/shard_map/ppermute | solution.py:33
  40.0 1.3 %collective-permute-start.17 = (bf16[16,2176]{1,0:T(8,128)(2,1)S(1)}, bf16[16,2176]{1,0:T(8,128)(2,1)S(1)}, u32[]{:S(2)}, u32[]{:S(2)}) collective-permute-start(bf16[16,2176]{1,0:T(8,128)(2,1)S(1)} %collective-permute-done.9.refs_6_), channel_id=1, source_target_pairs={{0,1},{1,0},{2,3},{3,2},{4,5},{5,4},{6,7},{7,6},{8,9},{9,8},{10,11... | collective-permute-start | bytes 208904 | tf_op jit(solution)/shard_map/ppermute | solution.py:33
  41.1 1.3 %collective-permute-start.16 = (bf16[16,2176]{1,0:T(8,128)(2,1)S(1)}, bf16[16,2176]{1,0:T(8,128)(2,1)S(1)}, u32[]{:S(2)}, u32[]{:S(2)}) collective-permute-start(bf16[16,2176]{1,0:T(8,128)(2,1)S(1)} %collective-permute-done.8.refs_5_), channel_id=1, source_target_pairs={{0,1},{1,0},{2,3},{3,2},{4,5},{5,4},{6,7},{7,6},{8,9},{9,8},{10,11... | collective-permute-start | bytes 208904 | tf_op jit(solution)/shard_map/ppermute | solution.py:33
  61.5 2.0 %collective-permute-start.19 = (bf16[128,2048]{1,0:T(8,128)(2,1)S(1)}, bf16[128,2048]{1,0:T(8,128)(2,1)S(1)}, u32[]{:S(2)}, u32[]{:S(2)}) collective-permute-start(bf16[128,2048]{1,0:T(8,128)(2,1)S(1)} %get-tuple-element.50), channel_id=1, source_target_pairs={{0,1},{1,0},{2,3},{3,2},{4,5},{5,4},{6,7},{7,6},{8,9},{9,8},{10,11... | collective-permute-start | bytes 1572872 | tf_op jit(solution)/shard_map/ppermute | solution.py:33
  63.5 5.0 %collective-permute-start.20 = (bf16[16,2048]{1,0:T(8,128)(2,1)S(1)}, bf16[16,2048]{1,0:T(8,128)(2,1)S(1)}, u32[]{:S(2)}, u32[]{:S(2)}) collective-permute-start(bf16[16,2048]{1,0:T(8,128)(2,1)S(1)} %get-tuple-element.52), channel_id=1, source_target_pairs={{0,2},{2,0},{1,3},{3,1},{4,6},{6,4},{5,7},{7,5},{8,10},{10,8},{9,1... | collective-permute-start | bytes 196616 | tf_op jit(solution)/shard_map/ppermute | solution.py:33
  64.7 5.2 %collective-permute-start.22 = (bf16[16,2048]{1,0:T(8,128)(2,1)S(1)}, bf16[16,2048]{1,0:T(8,128)(2,1)S(1)}, u32[]{:S(2)}, u32[]{:S(2)}) collective-permute-start(bf16[16,2048]{1,0:T(8,128)(2,1)S(1)} %get-tuple-element.54), channel_id=1, source_target_pairs={{0,2},{2,0},{1,3},{3,1},{4,6},{6,4},{5,7},{7,5},{8,10},{10,8},{9,1... | collective-permute-start | bytes 196616 | tf_op jit(solution)/shard_map/ppermute | solution.py:33
  65.6 5.7 %collective-permute-start.24 = (bf16[16,2048]{1,0:T(8,128)(2,1)S(1)}, bf16[16,2048]{1,0:T(8,128)(2,1)S(1)}, u32[]{:S(2)}, u32[]{:S(2)}) collective-permute-start(bf16[16,2048]{1,0:T(8,128)(2,1)S(1)} %get-tuple-element.56), channel_id=1, source_target_pairs={{0,2},{2,0},{1,3},{3,1},{4,6},{6,4},{5,7},{7,5},{8,10},{10,8},{9,1... | collective-permute-start | bytes 196616 | tf_op jit(solution)/shard_map/ppermute | solution.py:33
  66.8 6.4 %collective-permute-start.26 = (bf16[16,2048]{1,0:T(8,128)(2,1)S(1)}, bf16[16,2048]{1,0:T(8,128)(2,1)S(1)}, u32[]{:S(2)}, u32[]{:S(2)}) collective-permute-start(bf16[16,2048]{1,0:T(8,128)(2,1)S(1)} %get-tuple-element.58), channel_id=1, source_target_pairs={{0,2},{2,0},{1,3},{3,1},{4,6},{6,4},{5,7},{7,5},{8,10},{10,8},{9,1... | collective-permute-start | bytes 196616 | tf_op jit(solution)/shard_map/ppermute | solution.py:33
  68.6 5.0 %collective-permute-start.21 = (bf16[16,2048]{1,0:T(8,128)(2,1)S(1)}, bf16[16,2048]{1,0:T(8,128)(2,1)S(1)}, u32[]{:S(2)}, u32[]{:S(2)}) collective-permute-start(bf16[16,2048]{1,0:T(8,128)(2,1)S(1)} %sum_x1.1), channel_id=1, source_target_pairs={{0,4},{4,0},{8,12},{12,8},{1,5},{5,1},{9,13},{13,9},{2,6},{6,2},{1... | collective-permute-start | bytes 196616 | tf_op jit(solution)/shard_map/ppermute | solution.py:33
  70.0 6.6 %collective-permute-start.23 = (bf16[16,2048]{1,0:T(8,128)(2,1)S(1)}, bf16[16,2048]{1,0:T(8,128)(2,1)S(1)}, u32[]{:S(2)}, u32[]{:S(2)}) collective-permute-start(bf16[16,2048]{1,0:T(8,128)(2,1)S(1)} %sum_x2.1), channel_id=1, source_target_pairs={{0,8},{4,12},{8,0},{12,4},{1,9},{5,13},{9,1},{13,5},{2,10},{6,14},... | collective-permute-start | bytes 196616 | tf_op jit(solution)/shard_map/ppermute | solution.py:33
  71.4 6.2 %collective-permute-start.25 = (bf16[16,2048]{1,0:T(8,128)(2,1)S(1)}, bf16[16,2048]{1,0:T(8,128)(2,1)S(1)}, u32[]{:S(2)}, u32[]{:S(2)}) collective-permute-start(bf16[16,2048]{1,0:T(8,128)(2,1)S(1)} %sum_x3.1), channel_id=1, source_target_pairs={{0,12},{4,8},{8,4},{12,0},{1,13},{5,9},{9,5},{13,1},{2,14},{6,10},... | collective-permute-start | bytes 196616 | tf_op jit(solution)/shard_map/ppermute | solution.py:33

commit v8 on v5

--- a/solution.py
+++ b/solution.py
@@ -271,7 +271,7 @@
         shares.append(jnp.sum(jnp.where(pick, share, 0.0), axis=1, keepdims=True))
         picks.append(jnp.where(pick, 1.0, 0.0).astype(jnp.bfloat16))
     pick_ref[...] = jnp.concatenate(picks, axis=0)
-    column = min(512, width)
+    column = min(256, width)
 
     for c in range(0, width, column):
         packed_ref[:, c : c + column] = dot(pick_ref[...], rows_ref[:, c : c + column]).astype(
@@ -414,7 +414,7 @@
     count = sec_count * block
     capacity = sec_count * MOSTB
     down = w_down[0]
-    tile = min(512, down.shape[0] // experts)
+    tile = min(256, down.shape[0] // experts)
     kept = count // pp_count
     keep, send = call(
         functools.partial(experts_kernel, experts, capacity, tile, halves, len(rows), experts, 1),

time: 72 us -> 72.1 us (level)
  no operation moved by 1% of the time
where the time goes in v8:
time: 72.1 us; the launch traced here: 71.8 us
  starting transfers between devices  26.3 us (36%)
  Pallas kernels  25.7 us (36%)
  waiting for transfers between devices  18.7 us (26%)
  local copies, waits for them, and re-layouts  0.78 us (1%)
    pallas_call x11, Pallas kernels, call(): pl.pallas_call(kernel, out_shape=out_shape, in_specs=[s for s, _ in args]...  25.7 us
    ppermute x25, waiting for transfers between devices, xor_swap(): return lax.ppermute(x, axis, [(i, i ^ k) for i in range(n)])  18.7 us
    ppermute x25, starting transfers between devices, xor_swap(): return lax.ppermute(x, axis, [(i, i ^ k) for i in range(n)])  16.9 us
    ppermute x2, starting transfers between devices, per_device(): lax.ppermute(kv, 'sec', [(i, i + k) for i in range(sec_count - k)])  9.43 us
  transfers between devices with their start and end apart: 27, of which 14 were waited for; matrix products, arithmetic and copies ran while one was open for 0% of the time, Pallas kernels for 15%

profile of v8, /device:TPU:0, one launch (start us, length us, event | category | flops | bytes accessed | tf_op | source)
XLA Modules:
  0.0 71.8 jit_solution(15864533814048726255)
XLA Ops:
  0.0 0.8 %constant_dynamic-slice_fusion = (bf16[64,256]{1,0:T(8,128)(2,1)S(1)}, bf16[64,256]{1,0:T(8,128)(2,1)S(1)}) fusion(bf16[64,512]{1,0:T(8,128)(2,1)} %param.14, s32[]{:T(128)S(6)} %select_n.10, bf16[64,512]{1,0:T(8,128)(2,1)} %param.13), kind=kLoop, calls=%fused_computation.1 | loop fusion | bytes 131076 | tf_op jit(solution)/shard_map/dynamic_slice | solution.py:336
  0.8 4.9 %collective-permute-start.1 = (bf16[64,512]{1,0:T(8,128)(2,1)S(1)}, bf16[64,512]{1,0:T(8,128)(2,1)S(1)}, u32[]{:S(2)}, u32[]{:S(2)}) collective-permute-start(bf16[64,512]{1,0:T(8,128)(2,1)S(1)} %pad_maximum_fusion.refs_2_), channel_id=1, source_target_pairs={{0,4},{4,8},{8,12},{1,5},{5,9},{9,13},{2,6},{6,10},{10,14},{3,7},{... | collective-permute-start | bytes 196616 | tf_op jit(solution)/shard_map/ppermute | solution.py:340
  5.7 4.5 %collective-permute-start = (bf16[64,512]{1,0:T(8,128)(2,1)S(1)}, bf16[64,512]{1,0:T(8,128)(2,1)S(1)}, u32[]{:S(2)}, u32[]{:S(2)}) collective-permute-start(bf16[64,512]{1,0:T(8,128)(2,1)S(1)} %pad_maximum_fusion.refs_2_), channel_id=1, source_target_pairs={{0,8},{4,12},{1,9},{5,13},{2,10},{6,14},{3,11},{7,15},{16,24},{20,... | collective-permute-start | bytes 196616 | tf_op jit(solution)/shard_map/ppermute | solution.py:340
  10.2 7.3 %prepare.1 = (bf16[64,1024]{1,0:T(8,128)(2,1)S(1)}, bf16[1024,2048]{1,0:T(8,128)(2,1)S(1)}, f32[1,2048]{1,0:T(1,128)S(1)}, f32[64,192]{1,0:T(8,128)S(1)}, bf16[6...) custom-call(s32[8]{0:T(128)} %lengths_hbm.1, ...), custom_call_target="tpu_custom_call" | custom-call | bytes 20400000 | tf_op jit(solution)/shard_map/prepare/pallas_call | solution.py:41
  17.6 1.4 %attention.1 = (f32[32,2048]{1,0:T(8,128)S(1)}, bf16[32,2048]{1,0:T(8,128)(2,1)S(1)}) custom-call(bf16[64,1024]{1,0:T(8,128)(2,1)S(1)} %get-tuple-element.35.q_ref, f32[64,192]{1,0:T(8,128)S(1)} %get-tuple-element.36.mask_ref, bf16[64,64]{1,0:T(8,128)(2,1)S(1)} %get-tuple-element.37.order_ref, bf16[64,512]{1,0:T(8,128)(2,1)S(1)} %collective-permute-done.refs_0_, ...), custom_call_target="tpu_custom_call" | custom-call | bytes 8160000 | tf_op jit(solution)/shard_map/attention/pallas_call | solution.py:41
  19.1 1.3 %collective-permute-done.2.refs_1_ = bf16[32,2048]{1,0:T(8,128)(2,1)S(1)} collective-permute-done((bf16[32,2048]{1,0:T(8,128)(2,1)S(1)}, bf16[32,2048]{1,0:T(8,128)(2,1)S(1)}, u32[]{:S(2)}, u32[]{:S(2)}) %collective-permute-start.2) | collective-permute-done | bytes 131104 | tf_op jit(solution)/shard_map/ppermute | solution.py:33
  20.5 1.6 %collective-permute-start.3 = (bf16[16,2048]{1,0:T(8,128)(2,1)S(1)}, bf16[16,2048]{1,0:T(8,128)(2,1)S(1)}, u32[]{:S(2)}, u32[]{:S(2)}) collective-permute-start(bf16[16,2048]{1,0:T(8,128)(2,1)S(1)} %get-tuple-element.42), channel_id=1, source_target_pairs={{0,2},{2,0},{1,3},{3,1},{4,6},{6,4},{5,7},{7,5},{8,10},{10,8},{9,1... | collective-permute-start | bytes 196616 | tf_op jit(solution)/shard_map/ppermute | solution.py:33
  22.0 3.4 %load_up.1 = (bf16[2048,2048]{1,0:T(8,128)(2,1)S(1)}, f32[8,128]{1,0:T(8,128)S(1)}) custom-call(bf16[2048,4096]{1,0:T(8,128)(2,1)} %bitcast.6, f32[16,2048]{1,0:T(8,128)S(1)} %get-tuple-element.41.refs_0_), custom_call_target="tpu_custom_call" | custom-call | bytes 8388607 | tf_op jit(solution)/shard_map/load_up/pallas_call | solution.py:41
  25.6 0.9 %collective-permute-start.7 = (bf16[16,2176]{1,0:T(8,128)(2,1)S(1)}, bf16[16,2176]{1,0:T(8,128)(2,1)S(1)}, u32[]{:S(2)}, u32[]{:S(2)}) collective-permute-start(bf16[16,2176]{1,0:T(8,128)(2,1)S(1)} %get-tuple-element.45.refs_0_), channel_id=1, source_target_pairs={{0,2},{2,0},{1,3},{3,1},{4,6},{6,4},{5,7},{7,5},{8,10},{10,8},{9,1... | collective-permute-start | bytes 208904 | tf_op jit(solution)/shard_map/ppermute | solution.py:33
  26.5 0.8 %collective-permute-start.5 = (bf16[16,2176]{1,0:T(8,128)(2,1)S(1)}, bf16[16,2176]{1,0:T(8,128)(2,1)S(1)}, u32[]{:S(2)}, u32[]{:S(2)}) collective-permute-start(bf16[16,2176]{1,0:T(8,128)(2,1)S(1)} %get-tuple-element.45.refs_0_), channel_id=1, source_target_pairs={{0,8},{4,12},{8,0},{12,4},{1,9},{5,13},{9,1},{13,5},{2,10},{6,14},... | collective-permute-start | bytes 208904 | tf_op jit(solution)/shard_map/ppermute | solution.py:33
  27.4 3.5 %collective-permute-start.4 = (bf16[16,2176]{1,0:T(8,128)(2,1)S(1)}, bf16[16,2176]{1,0:T(8,128)(2,1)S(1)}, u32[]{:S(2)}, u32[]{:S(2)}) collective-permute-start(bf16[16,2176]{1,0:T(8,128)(2,1)S(1)} %get-tuple-element.45.refs_0_), channel_id=1, source_target_pairs={{0,4},{4,0},{8,12},{12,8},{1,5},{5,1},{9,13},{13,9},{2,6},{6,2},{1... | collective-permute-start | bytes 208904 | tf_op jit(solution)/shard_map/ppermute | solution.py:33
  30.9 2.6 %collective-permute-done.6.refs_3_ = bf16[16,2176]{1,0:T(8,128)(2,1)S(1)} collective-permute-done((bf16[16,2176]{1,0:T(8,128)(2,1)S(1)}, bf16[16,2176]{1,0:T(8,128)(2,1)S(1)}, u32[]{:S(2)}, u32[]{:S(2)}) %collective-permute-start.6) | collective-permute-done | bytes 69664 | tf_op jit(solution)/shard_map/ppermute | solution.py:33
  33.5 1.1 %collective-permute-start.10 = (bf16[16,2176]{1,0:T(8,128)(2,1)S(1)}, bf16[16,2176]{1,0:T(8,128)(2,1)S(1)}, u32[]{:S(2)}, u32[]{:S(2)}) collective-permute-start(bf16[16,2176]{1,0:T(8,128)(2,1)S(1)} %collective-permute-done.6.refs_3_), channel_id=1, source_target_pairs={{0,2},{2,0},{1,3},{3,1},{4,6},{6,4},{5,7},{7,5},{8,10},{10,8},{9,1... | collective-permute-start | bytes 208904 | tf_op jit(solution)/shard_map/ppermute | solution.py:33
  34.6 1.5 %collective-permute-start.9 = (bf16[16,2176]{1,0:T(8,128)(2,1)S(1)}, bf16[16,2176]{1,0:T(8,128)(2,1)S(1)}, u32[]{:S(2)}, u32[]{:S(2)}) collective-permute-start(bf16[16,2176]{1,0:T(8,128)(2,1)S(1)} %collective-permute-done.5.refs_2_), channel_id=1, source_target_pairs={{0,2},{2,0},{1,3},{3,1},{4,6},{6,4},{5,7},{7,5},{8,10},{10,8},{9,1... | collective-permute-start | bytes 208904 | tf_op jit(solution)/shard_map/ppermute | solution.py:33
  36.2 0.5 collective-permute-start.8
  37.2 1.3 %collective-permute-done.10.refs_7_ = bf16[16,2176]{1,0:T(8,128)(2,1)S(1)} collective-permute-done((bf16[16,2176]{1,0:T(8,128)(2,1)S(1)}, bf16[16,2176]{1,0:T(8,128)(2,1)S(1)}, u32[]{:S(2)}, u32[]{:S(2)}) %collective-permute-start.10) | collective-permute-done | bytes 69664 | tf_op jit(solution)/shard_map/ppermute | solution.py:33
  38.5 1.5 %collective-permute-done.9.refs_6_ = bf16[16,2176]{1,0:T(8,128)(2,1)S(1)} collective-permute-done((bf16[16,2176]{1,0:T(8,128)(2,1)S(1)}, bf16[16,2176]{1,0:T(8,128)(2,1)S(1)}, u32[]{:S(2)}, u32[]{:S(2)}) %collective-permute-start.9) | collective-permute-done | bytes 69664 | tf_op jit(solution)/shard_map/ppermute | solution.py:33
  40.0 1.1 %collective-permute-done.8.refs_5_ = bf16[16,2176]{1,0:T(8,128)(2,1)S(1)} collective-permute-done((bf16[16,2176]{1,0:T(8,128)(2,1)S(1)}, bf16[16,2176]{1,0:T(8,128)(2,1)S(1)}, u32[]{:S(2)}, u32[]{:S(2)}) %collective-permute-start.8) | collective-permute-done | bytes 69664 | tf_op jit(solution)/shard_map/ppermute | solution.py:33
  41.2 1.1 %collective-permute-done.16.refs_13_ = bf16[16,2176]{1,0:T(8,128)(2,1)S(1)} collective-permute-done((bf16[16,2176]{1,0:T(8,128)(2,1)S(1)}, bf16[16,2176]{1,0:T(8,128)(2,1)S(1)}, u32[]{:S(2)}, u32[]{:S(2)}) %collective-permute-start.16) | collective-permute-done | bytes 69664 | tf_op jit(solution)/shard_map/ppermute | solution.py:33
  42.3 12.6 %experts.1 = (f32[128,2048]{1,0:T(8,128)S(1)}, bf16[128,2048]{1,0:T(8,128)(2,1)S(1)}) custom-call(bf16[16,2176]{1,0:T(8,128)(2,1)S(1)} %get-tuple-element.45.refs_0_, bf16[16,2176]{1,0:T(8,128)(2,1)S(1)} %collective-permute-done.4.refs_1_, bf16[16,2176]{1,0:T(8,128)(2,1)S(1)} %collective-permute-done.5.refs_2_, ...), custom_call_target="tpu_custom_call" | custom-call | bytes 40800000 | tf_op jit(solution)/shard_map/experts/pallas_call | solution.py:41
  55.2 1.8 %collective-permute-done.19.refs_1_ = bf16[128,2048]{1,0:T(8,128)(2,1)S(1)} collective-permute-done((bf16[128,2048]{1,0:T(8,128)(2,1)S(1)}, bf16[128,2048]{1,0:T(8,128)(2,1)S(1)}, u32[]{:S(2)}, u32[]{:S(2)}) %collective-permute-start.19) | collective-permute-done | bytes 524320 | tf_op jit(solution)/shard_map/ppermute | solution.py:33
  57.0 1.2 %collective-permute-start.20 = (bf16[16,2048]{1,0:T(8,128)(2,1)S(1)}, bf16[16,2048]{1,0:T(8,128)(2,1)S(1)}, u32[]{:S(2)}, u32[]{:S(2)}) collective-permute-start(bf16[16,2048]{1,0:T(8,128)(2,1)S(1)} %get-tuple-element.52), channel_id=1, source_target_pairs={{0,2},{2,0},{1,3},{3,1},{4,6},{6,4},{5,7},{7,5},{8,10},{10,8},{9,1... | collective-permute-start | bytes 196616 | tf_op jit(solution)/shard_map/ppermute | solution.py:33
  58.2 0.9 %collective-permute-start.22 = (bf16[16,2048]{1,0:T(8,128)(2,1)S(1)}, bf16[16,2048]{1,0:T(8,128)(2,1)S(1)}, u32[]{:S(2)}, u32[]{:S(2)}) collective-permute-start(bf16[16,2048]{1,0:T(8,128)(2,1)S(1)} %get-tuple-element.54), channel_id=1, source_target_pairs={{0,2},{2,0},{1,3},{3,1},{4,6},{6,4},{5,7},{7,5},{8,10},{10,8},{9,1... | collective-permute-start | bytes 196616 | tf_op jit(solution)/shard_map/ppermute | solution.py:33
  59.1 1.1 %collective-permute-start.24 = (bf16[16,2048]{1,0:T(8,128)(2,1)S(1)}, bf16[16,2048]{1,0:T(8,128)(2,1)S(1)}, u32[]{:S(2)}, u32[]{:S(2)}) collective-permute-start(bf16[16,2048]{1,0:T(8,128)(2,1)S(1)} %get-tuple-element.56), channel_id=1, source_target_pairs={{0,2},{2,0},{1,3},{3,1},{4,6},{6,4},{5,7},{7,5},{8,10},{10,8},{9,1... | collective-permute-start | bytes 196616 | tf_op jit(solution)/shard_map/ppermute | solution.py:33
  60.3 0.9 %collective-permute-start.26 = (bf16[16,2048]{1,0:T(8,128)(2,1)S(1)}, bf16[16,2048]{1,0:T(8,128)(2,1)S(1)}, u32[]{:S(2)}, u32[]{:S(2)}) collective-permute-start(bf16[16,2048]{1,0:T(8,128)(2,1)S(1)} %get-tuple-element.58), channel_id=1, source_target_pairs={{0,2},{2,0},{1,3},{3,1},{4,6},{6,4},{5,7},{7,5},{8,10},{10,8},{9,1... | collective-permute-start | bytes 196616 | tf_op jit(solution)/shard_map/ppermute | solution.py:33
  61.2 0.9 %collective-permute-done.20.refs_1_ = bf16[16,2048]{1,0:T(8,128)(2,1)S(1)} collective-permute-done((bf16[16,2048]{1,0:T(8,128)(2,1)S(1)}, bf16[16,2048]{1,0:T(8,128)(2,1)S(1)}, u32[]{:S(2)}, u32[]{:S(2)}) %collective-permute-start.20) | collective-permute-done | bytes 65568 | tf_op jit(solution)/shard_map/ppermute | solution.py:33
  62.1 1.3 %collective-permute-done.22.refs_1_ = bf16[16,2048]{1,0:T(8,128)(2,1)S(1)} collective-permute-done((bf16[16,2048]{1,0:T(8,128)(2,1)S(1)}, bf16[16,2048]{1,0:T(8,128)(2,1)S(1)}, u32[]{:S(2)}, u32[]{:S(2)}) %collective-permute-start.22) | collective-permute-done | bytes 65568 | tf_op jit(solution)/shard_map/ppermute | solution.py:33
  63.5 1.3 %collective-permute-done.24.refs_1_ = bf16[16,2048]{1,0:T(8,128)(2,1)S(1)} collective-permute-done((bf16[16,2048]{1,0:T(8,128)(2,1)S(1)}, bf16[16,2048]{1,0:T(8,128)(2,1)S(1)}, u32[]{:S(2)}, u32[]{:S(2)}) %collective-permute-start.24) | collective-permute-done | bytes 65568 | tf_op jit(solution)/shard_map/ppermute | solution.py:33
  64.9 1.8 %collective-permute-start.25 = (bf16[16,2048]{1,0:T(8,128)(2,1)S(1)}, bf16[16,2048]{1,0:T(8,128)(2,1)S(1)}, u32[]{:S(2)}, u32[]{:S(2)}) collective-permute-start(bf16[16,2048]{1,0:T(8,128)(2,1)S(1)} %sum_x3.1), channel_id=1, source_target_pairs={{0,12},{4,8},{8,4},{12,0},{1,13},{5,9},{9,5},{13,1},{2,14},{6,10},... | collective-permute-start | bytes 196616 | tf_op jit(solution)/shard_map/ppermute | solution.py:33
  67.1 3.0 %collective-permute-done.23.refs_2_ = bf16[16,2048]{1,0:T(8,128)(2,1)S(1)} collective-permute-done((bf16[16,2048]{1,0:T(8,128)(2,1)S(1)}, bf16[16,2048]{1,0:T(8,128)(2,1)S(1)}, u32[]{:S(2)}, u32[]{:S(2)}) %collective-permute-start.23) | collective-permute-done | bytes 65568 | tf_op jit(solution)/shard_map/ppermute | solution.py:33
  70.1 1.0 %collective-permute-done.25.refs_3_ = bf16[16,2048]{1,0:T(8,128)(2,1)S(1)} collective-permute-done((bf16[16,2048]{1,0:T(8,128)(2,1)S(1)}, bf16[16,2048]{1,0:T(8,128)(2,1)S(1)}, u32[]{:S(2)}, u32[]{:S(2)}) %collective-permute-start.25) | collective-permute-done | bytes 65568 | tf_op jit(solution)/shard_map/ppermute | solution.py:33
  71.1 0.7 total.1
  (35 shorter events, 1.8 us)
Async XLA Ops:
  0.8 16.8 %collective-permute-start.1 = (bf16[64,512]{1,0:T(8,128)(2,1)S(1)}, bf16[64,512]{1,0:T(8,128)(2,1)S(1)}, u32[]{:S(2)}, u32[]{:S(2)}) collective-permute-start(bf16[64,512]{1,0:T(8,128)(2,1)S(1)} %pad_maximum_fusion.refs_2_), channel_id=1, source_target_pairs={{0,4},{4,8},{8,12},{1,5},{5,9},{9,13},{2,6},{6,10},{10,14},{3,7},{... | collective-permute-start | bytes 196616 | tf_op jit(solution)/shard_map/ppermute | solution.py:340
  5.7 11.9 %collective-permute-start = (bf16[64,512]{1,0:T(8,128)(2,1)S(1)}, bf16[64,512]{1,0:T(8,128)(2,1)S(1)}, u32[]{:S(2)}, u32[]{:S(2)}) collective-permute-start(bf16[64,512]{1,0:T(8,128)(2,1)S(1)} %pad_maximum_fusion.refs_2_), channel_id=1, source_target_pairs={{0,8},{4,12},{1,9},{5,13},{2,10},{6,14},{3,11},{7,15},{16,24},{20,... | collective-permute-start | bytes 196616 | tf_op jit(solution)/shard_map/ppermute | solution.py:340
  19.0 1.4 %collective-permute-start.2 = (bf16[32,2048]{1,0:T(8,128)(2,1)S(1)}, bf16[32,2048]{1,0:T(8,128)(2,1)S(1)}, u32[]{:S(2)}, u32[]{:S(2)}) collective-permute-start(bf16[32,2048]{1,0:T(8,128)(2,1)S(1)} %get-tuple-element.40), channel_id=1, source_target_pairs={{0,1},{1,0},{2,3},{3,2},{4,5},{5,4},{6,7},{7,6},{8,9},{9,8},{10,11... | collective-permute-start | bytes 393224 | tf_op jit(solution)/shard_map/ppermute | solution.py:33
  20.5 5.0 %collective-permute-start.3 = (bf16[16,2048]{1,0:T(8,128)(2,1)S(1)}, bf16[16,2048]{1,0:T(8,128)(2,1)S(1)}, u32[]{:S(2)}, u32[]{:S(2)}) collective-permute-start(bf16[16,2048]{1,0:T(8,128)(2,1)S(1)} %get-tuple-element.42), channel_id=1, source_target_pairs={{0,2},{2,0},{1,3},{3,1},{4,6},{6,4},{5,7},{7,5},{8,10},{10,8},{9,1... | collective-permute-start | bytes 196616 | tf_op jit(solution)/shard_map/ppermute | solution.py:33
  25.6 5.3 %collective-permute-start.7 = (bf16[16,2176]{1,0:T(8,128)(2,1)S(1)}, bf16[16,2176]{1,0:T(8,128)(2,1)S(1)}, u32[]{:S(2)}, u32[]{:S(2)}) collective-permute-start(bf16[16,2176]{1,0:T(8,128)(2,1)S(1)} %get-tuple-element.45.refs_0_), channel_id=1, source_target_pairs={{0,2},{2,0},{1,3},{3,1},{4,6},{6,4},{5,7},{7,5},{8,10},{10,8},{9,1... | collective-permute-start | bytes 208904 | tf_op jit(solution)/shard_map/ppermute | solution.py:33
  26.5 7.0 %collective-permute-start.6 = (bf16[16,2176]{1,0:T(8,128)(2,1)S(1)}, bf16[16,2176]{1,0:T(8,128)(2,1)S(1)}, u32[]{:S(2)}, u32[]{:S(2)}) collective-permute-start(bf16[16,2176]{1,0:T(8,128)(2,1)S(1)} %get-tuple-element.45.refs_0_), channel_id=1, source_target_pairs={{0,12},{4,8},{8,4},{12,0},{1,13},{5,9},{9,5},{13,1},{2,14},{6,10},... | collective-permute-start | bytes 208904 | tf_op jit(solution)/shard_map/ppermute | solution.py:33
  26.5 7.0 %collective-permute-start.11 = (bf16[16,2176]{1,0:T(8,128)(2,1)S(1)}, bf16[16,2176]{1,0:T(8,128)(2,1)S(1)}, u32[]{:S(2)}, u32[]{:S(2)}) collective-permute-start(bf16[16,2176]{1,0:T(8,128)(2,1)S(1)} %get-tuple-element.45.refs_0_), channel_id=1, source_target_pairs={{0,1},{1,0},{2,3},{3,2},{4,5},{5,4},{6,7},{7,6},{8,9},{9,8},{10,11... | collective-permute-start | bytes 208904 | tf_op jit(solution)/shard_map/ppermute | solution.py:33
  26.5 8.1 %collective-permute-start.5 = (bf16[16,2176]{1,0:T(8,128)(2,1)S(1)}, bf16[16,2176]{1,0:T(8,128)(2,1)S(1)}, u32[]{:S(2)}, u32[]{:S(2)}) collective-permute-start(bf16[16,2176]{1,0:T(8,128)(2,1)S(1)} %get-tuple-element.45.refs_0_), channel_id=1, source_target_pairs={{0,8},{4,12},{8,0},{12,4},{1,9},{5,13},{9,1},{13,5},{2,10},{6,14},... | collective-permute-start | bytes 208904 | tf_op jit(solution)/shard_map/ppermute | solution.py:33
  27.4 8.8 %collective-permute-start.4 = (bf16[16,2176]{1,0:T(8,128)(2,1)S(1)}, bf16[16,2176]{1,0:T(8,128)(2,1)S(1)}, u32[]{:S(2)}, u32[]{:S(2)}) collective-permute-start(bf16[16,2176]{1,0:T(8,128)(2,1)S(1)} %get-tuple-element.45.refs_0_), channel_id=1, source_target_pairs={{0,4},{4,0},{8,12},{12,8},{1,5},{5,1},{9,13},{13,9},{2,6},{6,2},{1... | collective-permute-start | bytes 208904 | tf_op jit(solution)/shard_map/ppermute | solution.py:33
  30.9 5.8 %collective-permute-start.15 = (bf16[16,2176]{1,0:T(8,128)(2,1)S(1)}, bf16[16,2176]{1,0:T(8,128)(2,1)S(1)}, u32[]{:S(2)}, u32[]{:S(2)}) collective-permute-start(bf16[16,2176]{1,0:T(8,128)(2,1)S(1)} %collective-permute-done.7.refs_4_), channel_id=1, source_target_pairs={{0,1},{1,0},{2,3},{3,2},{4,5},{5,4},{6,7},{7,6},{8,9},{9,8},{10,11... | collective-permute-start | bytes 208904 | tf_op jit(solution)/shard_map/ppermute | solution.py:33
  33.5 3.2 %collective-permute-start.14 = (bf16[16,2176]{1,0:T(8,128)(2,1)S(1)}, bf16[16,2176]{1,0:T(8,128)(2,1)S(1)}, u32[]{:S(2)}, u32[]{:S(2)}) collective-permute-start(bf16[16,2176]{1,0:T(8,128)(2,1)S(1)} %collective-permute-done.6.refs_3_), channel_id=1, source_target_pairs={{0,1},{1,0},{2,3},{3,2},{4,5},{5,4},{6,7},{7,6},{8,9},{9,8},{10,11... | collective-permute-start | bytes 208904 | tf_op jit(solution)/shard_map/ppermute | solution.py:33
  33.5 5.0 %collective-permute-start.10 = (bf16[16,2176]{1,0:T(8,128)(2,1)S(1)}, bf16[16,2176]{1,0:T(8,128)(2,1)S(1)}, u32[]{:S(2)}, u32[]{:S(2)}) collective-permute-start(bf16[16,2176]{1,0:T(8,128)(2,1)S(1)} %collective-permute-done.6.refs_3_), channel_id=1, source_target_pairs={{0,2},{2,0},{1,3},{3,1},{4,6},{6,4},{5,7},{7,5},{8,10},{10,8},{9,1... | collective-permute-start | bytes 208904 | tf_op jit(solution)/shard_map/ppermute | solution.py:33
  34.6 5.3 %collective-permute-start.9 = (bf16[16,2176]{1,0:T(8,128)(2,1)S(1)}, bf16[16,2176]{1,0:T(8,128)(2,1)S(1)}, u32[]{:S(2)}, u32[]{:S(2)}) collective-permute-start(bf16[16,2176]{1,0:T(8,128)(2,1)S(1)} %collective-permute-done.5.refs_2_), channel_id=1, source_target_pairs={{0,2},{2,0},{1,3},{3,1},{4,6},{6,4},{5,7},{7,5},{8,10},{10,8},{9,1... | collective-permute-start | bytes 208904 | tf_op jit(solution)/shard_map/ppermute | solution.py:33
  36.2 4.9 %collective-permute-start.8 = (bf16[16,2176]{1,0:T(8,128)(2,1)S(1)}, bf16[16,2176]{1,0:T(8,128)(2,1)S(1)}, u32[]{:S(2)}, u32[]{:S(2)}) collective-permute-start(bf16[16,2176]{1,0:T(8,128)(2,1)S(1)} %collective-permute-done.4.refs_1_), channel_id=1, source_target_pairs={{0,2},{2,0},{1,3},{3,1},{4,6},{6,4},{5,7},{7,5},{8,10},{10,8},{9,1... | collective-permute-start | bytes 208904 | tf_op jit(solution)/shard_map/ppermute | solution.py:33
  36.7 4.4 %collective-permute-start.13 = (bf16[16,2176]{1,0:T(8,128)(2,1)S(1)}, bf16[16,2176]{1,0:T(8,128)(2,1)S(1)}, u32[]{:S(2)}, u32[]{:S(2)}) collective-permute-start(bf16[16,2176]{1,0:T(8,128)(2,1)S(1)} %collective-permute-done.5.refs_2_), channel_id=1, source_target_pairs={{0,1},{1,0},{2,3},{3,2},{4,5},{5,4},{6,7},{7,6},{8,9},{9,8},{10,11... | collective-permute-start | bytes 208904 | tf_op jit(solution)/shard_map/ppermute | solution.py:33
  36.7 4.4 %collective-permute-start.12 = (bf16[16,2176]{1,0:T(8,128)(2,1)S(1)}, bf16[16,2176]{1,0:T(8,128)(2,1)S(1)}, u32[]{:S(2)}, u32[]{:S(2)}) collective-permute-start(bf16[16,2176]{1,0:T(8,128)(2,1)S(1)} %collective-permute-done.4.refs_1_), channel_id=1, source_target_pairs={{0,1},{1,0},{2,3},{3,2},{4,5},{5,4},{6,7},{7,6},{8,9},{9,8},{10,11... | collective-permute-start | bytes 208904 | tf_op jit(solution)/shard_map/ppermute | solution.py:33
  38.5 2.6 %collective-permute-start.18 = (bf16[16,2176]{1,0:T(8,128)(2,1)S(1)}, bf16[16,2176]{1,0:T(8,128)(2,1)S(1)}, u32[]{:S(2)}, u32[]{:S(2)}) collective-permute-start(bf16[16,2176]{1,0:T(8,128)(2,1)S(1)} %collective-permute-done.10.refs_7_), channel_id=1, source_target_pairs={{0,1},{1,0},{2,3},{3,2},{4,5},{5,4},{6,7},{7,6},{8,9},{9,8},{10,11... | collective-permute-start | bytes 208904 | tf_op jit(solution)/shard_map/ppermute | solution.py:33
  40.0 1.3 %collective-permute-start.17 = (bf16[16,2176]{1,0:T(8,128)(2,1)S(1)}, bf16[16,2176]{1,0:T(8,128)(2,1)S(1)}, u32[]{:S(2)}, u32[]{:S(2)}) collective-permute-start(bf16[16,2176]{1,0:T(8,128)(2,1)S(1)} %collective-permute-done.9.refs_6_), channel_id=1, source_target_pairs={{0,1},{1,0},{2,3},{3,2},{4,5},{5,4},{6,7},{7,6},{8,9},{9,8},{10,11... | collective-permute-start | bytes 208904 | tf_op jit(solution)/shard_map/ppermute | solution.py:33
  41.1 1.3 %collective-permute-start.16 = (bf16[16,2176]{1,0:T(8,128)(2,1)S(1)}, bf16[16,2176]{1,0:T(8,128)(2,1)S(1)}, u32[]{:S(2)}, u32[]{:S(2)}) collective-permute-start(bf16[16,2176]{1,0:T(8,128)(2,1)S(1)} %collective-permute-done.8.refs_5_), channel_id=1, source_target_pairs={{0,1},{1,0},{2,3},{3,2},{4,5},{5,4},{6,7},{7,6},{8,9},{9,8},{10,11... | collective-permute-start | bytes 208904 | tf_op jit(solution)/shard_map/ppermute | solution.py:33
  55.0 2.0 %collective-permute-start.19 = (bf16[128,2048]{1,0:T(8,128)(2,1)S(1)}, bf16[128,2048]{1,0:T(8,128)(2,1)S(1)}, u32[]{:S(2)}, u32[]{:S(2)}) collective-permute-start(bf16[128,2048]{1,0:T(8,128)(2,1)S(1)} %get-tuple-element.50), channel_id=1, source_target_pairs={{0,1},{1,0},{2,3},{3,2},{4,5},{5,4},{6,7},{7,6},{8,9},{9,8},{10,11... | collective-permute-start | bytes 1572872 | tf_op jit(solution)/shard_map/ppermute | solution.py:33
  57.0 5.0 %collective-permute-start.20 = (bf16[16,2048]{1,0:T(8,128)(2,1)S(1)}, bf16[16,2048]{1,0:T(8,128)(2,1)S(1)}, u32[]{:S(2)}, u32[]{:S(2)}) collective-permute-start(bf16[16,2048]{1,0:T(8,128)(2,1)S(1)} %get-tuple-element.52), channel_id=1, source_target_pairs={{0,2},{2,0},{1,3},{3,1},{4,6},{6,4},{5,7},{7,5},{8,10},{10,8},{9,1... | collective-permute-start | bytes 196616 | tf_op jit(solution)/shard_map/ppermute | solution.py:33
  58.2 5.2 %collective-permute-start.22 = (bf16[16,2048]{1,0:T(8,128)(2,1)S(1)}, bf16[16,2048]{1,0:T(8,128)(2,1)S(1)}, u32[]{:S(2)}, u32[]{:S(2)}) collective-permute-start(bf16[16,2048]{1,0:T(8,128)(2,1)S(1)} %get-tuple-element.54), channel_id=1, source_target_pairs={{0,2},{2,0},{1,3},{3,1},{4,6},{6,4},{5,7},{7,5},{8,10},{10,8},{9,1... | collective-permute-start | bytes 196616 | tf_op jit(solution)/shard_map/ppermute | solution.py:33
  59.1 5.7 %collective-permute-start.24 = (bf16[16,2048]{1,0:T(8,128)(2,1)S(1)}, bf16[16,2048]{1,0:T(8,128)(2,1)S(1)}, u32[]{:S(2)}, u32[]{:S(2)}) collective-permute-start(bf16[16,2048]{1,0:T(8,128)(2,1)S(1)} %get-tuple-element.56), channel_id=1, source_target_pairs={{0,2},{2,0},{1,3},{3,1},{4,6},{6,4},{5,7},{7,5},{8,10},{10,8},{9,1... | collective-permute-start | bytes 196616 | tf_op jit(solution)/shard_map/ppermute | solution.py:33
  60.3 6.4 %collective-permute-start.26 = (bf16[16,2048]{1,0:T(8,128)(2,1)S(1)}, bf16[16,2048]{1,0:T(8,128)(2,1)S(1)}, u32[]{:S(2)}, u32[]{:S(2)}) collective-permute-start(bf16[16,2048]{1,0:T(8,128)(2,1)S(1)} %get-tuple-element.58), channel_id=1, source_target_pairs={{0,2},{2,0},{1,3},{3,1},{4,6},{6,4},{5,7},{7,5},{8,10},{10,8},{9,1... | collective-permute-start | bytes 196616 | tf_op jit(solution)/shard_map/ppermute | solution.py:33
  62.1 5.0 %collective-permute-start.21 = (bf16[16,2048]{1,0:T(8,128)(2,1)S(1)}, bf16[16,2048]{1,0:T(8,128)(2,1)S(1)}, u32[]{:S(2)}, u32[]{:S(2)}) collective-permute-start(bf16[16,2048]{1,0:T(8,128)(2,1)S(1)} %sum_x1.1), channel_id=1, source_target_pairs={{0,4},{4,0},{8,12},{12,8},{1,5},{5,1},{9,13},{13,9},{2,6},{6,2},{1... | collective-permute-start | bytes 196616 | tf_op jit(solution)/shard_map/ppermute | solution.py:33
  63.5 6.6 %collective-permute-start.23 = (bf16[16,2048]{1,0:T(8,128)(2,1)S(1)}, bf16[16,2048]{1,0:T(8,128)(2,1)S(1)}, u32[]{:S(2)}, u32[]{:S(2)}) collective-permute-start(bf16[16,2048]{1,0:T(8,128)(2,1)S(1)} %sum_x2.1), channel_id=1, source_target_pairs={{0,8},{4,12},{8,0},{12,4},{1,9},{5,13},{9,1},{13,5},{2,10},{6,14},... | collective-permute-start | bytes 196616 | tf_op jit(solution)/shard_map/ppermute | solution.py:33
  64.9 6.2 %collective-permute-start.25 = (bf16[16,2048]{1,0:T(8,128)(2,1)S(1)}, bf16[16,2048]{1,0:T(8,128)(2,1)S(1)}, u32[]{:S(2)}, u32[]{:S(2)}) collective-permute-start(bf16[16,2048]{1,0:T(8,128)(2,1)S(1)} %sum_x3.1), channel_id=1, source_target_pairs={{0,12},{4,8},{8,4},{12,0},{1,13},{5,9},{9,5},{13,1},{2,14},{6,10},... | collective-permute-start | bytes 196616 | tf_op jit(solution)/shard_map/ppermute | solution.py:33

commit v9 on v5

--- a/solution.py
+++ b/solution.py
@@ -227,9 +227,9 @@
     gate_refs = list(refs[n_rows : n_rows + n_gate])
     up_refs = list(refs[n_rows + n_gate : n_rows + n_gate + n_up])
     refs = refs[n_rows + n_gate + n_up :]
-    up_hbm, down_hbm, keep_ref, send_ref, rows_ref, pick_ref, packed_ref, hidden_ref = refs[:8]
-    up_late = list(refs[8 : 8 + experts - n_up])
-    down_ref, up_sem, down_sem = refs[8 + experts - n_up :]
+    up_hbm, down_hbm, keep_ref, send_ref, rows_ref, pick_ref, share_ref, packed_ref, hidden_ref = refs[:9]
+    up_late = list(refs[9 : 9 + experts - n_up])
+    down_ref, up_sem, down_sem = refs[9 + experts - n_up :]
     per_expert, width = down_hbm.shape[0] // experts, down_hbm.shape[1]
     up_copies = [
         pltpu.make_async_copy(a, b, up_sem.at[i])
@@ -258,7 +258,7 @@
     id0, id1, code0, code1 = (info[i : i + 1, :] for i in range(4))
     slot_of = lax.broadcasted_iota(jnp.int32, (capacity, count), 0).astype(jnp.float32)
     first = lax.axis_index("sec") * experts if halves == 1 else lax.axis_index("sec") // halves
-    picks, shares = [], []
+    picks, shares, taken = [], [], []
     for x in range(experts):
         e = (first + x).astype(jnp.float32)
         hit0 = jnp.where(id0 == e, 1.0, 0.0)
@@ -269,31 +269,56 @@
         slot = jnp.where(member > 0.5, slot, -1.0)
         pick = slot == slot_of
         shares.append(jnp.sum(jnp.where(pick, share, 0.0), axis=1, keepdims=True))
+        taken.append(jnp.sum(member).astype(jnp.int32))
         picks.append(jnp.where(pick, 1.0, 0.0).astype(jnp.bfloat16))
     pick_ref[...] = jnp.concatenate(picks, axis=0)
+    share_ref[...] = jnp.broadcast_to(jnp.concatenate(shares, axis=0), share_ref.shape)
     column = min(512, width)
 
     for c in range(0, width, column):
         packed_ref[:, c : c + column] = dot(pick_ref[...], rows_ref[:, c : c + column]).astype(
             jnp.bfloat16
         )
+    step = min(capacity, 32)
+    sizes = range(step, capacity + 1, step) if capacity <= 4 * step else [capacity]
+
+    def by_size(x, run):
+        for size in sizes:
+            fits = taken[x] <= size
+            if size > sizes[0]:
+                fits = fits & (taken[x] > size - step)
+            if len(sizes) > 1:
+                pl.when(fits)(functools.partial(run, slice(x * capacity, x * capacity + size)))
+            else:
+                run(slice(x * capacity, x * capacity + size))
+
     for x in range(experts):
-        mine = slice(x * capacity, (x + 1) * capacity)
         if x >= n_up:
             up_copies[x - n_up].wait()
-        gate_ref, up_ref = gate_refs[x], up_refs[x]
-
-        for s in range(0, per_expert, tile):
-            cut = slice(s, s + tile)
-            gate = dot(packed_ref[mine, :], gate_ref[:, cut])
-            up = dot(packed_ref[mine, :], up_ref[:, cut])
-            half = 0.5 * gate
-            hidden_ref[mine, cut] = ((half + half * jnp.tanh(half)) * up).astype(jnp.bfloat16)
+
+        def inner(mine, gate_ref=gate_refs[x], up_ref=up_refs[x]):
+            def body(s, _):
+                cut = pl.ds(pl.multiple_of(s * tile, tile), tile)
+                gate = dot(packed_ref[mine, :], gate_ref[:, cut])
+                up = dot(packed_ref[mine, :], up_ref[:, cut])
+                half = 0.5 * gate
+                hidden_ref[mine, cut] = ((half + half * jnp.tanh(half)) * up).astype(jnp.bfloat16)
+                return 0
+
+            lax.fori_loop(0, per_expert // tile, body, 0)
+
+        def outer(mine, x=x):
+            def body(c, _):
+                cut = pl.ds(pl.multiple_of(c * column, column), column)
+                out = dot(hidden_ref[mine, :], down_ref[:, cut])
+                packed_ref[mine, cut] = (out * share_ref[mine, :1]).astype(jnp.bfloat16)
+                return 0
+
+            lax.fori_loop(0, width // column, body, 0)
+
+        by_size(x, inner)
         down_copies[x].wait()
-
-        for c in range(0, width, column):
-            out = dot(hidden_ref[mine, :], down_ref[:, c : c + column])
-            packed_ref[mine, c : c + column] = (out * shares[x]).astype(jnp.bfloat16)
+        by_size(x, outer)
         if x + 1 < experts:
             down_copies[x + 1].start()
     kept = keep_ref.shape[0]
@@ -398,7 +423,9 @@
     )
 
     groups = min(4, sec_count)
-    near = [normed] + [xor_swap(normed, "sec", k) for k in range(1, sec_count)]
+    near = {k: xor_swap(normed, "sec", k) if k else normed for k in range(0, sec_count, 2)}
+    near.update({k + 1: xor_swap(near[k], "sec", 1) for k in list(near) if k + 1 < sec_count})
+    near = [near[k] for k in range(sec_count)]
     per_group = sec_count // groups
     near = [
         jnp.concatenate(near[g * per_group : (g + 1) * per_group], axis=0)
@@ -423,6 +450,7 @@
         scratch=[
             pltpu.VMEM((count, width + LANES), bf16),
             pltpu.VMEM((experts * capacity, count), bf16),
+            pltpu.VMEM((experts * capacity, LANES), f32),
             pltpu.VMEM((experts * capacity, width), bf16),
             pltpu.VMEM((experts * capacity, down.shape[0] // experts), bf16),
             *[pltpu.VMEM((width, per_expert), bf16)] * (experts - 1),

time: 72 us -> 72.2 us (level)
  starting transfers between devices: 26.3 us -> 23.9 us
  Pallas kernels: 25.7 us -> 27.1 us
  waiting for transfers between devices: 18.7 us -> 19.9 us
    ppermute x25, starting transfers between devices: 16.9 us -> 14.5 us  [xor_swap(): return lax.ppermute(x, axis, [(i, i ^ k) for i in range(n)])]
    pallas_call x11, Pallas kernels: 25.7 us -> 27.1 us  [call(): pl.pallas_call(kernel, out_shape=out_shape, in_specs=[s for s, _ in args]...]
    ppermute x25, waiting for transfers between devices: 18.7 us -> 19.9 us  [xor_swap(): return lax.ppermute(x, axis, [(i, i ^ k) for i in range(n)])]
  transfers between devices with their start and end apart: 27 -> 27, of which waited for: 14 -> 13; matrix products, arithmetic and copies ran while one was open for 0% -> 0% of each run, Pallas kernels for 15% -> 15%
where the time goes in v9:
time: 72.2 us; the launch traced here: 71.9 us
  Pallas kernels  27.1 us (38%)
  starting transfers between devices  23.9 us (33%)
  waiting for transfers between devices  19.9 us (28%)
  local copies, waits for them, and re-layouts  0.78 us (1%)
    pallas_call x11, Pallas kernels, call(): pl.pallas_call(kernel, out_shape=out_shape, in_specs=[s for s, _ in args]...  27.1 us
    ppermute x25, waiting for transfers between devices, xor_swap(): return lax.ppermute(x, axis, [(i, i ^ k) for i in range(n)])  19.9 us
    ppermute x25, starting transfers between devices, xor_swap(): return lax.ppermute(x, axis, [(i, i ^ k) for i in range(n)])  14.5 us
    ppermute x2, starting transfers between devices, per_device(): lax.ppermute(kv, 'sec', [(i, i + k) for i in range(sec_count - k)])  9.43 us
  transfers between devices with their start and end apart: 27, of which 13 were waited for; matrix products, arithmetic and copies ran while one was open for 0% of the time, Pallas kernels for 15%

profile of v9, /device:TPU:0, one launch (start us, length us, event | category | flops | bytes accessed | tf_op | source)
XLA Modules:
  0.0 71.9 jit_solution(1549648572501838797)
XLA Ops:
  0.0 0.8 %constant_dynamic-slice_fusion = (bf16[64,256]{1,0:T(8,128)(2,1)S(1)}, bf16[64,256]{1,0:T(8,128)(2,1)S(1)}) fusion(bf16[64,512]{1,0:T(8,128)(2,1)} %param.14, s32[]{:T(128)S(6)} %select_n.10, bf16[64,512]{1,0:T(8,128)(2,1)} %param.13), kind=kLoop, calls=%fused_computation.1 | loop fusion | bytes 131076 | tf_op jit(solution)/shard_map/dynamic_slice | solution.py:361
  0.8 4.9 %collective-permute-start.1 = (bf16[64,512]{1,0:T(8,128)(2,1)S(1)}, bf16[64,512]{1,0:T(8,128)(2,1)S(1)}, u32[]{:S(2)}, u32[]{:S(2)}) collective-permute-start(bf16[64,512]{1,0:T(8,128)(2,1)S(1)} %pad_maximum_fusion.refs_2_), channel_id=1, source_target_pairs={{0,4},{4,8},{8,12},{1,5},{5,9},{9,13},{2,6},{6,10},{10,14},{3,7},{... | collective-permute-start | bytes 196616 | tf_op jit(solution)/shard_map/ppermute | solution.py:365
  5.7 4.5 %collective-permute-start = (bf16[64,512]{1,0:T(8,128)(2,1)S(1)}, bf16[64,512]{1,0:T(8,128)(2,1)S(1)}, u32[]{:S(2)}, u32[]{:S(2)}) collective-permute-start(bf16[64,512]{1,0:T(8,128)(2,1)S(1)} %pad_maximum_fusion.refs_2_), channel_id=1, source_target_pairs={{0,8},{4,12},{1,9},{5,13},{2,10},{6,14},{3,11},{7,15},{16,24},{20,... | collective-permute-start | bytes 196616 | tf_op jit(solution)/shard_map/ppermute | solution.py:365
  10.2 7.3 %prepare.1 = (bf16[64,1024]{1,0:T(8,128)(2,1)S(1)}, bf16[1024,2048]{1,0:T(8,128)(2,1)S(1)}, f32[1,2048]{1,0:T(1,128)S(1)}, f32[64,192]{1,0:T(8,128)S(1)}, bf16[6...) custom-call(s32[8]{0:T(128)} %lengths_hbm.1, ...), custom_call_target="tpu_custom_call" | custom-call | bytes 20400000 | tf_op jit(solution)/shard_map/prepare/pallas_call | solution.py:41
  17.6 1.4 %attention.1 = (f32[32,2048]{1,0:T(8,128)S(1)}, bf16[32,2048]{1,0:T(8,128)(2,1)S(1)}) custom-call(bf16[64,1024]{1,0:T(8,128)(2,1)S(1)} %get-tuple-element.35.q_ref, f32[64,192]{1,0:T(8,128)S(1)} %get-tuple-element.36.mask_ref, bf16[64,64]{1,0:T(8,128)(2,1)S(1)} %get-tuple-element.37.order_ref, bf16[64,512]{1,0:T(8,128)(2,1)S(1)} %collective-permute-done.refs_0_, ...), custom_call_target="tpu_custom_call" | custom-call | bytes 8160000 | tf_op jit(solution)/shard_map/attention/pallas_call | solution.py:41
  19.1 1.3 %collective-permute-done.2.refs_1_ = bf16[32,2048]{1,0:T(8,128)(2,1)S(1)} collective-permute-done((bf16[32,2048]{1,0:T(8,128)(2,1)S(1)}, bf16[32,2048]{1,0:T(8,128)(2,1)S(1)}, u32[]{:S(2)}, u32[]{:S(2)}) %collective-permute-start.2) | collective-permute-done | bytes 131104 | tf_op jit(solution)/shard_map/ppermute | solution.py:33
  20.5 1.6 %collective-permute-start.3 = (bf16[16,2048]{1,0:T(8,128)(2,1)S(1)}, bf16[16,2048]{1,0:T(8,128)(2,1)S(1)}, u32[]{:S(2)}, u32[]{:S(2)}) collective-permute-start(bf16[16,2048]{1,0:T(8,128)(2,1)S(1)} %get-tuple-element.42), channel_id=1, source_target_pairs={{0,2},{2,0},{1,3},{3,1},{4,6},{6,4},{5,7},{7,5},{8,10},{10,8},{9,1... | collective-permute-start | bytes 196616 | tf_op jit(solution)/shard_map/ppermute | solution.py:33
  22.0 3.4 %load_up.1 = (bf16[2048,2048]{1,0:T(8,128)(2,1)S(1)}, f32[8,128]{1,0:T(8,128)S(1)}) custom-call(bf16[2048,4096]{1,0:T(8,128)(2,1)} %bitcast.6, f32[16,2048]{1,0:T(8,128)S(1)} %get-tuple-element.41.refs_0_), custom_call_target="tpu_custom_call" | custom-call | bytes 8388607 | tf_op jit(solution)/shard_map/load_up/pallas_call | solution.py:41
  25.7 0.9 %collective-permute-start.7 = (bf16[16,2176]{1,0:T(8,128)(2,1)S(1)}, bf16[16,2176]{1,0:T(8,128)(2,1)S(1)}, u32[]{:S(2)}, u32[]{:S(2)}) collective-permute-start(bf16[16,2176]{1,0:T(8,128)(2,1)S(1)} %get-tuple-element.45.refs_0_), channel_id=1, source_target_pairs={{0,2},{2,0},{1,3},{3,1},{4,6},{6,4},{5,7},{7,5},{8,10},{10,8},{9,1... | collective-permute-start | bytes 208904 | tf_op jit(solution)/shard_map/ppermute | solution.py:33
  26.6 4.7 %collective-permute-done.5.refs_2_ = bf16[16,2176]{1,0:T(8,128)(2,1)S(1)} collective-permute-done((bf16[16,2176]{1,0:T(8,128)(2,1)S(1)}, bf16[16,2176]{1,0:T(8,128)(2,1)S(1)}, u32[]{:S(2)}, u32[]{:S(2)}) %collective-permute-start.5) | collective-permute-done | bytes 69664 | tf_op jit(solution)/shard_map/ppermute | solution.py:33
  31.3 0.5 collective-permute-start.13
  31.8 0.6 collective-permute-start.9
  32.6 1.2 %collective-permute-start.8 = (bf16[16,2176]{1,0:T(8,128)(2,1)S(1)}, bf16[16,2176]{1,0:T(8,128)(2,1)S(1)}, u32[]{:S(2)}, u32[]{:S(2)}) collective-permute-start(bf16[16,2176]{1,0:T(8,128)(2,1)S(1)} %collective-permute-done.4.refs_1_), channel_id=1, source_target_pairs={{0,2},{2,0},{1,3},{3,1},{4,6},{6,4},{5,7},{7,5},{8,10},{10,8},{9,1... | collective-permute-start | bytes 208904 | tf_op jit(solution)/shard_map/ppermute | solution.py:33
  33.8 1.8 %collective-permute-done.6.refs_3_ = bf16[16,2176]{1,0:T(8,128)(2,1)S(1)} collective-permute-done((bf16[16,2176]{1,0:T(8,128)(2,1)S(1)}, bf16[16,2176]{1,0:T(8,128)(2,1)S(1)}, u32[]{:S(2)}, u32[]{:S(2)}) %collective-permute-start.6) | collective-permute-done | bytes 69664 | tf_op jit(solution)/shard_map/ppermute | solution.py:33
  35.6 0.6 collective-permute-start.10
  36.2 0.5 collective-permute-start.14
  36.8 1.4 %collective-permute-done.8.refs_5_ = bf16[16,2176]{1,0:T(8,128)(2,1)S(1)} collective-permute-done((bf16[16,2176]{1,0:T(8,128)(2,1)S(1)}, bf16[16,2176]{1,0:T(8,128)(2,1)S(1)}, u32[]{:S(2)}, u32[]{:S(2)}) %collective-permute-start.8) | collective-permute-done | bytes 69664 | tf_op jit(solution)/shard_map/ppermute | solution.py:33
  38.2 1.7 %collective-permute-done.10.refs_7_ = bf16[16,2176]{1,0:T(8,128)(2,1)S(1)} collective-permute-done((bf16[16,2176]{1,0:T(8,128)(2,1)S(1)}, bf16[16,2176]{1,0:T(8,128)(2,1)S(1)}, u32[]{:S(2)}, u32[]{:S(2)}) %collective-permute-start.10) | collective-permute-done | bytes 69664 | tf_op jit(solution)/shard_map/ppermute | solution.py:33
  39.9 1.2 %collective-permute-done.18.refs_15_ = bf16[16,2176]{1,0:T(8,128)(2,1)S(1)} collective-permute-done((bf16[16,2176]{1,0:T(8,128)(2,1)S(1)}, bf16[16,2176]{1,0:T(8,128)(2,1)S(1)}, u32[]{:S(2)}, u32[]{:S(2)}) %collective-permute-start.18) | collective-permute-done | bytes 69664 | tf_op jit(solution)/shard_map/ppermute | solution.py:33
  41.2 14.0 %experts.1 = (f32[128,2048]{1,0:T(8,128)S(1)}, bf16[128,2048]{1,0:T(8,128)(2,1)S(1)}) custom-call(bf16[16,2176]{1,0:T(8,128)(2,1)S(1)} %get-tuple-element.45.refs_0_, bf16[16,2176]{1,0:T(8,128)(2,1)S(1)} %collective-permute-done.4.refs_1_, bf16[16,2176]{1,0:T(8,128)(2,1)S(1)} %collective-permute-done.5.refs_2_, ...), custom_call_target="tpu_custom_call" | custom-call | bytes 40800000 | tf_op jit(solution)/shard_map/experts/pallas_call | solution.py:41
  55.4 1.8 %collective-permute-done.19.refs_1_ = bf16[128,2048]{1,0:T(8,128)(2,1)S(1)} collective-permute-done((bf16[128,2048]{1,0:T(8,128)(2,1)S(1)}, bf16[128,2048]{1,0:T(8,128)(2,1)S(1)}, u32[]{:S(2)}, u32[]{:S(2)}) %collective-permute-start.19) | collective-permute-done | bytes 524320 | tf_op jit(solution)/shard_map/ppermute | solution.py:33
  57.3 0.7 collective-permute-start.20
  57.9 1.4 %collective-permute-start.22 = (bf16[16,2048]{1,0:T(8,128)(2,1)S(1)}, bf16[16,2048]{1,0:T(8,128)(2,1)S(1)}, u32[]{:S(2)}, u32[]{:S(2)}) collective-permute-start(bf16[16,2048]{1,0:T(8,128)(2,1)S(1)} %get-tuple-element.54), channel_id=1, source_target_pairs={{0,2},{2,0},{1,3},{3,1},{4,6},{6,4},{5,7},{7,5},{8,10},{10,8},{9,1... | collective-permute-start | bytes 196616 | tf_op jit(solution)/shard_map/ppermute | solution.py:33
  59.3 0.6 collective-permute-start.24
  60.0 1.4 %collective-permute-start.26 = (bf16[16,2048]{1,0:T(8,128)(2,1)S(1)}, bf16[16,2048]{1,0:T(8,128)(2,1)S(1)}, u32[]{:S(2)}, u32[]{:S(2)}) collective-permute-start(bf16[16,2048]{1,0:T(8,128)(2,1)S(1)} %get-tuple-element.58), channel_id=1, source_target_pairs={{0,2},{2,0},{1,3},{3,1},{4,6},{6,4},{5,7},{7,5},{8,10},{10,8},{9,1... | collective-permute-start | bytes 196616 | tf_op jit(solution)/shard_map/ppermute | solution.py:33
  61.4 0.9 %collective-permute-done.20.refs_1_ = bf16[16,2048]{1,0:T(8,128)(2,1)S(1)} collective-permute-done((bf16[16,2048]{1,0:T(8,128)(2,1)S(1)}, bf16[16,2048]{1,0:T(8,128)(2,1)S(1)}, u32[]{:S(2)}, u32[]{:S(2)}) %collective-permute-start.20) | collective-permute-done | bytes 65568 | tf_op jit(solution)/shard_map/ppermute | solution.py:33
  62.3 1.0 %collective-permute-start.21 = (bf16[16,2048]{1,0:T(8,128)(2,1)S(1)}, bf16[16,2048]{1,0:T(8,128)(2,1)S(1)}, u32[]{:S(2)}, u32[]{:S(2)}) collective-permute-start(bf16[16,2048]{1,0:T(8,128)(2,1)S(1)} %sum_x1.1), channel_id=1, source_target_pairs={{0,4},{4,0},{8,12},{12,8},{1,5},{5,1},{9,13},{13,9},{2,6},{6,2},{1... | collective-permute-start | bytes 196616 | tf_op jit(solution)/shard_map/ppermute | solution.py:33
  63.7 0.8 %collective-permute-start.23 = (bf16[16,2048]{1,0:T(8,128)(2,1)S(1)}, bf16[16,2048]{1,0:T(8,128)(2,1)S(1)}, u32[]{:S(2)}, u32[]{:S(2)}) collective-permute-start(bf16[16,2048]{1,0:T(8,128)(2,1)S(1)} %sum_x2.1), channel_id=1, source_target_pairs={{0,8},{4,12},{8,0},{12,4},{1,9},{5,13},{9,1},{13,5},{2,10},{6,14},... | collective-permute-start | bytes 196616 | tf_op jit(solution)/shard_map/ppermute | solution.py:33
  65.0 2.2 %collective-permute-start.25 = (bf16[16,2048]{1,0:T(8,128)(2,1)S(1)}, bf16[16,2048]{1,0:T(8,128)(2,1)S(1)}, u32[]{:S(2)}, u32[]{:S(2)}) collective-permute-start(bf16[16,2048]{1,0:T(8,128)(2,1)S(1)} %sum_x3.1), channel_id=1, source_target_pairs={{0,12},{4,8},{8,4},{12,0},{1,13},{5,9},{9,5},{13,1},{2,14},{6,10},... | collective-permute-start | bytes 196616 | tf_op jit(solution)/shard_map/ppermute | solution.py:33
  67.2 3.0 %collective-permute-done.23.refs_2_ = bf16[16,2048]{1,0:T(8,128)(2,1)S(1)} collective-permute-done((bf16[16,2048]{1,0:T(8,128)(2,1)S(1)}, bf16[16,2048]{1,0:T(8,128)(2,1)S(1)}, u32[]{:S(2)}, u32[]{:S(2)}) %collective-permute-start.23) | collective-permute-done | bytes 65568 | tf_op jit(solution)/shard_map/ppermute | solution.py:33
  70.2 1.1 %collective-permute-done.25.refs_3_ = bf16[16,2048]{1,0:T(8,128)(2,1)S(1)} collective-permute-done((bf16[16,2048]{1,0:T(8,128)(2,1)S(1)}, bf16[16,2048]{1,0:T(8,128)(2,1)S(1)}, u32[]{:S(2)}, u32[]{:S(2)}) %collective-permute-start.25) | collective-permute-done | bytes 65568 | tf_op jit(solution)/shard_map/ppermute | solution.py:33
  71.2 0.7 total.1
  (35 shorter events, 1.8 us)
Async XLA Ops:
  0.8 16.8 %collective-permute-start.1 = (bf16[64,512]{1,0:T(8,128)(2,1)S(1)}, bf16[64,512]{1,0:T(8,128)(2,1)S(1)}, u32[]{:S(2)}, u32[]{:S(2)}) collective-permute-start(bf16[64,512]{1,0:T(8,128)(2,1)S(1)} %pad_maximum_fusion.refs_2_), channel_id=1, source_target_pairs={{0,4},{4,8},{8,12},{1,5},{5,9},{9,13},{2,6},{6,10},{10,14},{3,7},{... | collective-permute-start | bytes 196616 | tf_op jit(solution)/shard_map/ppermute | solution.py:365
  5.7 11.9 %collective-permute-start = (bf16[64,512]{1,0:T(8,128)(2,1)S(1)}, bf16[64,512]{1,0:T(8,128)(2,1)S(1)}, u32[]{:S(2)}, u32[]{:S(2)}) collective-permute-start(bf16[64,512]{1,0:T(8,128)(2,1)S(1)} %pad_maximum_fusion.refs_2_), channel_id=1, source_target_pairs={{0,8},{4,12},{1,9},{5,13},{2,10},{6,14},{3,11},{7,15},{16,24},{20,... | collective-permute-start | bytes 196616 | tf_op jit(solution)/shard_map/ppermute | solution.py:365
  19.0 1.4 %collective-permute-start.2 = (bf16[32,2048]{1,0:T(8,128)(2,1)S(1)}, bf16[32,2048]{1,0:T(8,128)(2,1)S(1)}, u32[]{:S(2)}, u32[]{:S(2)}) collective-permute-start(bf16[32,2048]{1,0:T(8,128)(2,1)S(1)} %get-tuple-element.40), channel_id=1, source_target_pairs={{0,1},{1,0},{2,3},{3,2},{4,5},{5,4},{6,7},{7,6},{8,9},{9,8},{10,11... | collective-permute-start | bytes 393224 | tf_op jit(solution)/shard_map/ppermute | solution.py:33
  20.5 5.0 %collective-permute-start.3 = (bf16[16,2048]{1,0:T(8,128)(2,1)S(1)}, bf16[16,2048]{1,0:T(8,128)(2,1)S(1)}, u32[]{:S(2)}, u32[]{:S(2)}) collective-permute-start(bf16[16,2048]{1,0:T(8,128)(2,1)S(1)} %get-tuple-element.42), channel_id=1, source_target_pairs={{0,2},{2,0},{1,3},{3,1},{4,6},{6,4},{5,7},{7,5},{8,10},{10,8},{9,1... | collective-permute-start | bytes 196616 | tf_op jit(solution)/shard_map/ppermute | solution.py:33
  25.6 5.7 %collective-permute-start.5 = (bf16[16,2176]{1,0:T(8,128)(2,1)S(1)}, bf16[16,2176]{1,0:T(8,128)(2,1)S(1)}, u32[]{:S(2)}, u32[]{:S(2)}) collective-permute-start(bf16[16,2176]{1,0:T(8,128)(2,1)S(1)} %get-tuple-element.45.refs_0_), channel_id=1, source_target_pairs={{0,8},{4,12},{8,0},{12,4},{1,9},{5,13},{9,1},{13,5},{2,10},{6,14},... | collective-permute-start | bytes 208904 | tf_op jit(solution)/shard_map/ppermute | solution.py:33
  25.7 5.6 %collective-permute-start.7 = (bf16[16,2176]{1,0:T(8,128)(2,1)S(1)}, bf16[16,2176]{1,0:T(8,128)(2,1)S(1)}, u32[]{:S(2)}, u32[]{:S(2)}) collective-permute-start(bf16[16,2176]{1,0:T(8,128)(2,1)S(1)} %get-tuple-element.45.refs_0_), channel_id=1, source_target_pairs={{0,2},{2,0},{1,3},{3,1},{4,6},{6,4},{5,7},{7,5},{8,10},{10,8},{9,1... | collective-permute-start | bytes 208904 | tf_op jit(solution)/shard_map/ppermute | solution.py:33
  26.6 5.2 %collective-permute-start.11 = (bf16[16,2176]{1,0:T(8,128)(2,1)S(1)}, bf16[16,2176]{1,0:T(8,128)(2,1)S(1)}, u32[]{:S(2)}, u32[]{:S(2)}) collective-permute-start(bf16[16,2176]{1,0:T(8,128)(2,1)S(1)} %get-tuple-element.45.refs_0_), channel_id=1, source_target_pairs={{0,1},{1,0},{2,3},{3,2},{4,5},{5,4},{6,7},{7,6},{8,9},{9,8},{10,11... | collective-permute-start | bytes 208904 | tf_op jit(solution)/shard_map/ppermute | solution.py:33
  26.6 6.0 %collective-permute-start.4 = (bf16[16,2176]{1,0:T(8,128)(2,1)S(1)}, bf16[16,2176]{1,0:T(8,128)(2,1)S(1)}, u32[]{:S(2)}, u32[]{:S(2)}) collective-permute-start(bf16[16,2176]{1,0:T(8,128)(2,1)S(1)} %get-tuple-element.45.refs_0_), channel_id=1, source_target_pairs={{0,4},{4,0},{8,12},{12,8},{1,5},{5,1},{9,13},{13,9},{2,6},{6,2},{1... | collective-permute-start | bytes 208904 | tf_op jit(solution)/shard_map/ppermute | solution.py:33
  31.3 4.3 %collective-permute-start.6 = (bf16[16,2176]{1,0:T(8,128)(2,1)S(1)}, bf16[16,2176]{1,0:T(8,128)(2,1)S(1)}, u32[]{:S(2)}, u32[]{:S(2)}) collective-permute-start(bf16[16,2176]{1,0:T(8,128)(2,1)S(1)} %collective-permute-done.5.refs_2_), channel_id=1, source_target_pairs={{0,4},{4,0},{8,12},{12,8},{1,5},{5,1},{9,13},{13,9},{2,6},{6,2},{1... | collective-permute-start | bytes 208904 | tf_op jit(solution)/shard_map/ppermute | solution.py:33
  31.3 4.9 %collective-permute-start.15 = (bf16[16,2176]{1,0:T(8,128)(2,1)S(1)}, bf16[16,2176]{1,0:T(8,128)(2,1)S(1)}, u32[]{:S(2)}, u32[]{:S(2)}) collective-permute-start(bf16[16,2176]{1,0:T(8,128)(2,1)S(1)} %collective-permute-done.7.refs_4_), channel_id=1, source_target_pairs={{0,1},{1,0},{2,3},{3,2},{4,5},{5,4},{6,7},{7,6},{8,9},{9,8},{10,11... | collective-permute-start | bytes 208904 | tf_op jit(solution)/shard_map/ppermute | solution.py:33
  31.3 4.9 %collective-permute-start.13 = (bf16[16,2176]{1,0:T(8,128)(2,1)S(1)}, bf16[16,2176]{1,0:T(8,128)(2,1)S(1)}, u32[]{:S(2)}, u32[]{:S(2)}) collective-permute-start(bf16[16,2176]{1,0:T(8,128)(2,1)S(1)} %collective-permute-done.5.refs_2_), channel_id=1, source_target_pairs={{0,1},{1,0},{2,3},{3,2},{4,5},{5,4},{6,7},{7,6},{8,9},{9,8},{10,11... | collective-permute-start | bytes 208904 | tf_op jit(solution)/shard_map/ppermute | solution.py:33
  31.8 4.9 %collective-permute-start.9 = (bf16[16,2176]{1,0:T(8,128)(2,1)S(1)}, bf16[16,2176]{1,0:T(8,128)(2,1)S(1)}, u32[]{:S(2)}, u32[]{:S(2)}) collective-permute-start(bf16[16,2176]{1,0:T(8,128)(2,1)S(1)} %collective-permute-done.5.refs_2_), channel_id=1, source_target_pairs={{0,2},{2,0},{1,3},{3,1},{4,6},{6,4},{5,7},{7,5},{8,10},{10,8},{9,1... | collective-permute-start | bytes 208904 | tf_op jit(solution)/shard_map/ppermute | solution.py:33
  32.6 5.6 %collective-permute-start.8 = (bf16[16,2176]{1,0:T(8,128)(2,1)S(1)}, bf16[16,2176]{1,0:T(8,128)(2,1)S(1)}, u32[]{:S(2)}, u32[]{:S(2)}) collective-permute-start(bf16[16,2176]{1,0:T(8,128)(2,1)S(1)} %collective-permute-done.4.refs_1_), channel_id=1, source_target_pairs={{0,2},{2,0},{1,3},{3,1},{4,6},{6,4},{5,7},{7,5},{8,10},{10,8},{9,1... | collective-permute-start | bytes 208904 | tf_op jit(solution)/shard_map/ppermute | solution.py:33
  35.6 4.3 %collective-permute-start.10 = (bf16[16,2176]{1,0:T(8,128)(2,1)S(1)}, bf16[16,2176]{1,0:T(8,128)(2,1)S(1)}, u32[]{:S(2)}, u32[]{:S(2)}) collective-permute-start(bf16[16,2176]{1,0:T(8,128)(2,1)S(1)} %collective-permute-done.6.refs_3_), channel_id=1, source_target_pairs={{0,2},{2,0},{1,3},{3,1},{4,6},{6,4},{5,7},{7,5},{8,10},{10,8},{9,1... | collective-permute-start | bytes 208904 | tf_op jit(solution)/shard_map/ppermute | solution.py:33
  36.2 3.7 %collective-permute-start.12 = (bf16[16,2176]{1,0:T(8,128)(2,1)S(1)}, bf16[16,2176]{1,0:T(8,128)(2,1)S(1)}, u32[]{:S(2)}, u32[]{:S(2)}) collective-permute-start(bf16[16,2176]{1,0:T(8,128)(2,1)S(1)} %collective-permute-done.4.refs_1_), channel_id=1, source_target_pairs={{0,1},{1,0},{2,3},{3,2},{4,5},{5,4},{6,7},{7,6},{8,9},{9,8},{10,11... | collective-permute-start | bytes 208904 | tf_op jit(solution)/shard_map/ppermute | solution.py:33
  36.2 3.7 %collective-permute-start.14 = (bf16[16,2176]{1,0:T(8,128)(2,1)S(1)}, bf16[16,2176]{1,0:T(8,128)(2,1)S(1)}, u32[]{:S(2)}, u32[]{:S(2)}) collective-permute-start(bf16[16,2176]{1,0:T(8,128)(2,1)S(1)} %collective-permute-done.6.refs_3_), channel_id=1, source_target_pairs={{0,1},{1,0},{2,3},{3,2},{4,5},{5,4},{6,7},{7,6},{8,9},{9,8},{10,11... | collective-permute-start | bytes 208904 | tf_op jit(solution)/shard_map/ppermute | solution.py:33
  36.7 3.2 %collective-permute-start.17 = (bf16[16,2176]{1,0:T(8,128)(2,1)S(1)}, bf16[16,2176]{1,0:T(8,128)(2,1)S(1)}, u32[]{:S(2)}, u32[]{:S(2)}) collective-permute-start(bf16[16,2176]{1,0:T(8,128)(2,1)S(1)} %collective-permute-done.9.refs_6_), channel_id=1, source_target_pairs={{0,1},{1,0},{2,3},{3,2},{4,5},{5,4},{6,7},{7,6},{8,9},{9,8},{10,11... | collective-permute-start | bytes 208904 | tf_op jit(solution)/shard_map/ppermute | solution.py:33
  38.2 1.7 %collective-permute-start.16 = (bf16[16,2176]{1,0:T(8,128)(2,1)S(1)}, bf16[16,2176]{1,0:T(8,128)(2,1)S(1)}, u32[]{:S(2)}, u32[]{:S(2)}) collective-permute-start(bf16[16,2176]{1,0:T(8,128)(2,1)S(1)} %collective-permute-done.8.refs_5_), channel_id=1, source_target_pairs={{0,1},{1,0},{2,3},{3,2},{4,5},{5,4},{6,7},{7,6},{8,9},{9,8},{10,11... | collective-permute-start | bytes 208904 | tf_op jit(solution)/shard_map/ppermute | solution.py:33
  39.9 1.3 %collective-permute-start.18 = (bf16[16,2176]{1,0:T(8,128)(2,1)S(1)}, bf16[16,2176]{1,0:T(8,128)(2,1)S(1)}, u32[]{:S(2)}, u32[]{:S(2)}) collective-permute-start(bf16[16,2176]{1,0:T(8,128)(2,1)S(1)} %collective-permute-done.10.refs_7_), channel_id=1, source_target_pairs={{0,1},{1,0},{2,3},{3,2},{4,5},{5,4},{6,7},{7,6},{8,9},{9,8},{10,11... | collective-permute-start | bytes 208904 | tf_op jit(solution)/shard_map/ppermute | solution.py:33
  55.2 2.0 %collective-permute-start.19 = (bf16[128,2048]{1,0:T(8,128)(2,1)S(1)}, bf16[128,2048]{1,0:T(8,128)(2,1)S(1)}, u32[]{:S(2)}, u32[]{:S(2)}) collective-permute-start(bf16[128,2048]{1,0:T(8,128)(2,1)S(1)} %get-tuple-element.50), channel_id=1, source_target_pairs={{0,1},{1,0},{2,3},{3,2},{4,5},{5,4},{6,7},{7,6},{8,9},{9,8},{10,11... | collective-permute-start | bytes 1572872 | tf_op jit(solution)/shard_map/ppermute | solution.py:33
  57.3 5.0 %collective-permute-start.20 = (bf16[16,2048]{1,0:T(8,128)(2,1)S(1)}, bf16[16,2048]{1,0:T(8,128)(2,1)S(1)}, u32[]{:S(2)}, u32[]{:S(2)}) collective-permute-start(bf16[16,2048]{1,0:T(8,128)(2,1)S(1)} %get-tuple-element.52), channel_id=1, source_target_pairs={{0,2},{2,0},{1,3},{3,1},{4,6},{6,4},{5,7},{7,5},{8,10},{10,8},{9,1... | collective-permute-start | bytes 196616 | tf_op jit(solution)/shard_map/ppermute | solution.py:33
  57.9 5.7 %collective-permute-start.22 = (bf16[16,2048]{1,0:T(8,128)(2,1)S(1)}, bf16[16,2048]{1,0:T(8,128)(2,1)S(1)}, u32[]{:S(2)}, u32[]{:S(2)}) collective-permute-start(bf16[16,2048]{1,0:T(8,128)(2,1)S(1)} %get-tuple-element.54), channel_id=1, source_target_pairs={{0,2},{2,0},{1,3},{3,1},{4,6},{6,4},{5,7},{7,5},{8,10},{10,8},{9,1... | collective-permute-start | bytes 196616 | tf_op jit(solution)/shard_map/ppermute | solution.py:33
  59.3 5.6 %collective-permute-start.24 = (bf16[16,2048]{1,0:T(8,128)(2,1)S(1)}, bf16[16,2048]{1,0:T(8,128)(2,1)S(1)}, u32[]{:S(2)}, u32[]{:S(2)}) collective-permute-start(bf16[16,2048]{1,0:T(8,128)(2,1)S(1)} %get-tuple-element.56), channel_id=1, source_target_pairs={{0,2},{2,0},{1,3},{3,1},{4,6},{6,4},{5,7},{7,5},{8,10},{10,8},{9,1... | collective-permute-start | bytes 196616 | tf_op jit(solution)/shard_map/ppermute | solution.py:33
  60.0 7.2 %collective-permute-start.26 = (bf16[16,2048]{1,0:T(8,128)(2,1)S(1)}, bf16[16,2048]{1,0:T(8,128)(2,1)S(1)}, u32[]{:S(2)}, u32[]{:S(2)}) collective-permute-start(bf16[16,2048]{1,0:T(8,128)(2,1)S(1)} %get-tuple-element.58), channel_id=1, source_target_pairs={{0,2},{2,0},{1,3},{3,1},{4,6},{6,4},{5,7},{7,5},{8,10},{10,8},{9,1... | collective-permute-start | bytes 196616 | tf_op jit(solution)/shard_map/ppermute | solution.py:33
  62.3 4.9 %collective-permute-start.21 = (bf16[16,2048]{1,0:T(8,128)(2,1)S(1)}, bf16[16,2048]{1,0:T(8,128)(2,1)S(1)}, u32[]{:S(2)}, u32[]{:S(2)}) collective-permute-start(bf16[16,2048]{1,0:T(8,128)(2,1)S(1)} %sum_x1.1), channel_id=1, source_target_pairs={{0,4},{4,0},{8,12},{12,8},{1,5},{5,1},{9,13},{13,9},{2,6},{6,2},{1... | collective-permute-start | bytes 196616 | tf_op jit(solution)/shard_map/ppermute | solution.py:33
  63.7 6.5 %collective-permute-start.23 = (bf16[16,2048]{1,0:T(8,128)(2,1)S(1)}, bf16[16,2048]{1,0:T(8,128)(2,1)S(1)}, u32[]{:S(2)}, u32[]{:S(2)}) collective-permute-start(bf16[16,2048]{1,0:T(8,128)(2,1)S(1)} %sum_x2.1), channel_id=1, source_target_pairs={{0,8},{4,12},{8,0},{12,4},{1,9},{5,13},{9,1},{13,5},{2,10},{6,14},... | collective-permute-start | bytes 196616 | tf_op jit(solution)/shard_map/ppermute | solution.py:33
  65.0 6.2 %collective-permute-start.25 = (bf16[16,2048]{1,0:T(8,128)(2,1)S(1)}, bf16[16,2048]{1,0:T(8,128)(2,1)S(1)}, u32[]{:S(2)}, u32[]{:S(2)}) collective-permute-start(bf16[16,2048]{1,0:T(8,128)(2,1)S(1)} %sum_x3.1), channel_id=1, source_target_pairs={{0,12},{4,8},{8,4},{12,0},{1,13},{5,9},{9,5},{13,1},{2,14},{6,10},... | collective-permute-start | bytes 196616 | tf_op jit(solution)/shard_map/ppermute | solution.py:33

commit v10 on v5

--- a/solution.py
+++ b/solution.py
@@ -337,7 +337,7 @@
     )
     back = -(-(sec_count * block // 2 - 1) // block)
     pieces = [
-        lax.ppermute(kv, "sec", [(i, i + k) for i in range(sec_count - k)])
+        lax.ppermute(kv, "sec", [(i, (i + k) % sec_count) for i in range(sec_count)])
         for k in range(back, 0, -1)
     ] + [kv]
 
@@ -398,7 +398,9 @@
     )
 
     groups = min(4, sec_count)
-    near = [normed] + [xor_swap(normed, "sec", k) for k in range(1, sec_count)]
+    near = {k: xor_swap(normed, "sec", k) if k else normed for k in range(0, sec_count, 2)}
+    near.update({k + 1: xor_swap(near[k], "sec", 1) for k in list(near) if k + 1 < sec_count})
+    near = [near[k] for k in range(sec_count)]
     per_group = sec_count // groups
     near = [
         jnp.concatenate(near[g * per_group : (g + 1) * per_group], axis=0)

time: 72 us -> 67.4 us (0.936)
  starting transfers between devices: 26.3 us -> 22.4 us
    ppermute x2, starting transfers between devices: 9.43 us -> 5.67 us  [per_device(): lax.ppermute(kv, 'sec', [(i, (i + k) % sec_count) for i in range(sec_coun...]
  transfers between devices with their start and end apart: 27 -> 27, of which waited for: 14 -> 13; matrix products, arithmetic and copies ran while one was open for 0% -> 0% of each run, Pallas kernels for 15% -> 16%
where the time goes in v10:
time: 67.4 us; the launch traced here: 67.2 us
  Pallas kernels  25.7 us (38%)
  starting transfers between devices  22.4 us (33%)
  waiting for transfers between devices  18.1 us (27%)
  local copies, waits for them, and re-layouts  0.78 us (1%)
    pallas_call x11, Pallas kernels, call(): pl.pallas_call(kernel, out_shape=out_shape, in_specs=[s for s, _ in args]...  25.7 us
    ppermute x25, waiting for transfers between devices, xor_swap(): return lax.ppermute(x, axis, [(i, i ^ k) for i in range(n)])  18.1 us
    ppermute x25, starting transfers between devices, xor_swap(): return lax.ppermute(x, axis, [(i, i ^ k) for i in range(n)])  16.8 us
    ppermute x2, starting transfers between devices, per_device(): lax.ppermute(kv, 'sec', [(i, (i + k) % sec_count) for i in range(sec_coun...  5.67 us
  transfers between devices with their start and end apart: 27, of which 13 were waited for; matrix products, arithmetic and copies ran while one was open for 0% of the time, Pallas kernels for 16%

profile of v10, /device:TPU:0, one launch (start us, length us, event | category | flops | bytes accessed | tf_op | source)
XLA Modules:
  0.0 67.2 jit_solution(16699138937424976896)
XLA Ops:
  0.0 0.8 %constant_dynamic-slice_fusion = (bf16[64,256]{1,0:T(8,128)(2,1)S(1)}, bf16[64,256]{1,0:T(8,128)(2,1)S(1)}) fusion(bf16[64,512]{1,0:T(8,128)(2,1)} %param.14, s32[]{:T(128)S(6)} %select_n.10, bf16[64,512]{1,0:T(8,128)(2,1)} %param.13), kind=kLoop, calls=%fused_computation.1 | loop fusion | bytes 131076 | tf_op jit(solution)/shard_map/dynamic_slice | solution.py:336
  0.8 3.1 %collective-permute-start.1 = (bf16[64,512]{1,0:T(8,128)(2,1)S(1)}, bf16[64,512]{1,0:T(8,128)(2,1)S(1)}, u32[]{:S(2)}, u32[]{:S(2)}) collective-permute-start(bf16[64,512]{1,0:T(8,128)(2,1)S(1)} %pad_maximum_fusion.refs_2_), channel_id=1, source_target_pairs={{0,4},{4,8},{8,12},{12,0},{1,5},{5,9},{9,13},{13,1},{2,6},{6,10},{... | collective-permute-start | bytes 196616 | tf_op jit(solution)/shard_map/ppermute | solution.py:340
  3.9 2.6 %collective-permute-start = (bf16[64,512]{1,0:T(8,128)(2,1)S(1)}, bf16[64,512]{1,0:T(8,128)(2,1)S(1)}, u32[]{:S(2)}, u32[]{:S(2)}) collective-permute-start(bf16[64,512]{1,0:T(8,128)(2,1)S(1)} %pad_maximum_fusion.refs_2_), channel_id=1, source_target_pairs={{0,8},{4,12},{8,0},{12,4},{1,9},{5,13},{9,1},{13,5},{2,10},{6,14},... | collective-permute-start | bytes 196616 | tf_op jit(solution)/shard_map/ppermute | solution.py:340
  6.5 7.3 %prepare.1 = (bf16[64,1024]{1,0:T(8,128)(2,1)S(1)}, bf16[1024,2048]{1,0:T(8,128)(2,1)S(1)}, f32[1,2048]{1,0:T(1,128)S(1)}, f32[64,192]{1,0:T(8,128)S(1)}, bf16[6...) custom-call(s32[8]{0:T(128)} %lengths_hbm.1, ...), custom_call_target="tpu_custom_call" | custom-call | bytes 20400000 | tf_op jit(solution)/shard_map/prepare/pallas_call | solution.py:41
  13.8 1.4 %attention.1 = (f32[32,2048]{1,0:T(8,128)S(1)}, bf16[32,2048]{1,0:T(8,128)(2,1)S(1)}) custom-call(bf16[64,1024]{1,0:T(8,128)(2,1)S(1)} %get-tuple-element.35.q_ref, f32[64,192]{1,0:T(8,128)S(1)} %get-tuple-element.36.mask_ref, bf16[64,64]{1,0:T(8,128)(2,1)S(1)} %get-tuple-element.37.order_ref, bf16[64,512]{1,0:T(8,128)(2,1)S(1)} %collective-permute-done.refs_0_, ...), custom_call_target="tpu_custom_call" | custom-call | bytes 8160000 | tf_op jit(solution)/shard_map/attention/pallas_call | solution.py:41
  15.3 1.3 %collective-permute-done.2.refs_1_ = bf16[32,2048]{1,0:T(8,128)(2,1)S(1)} collective-permute-done((bf16[32,2048]{1,0:T(8,128)(2,1)S(1)}, bf16[32,2048]{1,0:T(8,128)(2,1)S(1)}, u32[]{:S(2)}, u32[]{:S(2)}) %collective-permute-start.2) | collective-permute-done | bytes 131104 | tf_op jit(solution)/shard_map/ppermute | solution.py:33
  16.7 1.6 %collective-permute-start.3 = (bf16[16,2048]{1,0:T(8,128)(2,1)S(1)}, bf16[16,2048]{1,0:T(8,128)(2,1)S(1)}, u32[]{:S(2)}, u32[]{:S(2)}) collective-permute-start(bf16[16,2048]{1,0:T(8,128)(2,1)S(1)} %get-tuple-element.42), channel_id=1, source_target_pairs={{0,2},{2,0},{1,3},{3,1},{4,6},{6,4},{5,7},{7,5},{8,10},{10,8},{9,1... | collective-permute-start | bytes 196616 | tf_op jit(solution)/shard_map/ppermute | solution.py:33
  18.3 3.4 %load_up.1 = (bf16[2048,2048]{1,0:T(8,128)(2,1)S(1)}, f32[8,128]{1,0:T(8,128)S(1)}) custom-call(bf16[2048,4096]{1,0:T(8,128)(2,1)} %bitcast.6, f32[16,2048]{1,0:T(8,128)S(1)} %get-tuple-element.41.refs_0_), custom_call_target="tpu_custom_call" | custom-call | bytes 8388607 | tf_op jit(solution)/shard_map/load_up/pallas_call | solution.py:41
  22.2 0.9 %collective-permute-start.7 = (bf16[16,2176]{1,0:T(8,128)(2,1)S(1)}, bf16[16,2176]{1,0:T(8,128)(2,1)S(1)}, u32[]{:S(2)}, u32[]{:S(2)}) collective-permute-start(bf16[16,2176]{1,0:T(8,128)(2,1)S(1)} %get-tuple-element.45.refs_0_), channel_id=1, source_target_pairs={{0,2},{2,0},{1,3},{3,1},{4,6},{6,4},{5,7},{7,5},{8,10},{10,8},{9,1... | collective-permute-start | bytes 208904 | tf_op jit(solution)/shard_map/ppermute | solution.py:33
  23.1 1.6 %collective-permute-start.4 = (bf16[16,2176]{1,0:T(8,128)(2,1)S(1)}, bf16[16,2176]{1,0:T(8,128)(2,1)S(1)}, u32[]{:S(2)}, u32[]{:S(2)}) collective-permute-start(bf16[16,2176]{1,0:T(8,128)(2,1)S(1)} %get-tuple-element.45.refs_0_), channel_id=1, source_target_pairs={{0,4},{4,0},{8,12},{12,8},{1,5},{5,1},{9,13},{13,9},{2,6},{6,2},{1... | collective-permute-start | bytes 208904 | tf_op jit(solution)/shard_map/ppermute | solution.py:33
  24.6 3.3 %collective-permute-done.5.refs_2_ = bf16[16,2176]{1,0:T(8,128)(2,1)S(1)} collective-permute-done((bf16[16,2176]{1,0:T(8,128)(2,1)S(1)}, bf16[16,2176]{1,0:T(8,128)(2,1)S(1)}, u32[]{:S(2)}, u32[]{:S(2)}) %collective-permute-start.5) | collective-permute-done | bytes 69664 | tf_op jit(solution)/shard_map/ppermute | solution.py:33
  28.0 0.5 collective-permute-start.13
  28.5 0.5 collective-permute-start.9
  29.0 1.6 %collective-permute-start.8 = (bf16[16,2176]{1,0:T(8,128)(2,1)S(1)}, bf16[16,2176]{1,0:T(8,128)(2,1)S(1)}, u32[]{:S(2)}, u32[]{:S(2)}) collective-permute-start(bf16[16,2176]{1,0:T(8,128)(2,1)S(1)} %collective-permute-done.4.refs_1_), channel_id=1, source_target_pairs={{0,2},{2,0},{1,3},{3,1},{4,6},{6,4},{5,7},{7,5},{8,10},{10,8},{9,1... | collective-permute-start | bytes 208904 | tf_op jit(solution)/shard_map/ppermute | solution.py:33
  30.5 1.8 %collective-permute-done.6.refs_3_ = bf16[16,2176]{1,0:T(8,128)(2,1)S(1)} collective-permute-done((bf16[16,2176]{1,0:T(8,128)(2,1)S(1)}, bf16[16,2176]{1,0:T(8,128)(2,1)S(1)}, u32[]{:S(2)}, u32[]{:S(2)}) %collective-permute-start.6) | collective-permute-done | bytes 69664 | tf_op jit(solution)/shard_map/ppermute | solution.py:33
  32.8 0.5 collective-permute-start.14
  33.4 1.5 %collective-permute-done.8.refs_5_ = bf16[16,2176]{1,0:T(8,128)(2,1)S(1)} collective-permute-done((bf16[16,2176]{1,0:T(8,128)(2,1)S(1)}, bf16[16,2176]{1,0:T(8,128)(2,1)S(1)}, u32[]{:S(2)}, u32[]{:S(2)}) %collective-permute-start.8) | collective-permute-done | bytes 69664 | tf_op jit(solution)/shard_map/ppermute | solution.py:33
  34.9 1.7 %collective-permute-done.10.refs_7_ = bf16[16,2176]{1,0:T(8,128)(2,1)S(1)} collective-permute-done((bf16[16,2176]{1,0:T(8,128)(2,1)S(1)}, bf16[16,2176]{1,0:T(8,128)(2,1)S(1)}, u32[]{:S(2)}, u32[]{:S(2)}) %collective-permute-start.10) | collective-permute-done | bytes 69664 | tf_op jit(solution)/shard_map/ppermute | solution.py:33
  36.6 1.2 %collective-permute-done.18.refs_15_ = bf16[16,2176]{1,0:T(8,128)(2,1)S(1)} collective-permute-done((bf16[16,2176]{1,0:T(8,128)(2,1)S(1)}, bf16[16,2176]{1,0:T(8,128)(2,1)S(1)}, u32[]{:S(2)}, u32[]{:S(2)}) %collective-permute-start.18) | collective-permute-done | bytes 69664 | tf_op jit(solution)/shard_map/ppermute | solution.py:33
  37.9 12.6 %experts.1 = (f32[128,2048]{1,0:T(8,128)S(1)}, bf16[128,2048]{1,0:T(8,128)(2,1)S(1)}) custom-call(bf16[16,2176]{1,0:T(8,128)(2,1)S(1)} %get-tuple-element.45.refs_0_, bf16[16,2176]{1,0:T(8,128)(2,1)S(1)} %collective-permute-done.4.refs_1_, bf16[16,2176]{1,0:T(8,128)(2,1)S(1)} %collective-permute-done.5.refs_2_, ...), custom_call_target="tpu_custom_call" | custom-call | bytes 40800000 | tf_op jit(solution)/shard_map/experts/pallas_call | solution.py:41
  50.6 1.7 %collective-permute-done.19.refs_1_ = bf16[128,2048]{1,0:T(8,128)(2,1)S(1)} collective-permute-done((bf16[128,2048]{1,0:T(8,128)(2,1)S(1)}, bf16[128,2048]{1,0:T(8,128)(2,1)S(1)}, u32[]{:S(2)}, u32[]{:S(2)}) %collective-permute-start.19) | collective-permute-done | bytes 524320 | tf_op jit(solution)/shard_map/ppermute | solution.py:33
  52.5 0.5 collective-permute-start.20
  53.0 1.6 %collective-permute-start.22 = (bf16[16,2048]{1,0:T(8,128)(2,1)S(1)}, bf16[16,2048]{1,0:T(8,128)(2,1)S(1)}, u32[]{:S(2)}, u32[]{:S(2)}) collective-permute-start(bf16[16,2048]{1,0:T(8,128)(2,1)S(1)} %get-tuple-element.54), channel_id=1, source_target_pairs={{0,2},{2,0},{1,3},{3,1},{4,6},{6,4},{5,7},{7,5},{8,10},{10,8},{9,1... | collective-permute-start | bytes 196616 | tf_op jit(solution)/shard_map/ppermute | solution.py:33
  54.6 0.5 collective-permute-start.24
  55.1 1.6 %collective-permute-start.26 = (bf16[16,2048]{1,0:T(8,128)(2,1)S(1)}, bf16[16,2048]{1,0:T(8,128)(2,1)S(1)}, u32[]{:S(2)}, u32[]{:S(2)}) collective-permute-start(bf16[16,2048]{1,0:T(8,128)(2,1)S(1)} %get-tuple-element.58), channel_id=1, source_target_pairs={{0,2},{2,0},{1,3},{3,1},{4,6},{6,4},{5,7},{7,5},{8,10},{10,8},{9,1... | collective-permute-start | bytes 196616 | tf_op jit(solution)/shard_map/ppermute | solution.py:33
  56.6 0.9 %collective-permute-done.20.refs_1_ = bf16[16,2048]{1,0:T(8,128)(2,1)S(1)} collective-permute-done((bf16[16,2048]{1,0:T(8,128)(2,1)S(1)}, bf16[16,2048]{1,0:T(8,128)(2,1)S(1)}, u32[]{:S(2)}, u32[]{:S(2)}) %collective-permute-start.20) | collective-permute-done | bytes 65568 | tf_op jit(solution)/shard_map/ppermute | solution.py:33
  57.5 1.1 %collective-permute-start.21 = (bf16[16,2048]{1,0:T(8,128)(2,1)S(1)}, bf16[16,2048]{1,0:T(8,128)(2,1)S(1)}, u32[]{:S(2)}, u32[]{:S(2)}) collective-permute-start(bf16[16,2048]{1,0:T(8,128)(2,1)S(1)} %sum_x1.1), channel_id=1, source_target_pairs={{0,4},{4,0},{8,12},{12,8},{1,5},{5,1},{9,13},{13,9},{2,6},{6,2},{1... | collective-permute-start | bytes 196616 | tf_op jit(solution)/shard_map/ppermute | solution.py:33
  58.9 1.2 %collective-permute-start.23 = (bf16[16,2048]{1,0:T(8,128)(2,1)S(1)}, bf16[16,2048]{1,0:T(8,128)(2,1)S(1)}, u32[]{:S(2)}, u32[]{:S(2)}) collective-permute-start(bf16[16,2048]{1,0:T(8,128)(2,1)S(1)} %sum_x2.1), channel_id=1, source_target_pairs={{0,8},{4,12},{8,0},{12,4},{1,9},{5,13},{9,1},{13,5},{2,10},{6,14},... | collective-permute-start | bytes 196616 | tf_op jit(solution)/shard_map/ppermute | solution.py:33
  60.2 2.2 %collective-permute-start.25 = (bf16[16,2048]{1,0:T(8,128)(2,1)S(1)}, bf16[16,2048]{1,0:T(8,128)(2,1)S(1)}, u32[]{:S(2)}, u32[]{:S(2)}) collective-permute-start(bf16[16,2048]{1,0:T(8,128)(2,1)S(1)} %sum_x3.1), channel_id=1, source_target_pairs={{0,12},{4,8},{8,4},{12,0},{1,13},{5,9},{9,5},{13,1},{2,14},{6,10},... | collective-permute-start | bytes 196616 | tf_op jit(solution)/shard_map/ppermute | solution.py:33
  62.4 3.0 %collective-permute-done.23.refs_2_ = bf16[16,2048]{1,0:T(8,128)(2,1)S(1)} collective-permute-done((bf16[16,2048]{1,0:T(8,128)(2,1)S(1)}, bf16[16,2048]{1,0:T(8,128)(2,1)S(1)}, u32[]{:S(2)}, u32[]{:S(2)}) %collective-permute-start.23) | collective-permute-done | bytes 65568 | tf_op jit(solution)/shard_map/ppermute | solution.py:33
  65.4 1.0 %collective-permute-done.25.refs_3_ = bf16[16,2048]{1,0:T(8,128)(2,1)S(1)} collective-permute-done((bf16[16,2048]{1,0:T(8,128)(2,1)S(1)}, bf16[16,2048]{1,0:T(8,128)(2,1)S(1)}, u32[]{:S(2)}, u32[]{:S(2)}) %collective-permute-start.25) | collective-permute-done | bytes 65568 | tf_op jit(solution)/shard_map/ppermute | solution.py:33
  66.5 0.7 %total.1 = bf16[16,2048]{1,0:T(8,128)(2,1)} custom-call(f32[16,2048]{1,0:T(8,128)S(1)} %get-tuple-element.44.refs_0_, bf16[16,2048]{1,0:T(8,128)(2,1)S(1)} %collective-permute-done.21.refs_1_, bf16[16,2048]{1,0:T(8,128)(2,1)S(1)} %collective-permute-done.23.refs_2_, bf16[16,2048]{1,0:T(8,128)(2,1)S(1)} %collective-permute-done.25.refs_3_, ...), custom_call_target="tpu_custom_call" | custom-call | bytes 680000 | tf_op jit(solution)/shard_map/total/pallas_call | solution.py:41
  (35 shorter events, 2.1 us)
Async XLA Ops:
  0.8 13.0 %collective-permute-start.1 = (bf16[64,512]{1,0:T(8,128)(2,1)S(1)}, bf16[64,512]{1,0:T(8,128)(2,1)S(1)}, u32[]{:S(2)}, u32[]{:S(2)}) collective-permute-start(bf16[64,512]{1,0:T(8,128)(2,1)S(1)} %pad_maximum_fusion.refs_2_), channel_id=1, source_target_pairs={{0,4},{4,8},{8,12},{12,0},{1,5},{5,9},{9,13},{13,1},{2,6},{6,10},{... | collective-permute-start | bytes 196616 | tf_op jit(solution)/shard_map/ppermute | solution.py:340
  3.9 9.9 %collective-permute-start = (bf16[64,512]{1,0:T(8,128)(2,1)S(1)}, bf16[64,512]{1,0:T(8,128)(2,1)S(1)}, u32[]{:S(2)}, u32[]{:S(2)}) collective-permute-start(bf16[64,512]{1,0:T(8,128)(2,1)S(1)} %pad_maximum_fusion.refs_2_), channel_id=1, source_target_pairs={{0,8},{4,12},{8,0},{12,4},{1,9},{5,13},{9,1},{13,5},{2,10},{6,14},... | collective-permute-start | bytes 196616 | tf_op jit(solution)/shard_map/ppermute | solution.py:340
  15.3 1.4 %collective-permute-start.2 = (bf16[32,2048]{1,0:T(8,128)(2,1)S(1)}, bf16[32,2048]{1,0:T(8,128)(2,1)S(1)}, u32[]{:S(2)}, u32[]{:S(2)}) collective-permute-start(bf16[32,2048]{1,0:T(8,128)(2,1)S(1)} %get-tuple-element.40), channel_id=1, source_target_pairs={{0,1},{1,0},{2,3},{3,2},{4,5},{5,4},{6,7},{7,6},{8,9},{9,8},{10,11... | collective-permute-start | bytes 393224 | tf_op jit(solution)/shard_map/ppermute | solution.py:33
  16.7 5.0 %collective-permute-start.3 = (bf16[16,2048]{1,0:T(8,128)(2,1)S(1)}, bf16[16,2048]{1,0:T(8,128)(2,1)S(1)}, u32[]{:S(2)}, u32[]{:S(2)}) collective-permute-start(bf16[16,2048]{1,0:T(8,128)(2,1)S(1)} %get-tuple-element.42), channel_id=1, source_target_pairs={{0,2},{2,0},{1,3},{3,1},{4,6},{6,4},{5,7},{7,5},{8,10},{10,8},{9,1... | collective-permute-start | bytes 196616 | tf_op jit(solution)/shard_map/ppermute | solution.py:33
  21.8 6.2 %collective-permute-start.5 = (bf16[16,2176]{1,0:T(8,128)(2,1)S(1)}, bf16[16,2176]{1,0:T(8,128)(2,1)S(1)}, u32[]{:S(2)}, u32[]{:S(2)}) collective-permute-start(bf16[16,2176]{1,0:T(8,128)(2,1)S(1)} %get-tuple-element.45.refs_0_), channel_id=1, source_target_pairs={{0,8},{4,12},{8,0},{12,4},{1,9},{5,13},{9,1},{13,5},{2,10},{6,14},... | collective-permute-start | bytes 208904 | tf_op jit(solution)/shard_map/ppermute | solution.py:33
  22.2 5.8 %collective-permute-start.7 = (bf16[16,2176]{1,0:T(8,128)(2,1)S(1)}, bf16[16,2176]{1,0:T(8,128)(2,1)S(1)}, u32[]{:S(2)}, u32[]{:S(2)}) collective-permute-start(bf16[16,2176]{1,0:T(8,128)(2,1)S(1)} %get-tuple-element.45.refs_0_), channel_id=1, source_target_pairs={{0,2},{2,0},{1,3},{3,1},{4,6},{6,4},{5,7},{7,5},{8,10},{10,8},{9,1... | collective-permute-start | bytes 208904 | tf_op jit(solution)/shard_map/ppermute | solution.py:33
  23.1 5.4 %collective-permute-start.11 = (bf16[16,2176]{1,0:T(8,128)(2,1)S(1)}, bf16[16,2176]{1,0:T(8,128)(2,1)S(1)}, u32[]{:S(2)}, u32[]{:S(2)}) collective-permute-start(bf16[16,2176]{1,0:T(8,128)(2,1)S(1)} %get-tuple-element.45.refs_0_), channel_id=1, source_target_pairs={{0,1},{1,0},{2,3},{3,2},{4,5},{5,4},{6,7},{7,6},{8,9},{9,8},{10,11... | collective-permute-start | bytes 208904 | tf_op jit(solution)/shard_map/ppermute | solution.py:33
  23.1 5.9 %collective-permute-start.4 = (bf16[16,2176]{1,0:T(8,128)(2,1)S(1)}, bf16[16,2176]{1,0:T(8,128)(2,1)S(1)}, u32[]{:S(2)}, u32[]{:S(2)}) collective-permute-start(bf16[16,2176]{1,0:T(8,128)(2,1)S(1)} %get-tuple-element.45.refs_0_), channel_id=1, source_target_pairs={{0,4},{4,0},{8,12},{12,8},{1,5},{5,1},{9,13},{13,9},{2,6},{6,2},{1... | collective-permute-start | bytes 208904 | tf_op jit(solution)/shard_map/ppermute | solution.py:33
  28.0 4.3 %collective-permute-start.6 = (bf16[16,2176]{1,0:T(8,128)(2,1)S(1)}, bf16[16,2176]{1,0:T(8,128)(2,1)S(1)}, u32[]{:S(2)}, u32[]{:S(2)}) collective-permute-start(bf16[16,2176]{1,0:T(8,128)(2,1)S(1)} %collective-permute-done.5.refs_2_), channel_id=1, source_target_pairs={{0,4},{4,0},{8,12},{12,8},{1,5},{5,1},{9,13},{13,9},{2,6},{6,2},{1... | collective-permute-start | bytes 208904 | tf_op jit(solution)/shard_map/ppermute | solution.py:33
  28.0 4.8 %collective-permute-start.15 = (bf16[16,2176]{1,0:T(8,128)(2,1)S(1)}, bf16[16,2176]{1,0:T(8,128)(2,1)S(1)}, u32[]{:S(2)}, u32[]{:S(2)}) collective-permute-start(bf16[16,2176]{1,0:T(8,128)(2,1)S(1)} %collective-permute-done.7.refs_4_), channel_id=1, source_target_pairs={{0,1},{1,0},{2,3},{3,2},{4,5},{5,4},{6,7},{7,6},{8,9},{9,8},{10,11... | collective-permute-start | bytes 208904 | tf_op jit(solution)/shard_map/ppermute | solution.py:33
  28.0 4.8 %collective-permute-start.13 = (bf16[16,2176]{1,0:T(8,128)(2,1)S(1)}, bf16[16,2176]{1,0:T(8,128)(2,1)S(1)}, u32[]{:S(2)}, u32[]{:S(2)}) collective-permute-start(bf16[16,2176]{1,0:T(8,128)(2,1)S(1)} %collective-permute-done.5.refs_2_), channel_id=1, source_target_pairs={{0,1},{1,0},{2,3},{3,2},{4,5},{5,4},{6,7},{7,6},{8,9},{9,8},{10,11... | collective-permute-start | bytes 208904 | tf_op jit(solution)/shard_map/ppermute | solution.py:33
  28.5 4.9 %collective-permute-start.9 = (bf16[16,2176]{1,0:T(8,128)(2,1)S(1)}, bf16[16,2176]{1,0:T(8,128)(2,1)S(1)}, u32[]{:S(2)}, u32[]{:S(2)}) collective-permute-start(bf16[16,2176]{1,0:T(8,128)(2,1)S(1)} %collective-permute-done.5.refs_2_), channel_id=1, source_target_pairs={{0,2},{2,0},{1,3},{3,1},{4,6},{6,4},{5,7},{7,5},{8,10},{10,8},{9,1... | collective-permute-start | bytes 208904 | tf_op jit(solution)/shard_map/ppermute | solution.py:33
  29.0 5.9 %collective-permute-start.8 = (bf16[16,2176]{1,0:T(8,128)(2,1)S(1)}, bf16[16,2176]{1,0:T(8,128)(2,1)S(1)}, u32[]{:S(2)}, u32[]{:S(2)}) collective-permute-start(bf16[16,2176]{1,0:T(8,128)(2,1)S(1)} %collective-permute-done.4.refs_1_), channel_id=1, source_target_pairs={{0,2},{2,0},{1,3},{3,1},{4,6},{6,4},{5,7},{7,5},{8,10},{10,8},{9,1... | collective-permute-start | bytes 208904 | tf_op jit(solution)/shard_map/ppermute | solution.py:33
  32.3 4.3 %collective-permute-start.10 = (bf16[16,2176]{1,0:T(8,128)(2,1)S(1)}, bf16[16,2176]{1,0:T(8,128)(2,1)S(1)}, u32[]{:S(2)}, u32[]{:S(2)}) collective-permute-start(bf16[16,2176]{1,0:T(8,128)(2,1)S(1)} %collective-permute-done.6.refs_3_), channel_id=1, source_target_pairs={{0,2},{2,0},{1,3},{3,1},{4,6},{6,4},{5,7},{7,5},{8,10},{10,8},{9,1... | collective-permute-start | bytes 208904 | tf_op jit(solution)/shard_map/ppermute | solution.py:33
  32.8 3.8 %collective-permute-start.12 = (bf16[16,2176]{1,0:T(8,128)(2,1)S(1)}, bf16[16,2176]{1,0:T(8,128)(2,1)S(1)}, u32[]{:S(2)}, u32[]{:S(2)}) collective-permute-start(bf16[16,2176]{1,0:T(8,128)(2,1)S(1)} %collective-permute-done.4.refs_1_), channel_id=1, source_target_pairs={{0,1},{1,0},{2,3},{3,2},{4,5},{5,4},{6,7},{7,6},{8,9},{9,8},{10,11... | collective-permute-start | bytes 208904 | tf_op jit(solution)/shard_map/ppermute | solution.py:33
  32.8 3.8 %collective-permute-start.14 = (bf16[16,2176]{1,0:T(8,128)(2,1)S(1)}, bf16[16,2176]{1,0:T(8,128)(2,1)S(1)}, u32[]{:S(2)}, u32[]{:S(2)}) collective-permute-start(bf16[16,2176]{1,0:T(8,128)(2,1)S(1)} %collective-permute-done.6.refs_3_), channel_id=1, source_target_pairs={{0,1},{1,0},{2,3},{3,2},{4,5},{5,4},{6,7},{7,6},{8,9},{9,8},{10,11... | collective-permute-start | bytes 208904 | tf_op jit(solution)/shard_map/ppermute | solution.py:33
  33.4 3.2 %collective-permute-start.17 = (bf16[16,2176]{1,0:T(8,128)(2,1)S(1)}, bf16[16,2176]{1,0:T(8,128)(2,1)S(1)}, u32[]{:S(2)}, u32[]{:S(2)}) collective-permute-start(bf16[16,2176]{1,0:T(8,128)(2,1)S(1)} %collective-permute-done.9.refs_6_), channel_id=1, source_target_pairs={{0,1},{1,0},{2,3},{3,2},{4,5},{5,4},{6,7},{7,6},{8,9},{9,8},{10,11... | collective-permute-start | bytes 208904 | tf_op jit(solution)/shard_map/ppermute | solution.py:33
  34.9 1.7 %collective-permute-start.16 = (bf16[16,2176]{1,0:T(8,128)(2,1)S(1)}, bf16[16,2176]{1,0:T(8,128)(2,1)S(1)}, u32[]{:S(2)}, u32[]{:S(2)}) collective-permute-start(bf16[16,2176]{1,0:T(8,128)(2,1)S(1)} %collective-permute-done.8.refs_5_), channel_id=1, source_target_pairs={{0,1},{1,0},{2,3},{3,2},{4,5},{5,4},{6,7},{7,6},{8,9},{9,8},{10,11... | collective-permute-start | bytes 208904 | tf_op jit(solution)/shard_map/ppermute | solution.py:33
  36.6 1.3 %collective-permute-start.18 = (bf16[16,2176]{1,0:T(8,128)(2,1)S(1)}, bf16[16,2176]{1,0:T(8,128)(2,1)S(1)}, u32[]{:S(2)}, u32[]{:S(2)}) collective-permute-start(bf16[16,2176]{1,0:T(8,128)(2,1)S(1)} %collective-permute-done.10.refs_7_), channel_id=1, source_target_pairs={{0,1},{1,0},{2,3},{3,2},{4,5},{5,4},{6,7},{7,6},{8,9},{9,8},{10,11... | collective-permute-start | bytes 208904 | tf_op jit(solution)/shard_map/ppermute | solution.py:33
  50.4 2.0 %collective-permute-start.19 = (bf16[128,2048]{1,0:T(8,128)(2,1)S(1)}, bf16[128,2048]{1,0:T(8,128)(2,1)S(1)}, u32[]{:S(2)}, u32[]{:S(2)}) collective-permute-start(bf16[128,2048]{1,0:T(8,128)(2,1)S(1)} %get-tuple-element.50), channel_id=1, source_target_pairs={{0,1},{1,0},{2,3},{3,2},{4,5},{5,4},{6,7},{7,6},{8,9},{9,8},{10,11... | collective-permute-start | bytes 1572872 | tf_op jit(solution)/shard_map/ppermute | solution.py:33
  52.5 5.0 %collective-permute-start.20 = (bf16[16,2048]{1,0:T(8,128)(2,1)S(1)}, bf16[16,2048]{1,0:T(8,128)(2,1)S(1)}, u32[]{:S(2)}, u32[]{:S(2)}) collective-permute-start(bf16[16,2048]{1,0:T(8,128)(2,1)S(1)} %get-tuple-element.52), channel_id=1, source_target_pairs={{0,2},{2,0},{1,3},{3,1},{4,6},{6,4},{5,7},{7,5},{8,10},{10,8},{9,1... | collective-permute-start | bytes 196616 | tf_op jit(solution)/shard_map/ppermute | solution.py:33
  53.0 5.9 %collective-permute-start.22 = (bf16[16,2048]{1,0:T(8,128)(2,1)S(1)}, bf16[16,2048]{1,0:T(8,128)(2,1)S(1)}, u32[]{:S(2)}, u32[]{:S(2)}) collective-permute-start(bf16[16,2048]{1,0:T(8,128)(2,1)S(1)} %get-tuple-element.54), channel_id=1, source_target_pairs={{0,2},{2,0},{1,3},{3,1},{4,6},{6,4},{5,7},{7,5},{8,10},{10,8},{9,1... | collective-permute-start | bytes 196616 | tf_op jit(solution)/shard_map/ppermute | solution.py:33
  54.6 5.6 %collective-permute-start.24 = (bf16[16,2048]{1,0:T(8,128)(2,1)S(1)}, bf16[16,2048]{1,0:T(8,128)(2,1)S(1)}, u32[]{:S(2)}, u32[]{:S(2)}) collective-permute-start(bf16[16,2048]{1,0:T(8,128)(2,1)S(1)} %get-tuple-element.56), channel_id=1, source_target_pairs={{0,2},{2,0},{1,3},{3,1},{4,6},{6,4},{5,7},{7,5},{8,10},{10,8},{9,1... | collective-permute-start | bytes 196616 | tf_op jit(solution)/shard_map/ppermute | solution.py:33
  55.1 7.4 %collective-permute-start.26 = (bf16[16,2048]{1,0:T(8,128)(2,1)S(1)}, bf16[16,2048]{1,0:T(8,128)(2,1)S(1)}, u32[]{:S(2)}, u32[]{:S(2)}) collective-permute-start(bf16[16,2048]{1,0:T(8,128)(2,1)S(1)} %get-tuple-element.58), channel_id=1, source_target_pairs={{0,2},{2,0},{1,3},{3,1},{4,6},{6,4},{5,7},{7,5},{8,10},{10,8},{9,1... | collective-permute-start | bytes 196616 | tf_op jit(solution)/shard_map/ppermute | solution.py:33
  57.5 4.9 %collective-permute-start.21 = (bf16[16,2048]{1,0:T(8,128)(2,1)S(1)}, bf16[16,2048]{1,0:T(8,128)(2,1)S(1)}, u32[]{:S(2)}, u32[]{:S(2)}) collective-permute-start(bf16[16,2048]{1,0:T(8,128)(2,1)S(1)} %sum_x1.1), channel_id=1, source_target_pairs={{0,4},{4,0},{8,12},{12,8},{1,5},{5,1},{9,13},{13,9},{2,6},{6,2},{1... | collective-permute-start | bytes 196616 | tf_op jit(solution)/shard_map/ppermute | solution.py:33
  58.9 6.5 %collective-permute-start.23 = (bf16[16,2048]{1,0:T(8,128)(2,1)S(1)}, bf16[16,2048]{1,0:T(8,128)(2,1)S(1)}, u32[]{:S(2)}, u32[]{:S(2)}) collective-permute-start(bf16[16,2048]{1,0:T(8,128)(2,1)S(1)} %sum_x2.1), channel_id=1, source_target_pairs={{0,8},{4,12},{8,0},{12,4},{1,9},{5,13},{9,1},{13,5},{2,10},{6,14},... | collective-permute-start | bytes 196616 | tf_op jit(solution)/shard_map/ppermute | solution.py:33
  60.2 6.2 %collective-permute-start.25 = (bf16[16,2048]{1,0:T(8,128)(2,1)S(1)}, bf16[16,2048]{1,0:T(8,128)(2,1)S(1)}, u32[]{:S(2)}, u32[]{:S(2)}) collective-permute-start(bf16[16,2048]{1,0:T(8,128)(2,1)S(1)} %sum_x3.1), channel_id=1, source_target_pairs={{0,12},{4,8},{8,4},{12,0},{1,13},{5,9},{9,5},{13,1},{2,14},{6,10},... | collective-permute-start | bytes 196616 | tf_op jit(solution)/shard_map/ppermute | solution.py:33

commit v11 on v10

--- a/solution.py
+++ b/solution.py
@@ -222,28 +222,71 @@
     normed_ref[:, width:] = info_ref[...]
 
 
-def experts_kernel(experts, capacity, tile, halves, n_rows, n_gate, n_up, *refs):
+class Stream:
+    def __init__(self, groups, sem, window):
+        self.copies, self.last, self.window = [], {}, window
+        for name, pairs in groups:
+            for source, target in pairs:
+                at = len(self.copies)
+                self.copies.append(pltpu.make_async_copy(source, target, sem.at[at]))
+            self.last[name] = len(self.copies)
+        self.started = self.ended = 0
+        self.limit = len(self.copies)
+        self.clock = 0.0
+
+    def fill(self):
+        while self.started < self.limit and self.started - self.ended < self.window:
+            self.copies[self.started].start()
+            self.started += 1
+
+    def end_one(self):
+        self.copies[self.ended].wait()
+        self.ended += 1
+        self.fill()
+
+    def need(self, name):
+        while self.ended < self.last[name]:
+            self.end_one()
+
+    def step(self, cost):
+        self.clock += cost
+        while self.ended < self.started and self.ended + 2 <= self.clock:
+            self.end_one()
+
+
+def experts_kernel(experts, capacity, tile, halves, n_rows, *refs):
     rows_in = refs[:n_rows]
-    gate_refs = list(refs[n_rows : n_rows + n_gate])
-    up_refs = list(refs[n_rows + n_gate : n_rows + n_gate + n_up])
-    refs = refs[n_rows + n_gate + n_up :]
-    up_hbm, down_hbm, keep_ref, send_ref, rows_ref, pick_ref, packed_ref, hidden_ref = refs[:8]
-    up_late = list(refs[8 : 8 + experts - n_up])
-    down_ref, up_sem, down_sem = refs[8 + experts - n_up :]
+    gate_first, up_first, gate_hbm, up_hbm, down_hbm, keep_ref, send_ref = refs[
+        n_rows : n_rows + 7
+    ]
+    rows_ref, pick_ref, packed_ref, hidden_ref, half_ref, gate_ref, up_ref, down_ref, sem = refs[
+        n_rows + 7 :
+    ]
     per_expert, width = down_hbm.shape[0] // experts, down_hbm.shape[1]
-    up_copies = [
-        pltpu.make_async_copy(a, b, up_sem.at[i])
-        for i, (a, b) in enumerate(columns(up_hbm, up_late, n_up))
-    ]
-    up_refs += up_late
-    down_copies = [
-        pltpu.make_async_copy(
-            down_hbm.at[pl.ds(x * per_expert, per_expert)], down_ref, down_sem.at[x]
-        )
-        for x in range(experts)
-    ]
-    for c in down_copies[:1] + up_copies:
-        c.start()
+    column = min(512, width)
+    cuts = 4
+
+    def quarters(source, target, x, columns):
+        rows = target.shape[0] // cuts
+        pairs = []
+        for i in range(cuts):
+            to = pl.ds(i * rows, rows)
+            if columns:
+                part = source.at[to, pl.ds(x * per_expert, per_expert)]
+            else:
+                part = source.at[pl.ds(x * per_expert + i * rows, rows)]
+            pairs.append((part, target.at[to]))
+        return pairs
+
+    groups = []
+    for x in range(experts):
+        if x:
+            groups.append((("gate", x), quarters(gate_hbm, gate_ref.at[x - 1], x, True)))
+            groups.append((("up", x), quarters(up_hbm, up_ref.at[x - 1], x, True)))
+        groups.append((("down", x), quarters(down_hbm, down_ref, x, False)))
+    stream = Stream(groups, sem, 3)
+    stream.limit = stream.last["up", 1] if experts > 1 else stream.limit
+    stream.fill()
     count = 0
     for r in rows_in:
         rows_ref[count : count + r.shape[0], :] = r[...]
@@ -279,23 +322,28 @@
         )
     for x in range(experts):
         mine = slice(x * capacity, (x + 1) * capacity)
-        if x >= n_up:
-            up_copies[x - n_up].wait()
-        gate_ref, up_ref = gate_refs[x], up_refs[x]
-
+        if x:
+            stream.need(("gate", x))
         for s in range(0, per_expert, tile):
             cut = slice(s, s + tile)
-            gate = dot(packed_ref[mine, :], gate_ref[:, cut])
-            up = dot(packed_ref[mine, :], up_ref[:, cut])
+            stream.step(0.7)
+            gate = dot(packed_ref[mine, :], gate_ref[x - 1, :, cut] if x else gate_first[:, cut])
             half = 0.5 * gate
-            hidden_ref[mine, cut] = ((half + half * jnp.tanh(half)) * up).astype(jnp.bfloat16)
-        down_copies[x].wait()
-
+            half_ref[:, cut] = half + half * jnp.tanh(half)
+        if x:
+            stream.need(("up", x))
+        for s in range(0, per_expert, tile):
+            cut = slice(s, s + tile)
+            stream.step(0.7)
+            up = dot(packed_ref[mine, :], up_ref[x - 1, :, cut] if x else up_first[:, cut])
+            hidden_ref[mine, cut] = (half_ref[:, cut] * up).astype(jnp.bfloat16)
+        stream.need(("down", x))
         for c in range(0, width, column):
+            stream.step(0.7)
             out = dot(hidden_ref[mine, :], down_ref[:, c : c + column])
             packed_ref[mine, c : c + column] = (out * shares[x]).astype(jnp.bfloat16)
-        if x + 1 < experts:
-            down_copies[x + 1].start()
+        stream.limit = stream.last["up", x + 2] if x + 2 < experts else len(stream.copies)
+        stream.fill()
     kept = keep_ref.shape[0]
 
     for c in range(0, width, column):
@@ -355,7 +403,7 @@
             sds((own_rows, width), f32),
             sds((own_rows, LANES), bf16),
         ]
-        + [sds((width, per_expert), bf16)] * experts,
+        + [sds((width, per_expert), bf16)],
         [
             (HBM, a)
             for a in (
@@ -368,11 +416,11 @@
             pltpu.VMEM((2, block), jnp.int32),
             pltpu.VMEM((2, block), jnp.int32),
             pltpu.VMEM(residual.shape, bf16),
-            pltpu.SemaphoreType.DMA((7 + experts,)),
+            pltpu.SemaphoreType.DMA((8,)),
         ],
         vmem=6,
         name="prepare",
-        cost_us=6.0,
+        cost_us=4.0,
     )
     half = block // pp_count
     keep, send = call(
@@ -419,20 +467,22 @@
     tile = min(512, down.shape[0] // experts)
     kept = count // pp_count
     keep, send = call(
-        functools.partial(experts_kernel, experts, capacity, tile, halves, len(rows), experts, 1),
+        functools.partial(experts_kernel, experts, capacity, tile, halves, len(rows)),
         [sds((kept, width), f32), sds((count - kept, width), bf16)],
-        [(VMEM, a) for a in (*rows, *gate_v, *up_v)] + [(HBM, w_up[0]), (HBM, down)],
+        [(VMEM, a) for a in (*rows, *gate_v, *up_v)]
+        + [(HBM, a) for a in (w_gate[0], w_up[0], down)],
         scratch=[
             pltpu.VMEM((count, width + LANES), bf16),
             pltpu.VMEM((experts * capacity, count), bf16),
             pltpu.VMEM((experts * capacity, width), bf16),
             pltpu.VMEM((experts * capacity, down.shape[0] // experts), bf16),
-            *[pltpu.VMEM((width, per_expert), bf16)] * (experts - 1),
+            pltpu.VMEM((capacity, per_expert), f32),
+            pltpu.VMEM((max(1, experts - 1), width, per_expert), bf16),
+            pltpu.VMEM((max(1, experts - 1), width, per_expert), bf16),
             pltpu.VMEM((per_expert, width), bf16),
-            pltpu.SemaphoreType.DMA((experts,)),
-            pltpu.SemaphoreType.DMA((experts,)),
+            pltpu.SemaphoreType.DMA((4 * (3 * experts - 2),)),
         ],
-        vmem=24,
+        vmem=33,
         name="experts",
         cost_us=12.0,
     )

time: 67.4 us -> 66.4 us (0.985)
  Pallas kernels: 25.7 us -> 24.6 us
    pallas_call x11, Pallas kernels: 25.7 us -> 24.6 us  [call(): pl.pallas_call(kernel, out_shape=out_shape, in_specs=[s for s, _ in args]...]
  transfers between devices with their start and end apart: 27 -> 27, of which waited for: 13 -> 13; matrix products, arithmetic and copies ran while one was open for 0% -> 0% of each run, Pallas kernels for 16% -> 13%
where the time goes in v11:
time: 66.4 us; the launch traced here: 66.1 us
  Pallas kernels  24.6 us (37%)
  starting transfers between devices  22.5 us (34%)
  waiting for transfers between devices  18.1 us (27%)
  local copies, waits for them, and re-layouts  0.78 us (1%)
    pallas_call x11, Pallas kernels, call(): pl.pallas_call(kernel, out_shape=out_shape, in_specs=[s for s, _ in args]...  24.6 us
    ppermute x25, waiting for transfers between devices, xor_swap(): return lax.ppermute(x, axis, [(i, i ^ k) for i in range(n)])  18.1 us
    ppermute x25, starting transfers between devices, xor_swap(): return lax.ppermute(x, axis, [(i, i ^ k) for i in range(n)])  16.8 us
    ppermute x2, starting transfers between devices, per_device(): lax.ppermute(kv, 'sec', [(i, (i + k) % sec_count) for i in range(sec_coun...  5.67 us
  transfers between devices with their start and end apart: 27, of which 13 were waited for; matrix products, arithmetic and copies ran while one was open for 0% of the time, Pallas kernels for 13%

profile of v11, /device:TPU:0, one launch (start us, length us, event | category | flops | bytes accessed | tf_op | source)
XLA Modules:
  0.0 66.1 jit_solution(16813399925381233366)
XLA Ops:
  0.0 0.8 %constant_dynamic-slice_fusion = (bf16[64,256]{1,0:T(8,128)(2,1)S(1)}, bf16[64,256]{1,0:T(8,128)(2,1)S(1)}) fusion(bf16[64,512]{1,0:T(8,128)(2,1)} %param.14, s32[]{:T(128)S(6)} %select_n.10, bf16[64,512]{1,0:T(8,128)(2,1)} %param.13), kind=kLoop, calls=%fused_computation.1 | loop fusion | bytes 131076 | tf_op jit(solution)/shard_map/dynamic_slice | solution.py:384
  0.8 3.1 %collective-permute-start.1 = (bf16[64,512]{1,0:T(8,128)(2,1)S(1)}, bf16[64,512]{1,0:T(8,128)(2,1)S(1)}, u32[]{:S(2)}, u32[]{:S(2)}) collective-permute-start(bf16[64,512]{1,0:T(8,128)(2,1)S(1)} %pad_maximum_fusion.refs_2_), channel_id=1, source_target_pairs={{0,4},{4,8},{8,12},{12,0},{1,5},{5,9},{9,13},{13,1},{2,6},{6,10},{... | collective-permute-start | bytes 196616 | tf_op jit(solution)/shard_map/ppermute | solution.py:388
  3.9 2.6 %collective-permute-start = (bf16[64,512]{1,0:T(8,128)(2,1)S(1)}, bf16[64,512]{1,0:T(8,128)(2,1)S(1)}, u32[]{:S(2)}, u32[]{:S(2)}) collective-permute-start(bf16[64,512]{1,0:T(8,128)(2,1)S(1)} %pad_maximum_fusion.refs_2_), channel_id=1, source_target_pairs={{0,8},{4,12},{8,0},{12,4},{1,9},{5,13},{9,1},{13,5},{2,10},{6,14},... | collective-permute-start | bytes 196616 | tf_op jit(solution)/shard_map/ppermute | solution.py:388
  6.5 4.9 %prepare.1 = (bf16[64,1024]{1,0:T(8,128)(2,1)S(1)}, bf16[1024,2048]{1,0:T(8,128)(2,1)S(1)}, f32[1,2048]{1,0:T(1,128)S(1)}, f32[64,192]{1,0:T(8,128)S(1)}, bf16[6...) custom-call(s32[8]{0:T(128)} %lengths_hbm.1, ...), custom_call_target="tpu_custom_call" | custom-call | bytes 13600000 | tf_op jit(solution)/shard_map/prepare/pallas_call | solution.py:41
  11.4 1.4 %attention.1 = (f32[32,2048]{1,0:T(8,128)S(1)}, bf16[32,2048]{1,0:T(8,128)(2,1)S(1)}) custom-call(bf16[64,1024]{1,0:T(8,128)(2,1)S(1)} %get-tuple-element.34.q_ref, f32[64,192]{1,0:T(8,128)S(1)} %get-tuple-element.35.mask_ref, bf16[64,64]{1,0:T(8,128)(2,1)S(1)} %get-tuple-element.36.order_ref, bf16[64,512]{1,0:T(8,128)(2,1)S(1)} %collective-permute-done.refs_0_, ...), custom_call_target="tpu_custom_call" | custom-call | bytes 8160000 | tf_op jit(solution)/shard_map/attention/pallas_call | solution.py:41
  12.9 1.3 %collective-permute-done.2.refs_1_ = bf16[32,2048]{1,0:T(8,128)(2,1)S(1)} collective-permute-done((bf16[32,2048]{1,0:T(8,128)(2,1)S(1)}, bf16[32,2048]{1,0:T(8,128)(2,1)S(1)}, u32[]{:S(2)}, u32[]{:S(2)}) %collective-permute-start.2) | collective-permute-done | bytes 131104 | tf_op jit(solution)/shard_map/ppermute | solution.py:33
  14.3 1.6 %collective-permute-start.3 = (bf16[16,2048]{1,0:T(8,128)(2,1)S(1)}, bf16[16,2048]{1,0:T(8,128)(2,1)S(1)}, u32[]{:S(2)}, u32[]{:S(2)}) collective-permute-start(bf16[16,2048]{1,0:T(8,128)(2,1)S(1)} %get-tuple-element.41), channel_id=1, source_target_pairs={{0,2},{2,0},{1,3},{3,1},{4,6},{6,4},{5,7},{7,5},{8,10},{10,8},{9,1... | collective-permute-start | bytes 196616 | tf_op jit(solution)/shard_map/ppermute | solution.py:33
  15.9 3.4 %load_up.1 = (bf16[2048,2048]{1,0:T(8,128)(2,1)S(1)}, f32[8,128]{1,0:T(8,128)S(1)}) custom-call(bf16[2048,4096]{1,0:T(8,128)(2,1)} %bitcast.8, f32[16,2048]{1,0:T(8,128)S(1)} %get-tuple-element.40.refs_0_), custom_call_target="tpu_custom_call" | custom-call | bytes 8388607 | tf_op jit(solution)/shard_map/load_up/pallas_call | solution.py:41
  19.8 0.9 %collective-permute-start.7 = (bf16[16,2176]{1,0:T(8,128)(2,1)S(1)}, bf16[16,2176]{1,0:T(8,128)(2,1)S(1)}, u32[]{:S(2)}, u32[]{:S(2)}) collective-permute-start(bf16[16,2176]{1,0:T(8,128)(2,1)S(1)} %get-tuple-element.44.refs_0_), channel_id=1, source_target_pairs={{0,2},{2,0},{1,3},{3,1},{4,6},{6,4},{5,7},{7,5},{8,10},{10,8},{9,1... | collective-permute-start | bytes 208904 | tf_op jit(solution)/shard_map/ppermute | solution.py:33
  20.7 1.6 %collective-permute-start.4 = (bf16[16,2176]{1,0:T(8,128)(2,1)S(1)}, bf16[16,2176]{1,0:T(8,128)(2,1)S(1)}, u32[]{:S(2)}, u32[]{:S(2)}) collective-permute-start(bf16[16,2176]{1,0:T(8,128)(2,1)S(1)} %get-tuple-element.44.refs_0_), channel_id=1, source_target_pairs={{0,4},{4,0},{8,12},{12,8},{1,5},{5,1},{9,13},{13,9},{2,6},{6,2},{1... | collective-permute-start | bytes 208904 | tf_op jit(solution)/shard_map/ppermute | solution.py:33
  22.3 3.3 %collective-permute-done.5.refs_2_ = bf16[16,2176]{1,0:T(8,128)(2,1)S(1)} collective-permute-done((bf16[16,2176]{1,0:T(8,128)(2,1)S(1)}, bf16[16,2176]{1,0:T(8,128)(2,1)S(1)}, u32[]{:S(2)}, u32[]{:S(2)}) %collective-permute-start.5) | collective-permute-done | bytes 69664 | tf_op jit(solution)/shard_map/ppermute | solution.py:33
  25.6 0.5 collective-permute-start.13
  26.1 0.5 collective-permute-start.9
  26.6 1.6 %collective-permute-start.8 = (bf16[16,2176]{1,0:T(8,128)(2,1)S(1)}, bf16[16,2176]{1,0:T(8,128)(2,1)S(1)}, u32[]{:S(2)}, u32[]{:S(2)}) collective-permute-start(bf16[16,2176]{1,0:T(8,128)(2,1)S(1)} %collective-permute-done.4.refs_1_), channel_id=1, source_target_pairs={{0,2},{2,0},{1,3},{3,1},{4,6},{6,4},{5,7},{7,5},{8,10},{10,8},{9,1... | collective-permute-start | bytes 208904 | tf_op jit(solution)/shard_map/ppermute | solution.py:33
  28.1 1.8 %collective-permute-done.6.refs_3_ = bf16[16,2176]{1,0:T(8,128)(2,1)S(1)} collective-permute-done((bf16[16,2176]{1,0:T(8,128)(2,1)S(1)}, bf16[16,2176]{1,0:T(8,128)(2,1)S(1)}, u32[]{:S(2)}, u32[]{:S(2)}) %collective-permute-start.6) | collective-permute-done | bytes 69664 | tf_op jit(solution)/shard_map/ppermute | solution.py:33
  30.4 0.5 collective-permute-start.14
  31.0 1.5 %collective-permute-done.8.refs_5_ = bf16[16,2176]{1,0:T(8,128)(2,1)S(1)} collective-permute-done((bf16[16,2176]{1,0:T(8,128)(2,1)S(1)}, bf16[16,2176]{1,0:T(8,128)(2,1)S(1)}, u32[]{:S(2)}, u32[]{:S(2)}) %collective-permute-start.8) | collective-permute-done | bytes 69664 | tf_op jit(solution)/shard_map/ppermute | solution.py:33
  32.5 1.7 %collective-permute-done.10.refs_7_ = bf16[16,2176]{1,0:T(8,128)(2,1)S(1)} collective-permute-done((bf16[16,2176]{1,0:T(8,128)(2,1)S(1)}, bf16[16,2176]{1,0:T(8,128)(2,1)S(1)}, u32[]{:S(2)}, u32[]{:S(2)}) %collective-permute-start.10) | collective-permute-done | bytes 69664 | tf_op jit(solution)/shard_map/ppermute | solution.py:33
  34.2 1.2 %collective-permute-done.18.refs_15_ = bf16[16,2176]{1,0:T(8,128)(2,1)S(1)} collective-permute-done((bf16[16,2176]{1,0:T(8,128)(2,1)S(1)}, bf16[16,2176]{1,0:T(8,128)(2,1)S(1)}, u32[]{:S(2)}, u32[]{:S(2)}) %collective-permute-start.18) | collective-permute-done | bytes 69664 | tf_op jit(solution)/shard_map/ppermute | solution.py:33
  35.5 13.9 %experts.1 = (f32[128,2048]{1,0:T(8,128)S(1)}, bf16[128,2048]{1,0:T(8,128)(2,1)S(1)}) custom-call(bf16[16,2176]{1,0:T(8,128)(2,1)S(1)} %get-tuple-element.44.refs_0_, bf16[16,2176]{1,0:T(8,128)(2,1)S(1)} %collective-permute-done.4.refs_1_, bf16[16,2176]{1,0:T(8,128)(2,1)S(1)} %collective-permute-done.5.refs_2_, ...), custom_call_target="tpu_custom_call" | custom-call | bytes 40800000 | tf_op jit(solution)/shard_map/experts/pallas_call | solution.py:41
  49.6 1.8 %collective-permute-done.19.refs_1_ = bf16[128,2048]{1,0:T(8,128)(2,1)S(1)} collective-permute-done((bf16[128,2048]{1,0:T(8,128)(2,1)S(1)}, bf16[128,2048]{1,0:T(8,128)(2,1)S(1)}, u32[]{:S(2)}, u32[]{:S(2)}) %collective-permute-start.19) | collective-permute-done | bytes 524320 | tf_op jit(solution)/shard_map/ppermute | solution.py:33
  51.5 0.5 collective-permute-start.20
  52.0 1.6 %collective-permute-start.22 = (bf16[16,2048]{1,0:T(8,128)(2,1)S(1)}, bf16[16,2048]{1,0:T(8,128)(2,1)S(1)}, u32[]{:S(2)}, u32[]{:S(2)}) collective-permute-start(bf16[16,2048]{1,0:T(8,128)(2,1)S(1)} %get-tuple-element.52), channel_id=1, source_target_pairs={{0,2},{2,0},{1,3},{3,1},{4,6},{6,4},{5,7},{7,5},{8,10},{10,8},{9,1... | collective-permute-start | bytes 196616 | tf_op jit(solution)/shard_map/ppermute | solution.py:33
  53.6 0.5 collective-permute-start.24
  54.0 1.6 %collective-permute-start.26 = (bf16[16,2048]{1,0:T(8,128)(2,1)S(1)}, bf16[16,2048]{1,0:T(8,128)(2,1)S(1)}, u32[]{:S(2)}, u32[]{:S(2)}) collective-permute-start(bf16[16,2048]{1,0:T(8,128)(2,1)S(1)} %get-tuple-element.56), channel_id=1, source_target_pairs={{0,2},{2,0},{1,3},{3,1},{4,6},{6,4},{5,7},{7,5},{8,10},{10,8},{9,1... | collective-permute-start | bytes 196616 | tf_op jit(solution)/shard_map/ppermute | solution.py:33
  55.6 0.9 %collective-permute-done.20.refs_1_ = bf16[16,2048]{1,0:T(8,128)(2,1)S(1)} collective-permute-done((bf16[16,2048]{1,0:T(8,128)(2,1)S(1)}, bf16[16,2048]{1,0:T(8,128)(2,1)S(1)}, u32[]{:S(2)}, u32[]{:S(2)}) %collective-permute-start.20) | collective-permute-done | bytes 65568 | tf_op jit(solution)/shard_map/ppermute | solution.py:33
  56.5 1.1 %collective-permute-start.21 = (bf16[16,2048]{1,0:T(8,128)(2,1)S(1)}, bf16[16,2048]{1,0:T(8,128)(2,1)S(1)}, u32[]{:S(2)}, u32[]{:S(2)}) collective-permute-start(bf16[16,2048]{1,0:T(8,128)(2,1)S(1)} %sum_x1.1), channel_id=1, source_target_pairs={{0,4},{4,0},{8,12},{12,8},{1,5},{5,1},{9,13},{13,9},{2,6},{6,2},{1... | collective-permute-start | bytes 196616 | tf_op jit(solution)/shard_map/ppermute | solution.py:33
  57.9 1.2 %collective-permute-start.23 = (bf16[16,2048]{1,0:T(8,128)(2,1)S(1)}, bf16[16,2048]{1,0:T(8,128)(2,1)S(1)}, u32[]{:S(2)}, u32[]{:S(2)}) collective-permute-start(bf16[16,2048]{1,0:T(8,128)(2,1)S(1)} %sum_x2.1), channel_id=1, source_target_pairs={{0,8},{4,12},{8,0},{12,4},{1,9},{5,13},{9,1},{13,5},{2,10},{6,14},... | collective-permute-start | bytes 196616 | tf_op jit(solution)/shard_map/ppermute | solution.py:33
  59.2 2.2 %collective-permute-start.25 = (bf16[16,2048]{1,0:T(8,128)(2,1)S(1)}, bf16[16,2048]{1,0:T(8,128)(2,1)S(1)}, u32[]{:S(2)}, u32[]{:S(2)}) collective-permute-start(bf16[16,2048]{1,0:T(8,128)(2,1)S(1)} %sum_x3.1), channel_id=1, source_target_pairs={{0,12},{4,8},{8,4},{12,0},{1,13},{5,9},{9,5},{13,1},{2,14},{6,10},... | collective-permute-start | bytes 196616 | tf_op jit(solution)/shard_map/ppermute | solution.py:33
  61.4 3.0 %collective-permute-done.23.refs_2_ = bf16[16,2048]{1,0:T(8,128)(2,1)S(1)} collective-permute-done((bf16[16,2048]{1,0:T(8,128)(2,1)S(1)}, bf16[16,2048]{1,0:T(8,128)(2,1)S(1)}, u32[]{:S(2)}, u32[]{:S(2)}) %collective-permute-start.23) | collective-permute-done | bytes 65568 | tf_op jit(solution)/shard_map/ppermute | solution.py:33
  64.4 1.0 %collective-permute-done.25.refs_3_ = bf16[16,2048]{1,0:T(8,128)(2,1)S(1)} collective-permute-done((bf16[16,2048]{1,0:T(8,128)(2,1)S(1)}, bf16[16,2048]{1,0:T(8,128)(2,1)S(1)}, u32[]{:S(2)}, u32[]{:S(2)}) %collective-permute-start.25) | collective-permute-done | bytes 65568 | tf_op jit(solution)/shard_map/ppermute | solution.py:33
  65.5 0.7 %total.1 = bf16[16,2048]{1,0:T(8,128)(2,1)} custom-call(f32[16,2048]{1,0:T(8,128)S(1)} %get-tuple-element.43.refs_0_, bf16[16,2048]{1,0:T(8,128)(2,1)S(1)} %collective-permute-done.21.refs_1_, bf16[16,2048]{1,0:T(8,128)(2,1)S(1)} %collective-permute-done.23.refs_2_, bf16[16,2048]{1,0:T(8,128)(2,1)S(1)} %collective-permute-done.25.refs_3_, ...), custom_call_target="tpu_custom_call" | custom-call | bytes 680000 | tf_op jit(solution)/shard_map/total/pallas_call | solution.py:41
  (35 shorter events, 2.1 us)
Async XLA Ops:
  0.8 10.6 %collective-permute-start.1 = (bf16[64,512]{1,0:T(8,128)(2,1)S(1)}, bf16[64,512]{1,0:T(8,128)(2,1)S(1)}, u32[]{:S(2)}, u32[]{:S(2)}) collective-permute-start(bf16[64,512]{1,0:T(8,128)(2,1)S(1)} %pad_maximum_fusion.refs_2_), channel_id=1, source_target_pairs={{0,4},{4,8},{8,12},{12,0},{1,5},{5,9},{9,13},{13,1},{2,6},{6,10},{... | collective-permute-start | bytes 196616 | tf_op jit(solution)/shard_map/ppermute | solution.py:388
  3.9 7.5 %collective-permute-start = (bf16[64,512]{1,0:T(8,128)(2,1)S(1)}, bf16[64,512]{1,0:T(8,128)(2,1)S(1)}, u32[]{:S(2)}, u32[]{:S(2)}) collective-permute-start(bf16[64,512]{1,0:T(8,128)(2,1)S(1)} %pad_maximum_fusion.refs_2_), channel_id=1, source_target_pairs={{0,8},{4,12},{8,0},{12,4},{1,9},{5,13},{9,1},{13,5},{2,10},{6,14},... | collective-permute-start | bytes 196616 | tf_op jit(solution)/shard_map/ppermute | solution.py:388
  12.9 1.4 %collective-permute-start.2 = (bf16[32,2048]{1,0:T(8,128)(2,1)S(1)}, bf16[32,2048]{1,0:T(8,128)(2,1)S(1)}, u32[]{:S(2)}, u32[]{:S(2)}) collective-permute-start(bf16[32,2048]{1,0:T(8,128)(2,1)S(1)} %get-tuple-element.39), channel_id=1, source_target_pairs={{0,1},{1,0},{2,3},{3,2},{4,5},{5,4},{6,7},{7,6},{8,9},{9,8},{10,11... | collective-permute-start | bytes 393224 | tf_op jit(solution)/shard_map/ppermute | solution.py:33
  14.3 5.0 %collective-permute-start.3 = (bf16[16,2048]{1,0:T(8,128)(2,1)S(1)}, bf16[16,2048]{1,0:T(8,128)(2,1)S(1)}, u32[]{:S(2)}, u32[]{:S(2)}) collective-permute-start(bf16[16,2048]{1,0:T(8,128)(2,1)S(1)} %get-tuple-element.41), channel_id=1, source_target_pairs={{0,2},{2,0},{1,3},{3,1},{4,6},{6,4},{5,7},{7,5},{8,10},{10,8},{9,1... | collective-permute-start | bytes 196616 | tf_op jit(solution)/shard_map/ppermute | solution.py:33
  19.4 6.2 %collective-permute-start.5 = (bf16[16,2176]{1,0:T(8,128)(2,1)S(1)}, bf16[16,2176]{1,0:T(8,128)(2,1)S(1)}, u32[]{:S(2)}, u32[]{:S(2)}) collective-permute-start(bf16[16,2176]{1,0:T(8,128)(2,1)S(1)} %get-tuple-element.44.refs_0_), channel_id=1, source_target_pairs={{0,8},{4,12},{8,0},{12,4},{1,9},{5,13},{9,1},{13,5},{2,10},{6,14},... | collective-permute-start | bytes 208904 | tf_op jit(solution)/shard_map/ppermute | solution.py:33
  19.8 5.8 %collective-permute-start.7 = (bf16[16,2176]{1,0:T(8,128)(2,1)S(1)}, bf16[16,2176]{1,0:T(8,128)(2,1)S(1)}, u32[]{:S(2)}, u32[]{:S(2)}) collective-permute-start(bf16[16,2176]{1,0:T(8,128)(2,1)S(1)} %get-tuple-element.44.refs_0_), channel_id=1, source_target_pairs={{0,2},{2,0},{1,3},{3,1},{4,6},{6,4},{5,7},{7,5},{8,10},{10,8},{9,1... | collective-permute-start | bytes 208904 | tf_op jit(solution)/shard_map/ppermute | solution.py:33
  20.7 5.4 %collective-permute-start.11 = (bf16[16,2176]{1,0:T(8,128)(2,1)S(1)}, bf16[16,2176]{1,0:T(8,128)(2,1)S(1)}, u32[]{:S(2)}, u32[]{:S(2)}) collective-permute-start(bf16[16,2176]{1,0:T(8,128)(2,1)S(1)} %get-tuple-element.44.refs_0_), channel_id=1, source_target_pairs={{0,1},{1,0},{2,3},{3,2},{4,5},{5,4},{6,7},{7,6},{8,9},{9,8},{10,11... | collective-permute-start | bytes 208904 | tf_op jit(solution)/shard_map/ppermute | solution.py:33
  20.7 5.9 %collective-permute-start.4 = (bf16[16,2176]{1,0:T(8,128)(2,1)S(1)}, bf16[16,2176]{1,0:T(8,128)(2,1)S(1)}, u32[]{:S(2)}, u32[]{:S(2)}) collective-permute-start(bf16[16,2176]{1,0:T(8,128)(2,1)S(1)} %get-tuple-element.44.refs_0_), channel_id=1, source_target_pairs={{0,4},{4,0},{8,12},{12,8},{1,5},{5,1},{9,13},{13,9},{2,6},{6,2},{1... | collective-permute-start | bytes 208904 | tf_op jit(solution)/shard_map/ppermute | solution.py:33
  25.6 4.3 %collective-permute-start.6 = (bf16[16,2176]{1,0:T(8,128)(2,1)S(1)}, bf16[16,2176]{1,0:T(8,128)(2,1)S(1)}, u32[]{:S(2)}, u32[]{:S(2)}) collective-permute-start(bf16[16,2176]{1,0:T(8,128)(2,1)S(1)} %collective-permute-done.5.refs_2_), channel_id=1, source_target_pairs={{0,4},{4,0},{8,12},{12,8},{1,5},{5,1},{9,13},{13,9},{2,6},{6,2},{1... | collective-permute-start | bytes 208904 | tf_op jit(solution)/shard_map/ppermute | solution.py:33
  25.6 4.8 %collective-permute-start.15 = (bf16[16,2176]{1,0:T(8,128)(2,1)S(1)}, bf16[16,2176]{1,0:T(8,128)(2,1)S(1)}, u32[]{:S(2)}, u32[]{:S(2)}) collective-permute-start(bf16[16,2176]{1,0:T(8,128)(2,1)S(1)} %collective-permute-done.7.refs_4_), channel_id=1, source_target_pairs={{0,1},{1,0},{2,3},{3,2},{4,5},{5,4},{6,7},{7,6},{8,9},{9,8},{10,11... | collective-permute-start | bytes 208904 | tf_op jit(solution)/shard_map/ppermute | solution.py:33
  25.6 4.8 %collective-permute-start.13 = (bf16[16,2176]{1,0:T(8,128)(2,1)S(1)}, bf16[16,2176]{1,0:T(8,128)(2,1)S(1)}, u32[]{:S(2)}, u32[]{:S(2)}) collective-permute-start(bf16[16,2176]{1,0:T(8,128)(2,1)S(1)} %collective-permute-done.5.refs_2_), channel_id=1, source_target_pairs={{0,1},{1,0},{2,3},{3,2},{4,5},{5,4},{6,7},{7,6},{8,9},{9,8},{10,11... | collective-permute-start | bytes 208904 | tf_op jit(solution)/shard_map/ppermute | solution.py:33
  26.1 4.9 %collective-permute-start.9 = (bf16[16,2176]{1,0:T(8,128)(2,1)S(1)}, bf16[16,2176]{1,0:T(8,128)(2,1)S(1)}, u32[]{:S(2)}, u32[]{:S(2)}) collective-permute-start(bf16[16,2176]{1,0:T(8,128)(2,1)S(1)} %collective-permute-done.5.refs_2_), channel_id=1, source_target_pairs={{0,2},{2,0},{1,3},{3,1},{4,6},{6,4},{5,7},{7,5},{8,10},{10,8},{9,1... | collective-permute-start | bytes 208904 | tf_op jit(solution)/shard_map/ppermute | solution.py:33
  26.6 5.9 %collective-permute-start.8 = (bf16[16,2176]{1,0:T(8,128)(2,1)S(1)}, bf16[16,2176]{1,0:T(8,128)(2,1)S(1)}, u32[]{:S(2)}, u32[]{:S(2)}) collective-permute-start(bf16[16,2176]{1,0:T(8,128)(2,1)S(1)} %collective-permute-done.4.refs_1_), channel_id=1, source_target_pairs={{0,2},{2,0},{1,3},{3,1},{4,6},{6,4},{5,7},{7,5},{8,10},{10,8},{9,1... | collective-permute-start | bytes 208904 | tf_op jit(solution)/shard_map/ppermute | solution.py:33
  29.9 4.3 %collective-permute-start.10 = (bf16[16,2176]{1,0:T(8,128)(2,1)S(1)}, bf16[16,2176]{1,0:T(8,128)(2,1)S(1)}, u32[]{:S(2)}, u32[]{:S(2)}) collective-permute-start(bf16[16,2176]{1,0:T(8,128)(2,1)S(1)} %collective-permute-done.6.refs_3_), channel_id=1, source_target_pairs={{0,2},{2,0},{1,3},{3,1},{4,6},{6,4},{5,7},{7,5},{8,10},{10,8},{9,1... | collective-permute-start | bytes 208904 | tf_op jit(solution)/shard_map/ppermute | solution.py:33
  30.4 3.8 %collective-permute-start.12 = (bf16[16,2176]{1,0:T(8,128)(2,1)S(1)}, bf16[16,2176]{1,0:T(8,128)(2,1)S(1)}, u32[]{:S(2)}, u32[]{:S(2)}) collective-permute-start(bf16[16,2176]{1,0:T(8,128)(2,1)S(1)} %collective-permute-done.4.refs_1_), channel_id=1, source_target_pairs={{0,1},{1,0},{2,3},{3,2},{4,5},{5,4},{6,7},{7,6},{8,9},{9,8},{10,11... | collective-permute-start | bytes 208904 | tf_op jit(solution)/shard_map/ppermute | solution.py:33
  30.4 3.8 %collective-permute-start.14 = (bf16[16,2176]{1,0:T(8,128)(2,1)S(1)}, bf16[16,2176]{1,0:T(8,128)(2,1)S(1)}, u32[]{:S(2)}, u32[]{:S(2)}) collective-permute-start(bf16[16,2176]{1,0:T(8,128)(2,1)S(1)} %collective-permute-done.6.refs_3_), channel_id=1, source_target_pairs={{0,1},{1,0},{2,3},{3,2},{4,5},{5,4},{6,7},{7,6},{8,9},{9,8},{10,11... | collective-permute-start | bytes 208904 | tf_op jit(solution)/shard_map/ppermute | solution.py:33
  31.0 3.2 %collective-permute-start.17 = (bf16[16,2176]{1,0:T(8,128)(2,1)S(1)}, bf16[16,2176]{1,0:T(8,128)(2,1)S(1)}, u32[]{:S(2)}, u32[]{:S(2)}) collective-permute-start(bf16[16,2176]{1,0:T(8,128)(2,1)S(1)} %collective-permute-done.9.refs_6_), channel_id=1, source_target_pairs={{0,1},{1,0},{2,3},{3,2},{4,5},{5,4},{6,7},{7,6},{8,9},{9,8},{10,11... | collective-permute-start | bytes 208904 | tf_op jit(solution)/shard_map/ppermute | solution.py:33
  32.5 1.7 %collective-permute-start.16 = (bf16[16,2176]{1,0:T(8,128)(2,1)S(1)}, bf16[16,2176]{1,0:T(8,128)(2,1)S(1)}, u32[]{:S(2)}, u32[]{:S(2)}) collective-permute-start(bf16[16,2176]{1,0:T(8,128)(2,1)S(1)} %collective-permute-done.8.refs_5_), channel_id=1, source_target_pairs={{0,1},{1,0},{2,3},{3,2},{4,5},{5,4},{6,7},{7,6},{8,9},{9,8},{10,11... | collective-permute-start | bytes 208904 | tf_op jit(solution)/shard_map/ppermute | solution.py:33
  34.2 1.3 %collective-permute-start.18 = (bf16[16,2176]{1,0:T(8,128)(2,1)S(1)}, bf16[16,2176]{1,0:T(8,128)(2,1)S(1)}, u32[]{:S(2)}, u32[]{:S(2)}) collective-permute-start(bf16[16,2176]{1,0:T(8,128)(2,1)S(1)} %collective-permute-done.10.refs_7_), channel_id=1, source_target_pairs={{0,1},{1,0},{2,3},{3,2},{4,5},{5,4},{6,7},{7,6},{8,9},{9,8},{10,11... | collective-permute-start | bytes 208904 | tf_op jit(solution)/shard_map/ppermute | solution.py:33
  49.4 2.0 %collective-permute-start.19 = (bf16[128,2048]{1,0:T(8,128)(2,1)S(1)}, bf16[128,2048]{1,0:T(8,128)(2,1)S(1)}, u32[]{:S(2)}, u32[]{:S(2)}) collective-permute-start(bf16[128,2048]{1,0:T(8,128)(2,1)S(1)} %get-tuple-element.48), channel_id=1, source_target_pairs={{0,1},{1,0},{2,3},{3,2},{4,5},{5,4},{6,7},{7,6},{8,9},{9,8},{10,11... | collective-permute-start | bytes 1572872 | tf_op jit(solution)/shard_map/ppermute | solution.py:33
  51.5 5.0 %collective-permute-start.20 = (bf16[16,2048]{1,0:T(8,128)(2,1)S(1)}, bf16[16,2048]{1,0:T(8,128)(2,1)S(1)}, u32[]{:S(2)}, u32[]{:S(2)}) collective-permute-start(bf16[16,2048]{1,0:T(8,128)(2,1)S(1)} %get-tuple-element.50), channel_id=1, source_target_pairs={{0,2},{2,0},{1,3},{3,1},{4,6},{6,4},{5,7},{7,5},{8,10},{10,8},{9,1... | collective-permute-start | bytes 196616 | tf_op jit(solution)/shard_map/ppermute | solution.py:33
  52.0 5.9 %collective-permute-start.22 = (bf16[16,2048]{1,0:T(8,128)(2,1)S(1)}, bf16[16,2048]{1,0:T(8,128)(2,1)S(1)}, u32[]{:S(2)}, u32[]{:S(2)}) collective-permute-start(bf16[16,2048]{1,0:T(8,128)(2,1)S(1)} %get-tuple-element.52), channel_id=1, source_target_pairs={{0,2},{2,0},{1,3},{3,1},{4,6},{6,4},{5,7},{7,5},{8,10},{10,8},{9,1... | collective-permute-start | bytes 196616 | tf_op jit(solution)/shard_map/ppermute | solution.py:33
  53.6 5.6 %collective-permute-start.24 = (bf16[16,2048]{1,0:T(8,128)(2,1)S(1)}, bf16[16,2048]{1,0:T(8,128)(2,1)S(1)}, u32[]{:S(2)}, u32[]{:S(2)}) collective-permute-start(bf16[16,2048]{1,0:T(8,128)(2,1)S(1)} %get-tuple-element.54), channel_id=1, source_target_pairs={{0,2},{2,0},{1,3},{3,1},{4,6},{6,4},{5,7},{7,5},{8,10},{10,8},{9,1... | collective-permute-start | bytes 196616 | tf_op jit(solution)/shard_map/ppermute | solution.py:33
  54.0 7.4 %collective-permute-start.26 = (bf16[16,2048]{1,0:T(8,128)(2,1)S(1)}, bf16[16,2048]{1,0:T(8,128)(2,1)S(1)}, u32[]{:S(2)}, u32[]{:S(2)}) collective-permute-start(bf16[16,2048]{1,0:T(8,128)(2,1)S(1)} %get-tuple-element.56), channel_id=1, source_target_pairs={{0,2},{2,0},{1,3},{3,1},{4,6},{6,4},{5,7},{7,5},{8,10},{10,8},{9,1... | collective-permute-start | bytes 196616 | tf_op jit(solution)/shard_map/ppermute | solution.py:33
  56.5 4.9 %collective-permute-start.21 = (bf16[16,2048]{1,0:T(8,128)(2,1)S(1)}, bf16[16,2048]{1,0:T(8,128)(2,1)S(1)}, u32[]{:S(2)}, u32[]{:S(2)}) collective-permute-start(bf16[16,2048]{1,0:T(8,128)(2,1)S(1)} %sum_x1.1), channel_id=1, source_target_pairs={{0,4},{4,0},{8,12},{12,8},{1,5},{5,1},{9,13},{13,9},{2,6},{6,2},{1... | collective-permute-start | bytes 196616 | tf_op jit(solution)/shard_map/ppermute | solution.py:33
  57.9 6.5 %collective-permute-start.23 = (bf16[16,2048]{1,0:T(8,128)(2,1)S(1)}, bf16[16,2048]{1,0:T(8,128)(2,1)S(1)}, u32[]{:S(2)}, u32[]{:S(2)}) collective-permute-start(bf16[16,2048]{1,0:T(8,128)(2,1)S(1)} %sum_x2.1), channel_id=1, source_target_pairs={{0,8},{4,12},{8,0},{12,4},{1,9},{5,13},{9,1},{13,5},{2,10},{6,14},... | collective-permute-start | bytes 196616 | tf_op jit(solution)/shard_map/ppermute | solution.py:33
  59.2 6.2 %collective-permute-start.25 = (bf16[16,2048]{1,0:T(8,128)(2,1)S(1)}, bf16[16,2048]{1,0:T(8,128)(2,1)S(1)}, u32[]{:S(2)}, u32[]{:S(2)}) collective-permute-start(bf16[16,2048]{1,0:T(8,128)(2,1)S(1)} %sum_x3.1), channel_id=1, source_target_pairs={{0,12},{4,8},{8,4},{12,0},{1,13},{5,9},{9,5},{13,1},{2,14},{6,10},... | collective-permute-start | bytes 196616 | tf_op jit(solution)/shard_map/ppermute | solution.py:33

commit v12 on v11

--- a/solution.py
+++ b/solution.py
@@ -244,8 +244,8 @@
         self.ended += 1
         self.fill()
 
-    def need(self, name):
-        while self.ended < self.last[name]:
+    def need(self, name, but=0):
+        while self.ended < self.last[name] - but:
             self.end_one()
 
     def step(self, cost):
@@ -259,7 +259,7 @@
     gate_first, up_first, gate_hbm, up_hbm, down_hbm, keep_ref, send_ref = refs[
         n_rows : n_rows + 7
     ]
-    rows_ref, pick_ref, packed_ref, hidden_ref, half_ref, gate_ref, up_ref, down_ref, sem = refs[
+    rows_ref, pick_ref, packed_ref, hidden_ref, half_ref, sum_ref, gate_ref, up_ref, down_ref, sem = refs[
         n_rows + 7 :
     ]
     per_expert, width = down_hbm.shape[0] // experts, down_hbm.shape[1]
@@ -284,7 +284,7 @@
             groups.append((("gate", x), quarters(gate_hbm, gate_ref.at[x - 1], x, True)))
             groups.append((("up", x), quarters(up_hbm, up_ref.at[x - 1], x, True)))
         groups.append((("down", x), quarters(down_hbm, down_ref, x, False)))
-    stream = Stream(groups, sem, 3)
+    stream = Stream(groups, sem, 4)
     stream.limit = stream.last["up", 1] if experts > 1 else stream.limit
     stream.fill()
     count = 0
@@ -326,7 +326,7 @@
             stream.need(("gate", x))
         for s in range(0, per_expert, tile):
             cut = slice(s, s + tile)
-            stream.step(0.7)
+            stream.step(0.85)
             gate = dot(packed_ref[mine, :], gate_ref[x - 1, :, cut] if x else gate_first[:, cut])
             half = 0.5 * gate
             half_ref[:, cut] = half + half * jnp.tanh(half)
@@ -334,14 +334,21 @@
             stream.need(("up", x))
         for s in range(0, per_expert, tile):
             cut = slice(s, s + tile)
-            stream.step(0.7)
+            stream.step(0.85)
             up = dot(packed_ref[mine, :], up_ref[x - 1, :, cut] if x else up_first[:, cut])
             hidden_ref[mine, cut] = (half_ref[:, cut] * up).astype(jnp.bfloat16)
-        stream.need(("down", x))
-        for c in range(0, width, column):
-            stream.step(0.7)
-            out = dot(hidden_ref[mine, :], down_ref[:, c : c + column])
-            packed_ref[mine, c : c + column] = (out * shares[x]).astype(jnp.bfloat16)
+        rows = per_expert // cuts
+        for i in range(cuts):
+            stream.need(("down", x), cuts - 1 - i)
+            part = slice(i * rows, (i + 1) * rows)
+            out = dot(hidden_ref[mine, part], down_ref[part, :])
+            if i:
+                out = out + sum_ref[...]
+            if i < cuts - 1:
+                sum_ref[...] = out
+            else:
+                packed_ref[mine, :] = (out * shares[x]).astype(jnp.bfloat16)
+            stream.step(0.85)
         stream.limit = stream.last["up", x + 2] if x + 2 < experts else len(stream.copies)
         stream.fill()
     kept = keep_ref.shape[0]
@@ -477,6 +484,7 @@
             pltpu.VMEM((experts * capacity, width), bf16),
             pltpu.VMEM((experts * capacity, down.shape[0] // experts), bf16),
             pltpu.VMEM((capacity, per_expert), f32),
+            pltpu.VMEM((capacity, width), f32),
             pltpu.VMEM((max(1, experts - 1), width, per_expert), bf16),
             pltpu.VMEM((max(1, experts - 1), width, per_expert), bf16),
             pltpu.VMEM((per_expert, width), bf16),

time: 66.4 us -> 65 us (0.979)
  Pallas kernels: 24.6 us -> 23.3 us
    pallas_call x11, Pallas kernels: 24.6 us -> 23.3 us  [call(): pl.pallas_call(kernel, out_shape=out_shape, in_specs=[s for s, _ in args]...]
where the time goes in v12:
time: 65 us; the launch traced here: 64.8 us
  Pallas kernels  23.3 us (36%)
  starting transfers between devices  22.5 us (35%)
  waiting for transfers between devices  18.1 us (28%)
  local copies, waits for them, and re-layouts  0.78 us (1%)
    pallas_call x11, Pallas kernels, call(): pl.pallas_call(kernel, out_shape=out_shape, in_specs=[s for s, _ in args]...  23.3 us
    ppermute x25, waiting for transfers between devices, xor_swap(): return lax.ppermute(x, axis, [(i, i ^ k) for i in range(n)])  18.1 us
    ppermute x25, starting transfers between devices, xor_swap(): return lax.ppermute(x, axis, [(i, i ^ k) for i in range(n)])  16.8 us
    ppermute x2, starting transfers between devices, per_device(): lax.ppermute(kv, 'sec', [(i, (i + k) % sec_count) for i in range(sec_coun...  5.67 us
  transfers between devices with their start and end apart: 27, of which 13 were waited for; matrix products, arithmetic and copies ran while one was open for 0% of the time, Pallas kernels for 13%

profile of v12, /device:TPU:0, one launch (start us, length us, event | category | flops | bytes accessed | tf_op | source)
XLA Modules:
  0.0 64.8 jit_solution(6475652615052187811)
XLA Ops:
  0.0 0.8 %constant_dynamic-slice_fusion = (bf16[64,256]{1,0:T(8,128)(2,1)S(1)}, bf16[64,256]{1,0:T(8,128)(2,1)S(1)}) fusion(bf16[64,512]{1,0:T(8,128)(2,1)} %param.14, s32[]{:T(128)S(6)} %select_n.10, bf16[64,512]{1,0:T(8,128)(2,1)} %param.13), kind=kLoop, calls=%fused_computation.1 | loop fusion | bytes 131076 | tf_op jit(solution)/shard_map/dynamic_slice | solution.py:391
  0.8 3.1 %collective-permute-start.1 = (bf16[64,512]{1,0:T(8,128)(2,1)S(1)}, bf16[64,512]{1,0:T(8,128)(2,1)S(1)}, u32[]{:S(2)}, u32[]{:S(2)}) collective-permute-start(bf16[64,512]{1,0:T(8,128)(2,1)S(1)} %pad_maximum_fusion.refs_2_), channel_id=1, source_target_pairs={{0,4},{4,8},{8,12},{12,0},{1,5},{5,9},{9,13},{13,1},{2,6},{6,10},{... | collective-permute-start | bytes 196616 | tf_op jit(solution)/shard_map/ppermute | solution.py:395
  3.9 2.6 %collective-permute-start = (bf16[64,512]{1,0:T(8,128)(2,1)S(1)}, bf16[64,512]{1,0:T(8,128)(2,1)S(1)}, u32[]{:S(2)}, u32[]{:S(2)}) collective-permute-start(bf16[64,512]{1,0:T(8,128)(2,1)S(1)} %pad_maximum_fusion.refs_2_), channel_id=1, source_target_pairs={{0,8},{4,12},{8,0},{12,4},{1,9},{5,13},{9,1},{13,5},{2,10},{6,14},... | collective-permute-start | bytes 196616 | tf_op jit(solution)/shard_map/ppermute | solution.py:395
  6.5 4.9 %prepare.1 = (bf16[64,1024]{1,0:T(8,128)(2,1)S(1)}, bf16[1024,2048]{1,0:T(8,128)(2,1)S(1)}, f32[1,2048]{1,0:T(1,128)S(1)}, f32[64,192]{1,0:T(8,128)S(1)}, bf16[6...) custom-call(s32[8]{0:T(128)} %lengths_hbm.1, ...), custom_call_target="tpu_custom_call" | custom-call | bytes 13600000 | tf_op jit(solution)/shard_map/prepare/pallas_call | solution.py:41
  11.4 1.4 %attention.1 = (f32[32,2048]{1,0:T(8,128)S(1)}, bf16[32,2048]{1,0:T(8,128)(2,1)S(1)}) custom-call(bf16[64,1024]{1,0:T(8,128)(2,1)S(1)} %get-tuple-element.34.q_ref, f32[64,192]{1,0:T(8,128)S(1)} %get-tuple-element.35.mask_ref, bf16[64,64]{1,0:T(8,128)(2,1)S(1)} %get-tuple-element.36.order_ref, bf16[64,512]{1,0:T(8,128)(2,1)S(1)} %collective-permute-done.refs_0_, ...), custom_call_target="tpu_custom_call" | custom-call | bytes 8160000 | tf_op jit(solution)/shard_map/attention/pallas_call | solution.py:41
  12.9 1.3 %collective-permute-done.2.refs_1_ = bf16[32,2048]{1,0:T(8,128)(2,1)S(1)} collective-permute-done((bf16[32,2048]{1,0:T(8,128)(2,1)S(1)}, bf16[32,2048]{1,0:T(8,128)(2,1)S(1)}, u32[]{:S(2)}, u32[]{:S(2)}) %collective-permute-start.2) | collective-permute-done | bytes 131104 | tf_op jit(solution)/shard_map/ppermute | solution.py:33
  14.3 1.6 %collective-permute-start.3 = (bf16[16,2048]{1,0:T(8,128)(2,1)S(1)}, bf16[16,2048]{1,0:T(8,128)(2,1)S(1)}, u32[]{:S(2)}, u32[]{:S(2)}) collective-permute-start(bf16[16,2048]{1,0:T(8,128)(2,1)S(1)} %get-tuple-element.41), channel_id=1, source_target_pairs={{0,2},{2,0},{1,3},{3,1},{4,6},{6,4},{5,7},{7,5},{8,10},{10,8},{9,1... | collective-permute-start | bytes 196616 | tf_op jit(solution)/shard_map/ppermute | solution.py:33
  15.9 3.4 %load_up.1 = (bf16[2048,2048]{1,0:T(8,128)(2,1)S(1)}, f32[8,128]{1,0:T(8,128)S(1)}) custom-call(bf16[2048,4096]{1,0:T(8,128)(2,1)} %bitcast.8, f32[16,2048]{1,0:T(8,128)S(1)} %get-tuple-element.40.refs_0_), custom_call_target="tpu_custom_call" | custom-call | bytes 8388607 | tf_op jit(solution)/shard_map/load_up/pallas_call | solution.py:41
  19.8 0.9 %collective-permute-start.7 = (bf16[16,2176]{1,0:T(8,128)(2,1)S(1)}, bf16[16,2176]{1,0:T(8,128)(2,1)S(1)}, u32[]{:S(2)}, u32[]{:S(2)}) collective-permute-start(bf16[16,2176]{1,0:T(8,128)(2,1)S(1)} %get-tuple-element.44.refs_0_), channel_id=1, source_target_pairs={{0,2},{2,0},{1,3},{3,1},{4,6},{6,4},{5,7},{7,5},{8,10},{10,8},{9,1... | collective-permute-start | bytes 208904 | tf_op jit(solution)/shard_map/ppermute | solution.py:33
  20.7 1.6 %collective-permute-start.4 = (bf16[16,2176]{1,0:T(8,128)(2,1)S(1)}, bf16[16,2176]{1,0:T(8,128)(2,1)S(1)}, u32[]{:S(2)}, u32[]{:S(2)}) collective-permute-start(bf16[16,2176]{1,0:T(8,128)(2,1)S(1)} %get-tuple-element.44.refs_0_), channel_id=1, source_target_pairs={{0,4},{4,0},{8,12},{12,8},{1,5},{5,1},{9,13},{13,9},{2,6},{6,2},{1... | collective-permute-start | bytes 208904 | tf_op jit(solution)/shard_map/ppermute | solution.py:33
  22.3 3.3 %collective-permute-done.5.refs_2_ = bf16[16,2176]{1,0:T(8,128)(2,1)S(1)} collective-permute-done((bf16[16,2176]{1,0:T(8,128)(2,1)S(1)}, bf16[16,2176]{1,0:T(8,128)(2,1)S(1)}, u32[]{:S(2)}, u32[]{:S(2)}) %collective-permute-start.5) | collective-permute-done | bytes 69664 | tf_op jit(solution)/shard_map/ppermute | solution.py:33
  25.6 0.5 collective-permute-start.13
  26.1 0.5 collective-permute-start.9
  26.6 1.6 %collective-permute-start.8 = (bf16[16,2176]{1,0:T(8,128)(2,1)S(1)}, bf16[16,2176]{1,0:T(8,128)(2,1)S(1)}, u32[]{:S(2)}, u32[]{:S(2)}) collective-permute-start(bf16[16,2176]{1,0:T(8,128)(2,1)S(1)} %collective-permute-done.4.refs_1_), channel_id=1, source_target_pairs={{0,2},{2,0},{1,3},{3,1},{4,6},{6,4},{5,7},{7,5},{8,10},{10,8},{9,1... | collective-permute-start | bytes 208904 | tf_op jit(solution)/shard_map/ppermute | solution.py:33
  28.1 1.8 %collective-permute-done.6.refs_3_ = bf16[16,2176]{1,0:T(8,128)(2,1)S(1)} collective-permute-done((bf16[16,2176]{1,0:T(8,128)(2,1)S(1)}, bf16[16,2176]{1,0:T(8,128)(2,1)S(1)}, u32[]{:S(2)}, u32[]{:S(2)}) %collective-permute-start.6) | collective-permute-done | bytes 69664 | tf_op jit(solution)/shard_map/ppermute | solution.py:33
  30.4 0.5 collective-permute-start.14
  31.0 1.5 %collective-permute-done.8.refs_5_ = bf16[16,2176]{1,0:T(8,128)(2,1)S(1)} collective-permute-done((bf16[16,2176]{1,0:T(8,128)(2,1)S(1)}, bf16[16,2176]{1,0:T(8,128)(2,1)S(1)}, u32[]{:S(2)}, u32[]{:S(2)}) %collective-permute-start.8) | collective-permute-done | bytes 69664 | tf_op jit(solution)/shard_map/ppermute | solution.py:33
  32.5 1.7 %collective-permute-done.10.refs_7_ = bf16[16,2176]{1,0:T(8,128)(2,1)S(1)} collective-permute-done((bf16[16,2176]{1,0:T(8,128)(2,1)S(1)}, bf16[16,2176]{1,0:T(8,128)(2,1)S(1)}, u32[]{:S(2)}, u32[]{:S(2)}) %collective-permute-start.10) | collective-permute-done | bytes 69664 | tf_op jit(solution)/shard_map/ppermute | solution.py:33
  34.2 1.2 %collective-permute-done.18.refs_15_ = bf16[16,2176]{1,0:T(8,128)(2,1)S(1)} collective-permute-done((bf16[16,2176]{1,0:T(8,128)(2,1)S(1)}, bf16[16,2176]{1,0:T(8,128)(2,1)S(1)}, u32[]{:S(2)}, u32[]{:S(2)}) %collective-permute-start.18) | collective-permute-done | bytes 69664 | tf_op jit(solution)/shard_map/ppermute | solution.py:33
  35.5 12.6 %experts.1 = (f32[128,2048]{1,0:T(8,128)S(1)}, bf16[128,2048]{1,0:T(8,128)(2,1)S(1)}) custom-call(bf16[16,2176]{1,0:T(8,128)(2,1)S(1)} %get-tuple-element.44.refs_0_, bf16[16,2176]{1,0:T(8,128)(2,1)S(1)} %collective-permute-done.4.refs_1_, bf16[16,2176]{1,0:T(8,128)(2,1)S(1)} %collective-permute-done.5.refs_2_, ...), custom_call_target="tpu_custom_call" | custom-call | bytes 40800000 | tf_op jit(solution)/shard_map/experts/pallas_call | solution.py:41
  48.3 1.8 %collective-permute-done.19.refs_1_ = bf16[128,2048]{1,0:T(8,128)(2,1)S(1)} collective-permute-done((bf16[128,2048]{1,0:T(8,128)(2,1)S(1)}, bf16[128,2048]{1,0:T(8,128)(2,1)S(1)}, u32[]{:S(2)}, u32[]{:S(2)}) %collective-permute-start.19) | collective-permute-done | bytes 524320 | tf_op jit(solution)/shard_map/ppermute | solution.py:33
  50.1 0.5 collective-permute-start.20
  50.6 1.6 %collective-permute-start.22 = (bf16[16,2048]{1,0:T(8,128)(2,1)S(1)}, bf16[16,2048]{1,0:T(8,128)(2,1)S(1)}, u32[]{:S(2)}, u32[]{:S(2)}) collective-permute-start(bf16[16,2048]{1,0:T(8,128)(2,1)S(1)} %get-tuple-element.52), channel_id=1, source_target_pairs={{0,2},{2,0},{1,3},{3,1},{4,6},{6,4},{5,7},{7,5},{8,10},{10,8},{9,1... | collective-permute-start | bytes 196616 | tf_op jit(solution)/shard_map/ppermute | solution.py:33
  52.2 0.5 collective-permute-start.24
  52.7 1.6 %collective-permute-start.26 = (bf16[16,2048]{1,0:T(8,128)(2,1)S(1)}, bf16[16,2048]{1,0:T(8,128)(2,1)S(1)}, u32[]{:S(2)}, u32[]{:S(2)}) collective-permute-start(bf16[16,2048]{1,0:T(8,128)(2,1)S(1)} %get-tuple-element.56), channel_id=1, source_target_pairs={{0,2},{2,0},{1,3},{3,1},{4,6},{6,4},{5,7},{7,5},{8,10},{10,8},{9,1... | collective-permute-start | bytes 196616 | tf_op jit(solution)/shard_map/ppermute | solution.py:33
  54.2 0.9 %collective-permute-done.20.refs_1_ = bf16[16,2048]{1,0:T(8,128)(2,1)S(1)} collective-permute-done((bf16[16,2048]{1,0:T(8,128)(2,1)S(1)}, bf16[16,2048]{1,0:T(8,128)(2,1)S(1)}, u32[]{:S(2)}, u32[]{:S(2)}) %collective-permute-start.20) | collective-permute-done | bytes 65568 | tf_op jit(solution)/shard_map/ppermute | solution.py:33
  55.1 1.1 %collective-permute-start.21 = (bf16[16,2048]{1,0:T(8,128)(2,1)S(1)}, bf16[16,2048]{1,0:T(8,128)(2,1)S(1)}, u32[]{:S(2)}, u32[]{:S(2)}) collective-permute-start(bf16[16,2048]{1,0:T(8,128)(2,1)S(1)} %sum_x1.1), channel_id=1, source_target_pairs={{0,4},{4,0},{8,12},{12,8},{1,5},{5,1},{9,13},{13,9},{2,6},{6,2},{1... | collective-permute-start | bytes 196616 | tf_op jit(solution)/shard_map/ppermute | solution.py:33
  56.5 1.2 %collective-permute-start.23 = (bf16[16,2048]{1,0:T(8,128)(2,1)S(1)}, bf16[16,2048]{1,0:T(8,128)(2,1)S(1)}, u32[]{:S(2)}, u32[]{:S(2)}) collective-permute-start(bf16[16,2048]{1,0:T(8,128)(2,1)S(1)} %sum_x2.1), channel_id=1, source_target_pairs={{0,8},{4,12},{8,0},{12,4},{1,9},{5,13},{9,1},{13,5},{2,10},{6,14},... | collective-permute-start | bytes 196616 | tf_op jit(solution)/shard_map/ppermute | solution.py:33
  57.9 2.2 %collective-permute-start.25 = (bf16[16,2048]{1,0:T(8,128)(2,1)S(1)}, bf16[16,2048]{1,0:T(8,128)(2,1)S(1)}, u32[]{:S(2)}, u32[]{:S(2)}) collective-permute-start(bf16[16,2048]{1,0:T(8,128)(2,1)S(1)} %sum_x3.1), channel_id=1, source_target_pairs={{0,12},{4,8},{8,4},{12,0},{1,13},{5,9},{9,5},{13,1},{2,14},{6,10},... | collective-permute-start | bytes 196616 | tf_op jit(solution)/shard_map/ppermute | solution.py:33
  60.1 3.0 %collective-permute-done.23.refs_2_ = bf16[16,2048]{1,0:T(8,128)(2,1)S(1)} collective-permute-done((bf16[16,2048]{1,0:T(8,128)(2,1)S(1)}, bf16[16,2048]{1,0:T(8,128)(2,1)S(1)}, u32[]{:S(2)}, u32[]{:S(2)}) %collective-permute-start.23) | collective-permute-done | bytes 65568 | tf_op jit(solution)/shard_map/ppermute | solution.py:33
  63.1 1.0 %collective-permute-done.25.refs_3_ = bf16[16,2048]{1,0:T(8,128)(2,1)S(1)} collective-permute-done((bf16[16,2048]{1,0:T(8,128)(2,1)S(1)}, bf16[16,2048]{1,0:T(8,128)(2,1)S(1)}, u32[]{:S(2)}, u32[]{:S(2)}) %collective-permute-start.25) | collective-permute-done | bytes 65568 | tf_op jit(solution)/shard_map/ppermute | solution.py:33
  64.1 0.7 %total.1 = bf16[16,2048]{1,0:T(8,128)(2,1)} custom-call(f32[16,2048]{1,0:T(8,128)S(1)} %get-tuple-element.43.refs_0_, bf16[16,2048]{1,0:T(8,128)(2,1)S(1)} %collective-permute-done.21.refs_1_, bf16[16,2048]{1,0:T(8,128)(2,1)S(1)} %collective-permute-done.23.refs_2_, bf16[16,2048]{1,0:T(8,128)(2,1)S(1)} %collective-permute-done.25.refs_3_, ...), custom_call_target="tpu_custom_call" | custom-call | bytes 680000 | tf_op jit(solution)/shard_map/total/pallas_call | solution.py:41
  (35 shorter events, 2.1 us)
Async XLA Ops:
  0.8 10.6 %collective-permute-start.1 = (bf16[64,512]{1,0:T(8,128)(2,1)S(1)}, bf16[64,512]{1,0:T(8,128)(2,1)S(1)}, u32[]{:S(2)}, u32[]{:S(2)}) collective-permute-start(bf16[64,512]{1,0:T(8,128)(2,1)S(1)} %pad_maximum_fusion.refs_2_), channel_id=1, source_target_pairs={{0,4},{4,8},{8,12},{12,0},{1,5},{5,9},{9,13},{13,1},{2,6},{6,10},{... | collective-permute-start | bytes 196616 | tf_op jit(solution)/shard_map/ppermute | solution.py:395
  3.9 7.5 %collective-permute-start = (bf16[64,512]{1,0:T(8,128)(2,1)S(1)}, bf16[64,512]{1,0:T(8,128)(2,1)S(1)}, u32[]{:S(2)}, u32[]{:S(2)}) collective-permute-start(bf16[64,512]{1,0:T(8,128)(2,1)S(1)} %pad_maximum_fusion.refs_2_), channel_id=1, source_target_pairs={{0,8},{4,12},{8,0},{12,4},{1,9},{5,13},{9,1},{13,5},{2,10},{6,14},... | collective-permute-start | bytes 196616 | tf_op jit(solution)/shard_map/ppermute | solution.py:395
  12.9 1.4 %collective-permute-start.2 = (bf16[32,2048]{1,0:T(8,128)(2,1)S(1)}, bf16[32,2048]{1,0:T(8,128)(2,1)S(1)}, u32[]{:S(2)}, u32[]{:S(2)}) collective-permute-start(bf16[32,2048]{1,0:T(8,128)(2,1)S(1)} %get-tuple-element.39), channel_id=1, source_target_pairs={{0,1},{1,0},{2,3},{3,2},{4,5},{5,4},{6,7},{7,6},{8,9},{9,8},{10,11... | collective-permute-start | bytes 393224 | tf_op jit(solution)/shard_map/ppermute | solution.py:33
  14.3 5.0 %collective-permute-start.3 = (bf16[16,2048]{1,0:T(8,128)(2,1)S(1)}, bf16[16,2048]{1,0:T(8,128)(2,1)S(1)}, u32[]{:S(2)}, u32[]{:S(2)}) collective-permute-start(bf16[16,2048]{1,0:T(8,128)(2,1)S(1)} %get-tuple-element.41), channel_id=1, source_target_pairs={{0,2},{2,0},{1,3},{3,1},{4,6},{6,4},{5,7},{7,5},{8,10},{10,8},{9,1... | collective-permute-start | bytes 196616 | tf_op jit(solution)/shard_map/ppermute | solution.py:33
  19.4 6.2 %collective-permute-start.5 = (bf16[16,2176]{1,0:T(8,128)(2,1)S(1)}, bf16[16,2176]{1,0:T(8,128)(2,1)S(1)}, u32[]{:S(2)}, u32[]{:S(2)}) collective-permute-start(bf16[16,2176]{1,0:T(8,128)(2,1)S(1)} %get-tuple-element.44.refs_0_), channel_id=1, source_target_pairs={{0,8},{4,12},{8,0},{12,4},{1,9},{5,13},{9,1},{13,5},{2,10},{6,14},... | collective-permute-start | bytes 208904 | tf_op jit(solution)/shard_map/ppermute | solution.py:33
  19.8 5.8 %collective-permute-start.7 = (bf16[16,2176]{1,0:T(8,128)(2,1)S(1)}, bf16[16,2176]{1,0:T(8,128)(2,1)S(1)}, u32[]{:S(2)}, u32[]{:S(2)}) collective-permute-start(bf16[16,2176]{1,0:T(8,128)(2,1)S(1)} %get-tuple-element.44.refs_0_), channel_id=1, source_target_pairs={{0,2},{2,0},{1,3},{3,1},{4,6},{6,4},{5,7},{7,5},{8,10},{10,8},{9,1... | collective-permute-start | bytes 208904 | tf_op jit(solution)/shard_map/ppermute | solution.py:33
  20.7 5.4 %collective-permute-start.11 = (bf16[16,2176]{1,0:T(8,128)(2,1)S(1)}, bf16[16,2176]{1,0:T(8,128)(2,1)S(1)}, u32[]{:S(2)}, u32[]{:S(2)}) collective-permute-start(bf16[16,2176]{1,0:T(8,128)(2,1)S(1)} %get-tuple-element.44.refs_0_), channel_id=1, source_target_pairs={{0,1},{1,0},{2,3},{3,2},{4,5},{5,4},{6,7},{7,6},{8,9},{9,8},{10,11... | collective-permute-start | bytes 208904 | tf_op jit(solution)/shard_map/ppermute | solution.py:33
  20.7 5.9 %collective-permute-start.4 = (bf16[16,2176]{1,0:T(8,128)(2,1)S(1)}, bf16[16,2176]{1,0:T(8,128)(2,1)S(1)}, u32[]{:S(2)}, u32[]{:S(2)}) collective-permute-start(bf16[16,2176]{1,0:T(8,128)(2,1)S(1)} %get-tuple-element.44.refs_0_), channel_id=1, source_target_pairs={{0,4},{4,0},{8,12},{12,8},{1,5},{5,1},{9,13},{13,9},{2,6},{6,2},{1... | collective-permute-start | bytes 208904 | tf_op jit(solution)/shard_map/ppermute | solution.py:33
  25.6 4.3 %collective-permute-start.6 = (bf16[16,2176]{1,0:T(8,128)(2,1)S(1)}, bf16[16,2176]{1,0:T(8,128)(2,1)S(1)}, u32[]{:S(2)}, u32[]{:S(2)}) collective-permute-start(bf16[16,2176]{1,0:T(8,128)(2,1)S(1)} %collective-permute-done.5.refs_2_), channel_id=1, source_target_pairs={{0,4},{4,0},{8,12},{12,8},{1,5},{5,1},{9,13},{13,9},{2,6},{6,2},{1... | collective-permute-start | bytes 208904 | tf_op jit(solution)/shard_map/ppermute | solution.py:33
  25.6 4.8 %collective-permute-start.15 = (bf16[16,2176]{1,0:T(8,128)(2,1)S(1)}, bf16[16,2176]{1,0:T(8,128)(2,1)S(1)}, u32[]{:S(2)}, u32[]{:S(2)}) collective-permute-start(bf16[16,2176]{1,0:T(8,128)(2,1)S(1)} %collective-permute-done.7.refs_4_), channel_id=1, source_target_pairs={{0,1},{1,0},{2,3},{3,2},{4,5},{5,4},{6,7},{7,6},{8,9},{9,8},{10,11... | collective-permute-start | bytes 208904 | tf_op jit(solution)/shard_map/ppermute | solution.py:33
  25.6 4.8 %collective-permute-start.13 = (bf16[16,2176]{1,0:T(8,128)(2,1)S(1)}, bf16[16,2176]{1,0:T(8,128)(2,1)S(1)}, u32[]{:S(2)}, u32[]{:S(2)}) collective-permute-start(bf16[16,2176]{1,0:T(8,128)(2,1)S(1)} %collective-permute-done.5.refs_2_), channel_id=1, source_target_pairs={{0,1},{1,0},{2,3},{3,2},{4,5},{5,4},{6,7},{7,6},{8,9},{9,8},{10,11... | collective-permute-start | bytes 208904 | tf_op jit(solution)/shard_map/ppermute | solution.py:33
  26.1 4.9 %collective-permute-start.9 = (bf16[16,2176]{1,0:T(8,128)(2,1)S(1)}, bf16[16,2176]{1,0:T(8,128)(2,1)S(1)}, u32[]{:S(2)}, u32[]{:S(2)}) collective-permute-start(bf16[16,2176]{1,0:T(8,128)(2,1)S(1)} %collective-permute-done.5.refs_2_), channel_id=1, source_target_pairs={{0,2},{2,0},{1,3},{3,1},{4,6},{6,4},{5,7},{7,5},{8,10},{10,8},{9,1... | collective-permute-start | bytes 208904 | tf_op jit(solution)/shard_map/ppermute | solution.py:33
  26.6 5.9 %collective-permute-start.8 = (bf16[16,2176]{1,0:T(8,128)(2,1)S(1)}, bf16[16,2176]{1,0:T(8,128)(2,1)S(1)}, u32[]{:S(2)}, u32[]{:S(2)}) collective-permute-start(bf16[16,2176]{1,0:T(8,128)(2,1)S(1)} %collective-permute-done.4.refs_1_), channel_id=1, source_target_pairs={{0,2},{2,0},{1,3},{3,1},{4,6},{6,4},{5,7},{7,5},{8,10},{10,8},{9,1... | collective-permute-start | bytes 208904 | tf_op jit(solution)/shard_map/ppermute | solution.py:33
  29.9 4.3 %collective-permute-start.10 = (bf16[16,2176]{1,0:T(8,128)(2,1)S(1)}, bf16[16,2176]{1,0:T(8,128)(2,1)S(1)}, u32[]{:S(2)}, u32[]{:S(2)}) collective-permute-start(bf16[16,2176]{1,0:T(8,128)(2,1)S(1)} %collective-permute-done.6.refs_3_), channel_id=1, source_target_pairs={{0,2},{2,0},{1,3},{3,1},{4,6},{6,4},{5,7},{7,5},{8,10},{10,8},{9,1... | collective-permute-start | bytes 208904 | tf_op jit(solution)/shard_map/ppermute | solution.py:33
  30.4 3.8 %collective-permute-start.12 = (bf16[16,2176]{1,0:T(8,128)(2,1)S(1)}, bf16[16,2176]{1,0:T(8,128)(2,1)S(1)}, u32[]{:S(2)}, u32[]{:S(2)}) collective-permute-start(bf16[16,2176]{1,0:T(8,128)(2,1)S(1)} %collective-permute-done.4.refs_1_), channel_id=1, source_target_pairs={{0,1},{1,0},{2,3},{3,2},{4,5},{5,4},{6,7},{7,6},{8,9},{9,8},{10,11... | collective-permute-start | bytes 208904 | tf_op jit(solution)/shard_map/ppermute | solution.py:33
  30.4 3.8 %collective-permute-start.14 = (bf16[16,2176]{1,0:T(8,128)(2,1)S(1)}, bf16[16,2176]{1,0:T(8,128)(2,1)S(1)}, u32[]{:S(2)}, u32[]{:S(2)}) collective-permute-start(bf16[16,2176]{1,0:T(8,128)(2,1)S(1)} %collective-permute-done.6.refs_3_), channel_id=1, source_target_pairs={{0,1},{1,0},{2,3},{3,2},{4,5},{5,4},{6,7},{7,6},{8,9},{9,8},{10,11... | collective-permute-start | bytes 208904 | tf_op jit(solution)/shard_map/ppermute | solution.py:33
  31.0 3.2 %collective-permute-start.17 = (bf16[16,2176]{1,0:T(8,128)(2,1)S(1)}, bf16[16,2176]{1,0:T(8,128)(2,1)S(1)}, u32[]{:S(2)}, u32[]{:S(2)}) collective-permute-start(bf16[16,2176]{1,0:T(8,128)(2,1)S(1)} %collective-permute-done.9.refs_6_), channel_id=1, source_target_pairs={{0,1},{1,0},{2,3},{3,2},{4,5},{5,4},{6,7},{7,6},{8,9},{9,8},{10,11... | collective-permute-start | bytes 208904 | tf_op jit(solution)/shard_map/ppermute | solution.py:33
  32.5 1.7 %collective-permute-start.16 = (bf16[16,2176]{1,0:T(8,128)(2,1)S(1)}, bf16[16,2176]{1,0:T(8,128)(2,1)S(1)}, u32[]{:S(2)}, u32[]{:S(2)}) collective-permute-start(bf16[16,2176]{1,0:T(8,128)(2,1)S(1)} %collective-permute-done.8.refs_5_), channel_id=1, source_target_pairs={{0,1},{1,0},{2,3},{3,2},{4,5},{5,4},{6,7},{7,6},{8,9},{9,8},{10,11... | collective-permute-start | bytes 208904 | tf_op jit(solution)/shard_map/ppermute | solution.py:33
  34.2 1.3 %collective-permute-start.18 = (bf16[16,2176]{1,0:T(8,128)(2,1)S(1)}, bf16[16,2176]{1,0:T(8,128)(2,1)S(1)}, u32[]{:S(2)}, u32[]{:S(2)}) collective-permute-start(bf16[16,2176]{1,0:T(8,128)(2,1)S(1)} %collective-permute-done.10.refs_7_), channel_id=1, source_target_pairs={{0,1},{1,0},{2,3},{3,2},{4,5},{5,4},{6,7},{7,6},{8,9},{9,8},{10,11... | collective-permute-start | bytes 208904 | tf_op jit(solution)/shard_map/ppermute | solution.py:33
  48.0 2.0 %collective-permute-start.19 = (bf16[128,2048]{1,0:T(8,128)(2,1)S(1)}, bf16[128,2048]{1,0:T(8,128)(2,1)S(1)}, u32[]{:S(2)}, u32[]{:S(2)}) collective-permute-start(bf16[128,2048]{1,0:T(8,128)(2,1)S(1)} %get-tuple-element.48), channel_id=1, source_target_pairs={{0,1},{1,0},{2,3},{3,2},{4,5},{5,4},{6,7},{7,6},{8,9},{9,8},{10,11... | collective-permute-start | bytes 1572872 | tf_op jit(solution)/shard_map/ppermute | solution.py:33
  50.1 5.0 %collective-permute-start.20 = (bf16[16,2048]{1,0:T(8,128)(2,1)S(1)}, bf16[16,2048]{1,0:T(8,128)(2,1)S(1)}, u32[]{:S(2)}, u32[]{:S(2)}) collective-permute-start(bf16[16,2048]{1,0:T(8,128)(2,1)S(1)} %get-tuple-element.50), channel_id=1, source_target_pairs={{0,2},{2,0},{1,3},{3,1},{4,6},{6,4},{5,7},{7,5},{8,10},{10,8},{9,1... | collective-permute-start | bytes 196616 | tf_op jit(solution)/shard_map/ppermute | solution.py:33
  50.6 5.9 %collective-permute-start.22 = (bf16[16,2048]{1,0:T(8,128)(2,1)S(1)}, bf16[16,2048]{1,0:T(8,128)(2,1)S(1)}, u32[]{:S(2)}, u32[]{:S(2)}) collective-permute-start(bf16[16,2048]{1,0:T(8,128)(2,1)S(1)} %get-tuple-element.52), channel_id=1, source_target_pairs={{0,2},{2,0},{1,3},{3,1},{4,6},{6,4},{5,7},{7,5},{8,10},{10,8},{9,1... | collective-permute-start | bytes 196616 | tf_op jit(solution)/shard_map/ppermute | solution.py:33
  52.2 5.6 %collective-permute-start.24 = (bf16[16,2048]{1,0:T(8,128)(2,1)S(1)}, bf16[16,2048]{1,0:T(8,128)(2,1)S(1)}, u32[]{:S(2)}, u32[]{:S(2)}) collective-permute-start(bf16[16,2048]{1,0:T(8,128)(2,1)S(1)} %get-tuple-element.54), channel_id=1, source_target_pairs={{0,2},{2,0},{1,3},{3,1},{4,6},{6,4},{5,7},{7,5},{8,10},{10,8},{9,1... | collective-permute-start | bytes 196616 | tf_op jit(solution)/shard_map/ppermute | solution.py:33
  52.7 7.4 %collective-permute-start.26 = (bf16[16,2048]{1,0:T(8,128)(2,1)S(1)}, bf16[16,2048]{1,0:T(8,128)(2,1)S(1)}, u32[]{:S(2)}, u32[]{:S(2)}) collective-permute-start(bf16[16,2048]{1,0:T(8,128)(2,1)S(1)} %get-tuple-element.56), channel_id=1, source_target_pairs={{0,2},{2,0},{1,3},{3,1},{4,6},{6,4},{5,7},{7,5},{8,10},{10,8},{9,1... | collective-permute-start | bytes 196616 | tf_op jit(solution)/shard_map/ppermute | solution.py:33
  55.1 4.9 %collective-permute-start.21 = (bf16[16,2048]{1,0:T(8,128)(2,1)S(1)}, bf16[16,2048]{1,0:T(8,128)(2,1)S(1)}, u32[]{:S(2)}, u32[]{:S(2)}) collective-permute-start(bf16[16,2048]{1,0:T(8,128)(2,1)S(1)} %sum_x1.1), channel_id=1, source_target_pairs={{0,4},{4,0},{8,12},{12,8},{1,5},{5,1},{9,13},{13,9},{2,6},{6,2},{1... | collective-permute-start | bytes 196616 | tf_op jit(solution)/shard_map/ppermute | solution.py:33
  56.5 6.5 %collective-permute-start.23 = (bf16[16,2048]{1,0:T(8,128)(2,1)S(1)}, bf16[16,2048]{1,0:T(8,128)(2,1)S(1)}, u32[]{:S(2)}, u32[]{:S(2)}) collective-permute-start(bf16[16,2048]{1,0:T(8,128)(2,1)S(1)} %sum_x2.1), channel_id=1, source_target_pairs={{0,8},{4,12},{8,0},{12,4},{1,9},{5,13},{9,1},{13,5},{2,10},{6,14},... | collective-permute-start | bytes 196616 | tf_op jit(solution)/shard_map/ppermute | solution.py:33
  57.9 6.2 %collective-permute-start.25 = (bf16[16,2048]{1,0:T(8,128)(2,1)S(1)}, bf16[16,2048]{1,0:T(8,128)(2,1)S(1)}, u32[]{:S(2)}, u32[]{:S(2)}) collective-permute-start(bf16[16,2048]{1,0:T(8,128)(2,1)S(1)} %sum_x3.1), channel_id=1, source_target_pairs={{0,12},{4,8},{8,4},{12,0},{1,13},{5,9},{9,5},{13,1},{2,14},{6,10},... | collective-permute-start | bytes 196616 | tf_op jit(solution)/shard_map/ppermute | solution.py:33

commit v13 on v12

--- a/solution.py
+++ b/solution.py
@@ -121,31 +121,44 @@
         c.wait()
 
 
-def load_kernel(n_after, source, *refs):
-    *targets, token_ref, sem = refs[n_after:]
-    copies = [
-        pltpu.make_async_copy(a, b, sem.at[i])
-        for i, (a, b) in enumerate(columns(source, targets))
-    ]
-    for c in copies:
-        c.start()
+def load_kernel(part, n_after, source, *refs):
+    target, token_ref, sem = refs[n_after:]
+    rows, cols = target.shape
+    copy = pltpu.make_async_copy(
+        source.at[pl.ds(0, rows), pl.ds(part * cols, cols)], target, sem
+    )
+    copy.start()
     token_ref[...] = jnp.zeros_like(token_ref)
-    for c in copies:
-        c.wait()
-
-
-def load(array, parts, wanted, after, name):
-    rows, cols = array.shape
-    out = call(
-        functools.partial(load_kernel, len(after)),
-        [sds((rows, cols // parts), array.dtype)] * wanted + [sds((8, LANES), jnp.float32)],
+    copy.wait()
+
+
+def load(array, rows, columns, part, after, name):
+    return call(
+        functools.partial(load_kernel, part, len(after)),
+        [sds((rows, columns), array.dtype), sds((8, LANES), jnp.float32)],
         [(HBM, array)] + [(ANY, a) for a in after],
-        scratch=[pltpu.SemaphoreType.DMA((wanted,))],
+        scratch=[pltpu.SemaphoreType.DMA],
         vmem=1,
         name=name,
-        cost_us=array.size * wanted / parts * 2 / 3.4e6,
-    )
-    return out[:-1], out[-1]
+        cost_us=rows * columns * 2 / 3.4e6,
+    )
+
+
+def join_kernel(n, *refs):
+    start = 0
+    for r in refs[:n]:
+        refs[-1][start : start + r.shape[0], :] = r[...]
+        start += r.shape[0]
+
+
+def join(arrays, name, after=()):
+    return call(
+        functools.partial(join_kernel, len(arrays)),
+        sds((sum(a.shape[0] for a in arrays), arrays[0].shape[1]), arrays[0].dtype),
+        [(VMEM, a) for a in arrays] + [(ANY, a) for a in after],
+        name=name,
+        cost_us=0.1,
+    )
 
 
 def attention_kernel(back, kv_heads, group, q_ref, mask_ref, order_ref, *refs):
@@ -254,25 +267,26 @@
             self.end_one()
 
 
-def experts_kernel(experts, capacity, tile, halves, n_rows, *refs):
+def experts_kernel(experts, capacity, tile, halves, n_rows, n_late, *refs):
     rows_in = refs[:n_rows]
-    gate_first, up_first, gate_hbm, up_hbm, down_hbm, keep_ref, send_ref = refs[
-        n_rows : n_rows + 7
-    ]
+    gate_first, up_first, *gate_late = refs[n_rows : n_rows + 2 + n_late]
+    n_rows += n_late
+    gate_hbm, up_hbm, down_hbm, keep_ref, send_ref = refs[n_rows + 2 : n_rows + 7]
     rows_ref, pick_ref, packed_ref, hidden_ref, half_ref, sum_ref, gate_ref, up_ref, down_ref, sem = refs[
         n_rows + 7 :
     ]
     per_expert, width = down_hbm.shape[0] // experts, down_hbm.shape[1]
     column = min(512, width)
     cuts = 4
-
-    def quarters(source, target, x, columns):
+    early = gate_late[0].shape[0] if n_late else 0
+
+    def pieces(source, target, x, columns, first=0, cuts=cuts):
         rows = target.shape[0] // cuts
         pairs = []
         for i in range(cuts):
             to = pl.ds(i * rows, rows)
             if columns:
-                part = source.at[to, pl.ds(x * per_expert, per_expert)]
+                part = source.at[pl.ds(first + i * rows, rows), pl.ds(x * per_expert, per_expert)]
             else:
                 part = source.at[pl.ds(x * per_expert + i * rows, rows)]
             pairs.append((part, target.at[to]))
@@ -281,9 +295,10 @@
     groups = []
     for x in range(experts):
         if x:
-            groups.append((("gate", x), quarters(gate_hbm, gate_ref.at[x - 1], x, True)))
-            groups.append((("up", x), quarters(up_hbm, up_ref.at[x - 1], x, True)))
-        groups.append((("down", x), quarters(down_hbm, down_ref, x, False)))
+            some = (early, cuts // 2) if early else (0, cuts)
+            groups.append((("gate", x), pieces(gate_hbm, gate_ref.at[x - 1], x, True, *some)))
+            groups.append((("up", x), pieces(up_hbm, up_ref.at[x - 1], x, True)))
+        groups.append((("down", x), pieces(down_hbm, down_ref, x, False)))
     stream = Stream(groups, sem, 4)
     stream.limit = stream.last["up", 1] if experts > 1 else stream.limit
     stream.fill()
@@ -327,7 +342,11 @@
         for s in range(0, per_expert, tile):
             cut = slice(s, s + tile)
             stream.step(0.85)
-            gate = dot(packed_ref[mine, :], gate_ref[x - 1, :, cut] if x else gate_first[:, cut])
+            if x == 1 and n_late:
+                gate = dot(packed_ref[mine, :early], gate_late[0][:, cut])
+                gate = gate + dot(packed_ref[mine, early:], gate_ref[0, :, cut])
+            else:
+                gate = dot(packed_ref[mine, :], gate_ref[x - 1, :, cut] if x else gate_first[:, cut])
             half = 0.5 * gate
             half_ref[:, cut] = half + half * jnp.tanh(half)
         if x:
@@ -443,7 +462,7 @@
         [keep] + [xor_swap(send, "pp", 1)], [own_rows], [own_rows] * (tp_count - 1), "sum_cores"
     )
     got = [xor_swap(sends[k - 1], "tp", k) for k in range(1, tp_count)]
-    up_v, token = load(w_up[0], experts, 1, [own], "load_up")
+    up_v, token = load(w_up[0], width, per_expert, 0, [own], "load_up")
     stream, normed = call(
         functools.partial(norm_kernel, tp_count),
         [sds((own_rows, width), f32), sds((own_rows, width + LANES), bf16)],
@@ -454,6 +473,11 @@
 
     groups = min(4, sec_count)
     near = {k: xor_swap(normed, "sec", k) if k else normed for k in range(0, sec_count, 2)}
+    gate_late, late_rows = [], 0
+    if experts == 2 and sec_count > 2:
+        gate_late, token = load(w_gate[0], width // 2, per_expert, 1, [normed], "load_gate")
+        gate_late, late_rows = [gate_late], width // 2
+        near[2] = join([near[2]], "join", [token])
     near.update({k + 1: xor_swap(near[k], "sec", 1) for k in list(near) if k + 1 < sec_count})
     near = [near[k] for k in range(sec_count)]
     per_group = sec_count // groups
@@ -474,9 +498,9 @@
     tile = min(512, down.shape[0] // experts)
     kept = count // pp_count
     keep, send = call(
-        functools.partial(experts_kernel, experts, capacity, tile, halves, len(rows)),
+        functools.partial(experts_kernel, experts, capacity, tile, halves, len(rows), len(gate_late)),
         [sds((kept, width), f32), sds((count - kept, width), bf16)],
-        [(VMEM, a) for a in (*rows, *gate_v, *up_v)]
+        [(VMEM, a) for a in (*rows, *gate_v, up_v, *gate_late)]
         + [(HBM, a) for a in (w_gate[0], w_up[0], down)],
         scratch=[
             pltpu.VMEM((count, width + LANES), bf16),
@@ -485,12 +509,12 @@
             pltpu.VMEM((experts * capacity, down.shape[0] // experts), bf16),
             pltpu.VMEM((capacity, per_expert), f32),
             pltpu.VMEM((capacity, width), f32),
-            pltpu.VMEM((max(1, experts - 1), width, per_expert), bf16),
+            pltpu.VMEM((max(1, experts - 1), width - late_rows, per_expert), bf16),
             pltpu.VMEM((max(1, experts - 1), width, per_expert), bf16),
             pltpu.VMEM((per_expert, width), bf16),
             pltpu.SemaphoreType.DMA((4 * (3 * experts - 2),)),
         ],
-        vmem=33,
+        vmem=30,
         name="experts",
         cost_us=12.0,
     )
@@ -500,7 +524,7 @@
         [keep, xor_swap(send, "pp", 1)], [piece] * groups, [piece] * (groups * (tp_count - 1)), "sum_cores2"
     )
     final = [stream]
-    for g in list(range(1, groups)) + [0]:
+    for g in range(groups - 1, -1, -1):
         got = [xor_swap(sends[(k - 1) * groups + g], "tp", k) for k in range(1, tp_count)]
         if g == 0 and per_group == 1:
             final += [own[0]] + got

time: 65 us -> 64.1 us (0.986)
  waiting for transfers between devices: 18.1 us -> 14.9 us
  Pallas kernels: 23.3 us -> 25.7 us
    ppermute x25, waiting for transfers between devices: 18.1 us -> 14.9 us  [xor_swap(): return lax.ppermute(x, axis, [(i, i ^ k) for i in range(n)])]
    pallas_call x11 -> x13, Pallas kernels: 23.3 us -> 25.7 us  [call(): pl.pallas_call(kernel, out_shape=out_shape, in_specs=[s for s, _ in args]...]
  transfers between devices with their start and end apart: 27 -> 27, of which waited for: 13 -> 12; matrix products, arithmetic and copies ran while one was open for 0% -> 0% of each run, Pallas kernels for 13% -> 17%
where the time goes in v13:
time: 64.1 us; the launch traced here: 63.8 us
  Pallas kernels  25.7 us (40%)
  starting transfers between devices  22.2 us (35%)
  waiting for transfers between devices  14.9 us (23%)
  local copies, waits for them, and re-layouts  0.78 us (1%)
    pallas_call x13, Pallas kernels, call(): pl.pallas_call(kernel, out_shape=out_shape, in_specs=[s for s, _ in args]...  25.7 us
    ppermute x25, starting transfers between devices, xor_swap(): return lax.ppermute(x, axis, [(i, i ^ k) for i in range(n)])  16.6 us
    ppermute x25, waiting for transfers between devices, xor_swap(): return lax.ppermute(x, axis, [(i, i ^ k) for i in range(n)])  14.9 us
    ppermute x2, starting transfers between devices, per_device(): lax.ppermute(kv, 'sec', [(i, (i + k) % sec_count) for i in range(sec_coun...  5.67 us
  transfers between devices with their start and end apart: 27, of which 12 were waited for; matrix products, arithmetic and copies ran while one was open for 0% of the time, Pallas kernels for 17%

profile of v13, /device:TPU:0, one launch (start us, length us, event | category | flops | bytes accessed | tf_op | source)
XLA Modules:
  0.0 63.8 jit_solution(16362318471225153651)
XLA Ops:
  0.0 0.8 %constant_dynamic-slice_fusion = (bf16[64,256]{1,0:T(8,128)(2,1)S(1)}, bf16[64,256]{1,0:T(8,128)(2,1)S(1)}) fusion(bf16[64,512]{1,0:T(8,128)(2,1)} %param.14, s32[]{:T(128)S(6)} %select_n.10, bf16[64,512]{1,0:T(8,128)(2,1)} %param.13), kind=kLoop, calls=%fused_computation.1 | loop fusion | bytes 131076 | tf_op jit(solution)/shard_map/dynamic_slice | solution.py:410
  0.8 3.1 %collective-permute-start.1 = (bf16[64,512]{1,0:T(8,128)(2,1)S(1)}, bf16[64,512]{1,0:T(8,128)(2,1)S(1)}, u32[]{:S(2)}, u32[]{:S(2)}) collective-permute-start(bf16[64,512]{1,0:T(8,128)(2,1)S(1)} %pad_maximum_fusion.refs_2_), channel_id=1, source_target_pairs={{0,4},{4,8},{8,12},{12,0},{1,5},{5,9},{9,13},{13,1},{2,6},{6,10},{... | collective-permute-start | bytes 196616 | tf_op jit(solution)/shard_map/ppermute | solution.py:414
  3.9 2.6 %collective-permute-start = (bf16[64,512]{1,0:T(8,128)(2,1)S(1)}, bf16[64,512]{1,0:T(8,128)(2,1)S(1)}, u32[]{:S(2)}, u32[]{:S(2)}) collective-permute-start(bf16[64,512]{1,0:T(8,128)(2,1)S(1)} %pad_maximum_fusion.refs_2_), channel_id=1, source_target_pairs={{0,8},{4,12},{8,0},{12,4},{1,9},{5,13},{9,1},{13,5},{2,10},{6,14},... | collective-permute-start | bytes 196616 | tf_op jit(solution)/shard_map/ppermute | solution.py:414
  6.5 4.9 %prepare.1 = (bf16[64,1024]{1,0:T(8,128)(2,1)S(1)}, bf16[1024,2048]{1,0:T(8,128)(2,1)S(1)}, f32[1,2048]{1,0:T(1,128)S(1)}, f32[64,192]{1,0:T(8,128)S(1)}, bf16[6...) custom-call(s32[8]{0:T(128)} %lengths_hbm.1, ...), custom_call_target="tpu_custom_call" | custom-call | bytes 13600000 | tf_op jit(solution)/shard_map/prepare/pallas_call | solution.py:41
  11.4 1.4 %attention.1 = (f32[32,2048]{1,0:T(8,128)S(1)}, bf16[32,2048]{1,0:T(8,128)(2,1)S(1)}) custom-call(bf16[64,1024]{1,0:T(8,128)(2,1)S(1)} %get-tuple-element.36.q_ref, f32[64,192]{1,0:T(8,128)S(1)} %get-tuple-element.37.mask_ref, bf16[64,64]{1,0:T(8,128)(2,1)S(1)} %get-tuple-element.38.order_ref, bf16[64,512]{1,0:T(8,128)(2,1)S(1)} %collective-permute-done.refs_0_, ...), custom_call_target="tpu_custom_call" | custom-call | bytes 8160000 | tf_op jit(solution)/shard_map/attention/pallas_call | solution.py:41
  12.9 1.3 %collective-permute-done.2.refs_1_ = bf16[32,2048]{1,0:T(8,128)(2,1)S(1)} collective-permute-done((bf16[32,2048]{1,0:T(8,128)(2,1)S(1)}, bf16[32,2048]{1,0:T(8,128)(2,1)S(1)}, u32[]{:S(2)}, u32[]{:S(2)}) %collective-permute-start.2) | collective-permute-done | bytes 131104 | tf_op jit(solution)/shard_map/ppermute | solution.py:33
  14.3 1.6 %collective-permute-start.3 = (bf16[16,2048]{1,0:T(8,128)(2,1)S(1)}, bf16[16,2048]{1,0:T(8,128)(2,1)S(1)}, u32[]{:S(2)}, u32[]{:S(2)}) collective-permute-start(bf16[16,2048]{1,0:T(8,128)(2,1)S(1)} %get-tuple-element.43), channel_id=1, source_target_pairs={{0,2},{2,0},{1,3},{3,1},{4,6},{6,4},{5,7},{7,5},{8,10},{10,8},{9,1... | collective-permute-start | bytes 196616 | tf_op jit(solution)/shard_map/ppermute | solution.py:33
  15.9 3.4 %load_up.1 = (bf16[2048,2048]{1,0:T(8,128)(2,1)S(1)}, f32[8,128]{1,0:T(8,128)S(1)}) custom-call(bf16[2048,4096]{1,0:T(8,128)(2,1)} %bitcast.9, f32[16,2048]{1,0:T(8,128)S(1)} %get-tuple-element.42.refs_0_), custom_call_target="tpu_custom_call" | custom-call | bytes 8388607 | tf_op jit(solution)/shard_map/load_up/pallas_call | solution.py:41
  19.8 0.9 %collective-permute-start.7 = (bf16[16,2176]{1,0:T(8,128)(2,1)S(1)}, bf16[16,2176]{1,0:T(8,128)(2,1)S(1)}, u32[]{:S(2)}, u32[]{:S(2)}) collective-permute-start(bf16[16,2176]{1,0:T(8,128)(2,1)S(1)} %get-tuple-element.46.refs_0_), channel_id=1, source_target_pairs={{0,2},{2,0},{1,3},{3,1},{4,6},{6,4},{5,7},{7,5},{8,10},{10,8},{9,1... | collective-permute-start | bytes 208904 | tf_op jit(solution)/shard_map/ppermute | solution.py:33
  20.7 1.6 %collective-permute-start.4 = (bf16[16,2176]{1,0:T(8,128)(2,1)S(1)}, bf16[16,2176]{1,0:T(8,128)(2,1)S(1)}, u32[]{:S(2)}, u32[]{:S(2)}) collective-permute-start(bf16[16,2176]{1,0:T(8,128)(2,1)S(1)} %get-tuple-element.46.refs_0_), channel_id=1, source_target_pairs={{0,4},{4,0},{8,12},{12,8},{1,5},{5,1},{9,13},{13,9},{2,6},{6,2},{1... | collective-permute-start | bytes 208904 | tf_op jit(solution)/shard_map/ppermute | solution.py:33
  22.3 2.2 %load_gate.1 = (bf16[1024,2048]{1,0:T(8,128)(2,1)S(1)}, f32[8,128]{1,0:T(8,128)S(1)}) custom-call(bf16[2048,4096]{1,0:T(8,128)(2,1)} %bitcast.7, bf16[16,2176]{1,0:T(8,128)(2,1)S(1)} %get-tuple-element.46.refs_0_), custom_call_target="tpu_custom_call" | custom-call | bytes 4194303 | tf_op jit(solution)/shard_map/load_gate/pallas_call | solution.py:41
  24.5 1.0 %collective-permute-done.5.refs_0_ = bf16[16,2176]{1,0:T(8,128)(2,1)S(1)} collective-permute-done((bf16[16,2176]{1,0:T(8,128)(2,1)S(1)}, bf16[16,2176]{1,0:T(8,128)(2,1)S(1)}, u32[]{:S(2)}, u32[]{:S(2)}) %collective-permute-start.5) | collective-permute-done | bytes 69664 | tf_op jit(solution)/shard_map/ppermute | solution.py:33
  26.1 0.6 collective-permute-start.8
  26.7 1.5 %collective-permute-start.9 = (bf16[16,2176]{1,0:T(8,128)(2,1)S(1)}, bf16[16,2176]{1,0:T(8,128)(2,1)S(1)}, u32[]{:S(2)}, u32[]{:S(2)}) collective-permute-start(bf16[16,2176]{1,0:T(8,128)(2,1)S(1)} %join.1.refs_2_), channel_id=1, source_target_pairs={{0,2},{2,0},{1,3},{3,1},{4,6},{6,4},{5,7},{7,5},{8,10},{10,8},{9,1... | collective-permute-start | bytes 208904 | tf_op jit(solution)/shard_map/ppermute | solution.py:33
  28.2 1.7 %collective-permute-done.6.refs_3_ = bf16[16,2176]{1,0:T(8,128)(2,1)S(1)} collective-permute-done((bf16[16,2176]{1,0:T(8,128)(2,1)S(1)}, bf16[16,2176]{1,0:T(8,128)(2,1)S(1)}, u32[]{:S(2)}, u32[]{:S(2)}) %collective-permute-start.6) | collective-permute-done | bytes 69664 | tf_op jit(solution)/shard_map/ppermute | solution.py:33
  29.8 0.5 collective-permute-start.10
  30.3 0.5 collective-permute-start.14
  31.1 1.5 %collective-permute-done.9.refs_6_ = bf16[16,2176]{1,0:T(8,128)(2,1)S(1)} collective-permute-done((bf16[16,2176]{1,0:T(8,128)(2,1)S(1)}, bf16[16,2176]{1,0:T(8,128)(2,1)S(1)}, u32[]{:S(2)}, u32[]{:S(2)}) %collective-permute-start.9) | collective-permute-done | bytes 69664 | tf_op jit(solution)/shard_map/ppermute | solution.py:33
  32.6 1.5 %collective-permute-done.10.refs_7_ = bf16[16,2176]{1,0:T(8,128)(2,1)S(1)} collective-permute-done((bf16[16,2176]{1,0:T(8,128)(2,1)S(1)}, bf16[16,2176]{1,0:T(8,128)(2,1)S(1)}, u32[]{:S(2)}, u32[]{:S(2)}) %collective-permute-start.10) | collective-permute-done | bytes 69664 | tf_op jit(solution)/shard_map/ppermute | solution.py:33
  34.2 1.2 %collective-permute-done.18.refs_15_ = bf16[16,2176]{1,0:T(8,128)(2,1)S(1)} collective-permute-done((bf16[16,2176]{1,0:T(8,128)(2,1)S(1)}, bf16[16,2176]{1,0:T(8,128)(2,1)S(1)}, u32[]{:S(2)}, u32[]{:S(2)}) %collective-permute-start.18) | collective-permute-done | bytes 69664 | tf_op jit(solution)/shard_map/ppermute | solution.py:33
  35.4 12.8 %experts.1 = (f32[128,2048]{1,0:T(8,128)S(1)}, bf16[128,2048]{1,0:T(8,128)(2,1)S(1)}) custom-call(bf16[16,2176]{1,0:T(8,128)(2,1)S(1)} %get-tuple-element.46.refs_0_, bf16[16,2176]{1,0:T(8,128)(2,1)S(1)} %collective-permute-done.4.refs_1_, bf16[16,2176]{1,0:T(8,128)(2,1)S(1)} %join.1.refs_2_, bf16[16,2176]{1,0:T(8,128)(2,1)S(1)} %collective-permute-done.6.refs_3_, ...), custom_call_target="tpu_custom_call" | custom-call | bytes 40800000 | tf_op jit(solution)/shard_map/experts/pallas_call | solution.py:41
  48.4 1.8 %collective-permute-done.19.refs_1_ = bf16[128,2048]{1,0:T(8,128)(2,1)S(1)} collective-permute-done((bf16[128,2048]{1,0:T(8,128)(2,1)S(1)}, bf16[128,2048]{1,0:T(8,128)(2,1)S(1)}, u32[]{:S(2)}, u32[]{:S(2)}) %collective-permute-start.19) | collective-permute-done | bytes 524320 | tf_op jit(solution)/shard_map/ppermute | solution.py:33
  50.3 0.6 collective-permute-start.20
  50.8 1.6 %collective-permute-start.22 = (bf16[16,2048]{1,0:T(8,128)(2,1)S(1)}, bf16[16,2048]{1,0:T(8,128)(2,1)S(1)}, u32[]{:S(2)}, u32[]{:S(2)}) collective-permute-start(bf16[16,2048]{1,0:T(8,128)(2,1)S(1)} %get-tuple-element.56), channel_id=1, source_target_pairs={{0,2},{2,0},{1,3},{3,1},{4,6},{6,4},{5,7},{7,5},{8,10},{10,8},{9,1... | collective-permute-start | bytes 196616 | tf_op jit(solution)/shard_map/ppermute | solution.py:33
  52.9 1.6 %collective-permute-start.26 = (bf16[16,2048]{1,0:T(8,128)(2,1)S(1)}, bf16[16,2048]{1,0:T(8,128)(2,1)S(1)}, u32[]{:S(2)}, u32[]{:S(2)}) collective-permute-start(bf16[16,2048]{1,0:T(8,128)(2,1)S(1)} %get-tuple-element.60), channel_id=1, source_target_pairs={{0,2},{2,0},{1,3},{3,1},{4,6},{6,4},{5,7},{7,5},{8,10},{10,8},{9,1... | collective-permute-start | bytes 196616 | tf_op jit(solution)/shard_map/ppermute | solution.py:33
  54.4 0.9 %collective-permute-done.20.refs_1_ = bf16[16,2048]{1,0:T(8,128)(2,1)S(1)} collective-permute-done((bf16[16,2048]{1,0:T(8,128)(2,1)S(1)}, bf16[16,2048]{1,0:T(8,128)(2,1)S(1)}, u32[]{:S(2)}, u32[]{:S(2)}) %collective-permute-start.20) | collective-permute-done | bytes 65568 | tf_op jit(solution)/shard_map/ppermute | solution.py:33
  55.3 1.8 %collective-permute-start.21 = (bf16[16,2048]{1,0:T(8,128)(2,1)S(1)}, bf16[16,2048]{1,0:T(8,128)(2,1)S(1)}, u32[]{:S(2)}, u32[]{:S(2)}) collective-permute-start(bf16[16,2048]{1,0:T(8,128)(2,1)S(1)} %sum_x3.1), channel_id=1, source_target_pairs={{0,12},{4,8},{8,4},{12,0},{1,13},{5,9},{9,5},{13,1},{2,14},{6,10},... | collective-permute-start | bytes 196616 | tf_op jit(solution)/shard_map/ppermute | solution.py:33
  57.1 1.0 %collective-permute-start.23 = (bf16[16,2048]{1,0:T(8,128)(2,1)S(1)}, bf16[16,2048]{1,0:T(8,128)(2,1)S(1)}, u32[]{:S(2)}, u32[]{:S(2)}) collective-permute-start(bf16[16,2048]{1,0:T(8,128)(2,1)S(1)} %sum_x2.1), channel_id=1, source_target_pairs={{0,8},{4,12},{8,0},{12,4},{1,9},{5,13},{9,1},{13,5},{2,10},{6,14},... | collective-permute-start | bytes 196616 | tf_op jit(solution)/shard_map/ppermute | solution.py:33
  58.1 1.8 %collective-permute-start.25 = (bf16[16,2048]{1,0:T(8,128)(2,1)S(1)}, bf16[16,2048]{1,0:T(8,128)(2,1)S(1)}, u32[]{:S(2)}, u32[]{:S(2)}) collective-permute-start(bf16[16,2048]{1,0:T(8,128)(2,1)S(1)} %sum_x1.1), channel_id=1, source_target_pairs={{0,4},{4,0},{8,12},{12,8},{1,5},{5,1},{9,13},{13,9},{2,6},{6,2},{1... | collective-permute-start | bytes 196616 | tf_op jit(solution)/shard_map/ppermute | solution.py:33
  59.9 1.7 %collective-permute-done.21.refs_1_ = bf16[16,2048]{1,0:T(8,128)(2,1)S(1)} collective-permute-done((bf16[16,2048]{1,0:T(8,128)(2,1)S(1)}, bf16[16,2048]{1,0:T(8,128)(2,1)S(1)}, u32[]{:S(2)}, u32[]{:S(2)}) %collective-permute-start.21) | collective-permute-done | bytes 65568 | tf_op jit(solution)/shard_map/ppermute | solution.py:33
  61.6 1.5 %collective-permute-done.23.refs_2_ = bf16[16,2048]{1,0:T(8,128)(2,1)S(1)} collective-permute-done((bf16[16,2048]{1,0:T(8,128)(2,1)S(1)}, bf16[16,2048]{1,0:T(8,128)(2,1)S(1)}, u32[]{:S(2)}, u32[]{:S(2)}) %collective-permute-start.23) | collective-permute-done | bytes 65568 | tf_op jit(solution)/shard_map/ppermute | solution.py:33
  63.1 0.7 %total.1 = bf16[16,2048]{1,0:T(8,128)(2,1)} custom-call(f32[16,2048]{1,0:T(8,128)S(1)} %get-tuple-element.45.refs_0_, bf16[16,2048]{1,0:T(8,128)(2,1)S(1)} %collective-permute-done.21.refs_1_, bf16[16,2048]{1,0:T(8,128)(2,1)S(1)} %collective-permute-done.23.refs_2_, bf16[16,2048]{1,0:T(8,128)(2,1)S(1)} %collective-permute-done.25.refs_3_, ...), custom_call_target="tpu_custom_call" | custom-call | bytes 680000 | tf_op jit(solution)/shard_map/total/pallas_call | solution.py:41
  (37 shorter events, 2.4 us)
Async XLA Ops:
  0.8 10.6 %collective-permute-start.1 = (bf16[64,512]{1,0:T(8,128)(2,1)S(1)}, bf16[64,512]{1,0:T(8,128)(2,1)S(1)}, u32[]{:S(2)}, u32[]{:S(2)}) collective-permute-start(bf16[64,512]{1,0:T(8,128)(2,1)S(1)} %pad_maximum_fusion.refs_2_), channel_id=1, source_target_pairs={{0,4},{4,8},{8,12},{12,0},{1,5},{5,9},{9,13},{13,1},{2,6},{6,10},{... | collective-permute-start | bytes 196616 | tf_op jit(solution)/shard_map/ppermute | solution.py:414
  3.9 7.5 %collective-permute-start = (bf16[64,512]{1,0:T(8,128)(2,1)S(1)}, bf16[64,512]{1,0:T(8,128)(2,1)S(1)}, u32[]{:S(2)}, u32[]{:S(2)}) collective-permute-start(bf16[64,512]{1,0:T(8,128)(2,1)S(1)} %pad_maximum_fusion.refs_2_), channel_id=1, source_target_pairs={{0,8},{4,12},{8,0},{12,4},{1,9},{5,13},{9,1},{13,5},{2,10},{6,14},... | collective-permute-start | bytes 196616 | tf_op jit(solution)/shard_map/ppermute | solution.py:414
  12.9 1.4 %collective-permute-start.2 = (bf16[32,2048]{1,0:T(8,128)(2,1)S(1)}, bf16[32,2048]{1,0:T(8,128)(2,1)S(1)}, u32[]{:S(2)}, u32[]{:S(2)}) collective-permute-start(bf16[32,2048]{1,0:T(8,128)(2,1)S(1)} %get-tuple-element.41), channel_id=1, source_target_pairs={{0,1},{1,0},{2,3},{3,2},{4,5},{5,4},{6,7},{7,6},{8,9},{9,8},{10,11... | collective-permute-start | bytes 393224 | tf_op jit(solution)/shard_map/ppermute | solution.py:33
  14.3 5.0 %collective-permute-start.3 = (bf16[16,2048]{1,0:T(8,128)(2,1)S(1)}, bf16[16,2048]{1,0:T(8,128)(2,1)S(1)}, u32[]{:S(2)}, u32[]{:S(2)}) collective-permute-start(bf16[16,2048]{1,0:T(8,128)(2,1)S(1)} %get-tuple-element.43), channel_id=1, source_target_pairs={{0,2},{2,0},{1,3},{3,1},{4,6},{6,4},{5,7},{7,5},{8,10},{10,8},{9,1... | collective-permute-start | bytes 196616 | tf_op jit(solution)/shard_map/ppermute | solution.py:33
  19.4 6.1 %collective-permute-start.5 = (bf16[16,2176]{1,0:T(8,128)(2,1)S(1)}, bf16[16,2176]{1,0:T(8,128)(2,1)S(1)}, u32[]{:S(2)}, u32[]{:S(2)}) collective-permute-start(bf16[16,2176]{1,0:T(8,128)(2,1)S(1)} %get-tuple-element.46.refs_0_), channel_id=1, source_target_pairs={{0,8},{4,12},{8,0},{12,4},{1,9},{5,13},{9,1},{13,5},{2,10},{6,14},... | collective-permute-start | bytes 208904 | tf_op jit(solution)/shard_map/ppermute | solution.py:33
  19.8 5.7 %collective-permute-start.7 = (bf16[16,2176]{1,0:T(8,128)(2,1)S(1)}, bf16[16,2176]{1,0:T(8,128)(2,1)S(1)}, u32[]{:S(2)}, u32[]{:S(2)}) collective-permute-start(bf16[16,2176]{1,0:T(8,128)(2,1)S(1)} %get-tuple-element.46.refs_0_), channel_id=1, source_target_pairs={{0,2},{2,0},{1,3},{3,1},{4,6},{6,4},{5,7},{7,5},{8,10},{10,8},{9,1... | collective-permute-start | bytes 208904 | tf_op jit(solution)/shard_map/ppermute | solution.py:33
  20.7 5.4 %collective-permute-start.4 = (bf16[16,2176]{1,0:T(8,128)(2,1)S(1)}, bf16[16,2176]{1,0:T(8,128)(2,1)S(1)}, u32[]{:S(2)}, u32[]{:S(2)}) collective-permute-start(bf16[16,2176]{1,0:T(8,128)(2,1)S(1)} %get-tuple-element.46.refs_0_), channel_id=1, source_target_pairs={{0,4},{4,0},{8,12},{12,8},{1,5},{5,1},{9,13},{13,9},{2,6},{6,2},{1... | collective-permute-start | bytes 208904 | tf_op jit(solution)/shard_map/ppermute | solution.py:33
  22.3 4.4 %collective-permute-start.11 = (bf16[16,2176]{1,0:T(8,128)(2,1)S(1)}, bf16[16,2176]{1,0:T(8,128)(2,1)S(1)}, u32[]{:S(2)}, u32[]{:S(2)}) collective-permute-start(bf16[16,2176]{1,0:T(8,128)(2,1)S(1)} %get-tuple-element.46.refs_0_), channel_id=1, source_target_pairs={{0,1},{1,0},{2,3},{3,2},{4,5},{5,4},{6,7},{7,6},{8,9},{9,8},{10,11... | collective-permute-start | bytes 208904 | tf_op jit(solution)/shard_map/ppermute | solution.py:33
  25.5 4.3 %collective-permute-start.6 = (bf16[16,2176]{1,0:T(8,128)(2,1)S(1)}, bf16[16,2176]{1,0:T(8,128)(2,1)S(1)}, u32[]{:S(2)}, u32[]{:S(2)}) collective-permute-start(bf16[16,2176]{1,0:T(8,128)(2,1)S(1)} %join.1.refs_2_), channel_id=1, source_target_pairs={{0,4},{4,0},{8,12},{12,8},{1,5},{5,1},{9,13},{13,9},{2,6},{6,2},{1... | collective-permute-start | bytes 208904 | tf_op jit(solution)/shard_map/ppermute | solution.py:33
  25.6 4.8 %collective-permute-start.15 = (bf16[16,2176]{1,0:T(8,128)(2,1)S(1)}, bf16[16,2176]{1,0:T(8,128)(2,1)S(1)}, u32[]{:S(2)}, u32[]{:S(2)}) collective-permute-start(bf16[16,2176]{1,0:T(8,128)(2,1)S(1)} %collective-permute-done.7.refs_4_), channel_id=1, source_target_pairs={{0,1},{1,0},{2,3},{3,2},{4,5},{5,4},{6,7},{7,6},{8,9},{9,8},{10,11... | collective-permute-start | bytes 208904 | tf_op jit(solution)/shard_map/ppermute | solution.py:33
  26.1 4.2 %collective-permute-start.12 = (bf16[16,2176]{1,0:T(8,128)(2,1)S(1)}, bf16[16,2176]{1,0:T(8,128)(2,1)S(1)}, u32[]{:S(2)}, u32[]{:S(2)}) collective-permute-start(bf16[16,2176]{1,0:T(8,128)(2,1)S(1)} %collective-permute-done.4.refs_1_), channel_id=1, source_target_pairs={{0,1},{1,0},{2,3},{3,2},{4,5},{5,4},{6,7},{7,6},{8,9},{9,8},{10,11... | collective-permute-start | bytes 208904 | tf_op jit(solution)/shard_map/ppermute | solution.py:33
  26.1 5.0 %collective-permute-start.8 = (bf16[16,2176]{1,0:T(8,128)(2,1)S(1)}, bf16[16,2176]{1,0:T(8,128)(2,1)S(1)}, u32[]{:S(2)}, u32[]{:S(2)}) collective-permute-start(bf16[16,2176]{1,0:T(8,128)(2,1)S(1)} %collective-permute-done.4.refs_1_), channel_id=1, source_target_pairs={{0,2},{2,0},{1,3},{3,1},{4,6},{6,4},{5,7},{7,5},{8,10},{10,8},{9,1... | collective-permute-start | bytes 208904 | tf_op jit(solution)/shard_map/ppermute | solution.py:33
  26.7 5.9 %collective-permute-start.9 = (bf16[16,2176]{1,0:T(8,128)(2,1)S(1)}, bf16[16,2176]{1,0:T(8,128)(2,1)S(1)}, u32[]{:S(2)}, u32[]{:S(2)}) collective-permute-start(bf16[16,2176]{1,0:T(8,128)(2,1)S(1)} %join.1.refs_2_), channel_id=1, source_target_pairs={{0,2},{2,0},{1,3},{3,1},{4,6},{6,4},{5,7},{7,5},{8,10},{10,8},{9,1... | collective-permute-start | bytes 208904 | tf_op jit(solution)/shard_map/ppermute | solution.py:33
  29.8 4.3 %collective-permute-start.10 = (bf16[16,2176]{1,0:T(8,128)(2,1)S(1)}, bf16[16,2176]{1,0:T(8,128)(2,1)S(1)}, u32[]{:S(2)}, u32[]{:S(2)}) collective-permute-start(bf16[16,2176]{1,0:T(8,128)(2,1)S(1)} %collective-permute-done.6.refs_3_), channel_id=1, source_target_pairs={{0,2},{2,0},{1,3},{3,1},{4,6},{6,4},{5,7},{7,5},{8,10},{10,8},{9,1... | collective-permute-start | bytes 208904 | tf_op jit(solution)/shard_map/ppermute | solution.py:33
  30.3 3.8 %collective-permute-start.13 = (bf16[16,2176]{1,0:T(8,128)(2,1)S(1)}, bf16[16,2176]{1,0:T(8,128)(2,1)S(1)}, u32[]{:S(2)}, u32[]{:S(2)}) collective-permute-start(bf16[16,2176]{1,0:T(8,128)(2,1)S(1)} %join.1.refs_2_), channel_id=1, source_target_pairs={{0,1},{1,0},{2,3},{3,2},{4,5},{5,4},{6,7},{7,6},{8,9},{9,8},{10,11... | collective-permute-start | bytes 208904 | tf_op jit(solution)/shard_map/ppermute | solution.py:33
  30.3 3.8 %collective-permute-start.14 = (bf16[16,2176]{1,0:T(8,128)(2,1)S(1)}, bf16[16,2176]{1,0:T(8,128)(2,1)S(1)}, u32[]{:S(2)}, u32[]{:S(2)}) collective-permute-start(bf16[16,2176]{1,0:T(8,128)(2,1)S(1)} %collective-permute-done.6.refs_3_), channel_id=1, source_target_pairs={{0,1},{1,0},{2,3},{3,2},{4,5},{5,4},{6,7},{7,6},{8,9},{9,8},{10,11... | collective-permute-start | bytes 208904 | tf_op jit(solution)/shard_map/ppermute | solution.py:33
  31.1 3.0 %collective-permute-start.16 = (bf16[16,2176]{1,0:T(8,128)(2,1)S(1)}, bf16[16,2176]{1,0:T(8,128)(2,1)S(1)}, u32[]{:S(2)}, u32[]{:S(2)}) collective-permute-start(bf16[16,2176]{1,0:T(8,128)(2,1)S(1)} %collective-permute-done.8.refs_5_), channel_id=1, source_target_pairs={{0,1},{1,0},{2,3},{3,2},{4,5},{5,4},{6,7},{7,6},{8,9},{9,8},{10,11... | collective-permute-start | bytes 208904 | tf_op jit(solution)/shard_map/ppermute | solution.py:33
  32.6 1.6 %collective-permute-start.17 = (bf16[16,2176]{1,0:T(8,128)(2,1)S(1)}, bf16[16,2176]{1,0:T(8,128)(2,1)S(1)}, u32[]{:S(2)}, u32[]{:S(2)}) collective-permute-start(bf16[16,2176]{1,0:T(8,128)(2,1)S(1)} %collective-permute-done.9.refs_6_), channel_id=1, source_target_pairs={{0,1},{1,0},{2,3},{3,2},{4,5},{5,4},{6,7},{7,6},{8,9},{9,8},{10,11... | collective-permute-start | bytes 208904 | tf_op jit(solution)/shard_map/ppermute | solution.py:33
  34.2 1.3 %collective-permute-start.18 = (bf16[16,2176]{1,0:T(8,128)(2,1)S(1)}, bf16[16,2176]{1,0:T(8,128)(2,1)S(1)}, u32[]{:S(2)}, u32[]{:S(2)}) collective-permute-start(bf16[16,2176]{1,0:T(8,128)(2,1)S(1)} %collective-permute-done.10.refs_7_), channel_id=1, source_target_pairs={{0,1},{1,0},{2,3},{3,2},{4,5},{5,4},{6,7},{7,6},{8,9},{9,8},{10,11... | collective-permute-start | bytes 208904 | tf_op jit(solution)/shard_map/ppermute | solution.py:33
  48.2 2.0 %collective-permute-start.19 = (bf16[128,2048]{1,0:T(8,128)(2,1)S(1)}, bf16[128,2048]{1,0:T(8,128)(2,1)S(1)}, u32[]{:S(2)}, u32[]{:S(2)}) collective-permute-start(bf16[128,2048]{1,0:T(8,128)(2,1)S(1)} %get-tuple-element.52), channel_id=1, source_target_pairs={{0,1},{1,0},{2,3},{3,2},{4,5},{5,4},{6,7},{7,6},{8,9},{9,8},{10,11... | collective-permute-start | bytes 1572872 | tf_op jit(solution)/shard_map/ppermute | solution.py:33
  50.3 5.0 %collective-permute-start.20 = (bf16[16,2048]{1,0:T(8,128)(2,1)S(1)}, bf16[16,2048]{1,0:T(8,128)(2,1)S(1)}, u32[]{:S(2)}, u32[]{:S(2)}) collective-permute-start(bf16[16,2048]{1,0:T(8,128)(2,1)S(1)} %get-tuple-element.54), channel_id=1, source_target_pairs={{0,2},{2,0},{1,3},{3,1},{4,6},{6,4},{5,7},{7,5},{8,10},{10,8},{9,1... | collective-permute-start | bytes 196616 | tf_op jit(solution)/shard_map/ppermute | solution.py:33
  50.8 6.3 %collective-permute-start.22 = (bf16[16,2048]{1,0:T(8,128)(2,1)S(1)}, bf16[16,2048]{1,0:T(8,128)(2,1)S(1)}, u32[]{:S(2)}, u32[]{:S(2)}) collective-permute-start(bf16[16,2048]{1,0:T(8,128)(2,1)S(1)} %get-tuple-element.56), channel_id=1, source_target_pairs={{0,2},{2,0},{1,3},{3,1},{4,6},{6,4},{5,7},{7,5},{8,10},{10,8},{9,1... | collective-permute-start | bytes 196616 | tf_op jit(solution)/shard_map/ppermute | solution.py:33
  52.4 5.8 %collective-permute-start.24 = (bf16[16,2048]{1,0:T(8,128)(2,1)S(1)}, bf16[16,2048]{1,0:T(8,128)(2,1)S(1)}, u32[]{:S(2)}, u32[]{:S(2)}) collective-permute-start(bf16[16,2048]{1,0:T(8,128)(2,1)S(1)} %get-tuple-element.58), channel_id=1, source_target_pairs={{0,2},{2,0},{1,3},{3,1},{4,6},{6,4},{5,7},{7,5},{8,10},{10,8},{9,1... | collective-permute-start | bytes 196616 | tf_op jit(solution)/shard_map/ppermute | solution.py:33
  52.9 7.1 %collective-permute-start.26 = (bf16[16,2048]{1,0:T(8,128)(2,1)S(1)}, bf16[16,2048]{1,0:T(8,128)(2,1)S(1)}, u32[]{:S(2)}, u32[]{:S(2)}) collective-permute-start(bf16[16,2048]{1,0:T(8,128)(2,1)S(1)} %get-tuple-element.60), channel_id=1, source_target_pairs={{0,2},{2,0},{1,3},{3,1},{4,6},{6,4},{5,7},{7,5},{8,10},{10,8},{9,1... | collective-permute-start | bytes 196616 | tf_op jit(solution)/shard_map/ppermute | solution.py:33
  55.3 6.3 %collective-permute-start.21 = (bf16[16,2048]{1,0:T(8,128)(2,1)S(1)}, bf16[16,2048]{1,0:T(8,128)(2,1)S(1)}, u32[]{:S(2)}, u32[]{:S(2)}) collective-permute-start(bf16[16,2048]{1,0:T(8,128)(2,1)S(1)} %sum_x3.1), channel_id=1, source_target_pairs={{0,12},{4,8},{8,4},{12,0},{1,13},{5,9},{9,5},{13,1},{2,14},{6,10},... | collective-permute-start | bytes 196616 | tf_op jit(solution)/shard_map/ppermute | solution.py:33
  57.1 6.0 %collective-permute-start.23 = (bf16[16,2048]{1,0:T(8,128)(2,1)S(1)}, bf16[16,2048]{1,0:T(8,128)(2,1)S(1)}, u32[]{:S(2)}, u32[]{:S(2)}) collective-permute-start(bf16[16,2048]{1,0:T(8,128)(2,1)S(1)} %sum_x2.1), channel_id=1, source_target_pairs={{0,8},{4,12},{8,0},{12,4},{1,9},{5,13},{9,1},{13,5},{2,10},{6,14},... | collective-permute-start | bytes 196616 | tf_op jit(solution)/shard_map/ppermute | solution.py:33
  58.1 5.0 %collective-permute-start.25 = (bf16[16,2048]{1,0:T(8,128)(2,1)S(1)}, bf16[16,2048]{1,0:T(8,128)(2,1)S(1)}, u32[]{:S(2)}, u32[]{:S(2)}) collective-permute-start(bf16[16,2048]{1,0:T(8,128)(2,1)S(1)} %sum_x1.1), channel_id=1, source_target_pairs={{0,4},{4,0},{8,12},{12,8},{1,5},{5,1},{9,13},{13,9},{2,6},{6,2},{1... | collective-permute-start | bytes 196616 | tf_op jit(solution)/shard_map/ppermute | solution.py:33

commit v14 on v13

--- a/solution.py
+++ b/solution.py
@@ -63,7 +63,10 @@
 
 def columns(source, targets, first=0):
     per = targets[0].shape[1] if targets else 0
-    return [(source.at[:, pl.ds((first + i) * per, per)], t) for i, t in enumerate(targets)]
+    return [
+        (source.at[pl.ds(0, t.shape[0]), pl.ds((first + i) * per, per)], t)
+        for i, t in enumerate(targets)
+    ]
 
 
 def prepare_kernel(
@@ -121,20 +124,20 @@
         c.wait()
 
 
-def load_kernel(part, n_after, source, *refs):
+def load_kernel(first, n_after, source, *refs):
     target, token_ref, sem = refs[n_after:]
     rows, cols = target.shape
     copy = pltpu.make_async_copy(
-        source.at[pl.ds(0, rows), pl.ds(part * cols, cols)], target, sem
+        source.at[pl.ds(first, rows), pl.ds(0, cols)], target, sem
     )
     copy.start()
     token_ref[...] = jnp.zeros_like(token_ref)
     copy.wait()
 
 
-def load(array, rows, columns, part, after, name):
+def load(array, first, rows, columns, after, name):
     return call(
-        functools.partial(load_kernel, part, len(after)),
+        functools.partial(load_kernel, first, len(after)),
         [sds((rows, columns), array.dtype), sds((8, LANES), jnp.float32)],
         [(HBM, array)] + [(ANY, a) for a in after],
         scratch=[pltpu.SemaphoreType.DMA],
@@ -267,26 +270,26 @@
             self.end_one()
 
 
-def experts_kernel(experts, capacity, tile, halves, n_rows, n_late, *refs):
+def experts_kernel(experts, capacity, tile, halves, n_rows, *refs):
     rows_in = refs[:n_rows]
-    gate_first, up_first, *gate_late = refs[n_rows : n_rows + 2 + n_late]
-    n_rows += n_late
-    gate_hbm, up_hbm, down_hbm, keep_ref, send_ref = refs[n_rows + 2 : n_rows + 7]
+    gate_top, gate_low, up_first, gate_hbm, up_hbm, down_hbm, keep_ref, send_ref = refs[
+        n_rows : n_rows + 8
+    ]
     rows_ref, pick_ref, packed_ref, hidden_ref, half_ref, sum_ref, gate_ref, up_ref, down_ref, sem = refs[
-        n_rows + 7 :
+        n_rows + 8 :
     ]
     per_expert, width = down_hbm.shape[0] // experts, down_hbm.shape[1]
     column = min(512, width)
     cuts = 4
-    early = gate_late[0].shape[0] if n_late else 0
-
-    def pieces(source, target, x, columns, first=0, cuts=cuts):
+    top = gate_top.shape[0]
+
+    def pieces(source, target, x, columns):
         rows = target.shape[0] // cuts
         pairs = []
         for i in range(cuts):
             to = pl.ds(i * rows, rows)
             if columns:
-                part = source.at[pl.ds(first + i * rows, rows), pl.ds(x * per_expert, per_expert)]
+                part = source.at[to, pl.ds(x * per_expert, per_expert)]
             else:
                 part = source.at[pl.ds(x * per_expert + i * rows, rows)]
             pairs.append((part, target.at[to]))
@@ -295,8 +298,7 @@
     groups = []
     for x in range(experts):
         if x:
-            some = (early, cuts // 2) if early else (0, cuts)
-            groups.append((("gate", x), pieces(gate_hbm, gate_ref.at[x - 1], x, True, *some)))
+            groups.append((("gate", x), pieces(gate_hbm, gate_ref.at[x - 1], x, True)))
             groups.append((("up", x), pieces(up_hbm, up_ref.at[x - 1], x, True)))
         groups.append((("down", x), pieces(down_hbm, down_ref, x, False)))
     stream = Stream(groups, sem, 4)
@@ -342,11 +344,11 @@
         for s in range(0, per_expert, tile):
             cut = slice(s, s + tile)
             stream.step(0.85)
-            if x == 1 and n_late:
-                gate = dot(packed_ref[mine, :early], gate_late[0][:, cut])
-                gate = gate + dot(packed_ref[mine, early:], gate_ref[0, :, cut])
+            if x:
+                gate = dot(packed_ref[mine, :], gate_ref[x - 1, :, cut])
             else:
-                gate = dot(packed_ref[mine, :], gate_ref[x - 1, :, cut] if x else gate_first[:, cut])
+                gate = dot(packed_ref[mine, :top], gate_top[:, cut])
+                gate = gate + dot(packed_ref[mine, top:], gate_low[:, cut])
             half = 0.5 * gate
             half_ref[:, cut] = half + half * jnp.tanh(half)
         if x:
@@ -429,7 +431,7 @@
             sds((own_rows, width), f32),
             sds((own_rows, LANES), bf16),
         ]
-        + [sds((width, per_expert), bf16)],
+        + [sds((width // 2, per_expert), bf16)],
         [
             (HBM, a)
             for a in (
@@ -446,7 +448,7 @@
         ],
         vmem=6,
         name="prepare",
-        cost_us=4.0,
+        cost_us=3.0,
     )
     half = block // pp_count
     keep, send = call(
@@ -462,7 +464,7 @@
         [keep] + [xor_swap(send, "pp", 1)], [own_rows], [own_rows] * (tp_count - 1), "sum_cores"
     )
     got = [xor_swap(sends[k - 1], "tp", k) for k in range(1, tp_count)]
-    up_v, token = load(w_up[0], width, per_expert, 0, [own], "load_up")
+    up_v, token = load(w_up[0], 0, width, per_expert, [own], "load_up")
     stream, normed = call(
         functools.partial(norm_kernel, tp_count),
         [sds((own_rows, width), f32), sds((own_rows, width + LANES), bf16)],
@@ -473,10 +475,8 @@
 
     groups = min(4, sec_count)
     near = {k: xor_swap(normed, "sec", k) if k else normed for k in range(0, sec_count, 2)}
-    gate_late, late_rows = [], 0
-    if experts == 2 and sec_count > 2:
-        gate_late, token = load(w_gate[0], width // 2, per_expert, 1, [normed], "load_gate")
-        gate_late, late_rows = [gate_late], width // 2
+    gate_late, token = load(w_gate[0], width // 2, width // 2, per_expert, [normed], "load_gate")
+    if sec_count > 2:
         near[2] = join([near[2]], "join", [token])
     near.update({k + 1: xor_swap(near[k], "sec", 1) for k in list(near) if k + 1 < sec_count})
     near = [near[k] for k in range(sec_count)]
@@ -498,9 +498,9 @@
     tile = min(512, down.shape[0] // experts)
     kept = count // pp_count
     keep, send = call(
-        functools.partial(experts_kernel, experts, capacity, tile, halves, len(rows), len(gate_late)),
+        functools.partial(experts_kernel, experts, capacity, tile, halves, len(rows)),
         [sds((kept, width), f32), sds((count - kept, width), bf16)],
-        [(VMEM, a) for a in (*rows, *gate_v, up_v, *gate_late)]
+        [(VMEM, a) for a in (*rows, *gate_v, gate_late, up_v)]
         + [(HBM, a) for a in (w_gate[0], w_up[0], down)],
         scratch=[
             pltpu.VMEM((count, width + LANES), bf16),
@@ -509,12 +509,12 @@
             pltpu.VMEM((experts * capacity, down.shape[0] // experts), bf16),
             pltpu.VMEM((capacity, per_expert), f32),
             pltpu.VMEM((capacity, width), f32),
-            pltpu.VMEM((max(1, experts - 1), width - late_rows, per_expert), bf16),
+            pltpu.VMEM((max(1, experts - 1), width, per_expert), bf16),
             pltpu.VMEM((max(1, experts - 1), width, per_expert), bf16),
             pltpu.VMEM((per_expert, width), bf16),
             pltpu.SemaphoreType.DMA((4 * (3 * experts - 2),)),
         ],
-        vmem=30,
+        vmem=33,
         name="experts",
         cost_us=12.0,
     )

time: 64.1 us -> 64.1 us (level)
  starting transfers between devices: 22.2 us -> 24.2 us
  Pallas kernels: 25.7 us -> 24.7 us
  waiting for transfers between devices: 14.9 us -> 14 us
    ppermute x25, starting transfers between devices: 16.6 us -> 18.6 us  [xor_swap(): return lax.ppermute(x, axis, [(i, i ^ k) for i in range(n)])]
    ppermute x25, waiting for transfers between devices: 14.9 us -> 13.4 us  [xor_swap(): return lax.ppermute(x, axis, [(i, i ^ k) for i in range(n)])]
    pallas_call x13, Pallas kernels: 25.7 us -> 24.7 us  [call(): pl.pallas_call(kernel, out_shape=out_shape, in_specs=[s for s, _ in args]...]
  transfers between devices with their start and end apart: 27 -> 27, of which waited for: 12 -> 13; matrix products, arithmetic and copies ran while one was open for 0% -> 0% of each run, Pallas kernels for 17% -> 15%
where the time goes in v14:
time: 64.1 us; the launch traced here: 63.9 us
  Pallas kernels  24.7 us (39%)
  starting transfers between devices  24.2 us (38%)
  waiting for transfers between devices  14 us (22%)
  local copies, waits for them, and re-layouts  0.78 us (1%)
    pallas_call x13, Pallas kernels, call(): pl.pallas_call(kernel, out_shape=out_shape, in_specs=[s for s, _ in args]...  24.7 us
    ppermute x25, starting transfers between devices, xor_swap(): return lax.ppermute(x, axis, [(i, i ^ k) for i in range(n)])  18.6 us
    ppermute x25, waiting for transfers between devices, xor_swap(): return lax.ppermute(x, axis, [(i, i ^ k) for i in range(n)])  13.4 us
    ppermute x2, starting transfers between devices, per_device(): lax.ppermute(kv, 'sec', [(i, (i + k) % sec_count) for i in range(sec_coun...  5.67 us
  transfers between devices with their start and end apart: 27, of which 13 were waited for; matrix products, arithmetic and copies ran while one was open for 0% of the time, Pallas kernels for 15%

profile of v14, /device:TPU:0, one launch (start us, length us, event | category | flops | bytes accessed | tf_op | source)
XLA Modules:
  0.0 63.9 jit_solution(12712860737081654929)
XLA Ops:
  0.0 0.8 %constant_dynamic-slice_fusion = (bf16[64,256]{1,0:T(8,128)(2,1)S(1)}, bf16[64,256]{1,0:T(8,128)(2,1)S(1)}) fusion(bf16[64,512]{1,0:T(8,128)(2,1)} %param.14, s32[]{:T(128)S(6)} %select_n.10, bf16[64,512]{1,0:T(8,128)(2,1)} %param.13), kind=kLoop, calls=%fused_computation.1 | loop fusion | bytes 131076 | tf_op jit(solution)/shard_map/dynamic_slice | solution.py:412
  0.8 3.1 %collective-permute-start.1 = (bf16[64,512]{1,0:T(8,128)(2,1)S(1)}, bf16[64,512]{1,0:T(8,128)(2,1)S(1)}, u32[]{:S(2)}, u32[]{:S(2)}) collective-permute-start(bf16[64,512]{1,0:T(8,128)(2,1)S(1)} %pad_maximum_fusion.refs_2_), channel_id=1, source_target_pairs={{0,4},{4,8},{8,12},{12,0},{1,5},{5,9},{9,13},{13,1},{2,6},{6,10},{... | collective-permute-start | bytes 196616 | tf_op jit(solution)/shard_map/ppermute | solution.py:416
  3.9 2.6 %collective-permute-start = (bf16[64,512]{1,0:T(8,128)(2,1)S(1)}, bf16[64,512]{1,0:T(8,128)(2,1)S(1)}, u32[]{:S(2)}, u32[]{:S(2)}) collective-permute-start(bf16[64,512]{1,0:T(8,128)(2,1)S(1)} %pad_maximum_fusion.refs_2_), channel_id=1, source_target_pairs={{0,8},{4,12},{8,0},{12,4},{1,9},{5,13},{9,1},{13,5},{2,10},{6,14},... | collective-permute-start | bytes 196616 | tf_op jit(solution)/shard_map/ppermute | solution.py:416
  6.5 3.7 %prepare.1 = (bf16[64,1024]{1,0:T(8,128)(2,1)S(1)}, bf16[1024,2048]{1,0:T(8,128)(2,1)S(1)}, f32[1,2048]{1,0:T(1,128)S(1)}, f32[64,192]{1,0:T(8,128)S(1)}, bf16[6...) custom-call(s32[8]{0:T(128)} %lengths_hbm.1, ...), custom_call_target="tpu_custom_call" | custom-call | bytes 10200000 | tf_op jit(solution)/shard_map/prepare/pallas_call | solution.py:41
  10.2 0.6 collective-permute-done.refs_0_
  10.8 1.4 %attention.1 = (f32[32,2048]{1,0:T(8,128)S(1)}, bf16[32,2048]{1,0:T(8,128)(2,1)S(1)}) custom-call(bf16[64,1024]{1,0:T(8,128)(2,1)S(1)} %get-tuple-element.36.q_ref, f32[64,192]{1,0:T(8,128)S(1)} %get-tuple-element.37.mask_ref, bf16[64,64]{1,0:T(8,128)(2,1)S(1)} %get-tuple-element.38.order_ref, bf16[64,512]{1,0:T(8,128)(2,1)S(1)} %collective-permute-done.refs_0_, ...), custom_call_target="tpu_custom_call" | custom-call | bytes 8160000 | tf_op jit(solution)/shard_map/attention/pallas_call | solution.py:41
  12.3 1.3 %collective-permute-done.2.refs_1_ = bf16[32,2048]{1,0:T(8,128)(2,1)S(1)} collective-permute-done((bf16[32,2048]{1,0:T(8,128)(2,1)S(1)}, bf16[32,2048]{1,0:T(8,128)(2,1)S(1)}, u32[]{:S(2)}, u32[]{:S(2)}) %collective-permute-start.2) | collective-permute-done | bytes 131104 | tf_op jit(solution)/shard_map/ppermute | solution.py:33
  13.7 1.6 %collective-permute-start.3 = (bf16[16,2048]{1,0:T(8,128)(2,1)S(1)}, bf16[16,2048]{1,0:T(8,128)(2,1)S(1)}, u32[]{:S(2)}, u32[]{:S(2)}) collective-permute-start(bf16[16,2048]{1,0:T(8,128)(2,1)S(1)} %get-tuple-element.43), channel_id=1, source_target_pairs={{0,2},{2,0},{1,3},{3,1},{4,6},{6,4},{5,7},{7,5},{8,10},{10,8},{9,1... | collective-permute-start | bytes 196616 | tf_op jit(solution)/shard_map/ppermute | solution.py:33
  15.2 3.4 %load_up.1 = (bf16[2048,2048]{1,0:T(8,128)(2,1)S(1)}, f32[8,128]{1,0:T(8,128)S(1)}) custom-call(bf16[2048,4096]{1,0:T(8,128)(2,1)} %bitcast.9, f32[16,2048]{1,0:T(8,128)S(1)} %get-tuple-element.42.refs_0_), custom_call_target="tpu_custom_call" | custom-call | bytes 8388607 | tf_op jit(solution)/shard_map/load_up/pallas_call | solution.py:41
  18.8 1.0 %collective-permute-start.5 = (bf16[16,2176]{1,0:T(8,128)(2,1)S(1)}, bf16[16,2176]{1,0:T(8,128)(2,1)S(1)}, u32[]{:S(2)}, u32[]{:S(2)}) collective-permute-start(bf16[16,2176]{1,0:T(8,128)(2,1)S(1)} %get-tuple-element.46.refs_0_), channel_id=1, source_target_pairs={{0,8},{4,12},{8,0},{12,4},{1,9},{5,13},{9,1},{13,5},{2,10},{6,14},... | collective-permute-start | bytes 208904 | tf_op jit(solution)/shard_map/ppermute | solution.py:33
  19.8 0.9 %collective-permute-start.7 = (bf16[16,2176]{1,0:T(8,128)(2,1)S(1)}, bf16[16,2176]{1,0:T(8,128)(2,1)S(1)}, u32[]{:S(2)}, u32[]{:S(2)}) collective-permute-start(bf16[16,2176]{1,0:T(8,128)(2,1)S(1)} %get-tuple-element.46.refs_0_), channel_id=1, source_target_pairs={{0,2},{2,0},{1,3},{3,1},{4,6},{6,4},{5,7},{7,5},{8,10},{10,8},{9,1... | collective-permute-start | bytes 208904 | tf_op jit(solution)/shard_map/ppermute | solution.py:33
  20.6 1.6 %collective-permute-start.4 = (bf16[16,2176]{1,0:T(8,128)(2,1)S(1)}, bf16[16,2176]{1,0:T(8,128)(2,1)S(1)}, u32[]{:S(2)}, u32[]{:S(2)}) collective-permute-start(bf16[16,2176]{1,0:T(8,128)(2,1)S(1)} %get-tuple-element.46.refs_0_), channel_id=1, source_target_pairs={{0,4},{4,0},{8,12},{12,8},{1,5},{5,1},{9,13},{13,9},{2,6},{6,2},{1... | collective-permute-start | bytes 208904 | tf_op jit(solution)/shard_map/ppermute | solution.py:33
  22.3 2.2 %load_gate.1 = (bf16[1024,2048]{1,0:T(8,128)(2,1)S(1)}, f32[8,128]{1,0:T(8,128)S(1)}) custom-call(bf16[2048,4096]{1,0:T(8,128)(2,1)} %bitcast.7, bf16[16,2176]{1,0:T(8,128)(2,1)S(1)} %get-tuple-element.46.refs_0_), custom_call_target="tpu_custom_call" | custom-call | bytes 4194303 | tf_op jit(solution)/shard_map/load_gate/pallas_call | solution.py:41
  25.5 1.2 %collective-permute-start.8 = (bf16[16,2176]{1,0:T(8,128)(2,1)S(1)}, bf16[16,2176]{1,0:T(8,128)(2,1)S(1)}, u32[]{:S(2)}, u32[]{:S(2)}) collective-permute-start(bf16[16,2176]{1,0:T(8,128)(2,1)S(1)} %collective-permute-done.4.refs_1_), channel_id=1, source_target_pairs={{0,2},{2,0},{1,3},{3,1},{4,6},{6,4},{5,7},{7,5},{8,10},{10,8},{9,1... | collective-permute-start | bytes 208904 | tf_op jit(solution)/shard_map/ppermute | solution.py:33
  26.6 0.9 %collective-permute-start.9 = (bf16[16,2176]{1,0:T(8,128)(2,1)S(1)}, bf16[16,2176]{1,0:T(8,128)(2,1)S(1)}, u32[]{:S(2)}, u32[]{:S(2)}) collective-permute-start(bf16[16,2176]{1,0:T(8,128)(2,1)S(1)} %join.1.refs_2_), channel_id=1, source_target_pairs={{0,2},{2,0},{1,3},{3,1},{4,6},{6,4},{5,7},{7,5},{8,10},{10,8},{9,1... | collective-permute-start | bytes 208904 | tf_op jit(solution)/shard_map/ppermute | solution.py:33
  27.5 1.7 %collective-permute-done.6.refs_3_ = bf16[16,2176]{1,0:T(8,128)(2,1)S(1)} collective-permute-done((bf16[16,2176]{1,0:T(8,128)(2,1)S(1)}, bf16[16,2176]{1,0:T(8,128)(2,1)S(1)}, u32[]{:S(2)}, u32[]{:S(2)}) %collective-permute-start.6) | collective-permute-done | bytes 69664 | tf_op jit(solution)/shard_map/ppermute | solution.py:33
  29.2 1.2 %collective-permute-start.10 = (bf16[16,2176]{1,0:T(8,128)(2,1)S(1)}, bf16[16,2176]{1,0:T(8,128)(2,1)S(1)}, u32[]{:S(2)}, u32[]{:S(2)}) collective-permute-start(bf16[16,2176]{1,0:T(8,128)(2,1)S(1)} %collective-permute-done.6.refs_3_), channel_id=1, source_target_pairs={{0,2},{2,0},{1,3},{3,1},{4,6},{6,4},{5,7},{7,5},{8,10},{10,8},{9,1... | collective-permute-start | bytes 208904 | tf_op jit(solution)/shard_map/ppermute | solution.py:33
  31.4 2.1 %collective-permute-done.10.refs_7_ = bf16[16,2176]{1,0:T(8,128)(2,1)S(1)} collective-permute-done((bf16[16,2176]{1,0:T(8,128)(2,1)S(1)}, bf16[16,2176]{1,0:T(8,128)(2,1)S(1)}, u32[]{:S(2)}, u32[]{:S(2)}) %collective-permute-start.10) | collective-permute-done | bytes 69664 | tf_op jit(solution)/shard_map/ppermute | solution.py:33
  33.5 1.2 %collective-permute-done.18.refs_15_ = bf16[16,2176]{1,0:T(8,128)(2,1)S(1)} collective-permute-done((bf16[16,2176]{1,0:T(8,128)(2,1)S(1)}, bf16[16,2176]{1,0:T(8,128)(2,1)S(1)}, u32[]{:S(2)}, u32[]{:S(2)}) %collective-permute-start.18) | collective-permute-done | bytes 69664 | tf_op jit(solution)/shard_map/ppermute | solution.py:33
  34.7 13.0 %experts.1 = (f32[128,2048]{1,0:T(8,128)S(1)}, bf16[128,2048]{1,0:T(8,128)(2,1)S(1)}) custom-call(bf16[16,2176]{1,0:T(8,128)(2,1)S(1)} %get-tuple-element.46.refs_0_, bf16[16,2176]{1,0:T(8,128)(2,1)S(1)} %collective-permute-done.4.refs_1_, bf16[16,2176]{1,0:T(8,128)(2,1)S(1)} %join.1.refs_2_, bf16[16,2176]{1,0:T(8,128)(2,1)S(1)} %collective-permute-done.6.refs_3_, ...), custom_call_target="tpu_custom_call" | custom-call | bytes 40800000 | tf_op jit(solution)/shard_map/experts/pallas_call | solution.py:41
  48.0 1.8 %collective-permute-done.19.refs_1_ = bf16[128,2048]{1,0:T(8,128)(2,1)S(1)} collective-permute-done((bf16[128,2048]{1,0:T(8,128)(2,1)S(1)}, bf16[128,2048]{1,0:T(8,128)(2,1)S(1)}, u32[]{:S(2)}, u32[]{:S(2)}) %collective-permute-start.19) | collective-permute-done | bytes 524320 | tf_op jit(solution)/shard_map/ppermute | solution.py:33
  49.8 1.2 %collective-permute-start.20 = (bf16[16,2048]{1,0:T(8,128)(2,1)S(1)}, bf16[16,2048]{1,0:T(8,128)(2,1)S(1)}, u32[]{:S(2)}, u32[]{:S(2)}) collective-permute-start(bf16[16,2048]{1,0:T(8,128)(2,1)S(1)} %get-tuple-element.54), channel_id=1, source_target_pairs={{0,2},{2,0},{1,3},{3,1},{4,6},{6,4},{5,7},{7,5},{8,10},{10,8},{9,1... | collective-permute-start | bytes 196616 | tf_op jit(solution)/shard_map/ppermute | solution.py:33
  51.0 0.9 %collective-permute-start.22 = (bf16[16,2048]{1,0:T(8,128)(2,1)S(1)}, bf16[16,2048]{1,0:T(8,128)(2,1)S(1)}, u32[]{:S(2)}, u32[]{:S(2)}) collective-permute-start(bf16[16,2048]{1,0:T(8,128)(2,1)S(1)} %get-tuple-element.56), channel_id=1, source_target_pairs={{0,2},{2,0},{1,3},{3,1},{4,6},{6,4},{5,7},{7,5},{8,10},{10,8},{9,1... | collective-permute-start | bytes 196616 | tf_op jit(solution)/shard_map/ppermute | solution.py:33
  51.9 1.2 %collective-permute-start.24 = (bf16[16,2048]{1,0:T(8,128)(2,1)S(1)}, bf16[16,2048]{1,0:T(8,128)(2,1)S(1)}, u32[]{:S(2)}, u32[]{:S(2)}) collective-permute-start(bf16[16,2048]{1,0:T(8,128)(2,1)S(1)} %get-tuple-element.58), channel_id=1, source_target_pairs={{0,2},{2,0},{1,3},{3,1},{4,6},{6,4},{5,7},{7,5},{8,10},{10,8},{9,1... | collective-permute-start | bytes 196616 | tf_op jit(solution)/shard_map/ppermute | solution.py:33
  53.1 0.9 %collective-permute-start.26 = (bf16[16,2048]{1,0:T(8,128)(2,1)S(1)}, bf16[16,2048]{1,0:T(8,128)(2,1)S(1)}, u32[]{:S(2)}, u32[]{:S(2)}) collective-permute-start(bf16[16,2048]{1,0:T(8,128)(2,1)S(1)} %get-tuple-element.60), channel_id=1, source_target_pairs={{0,2},{2,0},{1,3},{3,1},{4,6},{6,4},{5,7},{7,5},{8,10},{10,8},{9,1... | collective-permute-start | bytes 196616 | tf_op jit(solution)/shard_map/ppermute | solution.py:33
  53.9 0.8 %collective-permute-done.20.refs_1_ = bf16[16,2048]{1,0:T(8,128)(2,1)S(1)} collective-permute-done((bf16[16,2048]{1,0:T(8,128)(2,1)S(1)}, bf16[16,2048]{1,0:T(8,128)(2,1)S(1)}, u32[]{:S(2)}, u32[]{:S(2)}) %collective-permute-start.20) | collective-permute-done | bytes 65568 | tf_op jit(solution)/shard_map/ppermute | solution.py:33
  54.8 2.3 %collective-permute-start.21 = (bf16[16,2048]{1,0:T(8,128)(2,1)S(1)}, bf16[16,2048]{1,0:T(8,128)(2,1)S(1)}, u32[]{:S(2)}, u32[]{:S(2)}) collective-permute-start(bf16[16,2048]{1,0:T(8,128)(2,1)S(1)} %sum_x3.1), channel_id=1, source_target_pairs={{0,12},{4,8},{8,4},{12,0},{1,13},{5,9},{9,5},{13,1},{2,14},{6,10},... | collective-permute-start | bytes 196616 | tf_op jit(solution)/shard_map/ppermute | solution.py:33
  57.1 1.0 %collective-permute-start.23 = (bf16[16,2048]{1,0:T(8,128)(2,1)S(1)}, bf16[16,2048]{1,0:T(8,128)(2,1)S(1)}, u32[]{:S(2)}, u32[]{:S(2)}) collective-permute-start(bf16[16,2048]{1,0:T(8,128)(2,1)S(1)} %sum_x2.1), channel_id=1, source_target_pairs={{0,8},{4,12},{8,0},{12,4},{1,9},{5,13},{9,1},{13,5},{2,10},{6,14},... | collective-permute-start | bytes 196616 | tf_op jit(solution)/shard_map/ppermute | solution.py:33
  58.2 1.3 %collective-permute-start.25 = (bf16[16,2048]{1,0:T(8,128)(2,1)S(1)}, bf16[16,2048]{1,0:T(8,128)(2,1)S(1)}, u32[]{:S(2)}, u32[]{:S(2)}) collective-permute-start(bf16[16,2048]{1,0:T(8,128)(2,1)S(1)} %sum_x1.1), channel_id=1, source_target_pairs={{0,4},{4,0},{8,12},{12,8},{1,5},{5,1},{9,13},{13,9},{2,6},{6,2},{1... | collective-permute-start | bytes 196616 | tf_op jit(solution)/shard_map/ppermute | solution.py:33
  59.4 2.1 %collective-permute-done.21.refs_1_ = bf16[16,2048]{1,0:T(8,128)(2,1)S(1)} collective-permute-done((bf16[16,2048]{1,0:T(8,128)(2,1)S(1)}, bf16[16,2048]{1,0:T(8,128)(2,1)S(1)}, u32[]{:S(2)}, u32[]{:S(2)}) %collective-permute-start.21) | collective-permute-done | bytes 65568 | tf_op jit(solution)/shard_map/ppermute | solution.py:33
  61.5 1.6 %collective-permute-done.23.refs_2_ = bf16[16,2048]{1,0:T(8,128)(2,1)S(1)} collective-permute-done((bf16[16,2048]{1,0:T(8,128)(2,1)S(1)}, bf16[16,2048]{1,0:T(8,128)(2,1)S(1)}, u32[]{:S(2)}, u32[]{:S(2)}) %collective-permute-start.23) | collective-permute-done | bytes 65568 | tf_op jit(solution)/shard_map/ppermute | solution.py:33
  63.2 0.7 %total.1 = bf16[16,2048]{1,0:T(8,128)(2,1)} custom-call(f32[16,2048]{1,0:T(8,128)S(1)} %get-tuple-element.45.refs_0_, bf16[16,2048]{1,0:T(8,128)(2,1)S(1)} %collective-permute-done.21.refs_1_, bf16[16,2048]{1,0:T(8,128)(2,1)S(1)} %collective-permute-done.23.refs_2_, bf16[16,2048]{1,0:T(8,128)(2,1)S(1)} %collective-permute-done.25.refs_3_, ...), custom_call_target="tpu_custom_call" | custom-call | bytes 680000 | tf_op jit(solution)/shard_map/total/pallas_call | solution.py:41
  (37 shorter events, 2.8 us)
Async XLA Ops:
  0.8 9.4 %collective-permute-start.1 = (bf16[64,512]{1,0:T(8,128)(2,1)S(1)}, bf16[64,512]{1,0:T(8,128)(2,1)S(1)}, u32[]{:S(2)}, u32[]{:S(2)}) collective-permute-start(bf16[64,512]{1,0:T(8,128)(2,1)S(1)} %pad_maximum_fusion.refs_2_), channel_id=1, source_target_pairs={{0,4},{4,8},{8,12},{12,0},{1,5},{5,9},{9,13},{13,1},{2,6},{6,10},{... | collective-permute-start | bytes 196616 | tf_op jit(solution)/shard_map/ppermute | solution.py:416
  3.9 6.9 %collective-permute-start = (bf16[64,512]{1,0:T(8,128)(2,1)S(1)}, bf16[64,512]{1,0:T(8,128)(2,1)S(1)}, u32[]{:S(2)}, u32[]{:S(2)}) collective-permute-start(bf16[64,512]{1,0:T(8,128)(2,1)S(1)} %pad_maximum_fusion.refs_2_), channel_id=1, source_target_pairs={{0,8},{4,12},{8,0},{12,4},{1,9},{5,13},{9,1},{13,5},{2,10},{6,14},... | collective-permute-start | bytes 196616 | tf_op jit(solution)/shard_map/ppermute | solution.py:416
  12.2 1.4 %collective-permute-start.2 = (bf16[32,2048]{1,0:T(8,128)(2,1)S(1)}, bf16[32,2048]{1,0:T(8,128)(2,1)S(1)}, u32[]{:S(2)}, u32[]{:S(2)}) collective-permute-start(bf16[32,2048]{1,0:T(8,128)(2,1)S(1)} %get-tuple-element.41), channel_id=1, source_target_pairs={{0,1},{1,0},{2,3},{3,2},{4,5},{5,4},{6,7},{7,6},{8,9},{9,8},{10,11... | collective-permute-start | bytes 393224 | tf_op jit(solution)/shard_map/ppermute | solution.py:33
  13.7 5.0 %collective-permute-start.3 = (bf16[16,2048]{1,0:T(8,128)(2,1)S(1)}, bf16[16,2048]{1,0:T(8,128)(2,1)S(1)}, u32[]{:S(2)}, u32[]{:S(2)}) collective-permute-start(bf16[16,2048]{1,0:T(8,128)(2,1)S(1)} %get-tuple-element.43), channel_id=1, source_target_pairs={{0,2},{2,0},{1,3},{3,1},{4,6},{6,4},{5,7},{7,5},{8,10},{10,8},{9,1... | collective-permute-start | bytes 196616 | tf_op jit(solution)/shard_map/ppermute | solution.py:33
  18.8 5.8 %collective-permute-start.5 = (bf16[16,2176]{1,0:T(8,128)(2,1)S(1)}, bf16[16,2176]{1,0:T(8,128)(2,1)S(1)}, u32[]{:S(2)}, u32[]{:S(2)}) collective-permute-start(bf16[16,2176]{1,0:T(8,128)(2,1)S(1)} %get-tuple-element.46.refs_0_), channel_id=1, source_target_pairs={{0,8},{4,12},{8,0},{12,4},{1,9},{5,13},{9,1},{13,5},{2,10},{6,14},... | collective-permute-start | bytes 208904 | tf_op jit(solution)/shard_map/ppermute | solution.py:33
  19.8 5.2 %collective-permute-start.7 = (bf16[16,2176]{1,0:T(8,128)(2,1)S(1)}, bf16[16,2176]{1,0:T(8,128)(2,1)S(1)}, u32[]{:S(2)}, u32[]{:S(2)}) collective-permute-start(bf16[16,2176]{1,0:T(8,128)(2,1)S(1)} %get-tuple-element.46.refs_0_), channel_id=1, source_target_pairs={{0,2},{2,0},{1,3},{3,1},{4,6},{6,4},{5,7},{7,5},{8,10},{10,8},{9,1... | collective-permute-start | bytes 208904 | tf_op jit(solution)/shard_map/ppermute | solution.py:33
  20.6 4.7 %collective-permute-start.4 = (bf16[16,2176]{1,0:T(8,128)(2,1)S(1)}, bf16[16,2176]{1,0:T(8,128)(2,1)S(1)}, u32[]{:S(2)}, u32[]{:S(2)}) collective-permute-start(bf16[16,2176]{1,0:T(8,128)(2,1)S(1)} %get-tuple-element.46.refs_0_), channel_id=1, source_target_pairs={{0,4},{4,0},{8,12},{12,8},{1,5},{5,1},{9,13},{13,9},{2,6},{6,2},{1... | collective-permute-start | bytes 208904 | tf_op jit(solution)/shard_map/ppermute | solution.py:33
  22.3 4.4 %collective-permute-start.11 = (bf16[16,2176]{1,0:T(8,128)(2,1)S(1)}, bf16[16,2176]{1,0:T(8,128)(2,1)S(1)}, u32[]{:S(2)}, u32[]{:S(2)}) collective-permute-start(bf16[16,2176]{1,0:T(8,128)(2,1)S(1)} %get-tuple-element.46.refs_0_), channel_id=1, source_target_pairs={{0,1},{1,0},{2,3},{3,2},{4,5},{5,4},{6,7},{7,6},{8,9},{9,8},{10,11... | collective-permute-start | bytes 208904 | tf_op jit(solution)/shard_map/ppermute | solution.py:33
  24.6 4.6 %collective-permute-start.6 = (bf16[16,2176]{1,0:T(8,128)(2,1)S(1)}, bf16[16,2176]{1,0:T(8,128)(2,1)S(1)}, u32[]{:S(2)}, u32[]{:S(2)}) collective-permute-start(bf16[16,2176]{1,0:T(8,128)(2,1)S(1)} %join.1.refs_2_), channel_id=1, source_target_pairs={{0,4},{4,0},{8,12},{12,8},{1,5},{5,1},{9,13},{13,9},{2,6},{6,2},{1... | collective-permute-start | bytes 208904 | tf_op jit(solution)/shard_map/ppermute | solution.py:33
  24.9 5.4 %collective-permute-start.15 = (bf16[16,2176]{1,0:T(8,128)(2,1)S(1)}, bf16[16,2176]{1,0:T(8,128)(2,1)S(1)}, u32[]{:S(2)}, u32[]{:S(2)}) collective-permute-start(bf16[16,2176]{1,0:T(8,128)(2,1)S(1)} %collective-permute-done.7.refs_4_), channel_id=1, source_target_pairs={{0,1},{1,0},{2,3},{3,2},{4,5},{5,4},{6,7},{7,6},{8,9},{9,8},{10,11... | collective-permute-start | bytes 208904 | tf_op jit(solution)/shard_map/ppermute | solution.py:33
  25.3 5.0 %collective-permute-start.12 = (bf16[16,2176]{1,0:T(8,128)(2,1)S(1)}, bf16[16,2176]{1,0:T(8,128)(2,1)S(1)}, u32[]{:S(2)}, u32[]{:S(2)}) collective-permute-start(bf16[16,2176]{1,0:T(8,128)(2,1)S(1)} %collective-permute-done.4.refs_1_), channel_id=1, source_target_pairs={{0,1},{1,0},{2,3},{3,2},{4,5},{5,4},{6,7},{7,6},{8,9},{9,8},{10,11... | collective-permute-start | bytes 208904 | tf_op jit(solution)/shard_map/ppermute | solution.py:33
  25.5 5.4 %collective-permute-start.8 = (bf16[16,2176]{1,0:T(8,128)(2,1)S(1)}, bf16[16,2176]{1,0:T(8,128)(2,1)S(1)}, u32[]{:S(2)}, u32[]{:S(2)}) collective-permute-start(bf16[16,2176]{1,0:T(8,128)(2,1)S(1)} %collective-permute-done.4.refs_1_), channel_id=1, source_target_pairs={{0,2},{2,0},{1,3},{3,1},{4,6},{6,4},{5,7},{7,5},{8,10},{10,8},{9,1... | collective-permute-start | bytes 208904 | tf_op jit(solution)/shard_map/ppermute | solution.py:33
  26.6 4.7 %collective-permute-start.9 = (bf16[16,2176]{1,0:T(8,128)(2,1)S(1)}, bf16[16,2176]{1,0:T(8,128)(2,1)S(1)}, u32[]{:S(2)}, u32[]{:S(2)}) collective-permute-start(bf16[16,2176]{1,0:T(8,128)(2,1)S(1)} %join.1.refs_2_), channel_id=1, source_target_pairs={{0,2},{2,0},{1,3},{3,1},{4,6},{6,4},{5,7},{7,5},{8,10},{10,8},{9,1... | collective-permute-start | bytes 208904 | tf_op jit(solution)/shard_map/ppermute | solution.py:33
  29.2 4.3 %collective-permute-start.10 = (bf16[16,2176]{1,0:T(8,128)(2,1)S(1)}, bf16[16,2176]{1,0:T(8,128)(2,1)S(1)}, u32[]{:S(2)}, u32[]{:S(2)}) collective-permute-start(bf16[16,2176]{1,0:T(8,128)(2,1)S(1)} %collective-permute-done.6.refs_3_), channel_id=1, source_target_pairs={{0,2},{2,0},{1,3},{3,1},{4,6},{6,4},{5,7},{7,5},{8,10},{10,8},{9,1... | collective-permute-start | bytes 208904 | tf_op jit(solution)/shard_map/ppermute | solution.py:33
  30.3 3.1 %collective-permute-start.13 = (bf16[16,2176]{1,0:T(8,128)(2,1)S(1)}, bf16[16,2176]{1,0:T(8,128)(2,1)S(1)}, u32[]{:S(2)}, u32[]{:S(2)}) collective-permute-start(bf16[16,2176]{1,0:T(8,128)(2,1)S(1)} %join.1.refs_2_), channel_id=1, source_target_pairs={{0,1},{1,0},{2,3},{3,2},{4,5},{5,4},{6,7},{7,6},{8,9},{9,8},{10,11... | collective-permute-start | bytes 208904 | tf_op jit(solution)/shard_map/ppermute | solution.py:33
  30.3 3.2 %collective-permute-start.14 = (bf16[16,2176]{1,0:T(8,128)(2,1)S(1)}, bf16[16,2176]{1,0:T(8,128)(2,1)S(1)}, u32[]{:S(2)}, u32[]{:S(2)}) collective-permute-start(bf16[16,2176]{1,0:T(8,128)(2,1)S(1)} %collective-permute-done.6.refs_3_), channel_id=1, source_target_pairs={{0,1},{1,0},{2,3},{3,2},{4,5},{5,4},{6,7},{7,6},{8,9},{9,8},{10,11... | collective-permute-start | bytes 208904 | tf_op jit(solution)/shard_map/ppermute | solution.py:33
  30.9 2.6 %collective-permute-start.16 = (bf16[16,2176]{1,0:T(8,128)(2,1)S(1)}, bf16[16,2176]{1,0:T(8,128)(2,1)S(1)}, u32[]{:S(2)}, u32[]{:S(2)}) collective-permute-start(bf16[16,2176]{1,0:T(8,128)(2,1)S(1)} %collective-permute-done.8.refs_5_), channel_id=1, source_target_pairs={{0,1},{1,0},{2,3},{3,2},{4,5},{5,4},{6,7},{7,6},{8,9},{9,8},{10,11... | collective-permute-start | bytes 208904 | tf_op jit(solution)/shard_map/ppermute | solution.py:33
  31.4 2.1 %collective-permute-start.17 = (bf16[16,2176]{1,0:T(8,128)(2,1)S(1)}, bf16[16,2176]{1,0:T(8,128)(2,1)S(1)}, u32[]{:S(2)}, u32[]{:S(2)}) collective-permute-start(bf16[16,2176]{1,0:T(8,128)(2,1)S(1)} %collective-permute-done.9.refs_6_), channel_id=1, source_target_pairs={{0,1},{1,0},{2,3},{3,2},{4,5},{5,4},{6,7},{7,6},{8,9},{9,8},{10,11... | collective-permute-start | bytes 208904 | tf_op jit(solution)/shard_map/ppermute | solution.py:33
  33.5 1.3 %collective-permute-start.18 = (bf16[16,2176]{1,0:T(8,128)(2,1)S(1)}, bf16[16,2176]{1,0:T(8,128)(2,1)S(1)}, u32[]{:S(2)}, u32[]{:S(2)}) collective-permute-start(bf16[16,2176]{1,0:T(8,128)(2,1)S(1)} %collective-permute-done.10.refs_7_), channel_id=1, source_target_pairs={{0,1},{1,0},{2,3},{3,2},{4,5},{5,4},{6,7},{7,6},{8,9},{9,8},{10,11... | collective-permute-start | bytes 208904 | tf_op jit(solution)/shard_map/ppermute | solution.py:33
  47.7 2.0 %collective-permute-start.19 = (bf16[128,2048]{1,0:T(8,128)(2,1)S(1)}, bf16[128,2048]{1,0:T(8,128)(2,1)S(1)}, u32[]{:S(2)}, u32[]{:S(2)}) collective-permute-start(bf16[128,2048]{1,0:T(8,128)(2,1)S(1)} %get-tuple-element.52), channel_id=1, source_target_pairs={{0,1},{1,0},{2,3},{3,2},{4,5},{5,4},{6,7},{7,6},{8,9},{9,8},{10,11... | collective-permute-start | bytes 1572872 | tf_op jit(solution)/shard_map/ppermute | solution.py:33
  49.8 5.0 %collective-permute-start.20 = (bf16[16,2048]{1,0:T(8,128)(2,1)S(1)}, bf16[16,2048]{1,0:T(8,128)(2,1)S(1)}, u32[]{:S(2)}, u32[]{:S(2)}) collective-permute-start(bf16[16,2048]{1,0:T(8,128)(2,1)S(1)} %get-tuple-element.54), channel_id=1, source_target_pairs={{0,2},{2,0},{1,3},{3,1},{4,6},{6,4},{5,7},{7,5},{8,10},{10,8},{9,1... | collective-permute-start | bytes 196616 | tf_op jit(solution)/shard_map/ppermute | solution.py:33
  51.0 6.1 %collective-permute-start.22 = (bf16[16,2048]{1,0:T(8,128)(2,1)S(1)}, bf16[16,2048]{1,0:T(8,128)(2,1)S(1)}, u32[]{:S(2)}, u32[]{:S(2)}) collective-permute-start(bf16[16,2048]{1,0:T(8,128)(2,1)S(1)} %get-tuple-element.56), channel_id=1, source_target_pairs={{0,2},{2,0},{1,3},{3,1},{4,6},{6,4},{5,7},{7,5},{8,10},{10,8},{9,1... | collective-permute-start | bytes 196616 | tf_op jit(solution)/shard_map/ppermute | solution.py:33
  51.9 6.2 %collective-permute-start.24 = (bf16[16,2048]{1,0:T(8,128)(2,1)S(1)}, bf16[16,2048]{1,0:T(8,128)(2,1)S(1)}, u32[]{:S(2)}, u32[]{:S(2)}) collective-permute-start(bf16[16,2048]{1,0:T(8,128)(2,1)S(1)} %get-tuple-element.58), channel_id=1, source_target_pairs={{0,2},{2,0},{1,3},{3,1},{4,6},{6,4},{5,7},{7,5},{8,10},{10,8},{9,1... | collective-permute-start | bytes 196616 | tf_op jit(solution)/shard_map/ppermute | solution.py:33
  53.1 6.3 %collective-permute-start.26 = (bf16[16,2048]{1,0:T(8,128)(2,1)S(1)}, bf16[16,2048]{1,0:T(8,128)(2,1)S(1)}, u32[]{:S(2)}, u32[]{:S(2)}) collective-permute-start(bf16[16,2048]{1,0:T(8,128)(2,1)S(1)} %get-tuple-element.60), channel_id=1, source_target_pairs={{0,2},{2,0},{1,3},{3,1},{4,6},{6,4},{5,7},{7,5},{8,10},{10,8},{9,1... | collective-permute-start | bytes 196616 | tf_op jit(solution)/shard_map/ppermute | solution.py:33
  54.8 6.7 %collective-permute-start.21 = (bf16[16,2048]{1,0:T(8,128)(2,1)S(1)}, bf16[16,2048]{1,0:T(8,128)(2,1)S(1)}, u32[]{:S(2)}, u32[]{:S(2)}) collective-permute-start(bf16[16,2048]{1,0:T(8,128)(2,1)S(1)} %sum_x3.1), channel_id=1, source_target_pairs={{0,12},{4,8},{8,4},{12,0},{1,13},{5,9},{9,5},{13,1},{2,14},{6,10},... | collective-permute-start | bytes 196616 | tf_op jit(solution)/shard_map/ppermute | solution.py:33
  57.1 5.9 %collective-permute-start.23 = (bf16[16,2048]{1,0:T(8,128)(2,1)S(1)}, bf16[16,2048]{1,0:T(8,128)(2,1)S(1)}, u32[]{:S(2)}, u32[]{:S(2)}) collective-permute-start(bf16[16,2048]{1,0:T(8,128)(2,1)S(1)} %sum_x2.1), channel_id=1, source_target_pairs={{0,8},{4,12},{8,0},{12,4},{1,9},{5,13},{9,1},{13,5},{2,10},{6,14},... | collective-permute-start | bytes 196616 | tf_op jit(solution)/shard_map/ppermute | solution.py:33
  58.2 5.0 %collective-permute-start.25 = (bf16[16,2048]{1,0:T(8,128)(2,1)S(1)}, bf16[16,2048]{1,0:T(8,128)(2,1)S(1)}, u32[]{:S(2)}, u32[]{:S(2)}) collective-permute-start(bf16[16,2048]{1,0:T(8,128)(2,1)S(1)} %sum_x1.1), channel_id=1, source_target_pairs={{0,4},{4,0},{8,12},{12,8},{1,5},{5,1},{9,13},{13,9},{2,6},{6,2},{1... | collective-permute-start | bytes 196616 | tf_op jit(solution)/shard_map/ppermute | solution.py:33

commit v15 on v14

--- a/solution.py
+++ b/solution.py
@@ -272,16 +272,15 @@
 
 def experts_kernel(experts, capacity, tile, halves, n_rows, *refs):
     rows_in = refs[:n_rows]
-    gate_top, gate_low, up_first, gate_hbm, up_hbm, down_hbm, keep_ref, send_ref = refs[
-        n_rows : n_rows + 8
-    ]
-    rows_ref, pick_ref, packed_ref, hidden_ref, half_ref, sum_ref, gate_ref, up_ref, down_ref, sem = refs[
-        n_rows + 8 :
+    gate_top, gate_low, up_first, gate_hbm, up_hbm, down_hbm = refs[n_rows : n_rows + 6]
+    send_ref, pick_ref, packed_ref = refs[n_rows + 6 : n_rows + 9]
+    rows_ref, hidden_ref, half_ref, sum_ref, up_low, gate_ref, up_ref, down_ref, sem = refs[
+        n_rows + 9 :
     ]
     per_expert, width = down_hbm.shape[0] // experts, down_hbm.shape[1]
     column = min(512, width)
     cuts = 4
-    top = gate_top.shape[0]
+    top, high = gate_top.shape[0], up_first.shape[0]
 
     def pieces(source, target, x, columns):
         rows = target.shape[0] // cuts
@@ -296,6 +295,9 @@
         return pairs
 
     groups = []
+    if high < width:
+        low = up_hbm.at[pl.ds(high, width - high), pl.ds(0, per_expert)]
+        groups.append((("up", 0), [(low, up_low)]))
     for x in range(experts):
         if x:
             groups.append((("gate", x), pieces(gate_hbm, gate_ref.at[x - 1], x, True)))
@@ -351,12 +353,15 @@
                 gate = gate + dot(packed_ref[mine, top:], gate_low[:, cut])
             half = 0.5 * gate
             half_ref[:, cut] = half + half * jnp.tanh(half)
-        if x:
-            stream.need(("up", x))
+        stream.need(("up", x))
         for s in range(0, per_expert, tile):
             cut = slice(s, s + tile)
             stream.step(0.85)
-            up = dot(packed_ref[mine, :], up_ref[x - 1, :, cut] if x else up_first[:, cut])
+            if x:
+                up = dot(packed_ref[mine, :], up_ref[x - 1, :, cut])
+            else:
+                up = dot(packed_ref[mine, :high], up_first[:, cut])
+                up = up + dot(packed_ref[mine, high:], up_low[:, cut])
             hidden_ref[mine, cut] = (half_ref[:, cut] * up).astype(jnp.bfloat16)
         rows = per_expert // cuts
         for i in range(cuts):
@@ -372,15 +377,21 @@
             stream.step(0.85)
         stream.limit = stream.last["up", x + 2] if x + 2 < experts else len(stream.copies)
         stream.fill()
-    kept = keep_ref.shape[0]
-
+    spread(pick_ref, packed_ref, send_ref, pick_ref.shape[1] - send_ref.shape[0])
+
+
+def spread(pick_ref, packed_ref, out_ref, first):
+    rows, width = out_ref.shape
+    column = min(512, width)
     for c in range(0, width, column):
-        out = lax.dot_general(
-            pick_ref[...], packed_ref[:, c : c + column], (((0,), (0,)), ((), ())),
-            preferred_element_type=jnp.float32,
-        )
-        keep_ref[:, c : c + column] = out[:kept]
-        send_ref[:, c : c + column] = out[kept:].astype(jnp.bfloat16)
+        out_ref[:, c : c + column] = lax.dot_general(
+            pick_ref[:, first : first + rows], packed_ref[:, c : c + column],
+            (((0,), (0,)), ((), ())), preferred_element_type=jnp.float32,
+        ).astype(out_ref.dtype)
+
+
+def keep_kernel(pick_ref, packed_ref, out_ref):
+    spread(pick_ref, packed_ref, out_ref, 0)
 
 
 def per_device(
@@ -464,7 +475,7 @@
         [keep] + [xor_swap(send, "pp", 1)], [own_rows], [own_rows] * (tp_count - 1), "sum_cores"
     )
     got = [xor_swap(sends[k - 1], "tp", k) for k in range(1, tp_count)]
-    up_v, token = load(w_up[0], 0, width, per_expert, [own], "load_up")
+    up_v, token = load(w_up[0], 0, width * 3 // 4, per_expert, [own], "load_up")
     stream, normed = call(
         functools.partial(norm_kernel, tp_count),
         [sds((own_rows, width), f32), sds((own_rows, width + LANES), bf16)],
@@ -497,28 +508,35 @@
     down = w_down[0]
     tile = min(512, down.shape[0] // experts)
     kept = count // pp_count
-    keep, send = call(
+    slots = experts * capacity
+    send, pick, weighted = call(
         functools.partial(experts_kernel, experts, capacity, tile, halves, len(rows)),
-        [sds((kept, width), f32), sds((count - kept, width), bf16)],
+        [sds((count - kept, width), bf16), sds((slots, count), bf16), sds((slots, width), bf16)],
         [(VMEM, a) for a in (*rows, *gate_v, gate_late, up_v)]
         + [(HBM, a) for a in (w_gate[0], w_up[0], down)],
         scratch=[
             pltpu.VMEM((count, width + LANES), bf16),
-            pltpu.VMEM((experts * capacity, count), bf16),
-            pltpu.VMEM((experts * capacity, width), bf16),
-            pltpu.VMEM((experts * capacity, down.shape[0] // experts), bf16),
+            pltpu.VMEM((slots, down.shape[0] // experts), bf16),
             pltpu.VMEM((capacity, per_expert), f32),
             pltpu.VMEM((capacity, width), f32),
+            pltpu.VMEM((width - up_v.shape[0], per_expert), bf16),
             pltpu.VMEM((max(1, experts - 1), width, per_expert), bf16),
             pltpu.VMEM((max(1, experts - 1), width, per_expert), bf16),
             pltpu.VMEM((per_expert, width), bf16),
-            pltpu.SemaphoreType.DMA((4 * (3 * experts - 2),)),
+            pltpu.SemaphoreType.DMA((4 * (3 * experts - 2) + 1,)),
         ],
         vmem=33,
         name="experts",
         cost_us=12.0,
     )
 
+    keep = call(
+        keep_kernel,
+        sds((kept, width), f32),
+        [(VMEM, pick), (VMEM, weighted)],
+        name="keep",
+        cost_us=0.4,
+    )
     piece = kept // (tp_count * groups)
     own, sends = add(
         [keep, xor_swap(send, "pp", 1)], [piece] * groups, [piece] * (groups * (tp_count - 1)), "sum_cores2"

time: 64.1 us -> 63.6 us (level)
    pallas_call x13 -> x14, Pallas kernels: 24.7 us -> 24.5 us  [call(): pl.pallas_call(kernel, out_shape=out_shape, in_specs=[s for s, _ in args]...]
  transfers between devices with their start and end apart: 27 -> 27, of which waited for: 13 -> 11; matrix products, arithmetic and copies ran while one was open for 0% -> 0% of each run, Pallas kernels for 15% -> 14%
where the time goes in v15:
time: 63.6 us; the launch traced here: 63.3 us
  Pallas kernels  24.5 us (39%)
  starting transfers between devices  24.4 us (38%)
  waiting for transfers between devices  13.6 us (21%)
  local copies, waits for them, and re-layouts  0.78 us (1%)
    pallas_call x14, Pallas kernels, call(): pl.pallas_call(kernel, out_shape=out_shape, in_specs=[s for s, _ in args]...  24.5 us
    ppermute x25, starting transfers between devices, xor_swap(): return lax.ppermute(x, axis, [(i, i ^ k) for i in range(n)])  18.7 us
    ppermute x25, waiting for transfers between devices, xor_swap(): return lax.ppermute(x, axis, [(i, i ^ k) for i in range(n)])  13 us
    ppermute x2, starting transfers between devices, per_device(): lax.ppermute(kv, 'sec', [(i, (i + k) % sec_count) for i in range(sec_coun...  5.67 us
  transfers between devices with their start and end apart: 27, of which 11 were waited for; matrix products, arithmetic and copies ran while one was open for 0% of the time, Pallas kernels for 14%

profile of v15, /device:TPU:0, one launch (start us, length us, event | category | flops | bytes accessed | tf_op | source)
XLA Modules:
  0.0 63.3 jit_solution(15223103571311952598)
XLA Ops:
  0.0 0.8 %constant_dynamic-slice_fusion = (bf16[64,256]{1,0:T(8,128)(2,1)S(1)}, bf16[64,256]{1,0:T(8,128)(2,1)S(1)}) fusion(bf16[64,512]{1,0:T(8,128)(2,1)} %param.14, s32[]{:T(128)S(6)} %select_n.10, bf16[64,512]{1,0:T(8,128)(2,1)} %param.13), kind=kLoop, calls=%fused_computation.1 | loop fusion | bytes 131076 | tf_op jit(solution)/shard_map/dynamic_slice | solution.py:423
  0.8 3.1 %collective-permute-start.1 = (bf16[64,512]{1,0:T(8,128)(2,1)S(1)}, bf16[64,512]{1,0:T(8,128)(2,1)S(1)}, u32[]{:S(2)}, u32[]{:S(2)}) collective-permute-start(bf16[64,512]{1,0:T(8,128)(2,1)S(1)} %pad_maximum_fusion.refs_2_), channel_id=1, source_target_pairs={{0,4},{4,8},{8,12},{12,0},{1,5},{5,9},{9,13},{13,1},{2,6},{6,10},{... | collective-permute-start | bytes 196616 | tf_op jit(solution)/shard_map/ppermute | solution.py:427
  3.9 2.6 %collective-permute-start = (bf16[64,512]{1,0:T(8,128)(2,1)S(1)}, bf16[64,512]{1,0:T(8,128)(2,1)S(1)}, u32[]{:S(2)}, u32[]{:S(2)}) collective-permute-start(bf16[64,512]{1,0:T(8,128)(2,1)S(1)} %pad_maximum_fusion.refs_2_), channel_id=1, source_target_pairs={{0,8},{4,12},{8,0},{12,4},{1,9},{5,13},{9,1},{13,5},{2,10},{6,14},... | collective-permute-start | bytes 196616 | tf_op jit(solution)/shard_map/ppermute | solution.py:427
  6.5 3.7 %prepare.1 = (bf16[64,1024]{1,0:T(8,128)(2,1)S(1)}, bf16[1024,2048]{1,0:T(8,128)(2,1)S(1)}, f32[1,2048]{1,0:T(1,128)S(1)}, f32[64,192]{1,0:T(8,128)S(1)}, bf16[6...) custom-call(s32[8]{0:T(128)} %lengths_hbm.1, ...), custom_call_target="tpu_custom_call" | custom-call | bytes 10200000 | tf_op jit(solution)/shard_map/prepare/pallas_call | solution.py:41
  10.2 0.6 collective-permute-done.refs_0_
  10.8 1.4 %attention.1 = (f32[32,2048]{1,0:T(8,128)S(1)}, bf16[32,2048]{1,0:T(8,128)(2,1)S(1)}) custom-call(bf16[64,1024]{1,0:T(8,128)(2,1)S(1)} %get-tuple-element.37.q_ref, f32[64,192]{1,0:T(8,128)S(1)} %get-tuple-element.38.mask_ref, bf16[64,64]{1,0:T(8,128)(2,1)S(1)} %get-tuple-element.39.order_ref, bf16[64,512]{1,0:T(8,128)(2,1)S(1)} %collective-permute-done.refs_0_, ...), custom_call_target="tpu_custom_call" | custom-call | bytes 8160000 | tf_op jit(solution)/shard_map/attention/pallas_call | solution.py:41
  12.3 1.3 %collective-permute-done.2.refs_1_ = bf16[32,2048]{1,0:T(8,128)(2,1)S(1)} collective-permute-done((bf16[32,2048]{1,0:T(8,128)(2,1)S(1)}, bf16[32,2048]{1,0:T(8,128)(2,1)S(1)}, u32[]{:S(2)}, u32[]{:S(2)}) %collective-permute-start.2) | collective-permute-done | bytes 131104 | tf_op jit(solution)/shard_map/ppermute | solution.py:33
  13.7 1.6 %collective-permute-start.3 = (bf16[16,2048]{1,0:T(8,128)(2,1)S(1)}, bf16[16,2048]{1,0:T(8,128)(2,1)S(1)}, u32[]{:S(2)}, u32[]{:S(2)}) collective-permute-start(bf16[16,2048]{1,0:T(8,128)(2,1)S(1)} %get-tuple-element.44), channel_id=1, source_target_pairs={{0,2},{2,0},{1,3},{3,1},{4,6},{6,4},{5,7},{7,5},{8,10},{10,8},{9,1... | collective-permute-start | bytes 196616 | tf_op jit(solution)/shard_map/ppermute | solution.py:33
  15.2 2.8 %load_up.1 = (bf16[1536,2048]{1,0:T(8,128)(2,1)S(1)}, f32[8,128]{1,0:T(8,128)S(1)}) custom-call(bf16[2048,4096]{1,0:T(8,128)(2,1)} %bitcast.9, f32[16,2048]{1,0:T(8,128)S(1)} %get-tuple-element.43.refs_0_), custom_call_target="tpu_custom_call" | custom-call | bytes 6291456 | tf_op jit(solution)/shard_map/load_up/pallas_call | solution.py:41
  18.2 1.0 %collective-permute-start.5 = (bf16[16,2176]{1,0:T(8,128)(2,1)S(1)}, bf16[16,2176]{1,0:T(8,128)(2,1)S(1)}, u32[]{:S(2)}, u32[]{:S(2)}) collective-permute-start(bf16[16,2176]{1,0:T(8,128)(2,1)S(1)} %get-tuple-element.47.refs_0_), channel_id=1, source_target_pairs={{0,8},{4,12},{8,0},{12,4},{1,9},{5,13},{9,1},{13,5},{2,10},{6,14},... | collective-permute-start | bytes 208904 | tf_op jit(solution)/shard_map/ppermute | solution.py:33
  19.2 1.5 %collective-permute-start.7 = (bf16[16,2176]{1,0:T(8,128)(2,1)S(1)}, bf16[16,2176]{1,0:T(8,128)(2,1)S(1)}, u32[]{:S(2)}, u32[]{:S(2)}) collective-permute-start(bf16[16,2176]{1,0:T(8,128)(2,1)S(1)} %get-tuple-element.47.refs_0_), channel_id=1, source_target_pairs={{0,2},{2,0},{1,3},{3,1},{4,6},{6,4},{5,7},{7,5},{8,10},{10,8},{9,1... | collective-permute-start | bytes 208904 | tf_op jit(solution)/shard_map/ppermute | solution.py:33
  20.6 1.6 %collective-permute-start.4 = (bf16[16,2176]{1,0:T(8,128)(2,1)S(1)}, bf16[16,2176]{1,0:T(8,128)(2,1)S(1)}, u32[]{:S(2)}, u32[]{:S(2)}) collective-permute-start(bf16[16,2176]{1,0:T(8,128)(2,1)S(1)} %get-tuple-element.47.refs_0_), channel_id=1, source_target_pairs={{0,4},{4,0},{8,12},{12,8},{1,5},{5,1},{9,13},{13,9},{2,6},{6,2},{1... | collective-permute-start | bytes 208904 | tf_op jit(solution)/shard_map/ppermute | solution.py:33
  22.3 2.2 %load_gate.1 = (bf16[1024,2048]{1,0:T(8,128)(2,1)S(1)}, f32[8,128]{1,0:T(8,128)S(1)}) custom-call(bf16[2048,4096]{1,0:T(8,128)(2,1)} %bitcast.7, bf16[16,2176]{1,0:T(8,128)(2,1)S(1)} %get-tuple-element.47.refs_0_), custom_call_target="tpu_custom_call" | custom-call | bytes 4194303 | tf_op jit(solution)/shard_map/load_gate/pallas_call | solution.py:41
  26.0 1.5 %collective-permute-start.9 = (bf16[16,2176]{1,0:T(8,128)(2,1)S(1)}, bf16[16,2176]{1,0:T(8,128)(2,1)S(1)}, u32[]{:S(2)}, u32[]{:S(2)}) collective-permute-start(bf16[16,2176]{1,0:T(8,128)(2,1)S(1)} %join.1.refs_2_), channel_id=1, source_target_pairs={{0,2},{2,0},{1,3},{3,1},{4,6},{6,4},{5,7},{7,5},{8,10},{10,8},{9,1... | collective-permute-start | bytes 208904 | tf_op jit(solution)/shard_map/ppermute | solution.py:33
  27.5 1.7 %collective-permute-done.6.refs_3_ = bf16[16,2176]{1,0:T(8,128)(2,1)S(1)} collective-permute-done((bf16[16,2176]{1,0:T(8,128)(2,1)S(1)}, bf16[16,2176]{1,0:T(8,128)(2,1)S(1)}, u32[]{:S(2)}, u32[]{:S(2)}) %collective-permute-start.6) | collective-permute-done | bytes 69664 | tf_op jit(solution)/shard_map/ppermute | solution.py:33
  29.2 0.6 collective-permute-start.10
  30.5 0.8 %collective-permute-done.9.refs_6_ = bf16[16,2176]{1,0:T(8,128)(2,1)S(1)} collective-permute-done((bf16[16,2176]{1,0:T(8,128)(2,1)S(1)}, bf16[16,2176]{1,0:T(8,128)(2,1)S(1)}, u32[]{:S(2)}, u32[]{:S(2)}) %collective-permute-start.9) | collective-permute-done | bytes 69664 | tf_op jit(solution)/shard_map/ppermute | solution.py:33
  31.3 2.2 %collective-permute-done.10.refs_7_ = bf16[16,2176]{1,0:T(8,128)(2,1)S(1)} collective-permute-done((bf16[16,2176]{1,0:T(8,128)(2,1)S(1)}, bf16[16,2176]{1,0:T(8,128)(2,1)S(1)}, u32[]{:S(2)}, u32[]{:S(2)}) %collective-permute-start.10) | collective-permute-done | bytes 69664 | tf_op jit(solution)/shard_map/ppermute | solution.py:33
  33.5 1.2 %collective-permute-done.18.refs_15_ = bf16[16,2176]{1,0:T(8,128)(2,1)S(1)} collective-permute-done((bf16[16,2176]{1,0:T(8,128)(2,1)S(1)}, bf16[16,2176]{1,0:T(8,128)(2,1)S(1)}, u32[]{:S(2)}, u32[]{:S(2)}) %collective-permute-start.18) | collective-permute-done | bytes 69664 | tf_op jit(solution)/shard_map/ppermute | solution.py:33
  34.7 13.0 %experts.1 = (bf16[128,2048]{1,0:T(8,128)(2,1)S(1)}, bf16[256,256]{1,0:T(8,128)(2,1)S(1)}, bf16[256,2048]{1,0:T(8,128)(2,1)S(1)}) custom-call(bf16[16,2176]{1,0:T(8,128)(2,1)S(1)} %get-tuple-element.47.refs_0_, bf16[16,2176]{1,0:T(8,128)(2,1)S(1)} %collective-permute-done.4.refs_1_, bf16[16,2176]{1,0:T(8,128)(2,1)S(1)} %join.1.refs_2_, ...), custom_call_target="tpu_custom_call" | custom-call | bytes 40800000 | tf_op jit(solution)/shard_map/experts/pallas_call | solution.py:41
  48.3 1.4 %collective-permute-done.19.refs_1_ = bf16[128,2048]{1,0:T(8,128)(2,1)S(1)} collective-permute-done((bf16[128,2048]{1,0:T(8,128)(2,1)S(1)}, bf16[128,2048]{1,0:T(8,128)(2,1)S(1)}, u32[]{:S(2)}, u32[]{:S(2)}) %collective-permute-start.19) | collective-permute-done | bytes 524320 | tf_op jit(solution)/shard_map/ppermute | solution.py:33
  49.8 0.6 %collective-permute-start.20 = (bf16[16,2048]{1,0:T(8,128)(2,1)S(1)}, bf16[16,2048]{1,0:T(8,128)(2,1)S(1)}, u32[]{:S(2)}, u32[]{:S(2)}) collective-permute-start(bf16[16,2048]{1,0:T(8,128)(2,1)S(1)} %get-tuple-element.56), channel_id=1, source_target_pairs={{0,2},{2,0},{1,3},{3,1},{4,6},{6,4},{5,7},{7,5},{8,10},{10,8},{9,1... | collective-permute-start | bytes 196616 | tf_op jit(solution)/shard_map/ppermute | solution.py:33
  50.4 1.4 %collective-permute-start.22 = (bf16[16,2048]{1,0:T(8,128)(2,1)S(1)}, bf16[16,2048]{1,0:T(8,128)(2,1)S(1)}, u32[]{:S(2)}, u32[]{:S(2)}) collective-permute-start(bf16[16,2048]{1,0:T(8,128)(2,1)S(1)} %get-tuple-element.58), channel_id=1, source_target_pairs={{0,2},{2,0},{1,3},{3,1},{4,6},{6,4},{5,7},{7,5},{8,10},{10,8},{9,1... | collective-permute-start | bytes 196616 | tf_op jit(solution)/shard_map/ppermute | solution.py:33
  51.9 0.6 collective-permute-start.24
  52.5 1.4 %collective-permute-start.26 = (bf16[16,2048]{1,0:T(8,128)(2,1)S(1)}, bf16[16,2048]{1,0:T(8,128)(2,1)S(1)}, u32[]{:S(2)}, u32[]{:S(2)}) collective-permute-start(bf16[16,2048]{1,0:T(8,128)(2,1)S(1)} %get-tuple-element.62), channel_id=1, source_target_pairs={{0,2},{2,0},{1,3},{3,1},{4,6},{6,4},{5,7},{7,5},{8,10},{10,8},{9,1... | collective-permute-start | bytes 196616 | tf_op jit(solution)/shard_map/ppermute | solution.py:33
  53.9 0.9 %collective-permute-done.20.refs_1_ = bf16[16,2048]{1,0:T(8,128)(2,1)S(1)} collective-permute-done((bf16[16,2048]{1,0:T(8,128)(2,1)S(1)}, bf16[16,2048]{1,0:T(8,128)(2,1)S(1)}, u32[]{:S(2)}, u32[]{:S(2)}) %collective-permute-start.20) | collective-permute-done | bytes 65568 | tf_op jit(solution)/shard_map/ppermute | solution.py:33
  54.8 1.9 %collective-permute-start.21 = (bf16[16,2048]{1,0:T(8,128)(2,1)S(1)}, bf16[16,2048]{1,0:T(8,128)(2,1)S(1)}, u32[]{:S(2)}, u32[]{:S(2)}) collective-permute-start(bf16[16,2048]{1,0:T(8,128)(2,1)S(1)} %sum_x3.1), channel_id=1, source_target_pairs={{0,12},{4,8},{8,4},{12,0},{1,13},{5,9},{9,5},{13,1},{2,14},{6,10},... | collective-permute-start | bytes 196616 | tf_op jit(solution)/shard_map/ppermute | solution.py:33
  56.7 0.9 %collective-permute-start.23 = (bf16[16,2048]{1,0:T(8,128)(2,1)S(1)}, bf16[16,2048]{1,0:T(8,128)(2,1)S(1)}, u32[]{:S(2)}, u32[]{:S(2)}) collective-permute-start(bf16[16,2048]{1,0:T(8,128)(2,1)S(1)} %sum_x2.1), channel_id=1, source_target_pairs={{0,8},{4,12},{8,0},{12,4},{1,9},{5,13},{9,1},{13,5},{2,10},{6,14},... | collective-permute-start | bytes 196616 | tf_op jit(solution)/shard_map/ppermute | solution.py:33
  57.6 1.8 %collective-permute-start.25 = (bf16[16,2048]{1,0:T(8,128)(2,1)S(1)}, bf16[16,2048]{1,0:T(8,128)(2,1)S(1)}, u32[]{:S(2)}, u32[]{:S(2)}) collective-permute-start(bf16[16,2048]{1,0:T(8,128)(2,1)S(1)} %sum_x1.1), channel_id=1, source_target_pairs={{0,4},{4,0},{8,12},{12,8},{1,5},{5,1},{9,13},{13,9},{2,6},{6,2},{1... | collective-permute-start | bytes 196616 | tf_op jit(solution)/shard_map/ppermute | solution.py:33
  59.5 1.6 %collective-permute-done.21.refs_1_ = bf16[16,2048]{1,0:T(8,128)(2,1)S(1)} collective-permute-done((bf16[16,2048]{1,0:T(8,128)(2,1)S(1)}, bf16[16,2048]{1,0:T(8,128)(2,1)S(1)}, u32[]{:S(2)}, u32[]{:S(2)}) %collective-permute-start.21) | collective-permute-done | bytes 65568 | tf_op jit(solution)/shard_map/ppermute | solution.py:33
  61.1 1.6 %collective-permute-done.23.refs_2_ = bf16[16,2048]{1,0:T(8,128)(2,1)S(1)} collective-permute-done((bf16[16,2048]{1,0:T(8,128)(2,1)S(1)}, bf16[16,2048]{1,0:T(8,128)(2,1)S(1)}, u32[]{:S(2)}, u32[]{:S(2)}) %collective-permute-start.23) | collective-permute-done | bytes 65568 | tf_op jit(solution)/shard_map/ppermute | solution.py:33
  62.7 0.7 %total.1 = bf16[16,2048]{1,0:T(8,128)(2,1)} custom-call(f32[16,2048]{1,0:T(8,128)S(1)} %get-tuple-element.46.refs_0_, bf16[16,2048]{1,0:T(8,128)(2,1)S(1)} %collective-permute-done.21.refs_1_, bf16[16,2048]{1,0:T(8,128)(2,1)S(1)} %collective-permute-done.23.refs_2_, bf16[16,2048]{1,0:T(8,128)(2,1)S(1)} %collective-permute-done.25.refs_3_, ...), custom_call_target="tpu_custom_call" | custom-call | bytes 680000 | tf_op jit(solution)/shard_map/total/pallas_call | solution.py:41
  (38 shorter events, 3.2 us)
Async XLA Ops:
  0.8 9.4 %collective-permute-start.1 = (bf16[64,512]{1,0:T(8,128)(2,1)S(1)}, bf16[64,512]{1,0:T(8,128)(2,1)S(1)}, u32[]{:S(2)}, u32[]{:S(2)}) collective-permute-start(bf16[64,512]{1,0:T(8,128)(2,1)S(1)} %pad_maximum_fusion.refs_2_), channel_id=1, source_target_pairs={{0,4},{4,8},{8,12},{12,0},{1,5},{5,9},{9,13},{13,1},{2,6},{6,10},{... | collective-permute-start | bytes 196616 | tf_op jit(solution)/shard_map/ppermute | solution.py:427
  3.9 6.9 %collective-permute-start = (bf16[64,512]{1,0:T(8,128)(2,1)S(1)}, bf16[64,512]{1,0:T(8,128)(2,1)S(1)}, u32[]{:S(2)}, u32[]{:S(2)}) collective-permute-start(bf16[64,512]{1,0:T(8,128)(2,1)S(1)} %pad_maximum_fusion.refs_2_), channel_id=1, source_target_pairs={{0,8},{4,12},{8,0},{12,4},{1,9},{5,13},{9,1},{13,5},{2,10},{6,14},... | collective-permute-start | bytes 196616 | tf_op jit(solution)/shard_map/ppermute | solution.py:427
  12.2 1.4 %collective-permute-start.2 = (bf16[32,2048]{1,0:T(8,128)(2,1)S(1)}, bf16[32,2048]{1,0:T(8,128)(2,1)S(1)}, u32[]{:S(2)}, u32[]{:S(2)}) collective-permute-start(bf16[32,2048]{1,0:T(8,128)(2,1)S(1)} %get-tuple-element.42), channel_id=1, source_target_pairs={{0,1},{1,0},{2,3},{3,2},{4,5},{5,4},{6,7},{7,6},{8,9},{9,8},{10,11... | collective-permute-start | bytes 393224 | tf_op jit(solution)/shard_map/ppermute | solution.py:33
  13.7 4.4 %collective-permute-start.3 = (bf16[16,2048]{1,0:T(8,128)(2,1)S(1)}, bf16[16,2048]{1,0:T(8,128)(2,1)S(1)}, u32[]{:S(2)}, u32[]{:S(2)}) collective-permute-start(bf16[16,2048]{1,0:T(8,128)(2,1)S(1)} %get-tuple-element.44), channel_id=1, source_target_pairs={{0,2},{2,0},{1,3},{3,1},{4,6},{6,4},{5,7},{7,5},{8,10},{10,8},{9,1... | collective-permute-start | bytes 196616 | tf_op jit(solution)/shard_map/ppermute | solution.py:33
  18.2 6.3 %collective-permute-start.5 = (bf16[16,2176]{1,0:T(8,128)(2,1)S(1)}, bf16[16,2176]{1,0:T(8,128)(2,1)S(1)}, u32[]{:S(2)}, u32[]{:S(2)}) collective-permute-start(bf16[16,2176]{1,0:T(8,128)(2,1)S(1)} %get-tuple-element.47.refs_0_), channel_id=1, source_target_pairs={{0,8},{4,12},{8,0},{12,4},{1,9},{5,13},{9,1},{13,5},{2,10},{6,14},... | collective-permute-start | bytes 208904 | tf_op jit(solution)/shard_map/ppermute | solution.py:33
  19.2 5.8 %collective-permute-start.7 = (bf16[16,2176]{1,0:T(8,128)(2,1)S(1)}, bf16[16,2176]{1,0:T(8,128)(2,1)S(1)}, u32[]{:S(2)}, u32[]{:S(2)}) collective-permute-start(bf16[16,2176]{1,0:T(8,128)(2,1)S(1)} %get-tuple-element.47.refs_0_), channel_id=1, source_target_pairs={{0,2},{2,0},{1,3},{3,1},{4,6},{6,4},{5,7},{7,5},{8,10},{10,8},{9,1... | collective-permute-start | bytes 208904 | tf_op jit(solution)/shard_map/ppermute | solution.py:33
  20.6 4.6 %collective-permute-start.4 = (bf16[16,2176]{1,0:T(8,128)(2,1)S(1)}, bf16[16,2176]{1,0:T(8,128)(2,1)S(1)}, u32[]{:S(2)}, u32[]{:S(2)}) collective-permute-start(bf16[16,2176]{1,0:T(8,128)(2,1)S(1)} %get-tuple-element.47.refs_0_), channel_id=1, source_target_pairs={{0,4},{4,0},{8,12},{12,8},{1,5},{5,1},{9,13},{13,9},{2,6},{6,2},{1... | collective-permute-start | bytes 208904 | tf_op jit(solution)/shard_map/ppermute | solution.py:33
  22.3 3.8 %collective-permute-start.11 = (bf16[16,2176]{1,0:T(8,128)(2,1)S(1)}, bf16[16,2176]{1,0:T(8,128)(2,1)S(1)}, u32[]{:S(2)}, u32[]{:S(2)}) collective-permute-start(bf16[16,2176]{1,0:T(8,128)(2,1)S(1)} %get-tuple-element.47.refs_0_), channel_id=1, source_target_pairs={{0,1},{1,0},{2,3},{3,2},{4,5},{5,4},{6,7},{7,6},{8,9},{9,8},{10,11... | collective-permute-start | bytes 208904 | tf_op jit(solution)/shard_map/ppermute | solution.py:33
  24.5 4.7 %collective-permute-start.6 = (bf16[16,2176]{1,0:T(8,128)(2,1)S(1)}, bf16[16,2176]{1,0:T(8,128)(2,1)S(1)}, u32[]{:S(2)}, u32[]{:S(2)}) collective-permute-start(bf16[16,2176]{1,0:T(8,128)(2,1)S(1)} %join.1.refs_2_), channel_id=1, source_target_pairs={{0,4},{4,0},{8,12},{12,8},{1,5},{5,1},{9,13},{13,9},{2,6},{6,2},{1... | collective-permute-start | bytes 208904 | tf_op jit(solution)/shard_map/ppermute | solution.py:33
  24.9 4.8 %collective-permute-start.15 = (bf16[16,2176]{1,0:T(8,128)(2,1)S(1)}, bf16[16,2176]{1,0:T(8,128)(2,1)S(1)}, u32[]{:S(2)}, u32[]{:S(2)}) collective-permute-start(bf16[16,2176]{1,0:T(8,128)(2,1)S(1)} %collective-permute-done.7.refs_4_), channel_id=1, source_target_pairs={{0,1},{1,0},{2,3},{3,2},{4,5},{5,4},{6,7},{7,6},{8,9},{9,8},{10,11... | collective-permute-start | bytes 208904 | tf_op jit(solution)/shard_map/ppermute | solution.py:33
  25.2 4.6 %collective-permute-start.12 = (bf16[16,2176]{1,0:T(8,128)(2,1)S(1)}, bf16[16,2176]{1,0:T(8,128)(2,1)S(1)}, u32[]{:S(2)}, u32[]{:S(2)}) collective-permute-start(bf16[16,2176]{1,0:T(8,128)(2,1)S(1)} %collective-permute-done.4.refs_1_), channel_id=1, source_target_pairs={{0,1},{1,0},{2,3},{3,2},{4,5},{5,4},{6,7},{7,6},{8,9},{9,8},{10,11... | collective-permute-start | bytes 208904 | tf_op jit(solution)/shard_map/ppermute | solution.py:33
  25.5 5.0 %collective-permute-start.8 = (bf16[16,2176]{1,0:T(8,128)(2,1)S(1)}, bf16[16,2176]{1,0:T(8,128)(2,1)S(1)}, u32[]{:S(2)}, u32[]{:S(2)}) collective-permute-start(bf16[16,2176]{1,0:T(8,128)(2,1)S(1)} %collective-permute-done.4.refs_1_), channel_id=1, source_target_pairs={{0,2},{2,0},{1,3},{3,1},{4,6},{6,4},{5,7},{7,5},{8,10},{10,8},{9,1... | collective-permute-start | bytes 208904 | tf_op jit(solution)/shard_map/ppermute | solution.py:33
  26.0 5.2 %collective-permute-start.9 = (bf16[16,2176]{1,0:T(8,128)(2,1)S(1)}, bf16[16,2176]{1,0:T(8,128)(2,1)S(1)}, u32[]{:S(2)}, u32[]{:S(2)}) collective-permute-start(bf16[16,2176]{1,0:T(8,128)(2,1)S(1)} %join.1.refs_2_), channel_id=1, source_target_pairs={{0,2},{2,0},{1,3},{3,1},{4,6},{6,4},{5,7},{7,5},{8,10},{10,8},{9,1... | collective-permute-start | bytes 208904 | tf_op jit(solution)/shard_map/ppermute | solution.py:33
  29.2 4.3 %collective-permute-start.10 = (bf16[16,2176]{1,0:T(8,128)(2,1)S(1)}, bf16[16,2176]{1,0:T(8,128)(2,1)S(1)}, u32[]{:S(2)}, u32[]{:S(2)}) collective-permute-start(bf16[16,2176]{1,0:T(8,128)(2,1)S(1)} %collective-permute-done.6.refs_3_), channel_id=1, source_target_pairs={{0,2},{2,0},{1,3},{3,1},{4,6},{6,4},{5,7},{7,5},{8,10},{10,8},{9,1... | collective-permute-start | bytes 208904 | tf_op jit(solution)/shard_map/ppermute | solution.py:33
  29.7 3.7 %collective-permute-start.13 = (bf16[16,2176]{1,0:T(8,128)(2,1)S(1)}, bf16[16,2176]{1,0:T(8,128)(2,1)S(1)}, u32[]{:S(2)}, u32[]{:S(2)}) collective-permute-start(bf16[16,2176]{1,0:T(8,128)(2,1)S(1)} %join.1.refs_2_), channel_id=1, source_target_pairs={{0,1},{1,0},{2,3},{3,2},{4,5},{5,4},{6,7},{7,6},{8,9},{9,8},{10,11... | collective-permute-start | bytes 208904 | tf_op jit(solution)/shard_map/ppermute | solution.py:33
  29.7 3.7 %collective-permute-start.14 = (bf16[16,2176]{1,0:T(8,128)(2,1)S(1)}, bf16[16,2176]{1,0:T(8,128)(2,1)S(1)}, u32[]{:S(2)}, u32[]{:S(2)}) collective-permute-start(bf16[16,2176]{1,0:T(8,128)(2,1)S(1)} %collective-permute-done.6.refs_3_), channel_id=1, source_target_pairs={{0,1},{1,0},{2,3},{3,2},{4,5},{5,4},{6,7},{7,6},{8,9},{9,8},{10,11... | collective-permute-start | bytes 208904 | tf_op jit(solution)/shard_map/ppermute | solution.py:33
  30.5 3.0 %collective-permute-start.16 = (bf16[16,2176]{1,0:T(8,128)(2,1)S(1)}, bf16[16,2176]{1,0:T(8,128)(2,1)S(1)}, u32[]{:S(2)}, u32[]{:S(2)}) collective-permute-start(bf16[16,2176]{1,0:T(8,128)(2,1)S(1)} %collective-permute-done.8.refs_5_), channel_id=1, source_target_pairs={{0,1},{1,0},{2,3},{3,2},{4,5},{5,4},{6,7},{7,6},{8,9},{9,8},{10,11... | collective-permute-start | bytes 208904 | tf_op jit(solution)/shard_map/ppermute | solution.py:33
  31.3 2.2 %collective-permute-start.17 = (bf16[16,2176]{1,0:T(8,128)(2,1)S(1)}, bf16[16,2176]{1,0:T(8,128)(2,1)S(1)}, u32[]{:S(2)}, u32[]{:S(2)}) collective-permute-start(bf16[16,2176]{1,0:T(8,128)(2,1)S(1)} %collective-permute-done.9.refs_6_), channel_id=1, source_target_pairs={{0,1},{1,0},{2,3},{3,2},{4,5},{5,4},{6,7},{7,6},{8,9},{9,8},{10,11... | collective-permute-start | bytes 208904 | tf_op jit(solution)/shard_map/ppermute | solution.py:33
  33.5 1.3 %collective-permute-start.18 = (bf16[16,2176]{1,0:T(8,128)(2,1)S(1)}, bf16[16,2176]{1,0:T(8,128)(2,1)S(1)}, u32[]{:S(2)}, u32[]{:S(2)}) collective-permute-start(bf16[16,2176]{1,0:T(8,128)(2,1)S(1)} %collective-permute-done.10.refs_7_), channel_id=1, source_target_pairs={{0,1},{1,0},{2,3},{3,2},{4,5},{5,4},{6,7},{7,6},{8,9},{9,8},{10,11... | collective-permute-start | bytes 208904 | tf_op jit(solution)/shard_map/ppermute | solution.py:33
  47.7 2.0 %collective-permute-start.19 = (bf16[128,2048]{1,0:T(8,128)(2,1)S(1)}, bf16[128,2048]{1,0:T(8,128)(2,1)S(1)}, u32[]{:S(2)}, u32[]{:S(2)}) collective-permute-start(bf16[128,2048]{1,0:T(8,128)(2,1)S(1)} %get-tuple-element.54), channel_id=1, source_target_pairs={{0,1},{1,0},{2,3},{3,2},{4,5},{5,4},{6,7},{7,6},{8,9},{9,8},{10,11... | collective-permute-start | bytes 1572872 | tf_op jit(solution)/shard_map/ppermute | solution.py:33
  49.8 5.0 %collective-permute-start.20 = (bf16[16,2048]{1,0:T(8,128)(2,1)S(1)}, bf16[16,2048]{1,0:T(8,128)(2,1)S(1)}, u32[]{:S(2)}, u32[]{:S(2)}) collective-permute-start(bf16[16,2048]{1,0:T(8,128)(2,1)S(1)} %get-tuple-element.56), channel_id=1, source_target_pairs={{0,2},{2,0},{1,3},{3,1},{4,6},{6,4},{5,7},{7,5},{8,10},{10,8},{9,1... | collective-permute-start | bytes 196616 | tf_op jit(solution)/shard_map/ppermute | solution.py:33
  50.4 6.3 %collective-permute-start.22 = (bf16[16,2048]{1,0:T(8,128)(2,1)S(1)}, bf16[16,2048]{1,0:T(8,128)(2,1)S(1)}, u32[]{:S(2)}, u32[]{:S(2)}) collective-permute-start(bf16[16,2048]{1,0:T(8,128)(2,1)S(1)} %get-tuple-element.58), channel_id=1, source_target_pairs={{0,2},{2,0},{1,3},{3,1},{4,6},{6,4},{5,7},{7,5},{8,10},{10,8},{9,1... | collective-permute-start | bytes 196616 | tf_op jit(solution)/shard_map/ppermute | solution.py:33
  51.9 5.7 %collective-permute-start.24 = (bf16[16,2048]{1,0:T(8,128)(2,1)S(1)}, bf16[16,2048]{1,0:T(8,128)(2,1)S(1)}, u32[]{:S(2)}, u32[]{:S(2)}) collective-permute-start(bf16[16,2048]{1,0:T(8,128)(2,1)S(1)} %get-tuple-element.60), channel_id=1, source_target_pairs={{0,2},{2,0},{1,3},{3,1},{4,6},{6,4},{5,7},{7,5},{8,10},{10,8},{9,1... | collective-permute-start | bytes 196616 | tf_op jit(solution)/shard_map/ppermute | solution.py:33
  52.5 7.0 %collective-permute-start.26 = (bf16[16,2048]{1,0:T(8,128)(2,1)S(1)}, bf16[16,2048]{1,0:T(8,128)(2,1)S(1)}, u32[]{:S(2)}, u32[]{:S(2)}) collective-permute-start(bf16[16,2048]{1,0:T(8,128)(2,1)S(1)} %get-tuple-element.62), channel_id=1, source_target_pairs={{0,2},{2,0},{1,3},{3,1},{4,6},{6,4},{5,7},{7,5},{8,10},{10,8},{9,1... | collective-permute-start | bytes 196616 | tf_op jit(solution)/shard_map/ppermute | solution.py:33
  54.8 6.2 %collective-permute-start.21 = (bf16[16,2048]{1,0:T(8,128)(2,1)S(1)}, bf16[16,2048]{1,0:T(8,128)(2,1)S(1)}, u32[]{:S(2)}, u32[]{:S(2)}) collective-permute-start(bf16[16,2048]{1,0:T(8,128)(2,1)S(1)} %sum_x3.1), channel_id=1, source_target_pairs={{0,12},{4,8},{8,4},{12,0},{1,13},{5,9},{9,5},{13,1},{2,14},{6,10},... | collective-permute-start | bytes 196616 | tf_op jit(solution)/shard_map/ppermute | solution.py:33
  56.7 5.9 %collective-permute-start.23 = (bf16[16,2048]{1,0:T(8,128)(2,1)S(1)}, bf16[16,2048]{1,0:T(8,128)(2,1)S(1)}, u32[]{:S(2)}, u32[]{:S(2)}) collective-permute-start(bf16[16,2048]{1,0:T(8,128)(2,1)S(1)} %sum_x2.1), channel_id=1, source_target_pairs={{0,8},{4,12},{8,0},{12,4},{1,9},{5,13},{9,1},{13,5},{2,10},{6,14},... | collective-permute-start | bytes 196616 | tf_op jit(solution)/shard_map/ppermute | solution.py:33
  57.6 5.0 %collective-permute-start.25 = (bf16[16,2048]{1,0:T(8,128)(2,1)S(1)}, bf16[16,2048]{1,0:T(8,128)(2,1)S(1)}, u32[]{:S(2)}, u32[]{:S(2)}) collective-permute-start(bf16[16,2048]{1,0:T(8,128)(2,1)S(1)} %sum_x1.1), channel_id=1, source_target_pairs={{0,4},{4,0},{8,12},{12,8},{1,5},{5,1},{9,13},{13,9},{2,6},{6,2},{1... | collective-permute-start | bytes 196616 | tf_op jit(solution)/shard_map/ppermute | solution.py:33

commit v16 on v15

--- a/solution.py
+++ b/solution.py
@@ -442,7 +442,7 @@
             sds((own_rows, width), f32),
             sds((own_rows, LANES), bf16),
         ]
-        + [sds((width // 2, per_expert), bf16)],
+        + [sds((width * 3 // 4, per_expert), bf16)],
         [
             (HBM, a)
             for a in (
@@ -486,7 +486,7 @@
 
     groups = min(4, sec_count)
     near = {k: xor_swap(normed, "sec", k) if k else normed for k in range(0, sec_count, 2)}
-    gate_late, token = load(w_gate[0], width // 2, width // 2, per_expert, [normed], "load_gate")
+    gate_late, token = load(w_gate[0], width * 3 // 4, width // 4, per_expert, [normed], "load_gate")
     if sec_count > 2:
         near[2] = join([near[2]], "join", [token])
     near.update({k + 1: xor_swap(near[k], "sec", 1) for k in list(near) if k + 1 < sec_count})

time: 63.6 us -> 63.6 us (level)
    ppermute x25, waiting for transfers between devices: 13 us -> 13.6 us  [xor_swap(): return lax.ppermute(x, axis, [(i, i ^ k) for i in range(n)])]
  transfers between devices with their start and end apart: 27 -> 27, of which waited for: 11 -> 12; matrix products, arithmetic and copies ran while one was open for 0% -> 0% of each run, Pallas kernels for 14% -> 14%
where the time goes in v16:
time: 63.6 us; the launch traced here: 63.3 us
  Pallas kernels  24.5 us (39%)
  starting transfers between devices  24.3 us (38%)
  waiting for transfers between devices  13.6 us (21%)
  local copies, waits for them, and re-layouts  0.78 us (1%)
    pallas_call x14, Pallas kernels, call(): pl.pallas_call(kernel, out_shape=out_shape, in_specs=[s for s, _ in args]...  24.5 us
    ppermute x25, starting transfers between devices, xor_swap(): return lax.ppermute(x, axis, [(i, i ^ k) for i in range(n)])  18.6 us
    ppermute x25, waiting for transfers between devices, xor_swap(): return lax.ppermute(x, axis, [(i, i ^ k) for i in range(n)])  13.6 us
    ppermute x2, starting transfers between devices, per_device(): lax.ppermute(kv, 'sec', [(i, (i + k) % sec_count) for i in range(sec_coun...  5.67 us
  transfers between devices with their start and end apart: 27, of which 12 were waited for; matrix products, arithmetic and copies ran while one was open for 0% of the time, Pallas kernels for 14%

profile of v16, /device:TPU:0, one launch (start us, length us, event | category | flops | bytes accessed | tf_op | source)
XLA Modules:
  0.0 63.3 jit_solution(11188962402700938178)
XLA Ops:
  0.0 0.8 %constant_dynamic-slice_fusion = (bf16[64,256]{1,0:T(8,128)(2,1)S(1)}, bf16[64,256]{1,0:T(8,128)(2,1)S(1)}) fusion(bf16[64,512]{1,0:T(8,128)(2,1)} %param.14, s32[]{:T(128)S(6)} %select_n.10, bf16[64,512]{1,0:T(8,128)(2,1)} %param.13), kind=kLoop, calls=%fused_computation.1 | loop fusion | bytes 131076 | tf_op jit(solution)/shard_map/dynamic_slice | solution.py:423
  0.8 3.1 %collective-permute-start.1 = (bf16[64,512]{1,0:T(8,128)(2,1)S(1)}, bf16[64,512]{1,0:T(8,128)(2,1)S(1)}, u32[]{:S(2)}, u32[]{:S(2)}) collective-permute-start(bf16[64,512]{1,0:T(8,128)(2,1)S(1)} %pad_maximum_fusion.refs_2_), channel_id=1, source_target_pairs={{0,4},{4,8},{8,12},{12,0},{1,5},{5,9},{9,13},{13,1},{2,6},{6,10},{... | collective-permute-start | bytes 196616 | tf_op jit(solution)/shard_map/ppermute | solution.py:427
  3.9 2.6 %collective-permute-start = (bf16[64,512]{1,0:T(8,128)(2,1)S(1)}, bf16[64,512]{1,0:T(8,128)(2,1)S(1)}, u32[]{:S(2)}, u32[]{:S(2)}) collective-permute-start(bf16[64,512]{1,0:T(8,128)(2,1)S(1)} %pad_maximum_fusion.refs_2_), channel_id=1, source_target_pairs={{0,8},{4,12},{8,0},{12,4},{1,9},{5,13},{9,1},{13,5},{2,10},{6,14},... | collective-permute-start | bytes 196616 | tf_op jit(solution)/shard_map/ppermute | solution.py:427
  6.5 4.3 %prepare.1 = (bf16[64,1024]{1,0:T(8,128)(2,1)S(1)}, bf16[1024,2048]{1,0:T(8,128)(2,1)S(1)}, f32[1,2048]{1,0:T(1,128)S(1)}, f32[64,192]{1,0:T(8,128)S(1)}, bf16[6...) custom-call(s32[8]{0:T(128)} %lengths_hbm.1, ...), custom_call_target="tpu_custom_call" | custom-call | bytes 10200000 | tf_op jit(solution)/shard_map/prepare/pallas_call | solution.py:41
  10.8 1.4 %attention.1 = (f32[32,2048]{1,0:T(8,128)S(1)}, bf16[32,2048]{1,0:T(8,128)(2,1)S(1)}) custom-call(bf16[64,1024]{1,0:T(8,128)(2,1)S(1)} %get-tuple-element.37.q_ref, f32[64,192]{1,0:T(8,128)S(1)} %get-tuple-element.38.mask_ref, bf16[64,64]{1,0:T(8,128)(2,1)S(1)} %get-tuple-element.39.order_ref, bf16[64,512]{1,0:T(8,128)(2,1)S(1)} %collective-permute-done.refs_0_, ...), custom_call_target="tpu_custom_call" | custom-call | bytes 8160000 | tf_op jit(solution)/shard_map/attention/pallas_call | solution.py:41
  12.3 1.3 %collective-permute-done.2.refs_1_ = bf16[32,2048]{1,0:T(8,128)(2,1)S(1)} collective-permute-done((bf16[32,2048]{1,0:T(8,128)(2,1)S(1)}, bf16[32,2048]{1,0:T(8,128)(2,1)S(1)}, u32[]{:S(2)}, u32[]{:S(2)}) %collective-permute-start.2) | collective-permute-done | bytes 131104 | tf_op jit(solution)/shard_map/ppermute | solution.py:33
  13.7 1.6 %collective-permute-start.3 = (bf16[16,2048]{1,0:T(8,128)(2,1)S(1)}, bf16[16,2048]{1,0:T(8,128)(2,1)S(1)}, u32[]{:S(2)}, u32[]{:S(2)}) collective-permute-start(bf16[16,2048]{1,0:T(8,128)(2,1)S(1)} %get-tuple-element.44), channel_id=1, source_target_pairs={{0,2},{2,0},{1,3},{3,1},{4,6},{6,4},{5,7},{7,5},{8,10},{10,8},{9,1... | collective-permute-start | bytes 196616 | tf_op jit(solution)/shard_map/ppermute | solution.py:33
  15.3 2.8 %load_up.1 = (bf16[1536,2048]{1,0:T(8,128)(2,1)S(1)}, f32[8,128]{1,0:T(8,128)S(1)}) custom-call(bf16[2048,4096]{1,0:T(8,128)(2,1)} %bitcast.9, f32[16,2048]{1,0:T(8,128)S(1)} %get-tuple-element.43.refs_0_), custom_call_target="tpu_custom_call" | custom-call | bytes 6291456 | tf_op jit(solution)/shard_map/load_up/pallas_call | solution.py:41
  18.2 1.0 %collective-permute-start.5 = (bf16[16,2176]{1,0:T(8,128)(2,1)S(1)}, bf16[16,2176]{1,0:T(8,128)(2,1)S(1)}, u32[]{:S(2)}, u32[]{:S(2)}) collective-permute-start(bf16[16,2176]{1,0:T(8,128)(2,1)S(1)} %get-tuple-element.47.refs_0_), channel_id=1, source_target_pairs={{0,8},{4,12},{8,0},{12,4},{1,9},{5,13},{9,1},{13,5},{2,10},{6,14},... | collective-permute-start | bytes 208904 | tf_op jit(solution)/shard_map/ppermute | solution.py:33
  19.2 1.5 %collective-permute-start.7 = (bf16[16,2176]{1,0:T(8,128)(2,1)S(1)}, bf16[16,2176]{1,0:T(8,128)(2,1)S(1)}, u32[]{:S(2)}, u32[]{:S(2)}) collective-permute-start(bf16[16,2176]{1,0:T(8,128)(2,1)S(1)} %get-tuple-element.47.refs_0_), channel_id=1, source_target_pairs={{0,2},{2,0},{1,3},{3,1},{4,6},{6,4},{5,7},{7,5},{8,10},{10,8},{9,1... | collective-permute-start | bytes 208904 | tf_op jit(solution)/shard_map/ppermute | solution.py:33
  20.6 1.6 %collective-permute-start.4 = (bf16[16,2176]{1,0:T(8,128)(2,1)S(1)}, bf16[16,2176]{1,0:T(8,128)(2,1)S(1)}, u32[]{:S(2)}, u32[]{:S(2)}) collective-permute-start(bf16[16,2176]{1,0:T(8,128)(2,1)S(1)} %get-tuple-element.47.refs_0_), channel_id=1, source_target_pairs={{0,4},{4,0},{8,12},{12,8},{1,5},{5,1},{9,13},{13,9},{2,6},{6,2},{1... | collective-permute-start | bytes 208904 | tf_op jit(solution)/shard_map/ppermute | solution.py:33
  22.3 1.6 %load_gate.1 = (bf16[512,2048]{1,0:T(8,128)(2,1)S(1)}, f32[8,128]{1,0:T(8,128)S(1)}) custom-call(bf16[2048,4096]{1,0:T(8,128)(2,1)} %bitcast.7, bf16[16,2176]{1,0:T(8,128)(2,1)S(1)} %get-tuple-element.47.refs_0_), custom_call_target="tpu_custom_call" | custom-call | bytes 2097151 | tf_op jit(solution)/shard_map/load_gate/pallas_call | solution.py:41
  25.0 1.1 %collective-permute-start.8 = (bf16[16,2176]{1,0:T(8,128)(2,1)S(1)}, bf16[16,2176]{1,0:T(8,128)(2,1)S(1)}, u32[]{:S(2)}, u32[]{:S(2)}) collective-permute-start(bf16[16,2176]{1,0:T(8,128)(2,1)S(1)} %collective-permute-done.4.refs_1_), channel_id=1, source_target_pairs={{0,2},{2,0},{1,3},{3,1},{4,6},{6,4},{5,7},{7,5},{8,10},{10,8},{9,1... | collective-permute-start | bytes 208904 | tf_op jit(solution)/shard_map/ppermute | solution.py:33
  26.1 1.0 %collective-permute-start.9 = (bf16[16,2176]{1,0:T(8,128)(2,1)S(1)}, bf16[16,2176]{1,0:T(8,128)(2,1)S(1)}, u32[]{:S(2)}, u32[]{:S(2)}) collective-permute-start(bf16[16,2176]{1,0:T(8,128)(2,1)S(1)} %join.1.refs_2_), channel_id=1, source_target_pairs={{0,2},{2,0},{1,3},{3,1},{4,6},{6,4},{5,7},{7,5},{8,10},{10,8},{9,1... | collective-permute-start | bytes 208904 | tf_op jit(solution)/shard_map/ppermute | solution.py:33
  27.1 1.5 %collective-permute-done.6.refs_3_ = bf16[16,2176]{1,0:T(8,128)(2,1)S(1)} collective-permute-done((bf16[16,2176]{1,0:T(8,128)(2,1)S(1)}, bf16[16,2176]{1,0:T(8,128)(2,1)S(1)}, u32[]{:S(2)}, u32[]{:S(2)}) %collective-permute-start.6) | collective-permute-done | bytes 69664 | tf_op jit(solution)/shard_map/ppermute | solution.py:33
  28.6 1.1 %collective-permute-start.10 = (bf16[16,2176]{1,0:T(8,128)(2,1)S(1)}, bf16[16,2176]{1,0:T(8,128)(2,1)S(1)}, u32[]{:S(2)}, u32[]{:S(2)}) collective-permute-start(bf16[16,2176]{1,0:T(8,128)(2,1)S(1)} %collective-permute-done.6.refs_3_), channel_id=1, source_target_pairs={{0,2},{2,0},{1,3},{3,1},{4,6},{6,4},{5,7},{7,5},{8,10},{10,8},{9,1... | collective-permute-start | bytes 208904 | tf_op jit(solution)/shard_map/ppermute | solution.py:33
  30.3 1.2 %collective-permute-done.9.refs_6_ = bf16[16,2176]{1,0:T(8,128)(2,1)S(1)} collective-permute-done((bf16[16,2176]{1,0:T(8,128)(2,1)S(1)}, bf16[16,2176]{1,0:T(8,128)(2,1)S(1)}, u32[]{:S(2)}, u32[]{:S(2)}) %collective-permute-start.9) | collective-permute-done | bytes 69664 | tf_op jit(solution)/shard_map/ppermute | solution.py:33
  31.5 1.4 %collective-permute-done.10.refs_7_ = bf16[16,2176]{1,0:T(8,128)(2,1)S(1)} collective-permute-done((bf16[16,2176]{1,0:T(8,128)(2,1)S(1)}, bf16[16,2176]{1,0:T(8,128)(2,1)S(1)}, u32[]{:S(2)}, u32[]{:S(2)}) %collective-permute-start.10) | collective-permute-done | bytes 69664 | tf_op jit(solution)/shard_map/ppermute | solution.py:33
  32.9 1.2 %collective-permute-done.18.refs_15_ = bf16[16,2176]{1,0:T(8,128)(2,1)S(1)} collective-permute-done((bf16[16,2176]{1,0:T(8,128)(2,1)S(1)}, bf16[16,2176]{1,0:T(8,128)(2,1)S(1)}, u32[]{:S(2)}, u32[]{:S(2)}) %collective-permute-start.18) | collective-permute-done | bytes 69664 | tf_op jit(solution)/shard_map/ppermute | solution.py:33
  34.2 13.0 %experts.1 = (bf16[128,2048]{1,0:T(8,128)(2,1)S(1)}, bf16[256,256]{1,0:T(8,128)(2,1)S(1)}, bf16[256,2048]{1,0:T(8,128)(2,1)S(1)}) custom-call(bf16[16,2176]{1,0:T(8,128)(2,1)S(1)} %get-tuple-element.47.refs_0_, bf16[16,2176]{1,0:T(8,128)(2,1)S(1)} %collective-permute-done.4.refs_1_, bf16[16,2176]{1,0:T(8,128)(2,1)S(1)} %join.1.refs_2_, ...), custom_call_target="tpu_custom_call" | custom-call | bytes 40800000 | tf_op jit(solution)/shard_map/experts/pallas_call | solution.py:41
  47.7 1.4 %collective-permute-done.19.refs_1_ = bf16[128,2048]{1,0:T(8,128)(2,1)S(1)} collective-permute-done((bf16[128,2048]{1,0:T(8,128)(2,1)S(1)}, bf16[128,2048]{1,0:T(8,128)(2,1)S(1)}, u32[]{:S(2)}, u32[]{:S(2)}) %collective-permute-start.19) | collective-permute-done | bytes 524320 | tf_op jit(solution)/shard_map/ppermute | solution.py:33
  49.2 1.2 %collective-permute-start.20 = (bf16[16,2048]{1,0:T(8,128)(2,1)S(1)}, bf16[16,2048]{1,0:T(8,128)(2,1)S(1)}, u32[]{:S(2)}, u32[]{:S(2)}) collective-permute-start(bf16[16,2048]{1,0:T(8,128)(2,1)S(1)} %get-tuple-element.56), channel_id=1, source_target_pairs={{0,2},{2,0},{1,3},{3,1},{4,6},{6,4},{5,7},{7,5},{8,10},{10,8},{9,1... | collective-permute-start | bytes 196616 | tf_op jit(solution)/shard_map/ppermute | solution.py:33
  50.4 0.9 %collective-permute-start.22 = (bf16[16,2048]{1,0:T(8,128)(2,1)S(1)}, bf16[16,2048]{1,0:T(8,128)(2,1)S(1)}, u32[]{:S(2)}, u32[]{:S(2)}) collective-permute-start(bf16[16,2048]{1,0:T(8,128)(2,1)S(1)} %get-tuple-element.58), channel_id=1, source_target_pairs={{0,2},{2,0},{1,3},{3,1},{4,6},{6,4},{5,7},{7,5},{8,10},{10,8},{9,1... | collective-permute-start | bytes 196616 | tf_op jit(solution)/shard_map/ppermute | solution.py:33
  51.3 1.1 %collective-permute-start.24 = (bf16[16,2048]{1,0:T(8,128)(2,1)S(1)}, bf16[16,2048]{1,0:T(8,128)(2,1)S(1)}, u32[]{:S(2)}, u32[]{:S(2)}) collective-permute-start(bf16[16,2048]{1,0:T(8,128)(2,1)S(1)} %get-tuple-element.60), channel_id=1, source_target_pairs={{0,2},{2,0},{1,3},{3,1},{4,6},{6,4},{5,7},{7,5},{8,10},{10,8},{9,1... | collective-permute-start | bytes 196616 | tf_op jit(solution)/shard_map/ppermute | solution.py:33
  52.5 0.9 %collective-permute-start.26 = (bf16[16,2048]{1,0:T(8,128)(2,1)S(1)}, bf16[16,2048]{1,0:T(8,128)(2,1)S(1)}, u32[]{:S(2)}, u32[]{:S(2)}) collective-permute-start(bf16[16,2048]{1,0:T(8,128)(2,1)S(1)} %get-tuple-element.62), channel_id=1, source_target_pairs={{0,2},{2,0},{1,3},{3,1},{4,6},{6,4},{5,7},{7,5},{8,10},{10,8},{9,1... | collective-permute-start | bytes 196616 | tf_op jit(solution)/shard_map/ppermute | solution.py:33
  53.4 0.9 %collective-permute-done.20.refs_1_ = bf16[16,2048]{1,0:T(8,128)(2,1)S(1)} collective-permute-done((bf16[16,2048]{1,0:T(8,128)(2,1)S(1)}, bf16[16,2048]{1,0:T(8,128)(2,1)S(1)}, u32[]{:S(2)}, u32[]{:S(2)}) %collective-permute-start.20) | collective-permute-done | bytes 65568 | tf_op jit(solution)/shard_map/ppermute | solution.py:33
  54.3 2.3 %collective-permute-start.21 = (bf16[16,2048]{1,0:T(8,128)(2,1)S(1)}, bf16[16,2048]{1,0:T(8,128)(2,1)S(1)}, u32[]{:S(2)}, u32[]{:S(2)}) collective-permute-start(bf16[16,2048]{1,0:T(8,128)(2,1)S(1)} %sum_x3.1), channel_id=1, source_target_pairs={{0,12},{4,8},{8,4},{12,0},{1,13},{5,9},{9,5},{13,1},{2,14},{6,10},... | collective-permute-start | bytes 196616 | tf_op jit(solution)/shard_map/ppermute | solution.py:33
  56.6 1.0 %collective-permute-start.23 = (bf16[16,2048]{1,0:T(8,128)(2,1)S(1)}, bf16[16,2048]{1,0:T(8,128)(2,1)S(1)}, u32[]{:S(2)}, u32[]{:S(2)}) collective-permute-start(bf16[16,2048]{1,0:T(8,128)(2,1)S(1)} %sum_x2.1), channel_id=1, source_target_pairs={{0,8},{4,12},{8,0},{12,4},{1,9},{5,13},{9,1},{13,5},{2,10},{6,14},... | collective-permute-start | bytes 196616 | tf_op jit(solution)/shard_map/ppermute | solution.py:33
  57.6 1.3 %collective-permute-start.25 = (bf16[16,2048]{1,0:T(8,128)(2,1)S(1)}, bf16[16,2048]{1,0:T(8,128)(2,1)S(1)}, u32[]{:S(2)}, u32[]{:S(2)}) collective-permute-start(bf16[16,2048]{1,0:T(8,128)(2,1)S(1)} %sum_x1.1), channel_id=1, source_target_pairs={{0,4},{4,0},{8,12},{12,8},{1,5},{5,1},{9,13},{13,9},{2,6},{6,2},{1... | collective-permute-start | bytes 196616 | tf_op jit(solution)/shard_map/ppermute | solution.py:33
  58.9 2.1 %collective-permute-done.21.refs_1_ = bf16[16,2048]{1,0:T(8,128)(2,1)S(1)} collective-permute-done((bf16[16,2048]{1,0:T(8,128)(2,1)S(1)}, bf16[16,2048]{1,0:T(8,128)(2,1)S(1)}, u32[]{:S(2)}, u32[]{:S(2)}) %collective-permute-start.21) | collective-permute-done | bytes 65568 | tf_op jit(solution)/shard_map/ppermute | solution.py:33
  61.0 1.5 %collective-permute-done.23.refs_2_ = bf16[16,2048]{1,0:T(8,128)(2,1)S(1)} collective-permute-done((bf16[16,2048]{1,0:T(8,128)(2,1)S(1)}, bf16[16,2048]{1,0:T(8,128)(2,1)S(1)}, u32[]{:S(2)}, u32[]{:S(2)}) %collective-permute-start.23) | collective-permute-done | bytes 65568 | tf_op jit(solution)/shard_map/ppermute | solution.py:33
  62.7 0.7 %total.1 = bf16[16,2048]{1,0:T(8,128)(2,1)} custom-call(f32[16,2048]{1,0:T(8,128)S(1)} %get-tuple-element.46.refs_0_, bf16[16,2048]{1,0:T(8,128)(2,1)S(1)} %collective-permute-done.21.refs_1_, bf16[16,2048]{1,0:T(8,128)(2,1)S(1)} %collective-permute-done.23.refs_2_, bf16[16,2048]{1,0:T(8,128)(2,1)S(1)} %collective-permute-done.25.refs_3_, ...), custom_call_target="tpu_custom_call" | custom-call | bytes 680000 | tf_op jit(solution)/shard_map/total/pallas_call | solution.py:41
  (38 shorter events, 2.8 us)
Async XLA Ops:
  0.8 10.0 %collective-permute-start.1 = (bf16[64,512]{1,0:T(8,128)(2,1)S(1)}, bf16[64,512]{1,0:T(8,128)(2,1)S(1)}, u32[]{:S(2)}, u32[]{:S(2)}) collective-permute-start(bf16[64,512]{1,0:T(8,128)(2,1)S(1)} %pad_maximum_fusion.refs_2_), channel_id=1, source_target_pairs={{0,4},{4,8},{8,12},{12,0},{1,5},{5,9},{9,13},{13,1},{2,6},{6,10},{... | collective-permute-start | bytes 196616 | tf_op jit(solution)/shard_map/ppermute | solution.py:427
  3.9 6.9 %collective-permute-start = (bf16[64,512]{1,0:T(8,128)(2,1)S(1)}, bf16[64,512]{1,0:T(8,128)(2,1)S(1)}, u32[]{:S(2)}, u32[]{:S(2)}) collective-permute-start(bf16[64,512]{1,0:T(8,128)(2,1)S(1)} %pad_maximum_fusion.refs_2_), channel_id=1, source_target_pairs={{0,8},{4,12},{8,0},{12,4},{1,9},{5,13},{9,1},{13,5},{2,10},{6,14},... | collective-permute-start | bytes 196616 | tf_op jit(solution)/shard_map/ppermute | solution.py:427
  12.3 1.4 %collective-permute-start.2 = (bf16[32,2048]{1,0:T(8,128)(2,1)S(1)}, bf16[32,2048]{1,0:T(8,128)(2,1)S(1)}, u32[]{:S(2)}, u32[]{:S(2)}) collective-permute-start(bf16[32,2048]{1,0:T(8,128)(2,1)S(1)} %get-tuple-element.42), channel_id=1, source_target_pairs={{0,1},{1,0},{2,3},{3,2},{4,5},{5,4},{6,7},{7,6},{8,9},{9,8},{10,11... | collective-permute-start | bytes 393224 | tf_op jit(solution)/shard_map/ppermute | solution.py:33
  13.7 4.4 %collective-permute-start.3 = (bf16[16,2048]{1,0:T(8,128)(2,1)S(1)}, bf16[16,2048]{1,0:T(8,128)(2,1)S(1)}, u32[]{:S(2)}, u32[]{:S(2)}) collective-permute-start(bf16[16,2048]{1,0:T(8,128)(2,1)S(1)} %get-tuple-element.44), channel_id=1, source_target_pairs={{0,2},{2,0},{1,3},{3,1},{4,6},{6,4},{5,7},{7,5},{8,10},{10,8},{9,1... | collective-permute-start | bytes 196616 | tf_op jit(solution)/shard_map/ppermute | solution.py:33
  18.2 6.1 %collective-permute-start.5 = (bf16[16,2176]{1,0:T(8,128)(2,1)S(1)}, bf16[16,2176]{1,0:T(8,128)(2,1)S(1)}, u32[]{:S(2)}, u32[]{:S(2)}) collective-permute-start(bf16[16,2176]{1,0:T(8,128)(2,1)S(1)} %get-tuple-element.47.refs_0_), channel_id=1, source_target_pairs={{0,8},{4,12},{8,0},{12,4},{1,9},{5,13},{9,1},{13,5},{2,10},{6,14},... | collective-permute-start | bytes 208904 | tf_op jit(solution)/shard_map/ppermute | solution.py:33
  19.2 5.2 %collective-permute-start.7 = (bf16[16,2176]{1,0:T(8,128)(2,1)S(1)}, bf16[16,2176]{1,0:T(8,128)(2,1)S(1)}, u32[]{:S(2)}, u32[]{:S(2)}) collective-permute-start(bf16[16,2176]{1,0:T(8,128)(2,1)S(1)} %get-tuple-element.47.refs_0_), channel_id=1, source_target_pairs={{0,2},{2,0},{1,3},{3,1},{4,6},{6,4},{5,7},{7,5},{8,10},{10,8},{9,1... | collective-permute-start | bytes 208904 | tf_op jit(solution)/shard_map/ppermute | solution.py:33
  20.6 4.4 %collective-permute-start.4 = (bf16[16,2176]{1,0:T(8,128)(2,1)S(1)}, bf16[16,2176]{1,0:T(8,128)(2,1)S(1)}, u32[]{:S(2)}, u32[]{:S(2)}) collective-permute-start(bf16[16,2176]{1,0:T(8,128)(2,1)S(1)} %get-tuple-element.47.refs_0_), channel_id=1, source_target_pairs={{0,4},{4,0},{8,12},{12,8},{1,5},{5,1},{9,13},{13,9},{2,6},{6,2},{1... | collective-permute-start | bytes 208904 | tf_op jit(solution)/shard_map/ppermute | solution.py:33
  22.3 3.8 %collective-permute-start.11 = (bf16[16,2176]{1,0:T(8,128)(2,1)S(1)}, bf16[16,2176]{1,0:T(8,128)(2,1)S(1)}, u32[]{:S(2)}, u32[]{:S(2)}) collective-permute-start(bf16[16,2176]{1,0:T(8,128)(2,1)S(1)} %get-tuple-element.47.refs_0_), channel_id=1, source_target_pairs={{0,1},{1,0},{2,3},{3,2},{4,5},{5,4},{6,7},{7,6},{8,9},{9,8},{10,11... | collective-permute-start | bytes 208904 | tf_op jit(solution)/shard_map/ppermute | solution.py:33
  24.3 4.3 %collective-permute-start.6 = (bf16[16,2176]{1,0:T(8,128)(2,1)S(1)}, bf16[16,2176]{1,0:T(8,128)(2,1)S(1)}, u32[]{:S(2)}, u32[]{:S(2)}) collective-permute-start(bf16[16,2176]{1,0:T(8,128)(2,1)S(1)} %join.1.refs_2_), channel_id=1, source_target_pairs={{0,4},{4,0},{8,12},{12,8},{1,5},{5,1},{9,13},{13,9},{2,6},{6,2},{1... | collective-permute-start | bytes 208904 | tf_op jit(solution)/shard_map/ppermute | solution.py:33
  24.4 5.4 %collective-permute-start.15 = (bf16[16,2176]{1,0:T(8,128)(2,1)S(1)}, bf16[16,2176]{1,0:T(8,128)(2,1)S(1)}, u32[]{:S(2)}, u32[]{:S(2)}) collective-permute-start(bf16[16,2176]{1,0:T(8,128)(2,1)S(1)} %collective-permute-done.7.refs_4_), channel_id=1, source_target_pairs={{0,1},{1,0},{2,3},{3,2},{4,5},{5,4},{6,7},{7,6},{8,9},{9,8},{10,11... | collective-permute-start | bytes 208904 | tf_op jit(solution)/shard_map/ppermute | solution.py:33
  25.0 4.7 %collective-permute-start.12 = (bf16[16,2176]{1,0:T(8,128)(2,1)S(1)}, bf16[16,2176]{1,0:T(8,128)(2,1)S(1)}, u32[]{:S(2)}, u32[]{:S(2)}) collective-permute-start(bf16[16,2176]{1,0:T(8,128)(2,1)S(1)} %collective-permute-done.4.refs_1_), channel_id=1, source_target_pairs={{0,1},{1,0},{2,3},{3,2},{4,5},{5,4},{6,7},{7,6},{8,9},{9,8},{10,11... | collective-permute-start | bytes 208904 | tf_op jit(solution)/shard_map/ppermute | solution.py:33
  25.0 5.2 %collective-permute-start.8 = (bf16[16,2176]{1,0:T(8,128)(2,1)S(1)}, bf16[16,2176]{1,0:T(8,128)(2,1)S(1)}, u32[]{:S(2)}, u32[]{:S(2)}) collective-permute-start(bf16[16,2176]{1,0:T(8,128)(2,1)S(1)} %collective-permute-done.4.refs_1_), channel_id=1, source_target_pairs={{0,2},{2,0},{1,3},{3,1},{4,6},{6,4},{5,7},{7,5},{8,10},{10,8},{9,1... | collective-permute-start | bytes 208904 | tf_op jit(solution)/shard_map/ppermute | solution.py:33
  26.1 5.4 %collective-permute-start.9 = (bf16[16,2176]{1,0:T(8,128)(2,1)S(1)}, bf16[16,2176]{1,0:T(8,128)(2,1)S(1)}, u32[]{:S(2)}, u32[]{:S(2)}) collective-permute-start(bf16[16,2176]{1,0:T(8,128)(2,1)S(1)} %join.1.refs_2_), channel_id=1, source_target_pairs={{0,2},{2,0},{1,3},{3,1},{4,6},{6,4},{5,7},{7,5},{8,10},{10,8},{9,1... | collective-permute-start | bytes 208904 | tf_op jit(solution)/shard_map/ppermute | solution.py:33
  28.6 4.3 %collective-permute-start.10 = (bf16[16,2176]{1,0:T(8,128)(2,1)S(1)}, bf16[16,2176]{1,0:T(8,128)(2,1)S(1)}, u32[]{:S(2)}, u32[]{:S(2)}) collective-permute-start(bf16[16,2176]{1,0:T(8,128)(2,1)S(1)} %collective-permute-done.6.refs_3_), channel_id=1, source_target_pairs={{0,2},{2,0},{1,3},{3,1},{4,6},{6,4},{5,7},{7,5},{8,10},{10,8},{9,1... | collective-permute-start | bytes 208904 | tf_op jit(solution)/shard_map/ppermute | solution.py:33
  29.7 3.2 %collective-permute-start.13 = (bf16[16,2176]{1,0:T(8,128)(2,1)S(1)}, bf16[16,2176]{1,0:T(8,128)(2,1)S(1)}, u32[]{:S(2)}, u32[]{:S(2)}) collective-permute-start(bf16[16,2176]{1,0:T(8,128)(2,1)S(1)} %join.1.refs_2_), channel_id=1, source_target_pairs={{0,1},{1,0},{2,3},{3,2},{4,5},{5,4},{6,7},{7,6},{8,9},{9,8},{10,11... | collective-permute-start | bytes 208904 | tf_op jit(solution)/shard_map/ppermute | solution.py:33
  29.7 3.2 %collective-permute-start.14 = (bf16[16,2176]{1,0:T(8,128)(2,1)S(1)}, bf16[16,2176]{1,0:T(8,128)(2,1)S(1)}, u32[]{:S(2)}, u32[]{:S(2)}) collective-permute-start(bf16[16,2176]{1,0:T(8,128)(2,1)S(1)} %collective-permute-done.6.refs_3_), channel_id=1, source_target_pairs={{0,1},{1,0},{2,3},{3,2},{4,5},{5,4},{6,7},{7,6},{8,9},{9,8},{10,11... | collective-permute-start | bytes 208904 | tf_op jit(solution)/shard_map/ppermute | solution.py:33
  30.2 2.7 %collective-permute-start.16 = (bf16[16,2176]{1,0:T(8,128)(2,1)S(1)}, bf16[16,2176]{1,0:T(8,128)(2,1)S(1)}, u32[]{:S(2)}, u32[]{:S(2)}) collective-permute-start(bf16[16,2176]{1,0:T(8,128)(2,1)S(1)} %collective-permute-done.8.refs_5_), channel_id=1, source_target_pairs={{0,1},{1,0},{2,3},{3,2},{4,5},{5,4},{6,7},{7,6},{8,9},{9,8},{10,11... | collective-permute-start | bytes 208904 | tf_op jit(solution)/shard_map/ppermute | solution.py:33
  31.5 1.4 %collective-permute-start.17 = (bf16[16,2176]{1,0:T(8,128)(2,1)S(1)}, bf16[16,2176]{1,0:T(8,128)(2,1)S(1)}, u32[]{:S(2)}, u32[]{:S(2)}) collective-permute-start(bf16[16,2176]{1,0:T(8,128)(2,1)S(1)} %collective-permute-done.9.refs_6_), channel_id=1, source_target_pairs={{0,1},{1,0},{2,3},{3,2},{4,5},{5,4},{6,7},{7,6},{8,9},{9,8},{10,11... | collective-permute-start | bytes 208904 | tf_op jit(solution)/shard_map/ppermute | solution.py:33
  32.9 1.3 %collective-permute-start.18 = (bf16[16,2176]{1,0:T(8,128)(2,1)S(1)}, bf16[16,2176]{1,0:T(8,128)(2,1)S(1)}, u32[]{:S(2)}, u32[]{:S(2)}) collective-permute-start(bf16[16,2176]{1,0:T(8,128)(2,1)S(1)} %collective-permute-done.10.refs_7_), channel_id=1, source_target_pairs={{0,1},{1,0},{2,3},{3,2},{4,5},{5,4},{6,7},{7,6},{8,9},{9,8},{10,11... | collective-permute-start | bytes 208904 | tf_op jit(solution)/shard_map/ppermute | solution.py:33
  47.2 2.0 %collective-permute-start.19 = (bf16[128,2048]{1,0:T(8,128)(2,1)S(1)}, bf16[128,2048]{1,0:T(8,128)(2,1)S(1)}, u32[]{:S(2)}, u32[]{:S(2)}) collective-permute-start(bf16[128,2048]{1,0:T(8,128)(2,1)S(1)} %get-tuple-element.54), channel_id=1, source_target_pairs={{0,1},{1,0},{2,3},{3,2},{4,5},{5,4},{6,7},{7,6},{8,9},{9,8},{10,11... | collective-permute-start | bytes 1572872 | tf_op jit(solution)/shard_map/ppermute | solution.py:33
  49.2 5.0 %collective-permute-start.20 = (bf16[16,2048]{1,0:T(8,128)(2,1)S(1)}, bf16[16,2048]{1,0:T(8,128)(2,1)S(1)}, u32[]{:S(2)}, u32[]{:S(2)}) collective-permute-start(bf16[16,2048]{1,0:T(8,128)(2,1)S(1)} %get-tuple-element.56), channel_id=1, source_target_pairs={{0,2},{2,0},{1,3},{3,1},{4,6},{6,4},{5,7},{7,5},{8,10},{10,8},{9,1... | collective-permute-start | bytes 196616 | tf_op jit(solution)/shard_map/ppermute | solution.py:33
  50.4 6.1 %collective-permute-start.22 = (bf16[16,2048]{1,0:T(8,128)(2,1)S(1)}, bf16[16,2048]{1,0:T(8,128)(2,1)S(1)}, u32[]{:S(2)}, u32[]{:S(2)}) collective-permute-start(bf16[16,2048]{1,0:T(8,128)(2,1)S(1)} %get-tuple-element.58), channel_id=1, source_target_pairs={{0,2},{2,0},{1,3},{3,1},{4,6},{6,4},{5,7},{7,5},{8,10},{10,8},{9,1... | collective-permute-start | bytes 196616 | tf_op jit(solution)/shard_map/ppermute | solution.py:33
  51.3 6.3 %collective-permute-start.24 = (bf16[16,2048]{1,0:T(8,128)(2,1)S(1)}, bf16[16,2048]{1,0:T(8,128)(2,1)S(1)}, u32[]{:S(2)}, u32[]{:S(2)}) collective-permute-start(bf16[16,2048]{1,0:T(8,128)(2,1)S(1)} %get-tuple-element.60), channel_id=1, source_target_pairs={{0,2},{2,0},{1,3},{3,1},{4,6},{6,4},{5,7},{7,5},{8,10},{10,8},{9,1... | collective-permute-start | bytes 196616 | tf_op jit(solution)/shard_map/ppermute | solution.py:33
  52.5 6.4 %collective-permute-start.26 = (bf16[16,2048]{1,0:T(8,128)(2,1)S(1)}, bf16[16,2048]{1,0:T(8,128)(2,1)S(1)}, u32[]{:S(2)}, u32[]{:S(2)}) collective-permute-start(bf16[16,2048]{1,0:T(8,128)(2,1)S(1)} %get-tuple-element.62), channel_id=1, source_target_pairs={{0,2},{2,0},{1,3},{3,1},{4,6},{6,4},{5,7},{7,5},{8,10},{10,8},{9,1... | collective-permute-start | bytes 196616 | tf_op jit(solution)/shard_map/ppermute | solution.py:33
  54.3 6.7 %collective-permute-start.21 = (bf16[16,2048]{1,0:T(8,128)(2,1)S(1)}, bf16[16,2048]{1,0:T(8,128)(2,1)S(1)}, u32[]{:S(2)}, u32[]{:S(2)}) collective-permute-start(bf16[16,2048]{1,0:T(8,128)(2,1)S(1)} %sum_x3.1), channel_id=1, source_target_pairs={{0,12},{4,8},{8,4},{12,0},{1,13},{5,9},{9,5},{13,1},{2,14},{6,10},... | collective-permute-start | bytes 196616 | tf_op jit(solution)/shard_map/ppermute | solution.py:33
  56.6 5.9 %collective-permute-start.23 = (bf16[16,2048]{1,0:T(8,128)(2,1)S(1)}, bf16[16,2048]{1,0:T(8,128)(2,1)S(1)}, u32[]{:S(2)}, u32[]{:S(2)}) collective-permute-start(bf16[16,2048]{1,0:T(8,128)(2,1)S(1)} %sum_x2.1), channel_id=1, source_target_pairs={{0,8},{4,12},{8,0},{12,4},{1,9},{5,13},{9,1},{13,5},{2,10},{6,14},... | collective-permute-start | bytes 196616 | tf_op jit(solution)/shard_map/ppermute | solution.py:33
  57.6 5.0 %collective-permute-start.25 = (bf16[16,2048]{1,0:T(8,128)(2,1)S(1)}, bf16[16,2048]{1,0:T(8,128)(2,1)S(1)}, u32[]{:S(2)}, u32[]{:S(2)}) collective-permute-start(bf16[16,2048]{1,0:T(8,128)(2,1)S(1)} %sum_x1.1), channel_id=1, source_target_pairs={{0,4},{4,0},{8,12},{12,8},{1,5},{5,1},{9,13},{13,9},{2,6},{6,2},{1... | collective-permute-start | bytes 196616 | tf_op jit(solution)/shard_map/ppermute | solution.py:33

commit v17 on v16

--- a/solution.py
+++ b/solution.py
@@ -303,7 +303,7 @@
             groups.append((("gate", x), pieces(gate_hbm, gate_ref.at[x - 1], x, True)))
             groups.append((("up", x), pieces(up_hbm, up_ref.at[x - 1], x, True)))
         groups.append((("down", x), pieces(down_hbm, down_ref, x, False)))
-    stream = Stream(groups, sem, 4)
+    stream = Stream(groups, sem, 6)
     stream.limit = stream.last["up", 1] if experts > 1 else stream.limit
     stream.fill()
     count = 0

time: 63.6 us -> 63.6 us (level)
  no operation moved by 1% of the time
where the time goes in v17:
time: 63.6 us; the launch traced here: 63.4 us
  Pallas kernels  24.5 us (39%)
  starting transfers between devices  24.3 us (38%)
  waiting for transfers between devices  13.6 us (21%)
  local copies, waits for them, and re-layouts  0.78 us (1%)
    pallas_call x14, Pallas kernels, call(): pl.pallas_call(kernel, out_shape=out_shape, in_specs=[s for s, _ in args]...  24.5 us
    ppermute x25, starting transfers between devices, xor_swap(): return lax.ppermute(x, axis, [(i, i ^ k) for i in range(n)])  18.6 us
    ppermute x25, waiting for transfers between devices, xor_swap(): return lax.ppermute(x, axis, [(i, i ^ k) for i in range(n)])  13.6 us
    ppermute x2, starting transfers between devices, per_device(): lax.ppermute(kv, 'sec', [(i, (i + k) % sec_count) for i in range(sec_coun...  5.67 us
  transfers between devices with their start and end apart: 27, of which 12 were waited for; matrix products, arithmetic and copies ran while one was open for 0% of the time, Pallas kernels for 14%

profile of v17, /device:TPU:0, one launch (start us, length us, event | category | flops | bytes accessed | tf_op | source)
XLA Modules:
  0.0 63.4 jit_solution(10697445708439829408)
XLA Ops:
  0.0 0.8 %constant_dynamic-slice_fusion = (bf16[64,256]{1,0:T(8,128)(2,1)S(1)}, bf16[64,256]{1,0:T(8,128)(2,1)S(1)}) fusion(bf16[64,512]{1,0:T(8,128)(2,1)} %param.14, s32[]{:T(128)S(6)} %select_n.10, bf16[64,512]{1,0:T(8,128)(2,1)} %param.13), kind=kLoop, calls=%fused_computation.1 | loop fusion | bytes 131076 | tf_op jit(solution)/shard_map/dynamic_slice | solution.py:423
  0.8 3.1 %collective-permute-start.1 = (bf16[64,512]{1,0:T(8,128)(2,1)S(1)}, bf16[64,512]{1,0:T(8,128)(2,1)S(1)}, u32[]{:S(2)}, u32[]{:S(2)}) collective-permute-start(bf16[64,512]{1,0:T(8,128)(2,1)S(1)} %pad_maximum_fusion.refs_2_), channel_id=1, source_target_pairs={{0,4},{4,8},{8,12},{12,0},{1,5},{5,9},{9,13},{13,1},{2,6},{6,10},{... | collective-permute-start | bytes 196616 | tf_op jit(solution)/shard_map/ppermute | solution.py:427
  3.9 2.6 %collective-permute-start = (bf16[64,512]{1,0:T(8,128)(2,1)S(1)}, bf16[64,512]{1,0:T(8,128)(2,1)S(1)}, u32[]{:S(2)}, u32[]{:S(2)}) collective-permute-start(bf16[64,512]{1,0:T(8,128)(2,1)S(1)} %pad_maximum_fusion.refs_2_), channel_id=1, source_target_pairs={{0,8},{4,12},{8,0},{12,4},{1,9},{5,13},{9,1},{13,5},{2,10},{6,14},... | collective-permute-start | bytes 196616 | tf_op jit(solution)/shard_map/ppermute | solution.py:427
  6.5 4.3 %prepare.1 = (bf16[64,1024]{1,0:T(8,128)(2,1)S(1)}, bf16[1024,2048]{1,0:T(8,128)(2,1)S(1)}, f32[1,2048]{1,0:T(1,128)S(1)}, f32[64,192]{1,0:T(8,128)S(1)}, bf16[6...) custom-call(s32[8]{0:T(128)} %lengths_hbm.1, ...), custom_call_target="tpu_custom_call" | custom-call | bytes 10200000 | tf_op jit(solution)/shard_map/prepare/pallas_call | solution.py:41
  10.8 1.4 %attention.1 = (f32[32,2048]{1,0:T(8,128)S(1)}, bf16[32,2048]{1,0:T(8,128)(2,1)S(1)}) custom-call(bf16[64,1024]{1,0:T(8,128)(2,1)S(1)} %get-tuple-element.37.q_ref, f32[64,192]{1,0:T(8,128)S(1)} %get-tuple-element.38.mask_ref, bf16[64,64]{1,0:T(8,128)(2,1)S(1)} %get-tuple-element.39.order_ref, bf16[64,512]{1,0:T(8,128)(2,1)S(1)} %collective-permute-done.refs_0_, ...), custom_call_target="tpu_custom_call" | custom-call | bytes 8160000 | tf_op jit(solution)/shard_map/attention/pallas_call | solution.py:41
  12.3 1.3 %collective-permute-done.2.refs_1_ = bf16[32,2048]{1,0:T(8,128)(2,1)S(1)} collective-permute-done((bf16[32,2048]{1,0:T(8,128)(2,1)S(1)}, bf16[32,2048]{1,0:T(8,128)(2,1)S(1)}, u32[]{:S(2)}, u32[]{:S(2)}) %collective-permute-start.2) | collective-permute-done | bytes 131104 | tf_op jit(solution)/shard_map/ppermute | solution.py:33
  13.7 1.6 %collective-permute-start.3 = (bf16[16,2048]{1,0:T(8,128)(2,1)S(1)}, bf16[16,2048]{1,0:T(8,128)(2,1)S(1)}, u32[]{:S(2)}, u32[]{:S(2)}) collective-permute-start(bf16[16,2048]{1,0:T(8,128)(2,1)S(1)} %get-tuple-element.44), channel_id=1, source_target_pairs={{0,2},{2,0},{1,3},{3,1},{4,6},{6,4},{5,7},{7,5},{8,10},{10,8},{9,1... | collective-permute-start | bytes 196616 | tf_op jit(solution)/shard_map/ppermute | solution.py:33
  15.3 2.8 %load_up.1 = (bf16[1536,2048]{1,0:T(8,128)(2,1)S(1)}, f32[8,128]{1,0:T(8,128)S(1)}) custom-call(bf16[2048,4096]{1,0:T(8,128)(2,1)} %bitcast.9, f32[16,2048]{1,0:T(8,128)S(1)} %get-tuple-element.43.refs_0_), custom_call_target="tpu_custom_call" | custom-call | bytes 6291456 | tf_op jit(solution)/shard_map/load_up/pallas_call | solution.py:41
  18.2 1.0 %collective-permute-start.5 = (bf16[16,2176]{1,0:T(8,128)(2,1)S(1)}, bf16[16,2176]{1,0:T(8,128)(2,1)S(1)}, u32[]{:S(2)}, u32[]{:S(2)}) collective-permute-start(bf16[16,2176]{1,0:T(8,128)(2,1)S(1)} %get-tuple-element.47.refs_0_), channel_id=1, source_target_pairs={{0,8},{4,12},{8,0},{12,4},{1,9},{5,13},{9,1},{13,5},{2,10},{6,14},... | collective-permute-start | bytes 208904 | tf_op jit(solution)/shard_map/ppermute | solution.py:33
  19.2 1.5 %collective-permute-start.7 = (bf16[16,2176]{1,0:T(8,128)(2,1)S(1)}, bf16[16,2176]{1,0:T(8,128)(2,1)S(1)}, u32[]{:S(2)}, u32[]{:S(2)}) collective-permute-start(bf16[16,2176]{1,0:T(8,128)(2,1)S(1)} %get-tuple-element.47.refs_0_), channel_id=1, source_target_pairs={{0,2},{2,0},{1,3},{3,1},{4,6},{6,4},{5,7},{7,5},{8,10},{10,8},{9,1... | collective-permute-start | bytes 208904 | tf_op jit(solution)/shard_map/ppermute | solution.py:33
  20.6 1.6 %collective-permute-start.4 = (bf16[16,2176]{1,0:T(8,128)(2,1)S(1)}, bf16[16,2176]{1,0:T(8,128)(2,1)S(1)}, u32[]{:S(2)}, u32[]{:S(2)}) collective-permute-start(bf16[16,2176]{1,0:T(8,128)(2,1)S(1)} %get-tuple-element.47.refs_0_), channel_id=1, source_target_pairs={{0,4},{4,0},{8,12},{12,8},{1,5},{5,1},{9,13},{13,9},{2,6},{6,2},{1... | collective-permute-start | bytes 208904 | tf_op jit(solution)/shard_map/ppermute | solution.py:33
  22.3 1.6 %load_gate.1 = (bf16[512,2048]{1,0:T(8,128)(2,1)S(1)}, f32[8,128]{1,0:T(8,128)S(1)}) custom-call(bf16[2048,4096]{1,0:T(8,128)(2,1)} %bitcast.7, bf16[16,2176]{1,0:T(8,128)(2,1)S(1)} %get-tuple-element.47.refs_0_), custom_call_target="tpu_custom_call" | custom-call | bytes 2097151 | tf_op jit(solution)/shard_map/load_gate/pallas_call | solution.py:41
  25.0 1.1 %collective-permute-start.8 = (bf16[16,2176]{1,0:T(8,128)(2,1)S(1)}, bf16[16,2176]{1,0:T(8,128)(2,1)S(1)}, u32[]{:S(2)}, u32[]{:S(2)}) collective-permute-start(bf16[16,2176]{1,0:T(8,128)(2,1)S(1)} %collective-permute-done.4.refs_1_), channel_id=1, source_target_pairs={{0,2},{2,0},{1,3},{3,1},{4,6},{6,4},{5,7},{7,5},{8,10},{10,8},{9,1... | collective-permute-start | bytes 208904 | tf_op jit(solution)/shard_map/ppermute | solution.py:33
  26.1 1.0 %collective-permute-start.9 = (bf16[16,2176]{1,0:T(8,128)(2,1)S(1)}, bf16[16,2176]{1,0:T(8,128)(2,1)S(1)}, u32[]{:S(2)}, u32[]{:S(2)}) collective-permute-start(bf16[16,2176]{1,0:T(8,128)(2,1)S(1)} %join.1.refs_2_), channel_id=1, source_target_pairs={{0,2},{2,0},{1,3},{3,1},{4,6},{6,4},{5,7},{7,5},{8,10},{10,8},{9,1... | collective-permute-start | bytes 208904 | tf_op jit(solution)/shard_map/ppermute | solution.py:33
  27.1 1.5 %collective-permute-done.6.refs_3_ = bf16[16,2176]{1,0:T(8,128)(2,1)S(1)} collective-permute-done((bf16[16,2176]{1,0:T(8,128)(2,1)S(1)}, bf16[16,2176]{1,0:T(8,128)(2,1)S(1)}, u32[]{:S(2)}, u32[]{:S(2)}) %collective-permute-start.6) | collective-permute-done | bytes 69664 | tf_op jit(solution)/shard_map/ppermute | solution.py:33
  28.6 1.1 %collective-permute-start.10 = (bf16[16,2176]{1,0:T(8,128)(2,1)S(1)}, bf16[16,2176]{1,0:T(8,128)(2,1)S(1)}, u32[]{:S(2)}, u32[]{:S(2)}) collective-permute-start(bf16[16,2176]{1,0:T(8,128)(2,1)S(1)} %collective-permute-done.6.refs_3_), channel_id=1, source_target_pairs={{0,2},{2,0},{1,3},{3,1},{4,6},{6,4},{5,7},{7,5},{8,10},{10,8},{9,1... | collective-permute-start | bytes 208904 | tf_op jit(solution)/shard_map/ppermute | solution.py:33
  30.3 1.2 %collective-permute-done.9.refs_6_ = bf16[16,2176]{1,0:T(8,128)(2,1)S(1)} collective-permute-done((bf16[16,2176]{1,0:T(8,128)(2,1)S(1)}, bf16[16,2176]{1,0:T(8,128)(2,1)S(1)}, u32[]{:S(2)}, u32[]{:S(2)}) %collective-permute-start.9) | collective-permute-done | bytes 69664 | tf_op jit(solution)/shard_map/ppermute | solution.py:33
  31.5 1.4 %collective-permute-done.10.refs_7_ = bf16[16,2176]{1,0:T(8,128)(2,1)S(1)} collective-permute-done((bf16[16,2176]{1,0:T(8,128)(2,1)S(1)}, bf16[16,2176]{1,0:T(8,128)(2,1)S(1)}, u32[]{:S(2)}, u32[]{:S(2)}) %collective-permute-start.10) | collective-permute-done | bytes 69664 | tf_op jit(solution)/shard_map/ppermute | solution.py:33
  32.9 1.2 %collective-permute-done.18.refs_15_ = bf16[16,2176]{1,0:T(8,128)(2,1)S(1)} collective-permute-done((bf16[16,2176]{1,0:T(8,128)(2,1)S(1)}, bf16[16,2176]{1,0:T(8,128)(2,1)S(1)}, u32[]{:S(2)}, u32[]{:S(2)}) %collective-permute-start.18) | collective-permute-done | bytes 69664 | tf_op jit(solution)/shard_map/ppermute | solution.py:33
  34.2 13.0 %experts.1 = (bf16[128,2048]{1,0:T(8,128)(2,1)S(1)}, bf16[256,256]{1,0:T(8,128)(2,1)S(1)}, bf16[256,2048]{1,0:T(8,128)(2,1)S(1)}) custom-call(bf16[16,2176]{1,0:T(8,128)(2,1)S(1)} %get-tuple-element.47.refs_0_, bf16[16,2176]{1,0:T(8,128)(2,1)S(1)} %collective-permute-done.4.refs_1_, bf16[16,2176]{1,0:T(8,128)(2,1)S(1)} %join.1.refs_2_, ...), custom_call_target="tpu_custom_call" | custom-call | bytes 40800000 | tf_op jit(solution)/shard_map/experts/pallas_call | solution.py:41
  47.7 1.4 %collective-permute-done.19.refs_1_ = bf16[128,2048]{1,0:T(8,128)(2,1)S(1)} collective-permute-done((bf16[128,2048]{1,0:T(8,128)(2,1)S(1)}, bf16[128,2048]{1,0:T(8,128)(2,1)S(1)}, u32[]{:S(2)}, u32[]{:S(2)}) %collective-permute-start.19) | collective-permute-done | bytes 524320 | tf_op jit(solution)/shard_map/ppermute | solution.py:33
  49.3 1.2 %collective-permute-start.20 = (bf16[16,2048]{1,0:T(8,128)(2,1)S(1)}, bf16[16,2048]{1,0:T(8,128)(2,1)S(1)}, u32[]{:S(2)}, u32[]{:S(2)}) collective-permute-start(bf16[16,2048]{1,0:T(8,128)(2,1)S(1)} %get-tuple-element.56), channel_id=1, source_target_pairs={{0,2},{2,0},{1,3},{3,1},{4,6},{6,4},{5,7},{7,5},{8,10},{10,8},{9,1... | collective-permute-start | bytes 196616 | tf_op jit(solution)/shard_map/ppermute | solution.py:33
  50.4 0.9 %collective-permute-start.22 = (bf16[16,2048]{1,0:T(8,128)(2,1)S(1)}, bf16[16,2048]{1,0:T(8,128)(2,1)S(1)}, u32[]{:S(2)}, u32[]{:S(2)}) collective-permute-start(bf16[16,2048]{1,0:T(8,128)(2,1)S(1)} %get-tuple-element.58), channel_id=1, source_target_pairs={{0,2},{2,0},{1,3},{3,1},{4,6},{6,4},{5,7},{7,5},{8,10},{10,8},{9,1... | collective-permute-start | bytes 196616 | tf_op jit(solution)/shard_map/ppermute | solution.py:33
  51.4 1.1 %collective-permute-start.24 = (bf16[16,2048]{1,0:T(8,128)(2,1)S(1)}, bf16[16,2048]{1,0:T(8,128)(2,1)S(1)}, u32[]{:S(2)}, u32[]{:S(2)}) collective-permute-start(bf16[16,2048]{1,0:T(8,128)(2,1)S(1)} %get-tuple-element.60), channel_id=1, source_target_pairs={{0,2},{2,0},{1,3},{3,1},{4,6},{6,4},{5,7},{7,5},{8,10},{10,8},{9,1... | collective-permute-start | bytes 196616 | tf_op jit(solution)/shard_map/ppermute | solution.py:33
  52.5 0.9 %collective-permute-start.26 = (bf16[16,2048]{1,0:T(8,128)(2,1)S(1)}, bf16[16,2048]{1,0:T(8,128)(2,1)S(1)}, u32[]{:S(2)}, u32[]{:S(2)}) collective-permute-start(bf16[16,2048]{1,0:T(8,128)(2,1)S(1)} %get-tuple-element.62), channel_id=1, source_target_pairs={{0,2},{2,0},{1,3},{3,1},{4,6},{6,4},{5,7},{7,5},{8,10},{10,8},{9,1... | collective-permute-start | bytes 196616 | tf_op jit(solution)/shard_map/ppermute | solution.py:33
  53.4 0.9 %collective-permute-done.20.refs_1_ = bf16[16,2048]{1,0:T(8,128)(2,1)S(1)} collective-permute-done((bf16[16,2048]{1,0:T(8,128)(2,1)S(1)}, bf16[16,2048]{1,0:T(8,128)(2,1)S(1)}, u32[]{:S(2)}, u32[]{:S(2)}) %collective-permute-start.20) | collective-permute-done | bytes 65568 | tf_op jit(solution)/shard_map/ppermute | solution.py:33
  54.3 2.3 %collective-permute-start.21 = (bf16[16,2048]{1,0:T(8,128)(2,1)S(1)}, bf16[16,2048]{1,0:T(8,128)(2,1)S(1)}, u32[]{:S(2)}, u32[]{:S(2)}) collective-permute-start(bf16[16,2048]{1,0:T(8,128)(2,1)S(1)} %sum_x3.1), channel_id=1, source_target_pairs={{0,12},{4,8},{8,4},{12,0},{1,13},{5,9},{9,5},{13,1},{2,14},{6,10},... | collective-permute-start | bytes 196616 | tf_op jit(solution)/shard_map/ppermute | solution.py:33
  56.6 1.0 %collective-permute-start.23 = (bf16[16,2048]{1,0:T(8,128)(2,1)S(1)}, bf16[16,2048]{1,0:T(8,128)(2,1)S(1)}, u32[]{:S(2)}, u32[]{:S(2)}) collective-permute-start(bf16[16,2048]{1,0:T(8,128)(2,1)S(1)} %sum_x2.1), channel_id=1, source_target_pairs={{0,8},{4,12},{8,0},{12,4},{1,9},{5,13},{9,1},{13,5},{2,10},{6,14},... | collective-permute-start | bytes 196616 | tf_op jit(solution)/shard_map/ppermute | solution.py:33
  57.6 1.3 %collective-permute-start.25 = (bf16[16,2048]{1,0:T(8,128)(2,1)S(1)}, bf16[16,2048]{1,0:T(8,128)(2,1)S(1)}, u32[]{:S(2)}, u32[]{:S(2)}) collective-permute-start(bf16[16,2048]{1,0:T(8,128)(2,1)S(1)} %sum_x1.1), channel_id=1, source_target_pairs={{0,4},{4,0},{8,12},{12,8},{1,5},{5,1},{9,13},{13,9},{2,6},{6,2},{1... | collective-permute-start | bytes 196616 | tf_op jit(solution)/shard_map/ppermute | solution.py:33
  58.9 2.1 %collective-permute-done.21.refs_1_ = bf16[16,2048]{1,0:T(8,128)(2,1)S(1)} collective-permute-done((bf16[16,2048]{1,0:T(8,128)(2,1)S(1)}, bf16[16,2048]{1,0:T(8,128)(2,1)S(1)}, u32[]{:S(2)}, u32[]{:S(2)}) %collective-permute-start.21) | collective-permute-done | bytes 65568 | tf_op jit(solution)/shard_map/ppermute | solution.py:33
  61.0 1.5 %collective-permute-done.23.refs_2_ = bf16[16,2048]{1,0:T(8,128)(2,1)S(1)} collective-permute-done((bf16[16,2048]{1,0:T(8,128)(2,1)S(1)}, bf16[16,2048]{1,0:T(8,128)(2,1)S(1)}, u32[]{:S(2)}, u32[]{:S(2)}) %collective-permute-start.23) | collective-permute-done | bytes 65568 | tf_op jit(solution)/shard_map/ppermute | solution.py:33
  62.7 0.7 %total.1 = bf16[16,2048]{1,0:T(8,128)(2,1)} custom-call(f32[16,2048]{1,0:T(8,128)S(1)} %get-tuple-element.46.refs_0_, bf16[16,2048]{1,0:T(8,128)(2,1)S(1)} %collective-permute-done.21.refs_1_, bf16[16,2048]{1,0:T(8,128)(2,1)S(1)} %collective-permute-done.23.refs_2_, bf16[16,2048]{1,0:T(8,128)(2,1)S(1)} %collective-permute-done.25.refs_3_, ...), custom_call_target="tpu_custom_call" | custom-call | bytes 680000 | tf_op jit(solution)/shard_map/total/pallas_call | solution.py:41
  (38 shorter events, 2.8 us)
Async XLA Ops:
  0.8 10.0 %collective-permute-start.1 = (bf16[64,512]{1,0:T(8,128)(2,1)S(1)}, bf16[64,512]{1,0:T(8,128)(2,1)S(1)}, u32[]{:S(2)}, u32[]{:S(2)}) collective-permute-start(bf16[64,512]{1,0:T(8,128)(2,1)S(1)} %pad_maximum_fusion.refs_2_), channel_id=1, source_target_pairs={{0,4},{4,8},{8,12},{12,0},{1,5},{5,9},{9,13},{13,1},{2,6},{6,10},{... | collective-permute-start | bytes 196616 | tf_op jit(solution)/shard_map/ppermute | solution.py:427
  3.9 6.9 %collective-permute-start = (bf16[64,512]{1,0:T(8,128)(2,1)S(1)}, bf16[64,512]{1,0:T(8,128)(2,1)S(1)}, u32[]{:S(2)}, u32[]{:S(2)}) collective-permute-start(bf16[64,512]{1,0:T(8,128)(2,1)S(1)} %pad_maximum_fusion.refs_2_), channel_id=1, source_target_pairs={{0,8},{4,12},{8,0},{12,4},{1,9},{5,13},{9,1},{13,5},{2,10},{6,14},... | collective-permute-start | bytes 196616 | tf_op jit(solution)/shard_map/ppermute | solution.py:427
  12.3 1.4 %collective-permute-start.2 = (bf16[32,2048]{1,0:T(8,128)(2,1)S(1)}, bf16[32,2048]{1,0:T(8,128)(2,1)S(1)}, u32[]{:S(2)}, u32[]{:S(2)}) collective-permute-start(bf16[32,2048]{1,0:T(8,128)(2,1)S(1)} %get-tuple-element.42), channel_id=1, source_target_pairs={{0,1},{1,0},{2,3},{3,2},{4,5},{5,4},{6,7},{7,6},{8,9},{9,8},{10,11... | collective-permute-start | bytes 393224 | tf_op jit(solution)/shard_map/ppermute | solution.py:33
  13.7 4.4 %collective-permute-start.3 = (bf16[16,2048]{1,0:T(8,128)(2,1)S(1)}, bf16[16,2048]{1,0:T(8,128)(2,1)S(1)}, u32[]{:S(2)}, u32[]{:S(2)}) collective-permute-start(bf16[16,2048]{1,0:T(8,128)(2,1)S(1)} %get-tuple-element.44), channel_id=1, source_target_pairs={{0,2},{2,0},{1,3},{3,1},{4,6},{6,4},{5,7},{7,5},{8,10},{10,8},{9,1... | collective-permute-start | bytes 196616 | tf_op jit(solution)/shard_map/ppermute | solution.py:33
  18.2 6.1 %collective-permute-start.5 = (bf16[16,2176]{1,0:T(8,128)(2,1)S(1)}, bf16[16,2176]{1,0:T(8,128)(2,1)S(1)}, u32[]{:S(2)}, u32[]{:S(2)}) collective-permute-start(bf16[16,2176]{1,0:T(8,128)(2,1)S(1)} %get-tuple-element.47.refs_0_), channel_id=1, source_target_pairs={{0,8},{4,12},{8,0},{12,4},{1,9},{5,13},{9,1},{13,5},{2,10},{6,14},... | collective-permute-start | bytes 208904 | tf_op jit(solution)/shard_map/ppermute | solution.py:33
  19.2 5.2 %collective-permute-start.7 = (bf16[16,2176]{1,0:T(8,128)(2,1)S(1)}, bf16[16,2176]{1,0:T(8,128)(2,1)S(1)}, u32[]{:S(2)}, u32[]{:S(2)}) collective-permute-start(bf16[16,2176]{1,0:T(8,128)(2,1)S(1)} %get-tuple-element.47.refs_0_), channel_id=1, source_target_pairs={{0,2},{2,0},{1,3},{3,1},{4,6},{6,4},{5,7},{7,5},{8,10},{10,8},{9,1... | collective-permute-start | bytes 208904 | tf_op jit(solution)/shard_map/ppermute | solution.py:33
  20.6 4.4 %collective-permute-start.4 = (bf16[16,2176]{1,0:T(8,128)(2,1)S(1)}, bf16[16,2176]{1,0:T(8,128)(2,1)S(1)}, u32[]{:S(2)}, u32[]{:S(2)}) collective-permute-start(bf16[16,2176]{1,0:T(8,128)(2,1)S(1)} %get-tuple-element.47.refs_0_), channel_id=1, source_target_pairs={{0,4},{4,0},{8,12},{12,8},{1,5},{5,1},{9,13},{13,9},{2,6},{6,2},{1... | collective-permute-start | bytes 208904 | tf_op jit(solution)/shard_map/ppermute | solution.py:33
  22.3 3.8 %collective-permute-start.11 = (bf16[16,2176]{1,0:T(8,128)(2,1)S(1)}, bf16[16,2176]{1,0:T(8,128)(2,1)S(1)}, u32[]{:S(2)}, u32[]{:S(2)}) collective-permute-start(bf16[16,2176]{1,0:T(8,128)(2,1)S(1)} %get-tuple-element.47.refs_0_), channel_id=1, source_target_pairs={{0,1},{1,0},{2,3},{3,2},{4,5},{5,4},{6,7},{7,6},{8,9},{9,8},{10,11... | collective-permute-start | bytes 208904 | tf_op jit(solution)/shard_map/ppermute | solution.py:33
  24.3 4.3 %collective-permute-start.6 = (bf16[16,2176]{1,0:T(8,128)(2,1)S(1)}, bf16[16,2176]{1,0:T(8,128)(2,1)S(1)}, u32[]{:S(2)}, u32[]{:S(2)}) collective-permute-start(bf16[16,2176]{1,0:T(8,128)(2,1)S(1)} %join.1.refs_2_), channel_id=1, source_target_pairs={{0,4},{4,0},{8,12},{12,8},{1,5},{5,1},{9,13},{13,9},{2,6},{6,2},{1... | collective-permute-start | bytes 208904 | tf_op jit(solution)/shard_map/ppermute | solution.py:33
  24.4 5.4 %collective-permute-start.15 = (bf16[16,2176]{1,0:T(8,128)(2,1)S(1)}, bf16[16,2176]{1,0:T(8,128)(2,1)S(1)}, u32[]{:S(2)}, u32[]{:S(2)}) collective-permute-start(bf16[16,2176]{1,0:T(8,128)(2,1)S(1)} %collective-permute-done.7.refs_4_), channel_id=1, source_target_pairs={{0,1},{1,0},{2,3},{3,2},{4,5},{5,4},{6,7},{7,6},{8,9},{9,8},{10,11... | collective-permute-start | bytes 208904 | tf_op jit(solution)/shard_map/ppermute | solution.py:33
  25.0 4.7 %collective-permute-start.12 = (bf16[16,2176]{1,0:T(8,128)(2,1)S(1)}, bf16[16,2176]{1,0:T(8,128)(2,1)S(1)}, u32[]{:S(2)}, u32[]{:S(2)}) collective-permute-start(bf16[16,2176]{1,0:T(8,128)(2,1)S(1)} %collective-permute-done.4.refs_1_), channel_id=1, source_target_pairs={{0,1},{1,0},{2,3},{3,2},{4,5},{5,4},{6,7},{7,6},{8,9},{9,8},{10,11... | collective-permute-start | bytes 208904 | tf_op jit(solution)/shard_map/ppermute | solution.py:33
  25.0 5.2 %collective-permute-start.8 = (bf16[16,2176]{1,0:T(8,128)(2,1)S(1)}, bf16[16,2176]{1,0:T(8,128)(2,1)S(1)}, u32[]{:S(2)}, u32[]{:S(2)}) collective-permute-start(bf16[16,2176]{1,0:T(8,128)(2,1)S(1)} %collective-permute-done.4.refs_1_), channel_id=1, source_target_pairs={{0,2},{2,0},{1,3},{3,1},{4,6},{6,4},{5,7},{7,5},{8,10},{10,8},{9,1... | collective-permute-start | bytes 208904 | tf_op jit(solution)/shard_map/ppermute | solution.py:33
  26.1 5.4 %collective-permute-start.9 = (bf16[16,2176]{1,0:T(8,128)(2,1)S(1)}, bf16[16,2176]{1,0:T(8,128)(2,1)S(1)}, u32[]{:S(2)}, u32[]{:S(2)}) collective-permute-start(bf16[16,2176]{1,0:T(8,128)(2,1)S(1)} %join.1.refs_2_), channel_id=1, source_target_pairs={{0,2},{2,0},{1,3},{3,1},{4,6},{6,4},{5,7},{7,5},{8,10},{10,8},{9,1... | collective-permute-start | bytes 208904 | tf_op jit(solution)/shard_map/ppermute | solution.py:33
  28.6 4.3 %collective-permute-start.10 = (bf16[16,2176]{1,0:T(8,128)(2,1)S(1)}, bf16[16,2176]{1,0:T(8,128)(2,1)S(1)}, u32[]{:S(2)}, u32[]{:S(2)}) collective-permute-start(bf16[16,2176]{1,0:T(8,128)(2,1)S(1)} %collective-permute-done.6.refs_3_), channel_id=1, source_target_pairs={{0,2},{2,0},{1,3},{3,1},{4,6},{6,4},{5,7},{7,5},{8,10},{10,8},{9,1... | collective-permute-start | bytes 208904 | tf_op jit(solution)/shard_map/ppermute | solution.py:33
  29.7 3.2 %collective-permute-start.13 = (bf16[16,2176]{1,0:T(8,128)(2,1)S(1)}, bf16[16,2176]{1,0:T(8,128)(2,1)S(1)}, u32[]{:S(2)}, u32[]{:S(2)}) collective-permute-start(bf16[16,2176]{1,0:T(8,128)(2,1)S(1)} %join.1.refs_2_), channel_id=1, source_target_pairs={{0,1},{1,0},{2,3},{3,2},{4,5},{5,4},{6,7},{7,6},{8,9},{9,8},{10,11... | collective-permute-start | bytes 208904 | tf_op jit(solution)/shard_map/ppermute | solution.py:33
  29.7 3.2 %collective-permute-start.14 = (bf16[16,2176]{1,0:T(8,128)(2,1)S(1)}, bf16[16,2176]{1,0:T(8,128)(2,1)S(1)}, u32[]{:S(2)}, u32[]{:S(2)}) collective-permute-start(bf16[16,2176]{1,0:T(8,128)(2,1)S(1)} %collective-permute-done.6.refs_3_), channel_id=1, source_target_pairs={{0,1},{1,0},{2,3},{3,2},{4,5},{5,4},{6,7},{7,6},{8,9},{9,8},{10,11... | collective-permute-start | bytes 208904 | tf_op jit(solution)/shard_map/ppermute | solution.py:33
  30.2 2.7 %collective-permute-start.16 = (bf16[16,2176]{1,0:T(8,128)(2,1)S(1)}, bf16[16,2176]{1,0:T(8,128)(2,1)S(1)}, u32[]{:S(2)}, u32[]{:S(2)}) collective-permute-start(bf16[16,2176]{1,0:T(8,128)(2,1)S(1)} %collective-permute-done.8.refs_5_), channel_id=1, source_target_pairs={{0,1},{1,0},{2,3},{3,2},{4,5},{5,4},{6,7},{7,6},{8,9},{9,8},{10,11... | collective-permute-start | bytes 208904 | tf_op jit(solution)/shard_map/ppermute | solution.py:33
  31.5 1.4 %collective-permute-start.17 = (bf16[16,2176]{1,0:T(8,128)(2,1)S(1)}, bf16[16,2176]{1,0:T(8,128)(2,1)S(1)}, u32[]{:S(2)}, u32[]{:S(2)}) collective-permute-start(bf16[16,2176]{1,0:T(8,128)(2,1)S(1)} %collective-permute-done.9.refs_6_), channel_id=1, source_target_pairs={{0,1},{1,0},{2,3},{3,2},{4,5},{5,4},{6,7},{7,6},{8,9},{9,8},{10,11... | collective-permute-start | bytes 208904 | tf_op jit(solution)/shard_map/ppermute | solution.py:33
  32.9 1.3 %collective-permute-start.18 = (bf16[16,2176]{1,0:T(8,128)(2,1)S(1)}, bf16[16,2176]{1,0:T(8,128)(2,1)S(1)}, u32[]{:S(2)}, u32[]{:S(2)}) collective-permute-start(bf16[16,2176]{1,0:T(8,128)(2,1)S(1)} %collective-permute-done.10.refs_7_), channel_id=1, source_target_pairs={{0,1},{1,0},{2,3},{3,2},{4,5},{5,4},{6,7},{7,6},{8,9},{9,8},{10,11... | collective-permute-start | bytes 208904 | tf_op jit(solution)/shard_map/ppermute | solution.py:33
  47.2 2.0 %collective-permute-start.19 = (bf16[128,2048]{1,0:T(8,128)(2,1)S(1)}, bf16[128,2048]{1,0:T(8,128)(2,1)S(1)}, u32[]{:S(2)}, u32[]{:S(2)}) collective-permute-start(bf16[128,2048]{1,0:T(8,128)(2,1)S(1)} %get-tuple-element.54), channel_id=1, source_target_pairs={{0,1},{1,0},{2,3},{3,2},{4,5},{5,4},{6,7},{7,6},{8,9},{9,8},{10,11... | collective-permute-start | bytes 1572872 | tf_op jit(solution)/shard_map/ppermute | solution.py:33
  49.3 5.0 %collective-permute-start.20 = (bf16[16,2048]{1,0:T(8,128)(2,1)S(1)}, bf16[16,2048]{1,0:T(8,128)(2,1)S(1)}, u32[]{:S(2)}, u32[]{:S(2)}) collective-permute-start(bf16[16,2048]{1,0:T(8,128)(2,1)S(1)} %get-tuple-element.56), channel_id=1, source_target_pairs={{0,2},{2,0},{1,3},{3,1},{4,6},{6,4},{5,7},{7,5},{8,10},{10,8},{9,1... | collective-permute-start | bytes 196616 | tf_op jit(solution)/shard_map/ppermute | solution.py:33
  50.4 6.1 %collective-permute-start.22 = (bf16[16,2048]{1,0:T(8,128)(2,1)S(1)}, bf16[16,2048]{1,0:T(8,128)(2,1)S(1)}, u32[]{:S(2)}, u32[]{:S(2)}) collective-permute-start(bf16[16,2048]{1,0:T(8,128)(2,1)S(1)} %get-tuple-element.58), channel_id=1, source_target_pairs={{0,2},{2,0},{1,3},{3,1},{4,6},{6,4},{5,7},{7,5},{8,10},{10,8},{9,1... | collective-permute-start | bytes 196616 | tf_op jit(solution)/shard_map/ppermute | solution.py:33
  51.4 6.3 %collective-permute-start.24 = (bf16[16,2048]{1,0:T(8,128)(2,1)S(1)}, bf16[16,2048]{1,0:T(8,128)(2,1)S(1)}, u32[]{:S(2)}, u32[]{:S(2)}) collective-permute-start(bf16[16,2048]{1,0:T(8,128)(2,1)S(1)} %get-tuple-element.60), channel_id=1, source_target_pairs={{0,2},{2,0},{1,3},{3,1},{4,6},{6,4},{5,7},{7,5},{8,10},{10,8},{9,1... | collective-permute-start | bytes 196616 | tf_op jit(solution)/shard_map/ppermute | solution.py:33
  52.5 6.4 %collective-permute-start.26 = (bf16[16,2048]{1,0:T(8,128)(2,1)S(1)}, bf16[16,2048]{1,0:T(8,128)(2,1)S(1)}, u32[]{:S(2)}, u32[]{:S(2)}) collective-permute-start(bf16[16,2048]{1,0:T(8,128)(2,1)S(1)} %get-tuple-element.62), channel_id=1, source_target_pairs={{0,2},{2,0},{1,3},{3,1},{4,6},{6,4},{5,7},{7,5},{8,10},{10,8},{9,1... | collective-permute-start | bytes 196616 | tf_op jit(solution)/shard_map/ppermute | solution.py:33
  54.3 6.7 %collective-permute-start.21 = (bf16[16,2048]{1,0:T(8,128)(2,1)S(1)}, bf16[16,2048]{1,0:T(8,128)(2,1)S(1)}, u32[]{:S(2)}, u32[]{:S(2)}) collective-permute-start(bf16[16,2048]{1,0:T(8,128)(2,1)S(1)} %sum_x3.1), channel_id=1, source_target_pairs={{0,12},{4,8},{8,4},{12,0},{1,13},{5,9},{9,5},{13,1},{2,14},{6,10},... | collective-permute-start | bytes 196616 | tf_op jit(solution)/shard_map/ppermute | solution.py:33
  56.6 5.9 %collective-permute-start.23 = (bf16[16,2048]{1,0:T(8,128)(2,1)S(1)}, bf16[16,2048]{1,0:T(8,128)(2,1)S(1)}, u32[]{:S(2)}, u32[]{:S(2)}) collective-permute-start(bf16[16,2048]{1,0:T(8,128)(2,1)S(1)} %sum_x2.1), channel_id=1, source_target_pairs={{0,8},{4,12},{8,0},{12,4},{1,9},{5,13},{9,1},{13,5},{2,10},{6,14},... | collective-permute-start | bytes 196616 | tf_op jit(solution)/shard_map/ppermute | solution.py:33
  57.6 5.0 %collective-permute-start.25 = (bf16[16,2048]{1,0:T(8,128)(2,1)S(1)}, bf16[16,2048]{1,0:T(8,128)(2,1)S(1)}, u32[]{:S(2)}, u32[]{:S(2)}) collective-permute-start(bf16[16,2048]{1,0:T(8,128)(2,1)S(1)} %sum_x1.1), channel_id=1, source_target_pairs={{0,4},{4,0},{8,12},{12,8},{1,5},{5,1},{9,13},{13,9},{2,6},{6,2},{1... | collective-permute-start | bytes 196616 | tf_op jit(solution)/shard_map/ppermute | solution.py:33
